TPU v7x, 512 devices: a whole 4x8x8 slice. The times are simulated.
512 devices in a mesh: cells: 128 (over x, y_hi, z, core), vel: 4 (over y_lo).
Axes of the slice: x: 4, y: 8 (y_hi: 2, y_lo: 4; y = y_hi * 4 + y_lo), z: 8, core: 2. Of those that a mesh axis runs over, the one named last changes fastest.
Arguments:
- populations: float32 [2744, 128, 256], P('vel', 'cells'), may hold values from -6 to 6
- solid_mask: int32 [128, 256], P('cells'), may hold values 0 or 1
- collision: bfloat16 [2744, 2744], P('vel'), may hold values from -1 to 1
Outputs:
- evolved: float32 [2744, 128, 256], P('vel', 'cells')
All inputs are finite; a program needn't handle non-finite values. No bound on the sum of `solid_mask` on one device may be relied on, other than what follows from the above.
Results may differ from a plain program's by a relative error of at most 0.0031.
Values may be sent and summed in bfloat16 or wider, within the bound.
No kernel may reach another device: no remote copies, remote signals or barrier semaphores. Data moves between devices by JAX's collectives and lax.ppermute only.
A program may use at most 128 MiB of HBM per device.

v0:
```python
import jax
import jax.numpy as jnp
from jax import lax
from jax.sharding import PartitionSpec as P

K = 14
STEPS = 2
NZ = 16


def extended(cells, sides, width):
    for axis, dim in sides:
        count = lax.axis_size(axis)
        head = lax.slice_in_dim(cells, 0, width, axis=dim)
        tail = lax.slice_in_dim(cells, cells.shape[dim] - width, cells.shape[dim], axis=dim)
        cells = jnp.concatenate(
            [
                lax.ppermute(tail, axis, [(i, (i + 1) % count) for i in range(count)]),
                cells,
                lax.ppermute(head, axis, [((i + 1) % count, i) for i in range(count)]),
            ],
            axis=dim,
        )
    return cells


def from_partner(array, axis, apart):
    return lax.ppermute(array, axis, [(i, i ^ 1 << apart) for i in range(lax.axis_size(axis))])


def velocity_terms(first_row, row_count):
    velocity_ids = first_row + lax.iota(jnp.int32, row_count)
    components = (velocity_ids // (K * K), velocity_ids // K % K, velocity_ids % K)
    centre = (K - 1) / 2.0
    result = []
    for component in components:
        shifted = component.astype(jnp.float32) - centre
        factor = (0.3 * jnp.abs(shifted) / centre)[:, None, None]
        result.append((factor, (shifted > 0)[:, None, None]))
    return result


def lower_y(values):
    return jnp.roll(values, NZ, axis=-1)


def upper_y(values):
    return jnp.roll(values, -NZ, axis=-1)


def lower_z(values):
    z_place = lax.iota(jnp.int32, values.shape[-1]) % NZ
    return jnp.where(z_place == 0, jnp.roll(values, 1 - NZ, axis=-1), jnp.roll(values, 1, axis=-1))


def upper_z(values):
    z_place = lax.iota(jnp.int32, values.shape[-1]) % NZ
    return jnp.where(
        z_place == NZ - 1, jnp.roll(values, NZ - 1, axis=-1), jnp.roll(values, -1, axis=-1)
    )


def stream(tile_rows, padded, mirror, first_row, fluid_pad):
    fluid_cells = fluid_pad[1:-1]
    neighbours = (
        (padded[:, :-2], padded[:, 2:], fluid_pad[:-2], fluid_pad[2:]),
        (lower_y(tile_rows), upper_y(tile_rows), lower_y(fluid_cells), upper_y(fluid_cells)),
        (lower_z(tile_rows), upper_z(tile_rows), lower_z(fluid_cells), upper_z(fluid_cells)),
    )
    outflow = None
    for (factor, positive), (lower_side, upper_side, open_lower, open_upper) in zip(
        velocity_terms(first_row, tile_rows.shape[0]), neighbours
    ):
        upwind = jnp.where(
            positive,
            jnp.where(open_lower > 0, lower_side, mirror),
            jnp.where(open_upper > 0, upper_side, mirror),
        )
        flux_term = factor * (tile_rows - upwind)
        outflow = flux_term if outflow is None else outflow + flux_term
    return (tile_rows - outflow) * fluid_cells


def face_layers(tile_rows):
    return extended(tile_rows, (("cells", 1),), 1)


def mirror_values(tile_rows):
    partner = tile_rows
    for bit_number in range(lax.axis_size("vel").bit_length() - 1):
        partner = from_partner(partner, "vel", bit_number)
    return jnp.flip(partner, axis=0)


def per_device(populations, solid_mask, collision):
    tile_count = populations.shape[0]
    first_row = lax.axis_index("vel") * tile_count
    solid_pad = extended(solid_mask, (("cells", 0),), 1)
    fluid_pad = (solid_pad == 0).astype(jnp.float32)
    state = populations
    for step_index in range(STEPS):
        read = stream(state, face_layers(state), mirror_values(state), first_row, fluid_pad)
        lowered = read.astype(jnp.bfloat16)
        block_rows = lax.all_gather(lowered, "vel", axis=0, tiled=True)
        flat_rows = block_rows.reshape(block_rows.shape[0], -1)
        collided = jnp.dot(collision, flat_rows, preferred_element_type=jnp.float32)
        collided = collided.reshape(state.shape)
        state = stream(
            collided, face_layers(collided), mirror_values(collided), first_row, fluid_pad
        )
    return state


def solution(mesh):
    in_specs = (P("vel", "cells", None), P("cells", None), P("vel", None))
    out_specs = P("vel", "cells", None)
    return jax.shard_map(
        per_device, mesh=mesh, in_specs=in_specs, out_specs=out_specs, check_vma=False
    )
```

profile of v0, /device:TPU:6, one launch (start us, length us, event | category | flops | bytes accessed | tf_op | source)
XLA Modules:
  0.0 461.6 jit_solution(14547585777425873810)
XLA Ops:
  6.5 2.0 collective-permute-start
  8.6 15.9 %collective-permute-start.1 = (s32[1,256]{1,0:T(1,128)}, s32[1,256]{1,0:T(1,128)S(1)}, u32[]{:S(2)}, u32[]{:S(2)}) collective-permute-start(s32[1,256]{1,0:T(1,128)} %param.4), channel_id=1, source_target_pairs={{4,0},{8,4},{12,8},{16,12},{20,16},{24,20},{28,24},{32,28},{36,32}... | collective-permute-start | bytes 3080 | tf_op jit(solution)/shard_map/ppermute | solution.py:20
  24.5 2.6 collective-permute-start.3
  27.1 1.9 collective-permute-start.2
  29.0 10.6 %collective-permute-start.5 = (f32[686,1,256]{2,1,0:T(1,128)}, f32[686,1,256]{2,1,0:T(1,128)}, u32[]{:S(2)}, u32[]{:S(2)}) collective-permute-start(f32[686,1,256]{2,1,0:T(1,128)} %param.3), channel_id=1, source_target_pairs={{4,0},{8,4},{12,8},{16,12},{20,16},{24,20},{28,24},{32,28},{36,32}... | collective-permute-start | bytes 2107400 | tf_op jit(solution)/shard_map/ppermute | solution.py:20
  59.2 2.9 collective-permute-start.4
  65.3 21.4 %collective-permute-done.4 = f32[686,1,256]{2,1,0:T(1,128)S(1)} collective-permute-done((f32[686,1,256]{2,1,0:T(1,128)}, f32[686,1,256]{2,1,0:T(1,128)S(1)}, u32[]{:S(2)}, u32[]{:S(2)}) %collective-permute-start.4) | collective-permute-done | bytes 702496 | tf_op jit(solution)/shard_map/ppermute | solution.py:28
  86.8 4.0 rev.13
  90.8 4.3 fusion.19
  96.5 60.8 %all-gather.3.cloned.1.call-done = bf16[2744,1,256]{2,1,0:T(2,128)(2,1)} async-done(((bf16[686,1,256]{2,1,0:T(2,128)(2,1)}), bf16[2744,1,256]{2,1,0:T(2,128)(2,1)}) %all-gather.3.cloned.1.call-update) | async-done | bytes 1404944 | tf_op jit(solution)/shard_map/all_gather | solution.py:104
  157.3 4.1 fusion.6
  163.1 9.1 %collective-permute-start.9 = (f32[686,1,256]{2,1,0:T(1,128)}, f32[686,1,256]{2,1,0:T(1,128)}, u32[]{:S(2)}, u32[]{:S(2)}) collective-permute-start(f32[686,1,256]{2,1,0:T(1,128)} %copy.84), channel_id=1, source_target_pairs={{4,0},{8,4},{12,8},{16,12},{20,16},{24,20},{28,24},{32,28},{36,32}... | collective-permute-start | bytes 2107400 | tf_op jit(solution)/shard_map/ppermute | solution.py:20
  172.2 2.5 collective-permute-start.7
  174.6 1.9 collective-permute-start.6
  178.8 27.8 %collective-permute-done.7 = f32[686,1,256]{2,1,0:T(1,128)S(1)} collective-permute-done((f32[686,1,256]{2,1,0:T(1,128)}, f32[686,1,256]{2,1,0:T(1,128)S(1)}, u32[]{:S(2)}, u32[]{:S(2)}) %collective-permute-start.7) | collective-permute-done | bytes 702496 | tf_op jit(solution)/shard_map/ppermute | solution.py:28
  206.6 5.4 %collective-permute-start.8 = (f32[686,1,256]{2,1,0:T(1,128)S(1)}, f32[686,1,256]{2,1,0:T(1,128)S(1)}, u32[]{:S(2)}, u32[]{:S(2)}) collective-permute-start(f32[686,1,256]{2,1,0:T(1,128)S(1)} %collective-permute-done.7), channel_id=1, source_target_pairs={{0,2},{1,3},{2,0},{3,1},{4,6},{5,7},{6,4},{7,5},{8,10},{9,11},{10,... | collective-permute-start | bytes 2107400 | tf_op jit(solution)/shard_map/ppermute | solution.py:28
  215.6 12.9 %collective-permute-done.8 = f32[686,1,256]{2,1,0:T(1,128)S(1)} collective-permute-done((f32[686,1,256]{2,1,0:T(1,128)S(1)}, f32[686,1,256]{2,1,0:T(1,128)S(1)}, u32[]{:S(2)}, u32[]{:S(2)}) %collective-permute-start.8) | collective-permute-done | bytes 702496 | tf_op jit(solution)/shard_map/ppermute | solution.py:28
  229.6 4.4 fusion.31
  235.5 12.8 %collective-permute-start.13 = (f32[686,1,256]{2,1,0:T(1,128)}, f32[686,1,256]{2,1,0:T(1,128)}, u32[]{:S(2)}, u32[]{:S(2)}) collective-permute-start(f32[686,1,256]{2,1,0:T(1,128)} %copy.90), channel_id=1, source_target_pairs={{4,0},{8,4},{12,8},{16,12},{20,16},{24,20},{28,24},{32,28},{36,32}... | collective-permute-start | bytes 2107400 | tf_op jit(solution)/shard_map/ppermute | solution.py:20
  250.2 1.9 collective-permute-start.10
  254.3 24.6 %collective-permute-done.11 = f32[686,1,256]{2,1,0:T(1,128)S(1)} collective-permute-done((f32[686,1,256]{2,1,0:T(1,128)}, f32[686,1,256]{2,1,0:T(1,128)S(1)}, u32[]{:S(2)}, u32[]{:S(2)}) %collective-permute-start.11) | collective-permute-done | bytes 702496 | tf_op jit(solution)/shard_map/ppermute | solution.py:28
  278.9 4.3 collective-permute-start.12
  286.9 13.4 %collective-permute-done.12 = f32[686,1,256]{2,1,0:T(1,128)S(1)} collective-permute-done((f32[686,1,256]{2,1,0:T(1,128)S(1)}, f32[686,1,256]{2,1,0:T(1,128)S(1)}, u32[]{:S(2)}, u32[]{:S(2)}) %collective-permute-start.12) | collective-permute-done | bytes 702496 | tf_op jit(solution)/shard_map/ppermute | solution.py:28
  301.3 4.4 fusion.44
  307.1 69.5 %all-gather.5.cloned.1.call-done = bf16[2744,1,256]{2,1,0:T(2,128)(2,1)} async-done(((bf16[686,1,256]{2,1,0:T(2,128)(2,1)}), bf16[2744,1,256]{2,1,0:T(2,128)(2,1)}) %all-gather.5.cloned.1.call-update) | async-done | bytes 1404944 | tf_op jit(solution)/shard_map/all_gather | solution.py:104
  376.6 4.1 fusion.9
  382.3 9.1 %collective-permute-start.17 = (f32[686,1,256]{2,1,0:T(1,128)}, f32[686,1,256]{2,1,0:T(1,128)}, u32[]{:S(2)}, u32[]{:S(2)}) collective-permute-start(f32[686,1,256]{2,1,0:T(1,128)} %copy.97), channel_id=1, source_target_pairs={{4,0},{8,4},{12,8},{16,12},{20,16},{24,20},{28,24},{32,28},{36,32}... | collective-permute-start | bytes 2107400 | tf_op jit(solution)/shard_map/ppermute | solution.py:20
  391.4 2.5 collective-permute-start.15
  398.0 27.8 %collective-permute-done.15 = f32[686,1,256]{2,1,0:T(1,128)S(1)} collective-permute-done((f32[686,1,256]{2,1,0:T(1,128)}, f32[686,1,256]{2,1,0:T(1,128)S(1)}, u32[]{:S(2)}, u32[]{:S(2)}) %collective-permute-start.15) | collective-permute-done | bytes 702496 | tf_op jit(solution)/shard_map/ppermute | solution.py:28
  425.9 5.3 %collective-permute-start.16 = (f32[686,1,256]{2,1,0:T(1,128)S(1)}, f32[686,1,256]{2,1,0:T(1,128)S(1)}, u32[]{:S(2)}, u32[]{:S(2)}) collective-permute-start(f32[686,1,256]{2,1,0:T(1,128)S(1)} %collective-permute-done.15), channel_id=1, source_target_pairs={{0,2},{1,3},{2,0},{3,1},{4,6},{5,7},{6,4},{7,5},{8,10},{9,11},{10,... | collective-permute-start | bytes 2107400 | tf_op jit(solution)/shard_map/ppermute | solution.py:28
  434.9 12.9 %collective-permute-done.16 = f32[686,1,256]{2,1,0:T(1,128)S(1)} collective-permute-done((f32[686,1,256]{2,1,0:T(1,128)S(1)}, f32[686,1,256]{2,1,0:T(1,128)S(1)}, u32[]{:S(2)}, u32[]{:S(2)}) %collective-permute-start.16) | collective-permute-done | bytes 702496 | tf_op jit(solution)/shard_map/ppermute | solution.py:28
  448.8 4.4 fusion.56
  (86 shorter events, 56.3 us)
Async XLA Ops:
  6.5 37.5 %copy-start = (f32[686,1,256]{2,1,0:T(1,128)S(1)}, f32[686,1,256]{2,1,0:T(1,128)}, u32[]{:S(2)}) copy-start(f32[686,1,256]{2,1,0:T(1,128)} %param.3) | copy-start | bytes 2107396
  6.5 150.8 %all-gather.3.cloned.1.call-start = ((), (), s32[]{:S(2)}) async-start(), calls=%async_computation | async-start | bytes 3512320 | tf_op jit(solution)/shard_map/all_gather | solution.py:104
  6.5 51.8 %collective-permute-start = (s32[1,256]{1,0:T(1,128)}, s32[1,256]{1,0:T(1,128)S(1)}, u32[]{:S(2)}, u32[]{:S(2)}) collective-permute-start(s32[1,256]{1,0:T(1,128)} %param.4), channel_id=1, source_target_pairs={{0,4},{4,8},{8,12},{12,16},{16,20},{20,24},{24,28},{28,32},{32,36}... | collective-permute-start | bytes 3080 | tf_op jit(solution)/shard_map/ppermute | solution.py:18
  8.6 49.7 %collective-permute-start.1 = (s32[1,256]{1,0:T(1,128)}, s32[1,256]{1,0:T(1,128)S(1)}, u32[]{:S(2)}, u32[]{:S(2)}) collective-permute-start(s32[1,256]{1,0:T(1,128)} %param.4), channel_id=1, source_target_pairs={{4,0},{8,4},{12,8},{16,12},{20,16},{24,20},{28,24},{32,28},{36,32}... | collective-permute-start | bytes 3080 | tf_op jit(solution)/shard_map/ppermute | solution.py:20
  24.5 34.6 %collective-permute-start.3 = (f32[686,1,256]{2,1,0:T(1,128)}, f32[686,1,256]{2,1,0:T(1,128)}, u32[]{:S(2)}, u32[]{:S(2)}) collective-permute-start(f32[686,1,256]{2,1,0:T(1,128)} %param.3), channel_id=1, source_target_pairs={{0,1},{1,0},{2,3},{3,2},{4,5},{5,4},{6,7},{7,6},{8,9},{9,8},{10,11... | collective-permute-start | bytes 2107400 | tf_op jit(solution)/shard_map/ppermute | solution.py:28
  27.1 63.7 %collective-permute-start.2 = (f32[686,1,256]{2,1,0:T(1,128)}, f32[686,1,256]{2,1,0:T(1,128)}, u32[]{:S(2)}, u32[]{:S(2)}) collective-permute-start(f32[686,1,256]{2,1,0:T(1,128)} %param.3), channel_id=1, source_target_pairs={{0,4},{4,8},{8,12},{12,16},{16,20},{20,24},{24,28},{28,32},{32,36}... | collective-permute-start | bytes 2107400 | tf_op jit(solution)/shard_map/ppermute | solution.py:18
  29.0 61.8 %collective-permute-start.5 = (f32[686,1,256]{2,1,0:T(1,128)}, f32[686,1,256]{2,1,0:T(1,128)}, u32[]{:S(2)}, u32[]{:S(2)}) collective-permute-start(f32[686,1,256]{2,1,0:T(1,128)} %param.3), channel_id=1, source_target_pairs={{4,0},{8,4},{12,8},{16,12},{20,16},{24,20},{28,24},{32,28},{36,32}... | collective-permute-start | bytes 2107400 | tf_op jit(solution)/shard_map/ppermute | solution.py:20
  55.5 2.8 copy-start.1
  59.2 27.6 %collective-permute-start.4 = (f32[686,1,256]{2,1,0:T(1,128)}, f32[686,1,256]{2,1,0:T(1,128)S(1)}, u32[]{:S(2)}, u32[]{:S(2)}) collective-permute-start(f32[686,1,256]{2,1,0:T(1,128)} %collective-permute-done.3), channel_id=1, source_target_pairs={{0,2},{1,3},{2,0},{3,1},{4,6},{5,7},{6,4},{7,5},{8,10},{9,11},{10,... | collective-permute-start | bytes 2107400 | tf_op jit(solution)/shard_map/ppermute | solution.py:28
  96.5 280.1 %all-gather.5.cloned.1.call-start = ((), (), s32[]{:S(2)}) async-start(), calls=%async_computation.1 | async-start | bytes 3512320 | tf_op jit(solution)/shard_map/all_gather | solution.py:104
  163.1 66.5 %collective-permute-start.9 = (f32[686,1,256]{2,1,0:T(1,128)}, f32[686,1,256]{2,1,0:T(1,128)}, u32[]{:S(2)}, u32[]{:S(2)}) collective-permute-start(f32[686,1,256]{2,1,0:T(1,128)} %copy.84), channel_id=1, source_target_pairs={{4,0},{8,4},{12,8},{16,12},{20,16},{24,20},{28,24},{32,28},{36,32}... | collective-permute-start | bytes 2107400 | tf_op jit(solution)/shard_map/ppermute | solution.py:20
  172.2 34.4 %collective-permute-start.7 = (f32[686,1,256]{2,1,0:T(1,128)}, f32[686,1,256]{2,1,0:T(1,128)S(1)}, u32[]{:S(2)}, u32[]{:S(2)}) collective-permute-start(f32[686,1,256]{2,1,0:T(1,128)} %copy.84), channel_id=1, source_target_pairs={{0,1},{1,0},{2,3},{3,2},{4,5},{5,4},{6,7},{7,6},{8,9},{9,8},{10,11... | collective-permute-start | bytes 2107400 | tf_op jit(solution)/shard_map/ppermute | solution.py:28
  174.6 54.9 %collective-permute-start.6 = (f32[686,1,256]{2,1,0:T(1,128)}, f32[686,1,256]{2,1,0:T(1,128)}, u32[]{:S(2)}, u32[]{:S(2)}) collective-permute-start(f32[686,1,256]{2,1,0:T(1,128)} %copy.84), channel_id=1, source_target_pairs={{0,4},{4,8},{8,12},{12,16},{16,20},{20,24},{24,28},{28,32},{32,36}... | collective-permute-start | bytes 2107400 | tf_op jit(solution)/shard_map/ppermute | solution.py:18
  206.6 21.9 %collective-permute-start.8 = (f32[686,1,256]{2,1,0:T(1,128)S(1)}, f32[686,1,256]{2,1,0:T(1,128)S(1)}, u32[]{:S(2)}, u32[]{:S(2)}) collective-permute-start(f32[686,1,256]{2,1,0:T(1,128)S(1)} %collective-permute-done.7), channel_id=1, source_target_pairs={{0,2},{1,3},{2,0},{3,1},{4,6},{5,7},{6,4},{7,5},{8,10},{9,11},{10,... | collective-permute-start | bytes 2107400 | tf_op jit(solution)/shard_map/ppermute | solution.py:28
  235.5 65.8 %collective-permute-start.13 = (f32[686,1,256]{2,1,0:T(1,128)}, f32[686,1,256]{2,1,0:T(1,128)}, u32[]{:S(2)}, u32[]{:S(2)}) collective-permute-start(f32[686,1,256]{2,1,0:T(1,128)} %copy.90), channel_id=1, source_target_pairs={{4,0},{8,4},{12,8},{16,12},{20,16},{24,20},{28,24},{32,28},{36,32}... | collective-permute-start | bytes 2107400 | tf_op jit(solution)/shard_map/ppermute | solution.py:20
  248.3 30.7 %collective-permute-start.11 = (f32[686,1,256]{2,1,0:T(1,128)}, f32[686,1,256]{2,1,0:T(1,128)S(1)}, u32[]{:S(2)}, u32[]{:S(2)}) collective-permute-start(f32[686,1,256]{2,1,0:T(1,128)} %copy.90), channel_id=1, source_target_pairs={{0,1},{1,0},{2,3},{3,2},{4,5},{5,4},{6,7},{7,6},{8,9},{9,8},{10,11... | collective-permute-start | bytes 2107400 | tf_op jit(solution)/shard_map/ppermute | solution.py:28
  250.2 51.1 %collective-permute-start.10 = (f32[686,1,256]{2,1,0:T(1,128)}, f32[686,1,256]{2,1,0:T(1,128)}, u32[]{:S(2)}, u32[]{:S(2)}) collective-permute-start(f32[686,1,256]{2,1,0:T(1,128)} %copy.90), channel_id=1, source_target_pairs={{0,4},{4,8},{8,12},{12,16},{16,20},{20,24},{24,28},{28,32},{32,36}... | collective-permute-start | bytes 2107400 | tf_op jit(solution)/shard_map/ppermute | solution.py:18
  278.9 21.4 %collective-permute-start.12 = (f32[686,1,256]{2,1,0:T(1,128)S(1)}, f32[686,1,256]{2,1,0:T(1,128)S(1)}, u32[]{:S(2)}, u32[]{:S(2)}) collective-permute-start(f32[686,1,256]{2,1,0:T(1,128)S(1)} %collective-permute-done.11), channel_id=1, source_target_pairs={{0,2},{1,3},{2,0},{3,1},{4,6},{5,7},{6,4},{7,5},{8,10},{9,11},{10,... | collective-permute-start | bytes 2107400 | tf_op jit(solution)/shard_map/ppermute | solution.py:28
  382.3 66.5 %collective-permute-start.17 = (f32[686,1,256]{2,1,0:T(1,128)}, f32[686,1,256]{2,1,0:T(1,128)}, u32[]{:S(2)}, u32[]{:S(2)}) collective-permute-start(f32[686,1,256]{2,1,0:T(1,128)} %copy.97), channel_id=1, source_target_pairs={{4,0},{8,4},{12,8},{16,12},{20,16},{24,20},{28,24},{32,28},{36,32}... | collective-permute-start | bytes 2107400 | tf_op jit(solution)/shard_map/ppermute | solution.py:20
  391.4 34.4 %collective-permute-start.15 = (f32[686,1,256]{2,1,0:T(1,128)}, f32[686,1,256]{2,1,0:T(1,128)S(1)}, u32[]{:S(2)}, u32[]{:S(2)}) collective-permute-start(f32[686,1,256]{2,1,0:T(1,128)} %copy.97), channel_id=1, source_target_pairs={{0,1},{1,0},{2,3},{3,2},{4,5},{5,4},{6,7},{7,6},{8,9},{9,8},{10,11... | collective-permute-start | bytes 2107400 | tf_op jit(solution)/shard_map/ppermute | solution.py:28
  393.9 54.9 %collective-permute-start.14 = (f32[686,1,256]{2,1,0:T(1,128)}, f32[686,1,256]{2,1,0:T(1,128)}, u32[]{:S(2)}, u32[]{:S(2)}) collective-permute-start(f32[686,1,256]{2,1,0:T(1,128)} %copy.97), channel_id=1, source_target_pairs={{0,4},{4,8},{8,12},{12,16},{16,20},{20,24},{24,28},{28,32},{32,36}... | collective-permute-start | bytes 2107400 | tf_op jit(solution)/shard_map/ppermute | solution.py:18
  425.9 21.9 %collective-permute-start.16 = (f32[686,1,256]{2,1,0:T(1,128)S(1)}, f32[686,1,256]{2,1,0:T(1,128)S(1)}, u32[]{:S(2)}, u32[]{:S(2)}) collective-permute-start(f32[686,1,256]{2,1,0:T(1,128)S(1)} %collective-permute-done.15), channel_id=1, source_target_pairs={{0,2},{1,3},{2,0},{3,1},{4,6},{5,7},{6,4},{7,5},{8,10},{9,11},{10,... | collective-permute-start | bytes 2107400 | tf_op jit(solution)/shard_map/ppermute | solution.py:28
Sparse Core Ops, SparseCore 0:
  96.6 60.6 all-gather.2
  307.2 69.3 all-gather.4
where the time goes:
time: 462 us
  waiting for transfers between devices  271 us (59%)
  starting transfers between devices  94.6 us (20%)
  local copies, waits for them, and re-layouts  52.5 us (11%)
  other arithmetic  21.1 us (5%)
  between operations  13.8 us (3%)
  matrix products  8.25 us (2%)
    ppermute x8, waiting for transfers between devices, from_partner(): lax.ppermute(array, axis, [(i, i ^ 1 << apart) for i in range(lax.axis_si...  141 us
    all_gather x2, waiting for transfers between devices, per_device(): block_rows = lax.all_gather(lowered, 'vel', axis=0, tiled=True)  130 us
    ppermute x5, starting transfers between devices, extended(): lax.ppermute(head, axis, [((i + 1) % count, i) for i in range(count)])  57.4 us
    ppermute x8, starting transfers between devices, from_partner(): lax.ppermute(array, axis, [(i, i ^ 1 << apart) for i in range(lax.axis_si...  27.3 us
    slice x8, local copies, waits for them, and re-layouts, upper_z(): jnp.roll(values, NZ - 1, axis=-1)  10.8 us
    ppermute x5, starting transfers between devices, extended(): lax.ppermute(tail, axis, [(i, (i + 1) % count) for i in range(count)])  9.73 us
    slice x8, local copies, waits for them, and re-layouts, upper_z(): jnp.roll(values, -1, axis=-1)  9.71 us
  transfers between devices with their start and end apart: 20, of which 9 were waited for; matrix products, arithmetic and copies ran while one was open for 10% of the time, Pallas kernels for 0%

commit v1 on v0

v1 whole, which is shorter than its diff:
```python
import jax
import jax.numpy as jnp
from jax import lax
from jax.sharding import PartitionSpec as P

K = 14
STEPS = 2
NZ = 16
BOTH = ("cells", "vel")


def velocity_terms(first_row, row_count):
    velocity_ids = first_row + lax.iota(jnp.int32, row_count)
    components = (velocity_ids // (K * K), velocity_ids // K % K, velocity_ids % K)
    centre = (K - 1) / 2.0
    result = []
    for component in components:
        shifted = component.astype(jnp.float32) - centre
        factor = (0.3 * jnp.abs(shifted) / centre)[:, None]
        result.append((factor, (shifted > 0)[:, None]))
    return result


def lower_y(values):
    return jnp.roll(values, NZ, axis=-1)


def upper_y(values):
    return jnp.roll(values, -NZ, axis=-1)


def lower_z(values):
    z_place = lax.iota(jnp.int32, values.shape[-1]) % NZ
    return jnp.where(z_place == 0, jnp.roll(values, 1 - NZ, axis=-1), jnp.roll(values, 1, axis=-1))


def upper_z(values):
    z_place = lax.iota(jnp.int32, values.shape[-1]) % NZ
    return jnp.where(
        z_place == NZ - 1, jnp.roll(values, NZ - 1, axis=-1), jnp.roll(values, -1, axis=-1)
    )


def upwind_layer(array):
    cells, vel = lax.axis_size("cells"), lax.axis_size("vel")
    pairs = []
    for cell in range(cells):
        for part in range(vel):
            target = (cell + (1 if 2 * part >= vel else -1)) % cells
            pairs.append((cell * vel + part, target * vel + part))
    return lax.ppermute(array, BOTH, pairs)


def from_mirror(array):
    vel = lax.axis_size("vel")
    return lax.ppermute(array, "vel", [(i, vel - 1 - i) for i in range(vel)])


def gathered(array):
    vel = lax.axis_size("vel")
    mine = lax.axis_index("vel")
    parts = [array]
    for step in range(1, vel):
        parts.append(lax.ppermute(array, "vel", [(i, i ^ step) for i in range(vel)]))
    return [lax.select_n(mine, *[parts[i ^ j] for i in range(vel)]) for j in range(vel)]


def stream(rows, terms, fluid, open_x):
    low = rows.astype(jnp.bfloat16)
    mirror = jnp.flip(from_mirror(low), axis=0).astype(jnp.float32)
    layer = upwind_layer(low).astype(jnp.float32)
    upwind = [jnp.where(open_x > 0, layer, mirror)]
    for (factor, positive), (lower, upper) in zip(terms[1:], ((lower_y, upper_y), (lower_z, upper_z))):
        upwind.append(
            jnp.where(
                positive,
                jnp.where(lower(fluid) > 0, lower(rows), mirror),
                jnp.where(upper(fluid) > 0, upper(rows), mirror),
            )
        )
    outflow = 0.0
    for (factor, _), value in zip(terms, upwind):
        outflow = outflow + factor * (rows - value)
    return (rows - outflow) * fluid


def per_device(populations, solid_mask, collision):
    row_count = populations.shape[0]
    terms = velocity_terms(lax.axis_index("vel") * row_count, row_count)
    open_x = (upwind_layer(solid_mask) == 0).astype(jnp.float32)
    fluid = (solid_mask == 0).astype(jnp.float32)
    state = populations[:, 0, :]
    for _ in range(STEPS):
        read = stream(state, terms, fluid, open_x)
        blocks = gathered(read.astype(jnp.bfloat16))
        collided = jnp.dot(
            collision, jnp.concatenate(blocks, axis=0), preferred_element_type=jnp.float32
        )
        state = stream(collided, terms, fluid, open_x)
    return state[:, None, :]


def solution(mesh):
    in_specs = (P("vel", "cells", None), P("cells", None), P("vel", None))
    out_specs = P("vel", "cells", None)
    return jax.shard_map(
        per_device, mesh=mesh, in_specs=in_specs, out_specs=out_specs, check_vma=False
    )
```

time: 462 us -> 214 us (0.46)
  the two profiles are of different devices: /device:TPU:6 before, /device:TPU:8 now
where the time goes in v1:
time: 214 us; the launch traced here: 212 us
  starting transfers between devices  68.9 us (32%)
  waiting for transfers between devices  58.2 us (27%)
  local copies, waits for them, and re-layouts  54.6 us (26%)
  other arithmetic  21.8 us (10%)
  matrix products  8.01 us (4%)
    ppermute x6, waiting for transfers between devices, gathered(): lax.ppermute(array, 'vel', [(i, i ^ step) for i in range(vel)])  38.5 us
    ppermute x5, starting transfers between devices, upwind_layer(): return lax.ppermute(array, BOTH, pairs)  36.6 us
    rev x4, local copies, waits for them, and re-layouts, stream(): mirror = jnp.flip(from_mirror(low), axis=0).astype(jnp.float32)  23.1 us
    ppermute x4, waiting for transfers between devices, from_mirror(): return lax.ppermute(array, 'vel', [(i, vel - 1 - i) for i in range(vel)])  19.7 us
    ppermute x6, starting transfers between devices, gathered(): lax.ppermute(array, 'vel', [(i, i ^ step) for i in range(vel)])  18.9 us
    ppermute x4, starting transfers between devices, from_mirror(): return lax.ppermute(array, 'vel', [(i, vel - 1 - i) for i in range(vel)])  13.4 us
    dot_general x2, matrix products, per_device(): jnp.dot(collision, jnp.concatenate(blocks, axis=0), preferred_element_typ...  8.01 us
    convert_element_type x2, other arithmetic, per_device(): blocks = gathered(read.astype(jnp.bfloat16))  7.99 us
  transfers between devices with their start and end apart: 15, of which 7 were waited for; matrix products, arithmetic and copies ran while one was open for 24% of the time, Pallas kernels for 0%

profile of v1, /device:TPU:8, one launch (start us, length us, event | category | flops | bytes accessed | tf_op | source)
XLA Modules:
  0.0 211.8 jit_solution(3206944824525972768)
XLA Ops:
  0.0 1.9 copy.12
  1.9 3.5 %collective-permute-start.2 = (bf16[686,256]{1,0:T(8,128)(2,1)}, bf16[686,256]{1,0:T(8,128)(2,1)}, u32[]{:S(2)}, u32[]{:S(2)}) collective-permute-start(bf16[686,256]{1,0:T(8,128)(2,1)} %bitcast.34), channel_id=1, source_target_pairs={{0,3},{1,2},{2,1},{3,0},{4,7},{5,6},{6,5},{7,4},{8,11},{9,10},{10,... | collective-permute-start | bytes 1053704 | tf_op jit(solution)/shard_map/ppermute | solution.py:56
  5.4 15.8 %collective-permute-start.1 = (bf16[686,256]{1,0:T(8,128)(2,1)}, bf16[686,256]{1,0:T(8,128)(2,1)}, u32[]{:S(2)}, u32[]{:S(2)}) collective-permute-start(bf16[686,256]{1,0:T(8,128)(2,1)} %bitcast.34), channel_id=1, source_target_pairs={{0,508},{1,509},{2,6},{3,7},{4,0},{5,1},{6,10},{7,11},{8,4},{9,5},... | collective-permute-start | bytes 1053704 | tf_op jit(solution)/shard_map/ppermute | solution.py:51
  21.2 2.9 %collective-permute-start = (s32[1,256]{1,0:T(1,128)}, s32[1,256]{1,0:T(1,128)}, u32[]{:S(2)}, u32[]{:S(2)}) collective-permute-start(s32[1,256]{1,0:T(1,128)} %param.4), channel_id=1, source_target_pairs={{0,508},{1,509},{2,6},{3,7},{4,0},{5,1},{6,10},{7,11},{8,4},{9,5},... | collective-permute-start | bytes 3080 | tf_op jit(solution)/shard_map/ppermute | solution.py:51
  36.3 6.4 %rev.13 = bf16[686,256]{1,0:T(8,128)(2,1)} reverse(bf16[686,256]{1,0:T(8,128)(2,1)} %collective-permute-done.2), dimensions={0} | reverse | bytes 702464 | tf_op jit(solution)/shard_map/jit(_flip)/rev | solution.py:70
  42.7 4.3 %fusion.6 = bf16[686,256]{1,0:T(8,128)(2,1)} fusion(bf16[686,256]{1,0:T(8,128)(2,1)} %rev.13, f32[686,240]{1,0:T(8,128)S(1)} %get-tuple-element.60, f32[686,16]{1,0:T(8,128)} %get-tuple-element.62, f32[686,16]{1,0:T(8,128)} %get-tuple-element.61, f32[686,240]{1,0:T(8,128)S(1)} %get-tuple-element.59, f32[686,15]{1,0:T(8,128)} %get-tuple-element.56, ...), kind=kLoop, calls=%fused_computation.28 | loop fusion | flops 4917248 | bytes 5983364 | tf_op jit(solution)/shard_map/convert_element_type | solution.py:95
  48.9 5.8 %collective-permute-start.4 = (bf16[686,256]{1,0:T(8,128)(2,1)}, bf16[686,256]{1,0:T(8,128)(2,1)S(1)}, u32[]{:S(2)}, u32[]{:S(2)}) collective-permute-start(bf16[686,256]{1,0:T(8,128)(2,1)} %fusion.6), channel_id=1, source_target_pairs={{0,2},{1,3},{2,0},{3,1},{4,6},{5,7},{6,4},{7,5},{8,10},{9,11},{10,... | collective-permute-start | bytes 1053704 | tf_op jit(solution)/shard_map/ppermute | solution.py:64
  56.7 18.7 %collective-permute-done.5 = bf16[686,256]{1,0:T(8,128)(2,1)S(1)} collective-permute-done((bf16[686,256]{1,0:T(8,128)(2,1)}, bf16[686,256]{1,0:T(8,128)(2,1)S(1)}, u32[]{:S(2)}, u32[]{:S(2)}) %collective-permute-start.5) | collective-permute-done | bytes 351264 | tf_op jit(solution)/shard_map/ppermute | solution.py:64
  75.4 4.0 %collective-permute-done.4 = bf16[686,256]{1,0:T(8,128)(2,1)S(1)} collective-permute-done((bf16[686,256]{1,0:T(8,128)(2,1)}, bf16[686,256]{1,0:T(8,128)(2,1)S(1)}, u32[]{:S(2)}, u32[]{:S(2)}) %collective-permute-start.4) | collective-permute-done | bytes 351264 | tf_op jit(solution)/shard_map/ppermute | solution.py:64
  80.5 2.3 %concatenate.204 = bf16[2744,256]{1,0:T(8,128)(2,1)S(1)} concatenate(bf16[686,256]{1,0:T(8,128)(2,1)S(1)} %get-tuple-element.14, bf16[686,256]{1,0:T(8,128)(2,1)S(1)} %get-tuple-element.13, bf16[686,256]{1,0:T(8,128)(2,1)S(1)} %get-tuple-element.12, bf16[686,256]{1,0:T(8,128)(2,1)S(1)} %get-tuple-element.11), dimensions={0} | concatenate | bytes 2809856 | tf_op jit(solution)/shard_map/concatenate | solution.py:97
  82.9 4.0 %fusion.99 = (bf16[686,256]{1,0:T(8,128)(2,1)}, f32[686,256]{1,0:T(8,128)S(1)}) fusion(bf16[2744,256]{1,0:T(8,128)(2,1)S(1)} %concatenate.204, bf16[686,2744]{1,0:T(8,128)(2,1)} %param.5), kind=kOutput, calls=%fused_computation.161 | convolution fusion | flops 963956224 | bytes 6223392 | tf_op jit(solution)/shard_map/dot_general | solution.py:96
  86.9 3.6 %collective-permute-start.7 = (bf16[686,256]{1,0:T(8,128)(2,1)}, bf16[686,256]{1,0:T(8,128)(2,1)S(1)}, u32[]{:S(2)}, u32[]{:S(2)}) collective-permute-start(bf16[686,256]{1,0:T(8,128)(2,1)} %get-tuple-element.75), channel_id=1, source_target_pairs={{0,3},{1,2},{2,1},{3,0},{4,7},{5,6},{6,5},{7,4},{8,11},{9,10},{10,... | collective-permute-start | bytes 1053704 | tf_op jit(solution)/shard_map/ppermute | solution.py:56
  90.5 5.1 %collective-permute-start.6 = (bf16[686,256]{1,0:T(8,128)(2,1)}, bf16[686,256]{1,0:T(8,128)(2,1)S(1)}, u32[]{:S(2)}, u32[]{:S(2)}) collective-permute-start(bf16[686,256]{1,0:T(8,128)(2,1)} %get-tuple-element.75), channel_id=1, source_target_pairs={{0,508},{1,509},{2,6},{3,7},{4,0},{5,1},{6,10},{7,11},{8,4},{9,5},... | collective-permute-start | bytes 1053704 | tf_op jit(solution)/shard_map/ppermute | solution.py:51
  101.2 8.2 %collective-permute-done.7 = bf16[686,256]{1,0:T(8,128)(2,1)S(1)} collective-permute-done((bf16[686,256]{1,0:T(8,128)(2,1)}, bf16[686,256]{1,0:T(8,128)(2,1)S(1)}, u32[]{:S(2)}, u32[]{:S(2)}) %collective-permute-start.7) | collective-permute-done | bytes 351264 | tf_op jit(solution)/shard_map/ppermute | solution.py:56
  109.4 4.0 %rev.14 = bf16[686,256]{1,0:T(8,128)(2,1)} reverse(bf16[686,256]{1,0:T(8,128)(2,1)S(1)} %collective-permute-done.7), dimensions={0} | reverse | bytes 702464 | tf_op jit(solution)/shard_map/jit(_flip)/rev | solution.py:70
  114.2 4.3 %fusion.69 = (bf16[686,256]{1,0:T(8,128)(2,1)}, f32[686,256]{1,0:T(8,128)S(1)}) fusion(f32[256]{0:T(256)S(1)} %bitcast.42, f32[686,256]{1,0:T(8,128)S(1)} %get-tuple-element.76, f32[686,1]{1,0:T(8,128)} %get-tuple-element.48, f32[686,255]{1,0:T(8,128)S(1)} %get-tuple-element.50, f32[686,241]{1,0:T(8,128)} %get-tuple-element.44, ...), kind=kLoop, calls=%fused_computation.132 | loop fusion | flops 4917248 | bytes 6685828 | tf_op jit(solution)/shard_map/convert_element_type | solution.py:69
  118.4 3.3 %collective-permute-start.9 = (bf16[686,256]{1,0:T(8,128)(2,1)}, bf16[686,256]{1,0:T(8,128)(2,1)}, u32[]{:S(2)}, u32[]{:S(2)}) collective-permute-start(bf16[686,256]{1,0:T(8,128)(2,1)} %get-tuple-element.5), channel_id=1, source_target_pairs={{0,3},{1,2},{2,1},{3,0},{4,7},{5,6},{6,5},{7,4},{8,11},{9,10},{10,... | collective-permute-start | bytes 1053704 | tf_op jit(solution)/shard_map/ppermute | solution.py:56
  121.8 5.7 %collective-permute-start.8 = (bf16[686,256]{1,0:T(8,128)(2,1)}, bf16[686,256]{1,0:T(8,128)(2,1)}, u32[]{:S(2)}, u32[]{:S(2)}) collective-permute-start(bf16[686,256]{1,0:T(8,128)(2,1)} %get-tuple-element.5), channel_id=1, source_target_pairs={{0,508},{1,509},{2,6},{3,7},{4,0},{5,1},{6,10},{7,11},{8,4},{9,5},... | collective-permute-start | bytes 1053704 | tf_op jit(solution)/shard_map/ppermute | solution.py:51
  132.2 4.2 %collective-permute-done.9 = bf16[686,256]{1,0:T(8,128)(2,1)} collective-permute-done((bf16[686,256]{1,0:T(8,128)(2,1)}, bf16[686,256]{1,0:T(8,128)(2,1)}, u32[]{:S(2)}, u32[]{:S(2)}) %collective-permute-start.9) | collective-permute-done | bytes 351264 | tf_op jit(solution)/shard_map/ppermute | solution.py:56
  136.4 6.4 %rev.15 = bf16[686,256]{1,0:T(8,128)(2,1)} reverse(bf16[686,256]{1,0:T(8,128)(2,1)} %collective-permute-done.9), dimensions={0} | reverse | bytes 702464 | tf_op jit(solution)/shard_map/jit(_flip)/rev | solution.py:70
  142.8 3.7 %fusion.31 = bf16[686,256]{1,0:T(8,128)(2,1)S(1)} fusion(f32[686,256]{1,0:T(8,128)S(1)} %get-tuple-element.6, bf16[686,256]{1,0:T(8,128)(2,1)} %rev.15, f32[686,240]{1,0:T(8,128)S(1)} %get-tuple-element.36, f32[686,16]{1,0:T(8,128)} %get-tuple-element.38, f32[686,16]{1,0:T(8,128)} %get-tuple-element.37, f32[686,240]{1,0:T(8,128)S(1)} %get-tuple-element.35, ...), kind=kLoop, calls=%fused_computation.53 | loop fusion | flops 4917248 | bytes 5983364 | tf_op jit(solution)/shard_map/convert_element_type | solution.py:95
  146.5 3.0 %collective-permute-start.12 = (bf16[686,256]{1,0:T(8,128)(2,1)S(1)}, bf16[686,256]{1,0:T(8,128)(2,1)S(1)}, u32[]{:S(2)}, u32[]{:S(2)}) collective-permute-start(bf16[686,256]{1,0:T(8,128)(2,1)S(1)} %fusion.31), channel_id=1, source_target_pairs={{0,3},{1,2},{2,1},{3,0},{4,7},{5,6},{6,5},{7,4},{8,11},{9,10},{10,... | collective-permute-start | bytes 1053704 | tf_op jit(solution)/shard_map/ppermute | solution.py:64
  151.4 4.3 %collective-permute-start.10 = (bf16[686,256]{1,0:T(8,128)(2,1)S(1)}, bf16[686,256]{1,0:T(8,128)(2,1)S(1)}, u32[]{:S(2)}, u32[]{:S(2)}) collective-permute-start(bf16[686,256]{1,0:T(8,128)(2,1)S(1)} %fusion.31), channel_id=1, source_target_pairs={{0,1},{1,0},{2,3},{3,2},{4,5},{5,4},{6,7},{7,6},{8,9},{9,8},{10,11... | collective-permute-start | bytes 1053704 | tf_op jit(solution)/shard_map/ppermute | solution.py:64
  155.7 11.4 %collective-permute-done.12 = bf16[686,256]{1,0:T(8,128)(2,1)S(1)} collective-permute-done((bf16[686,256]{1,0:T(8,128)(2,1)S(1)}, bf16[686,256]{1,0:T(8,128)(2,1)S(1)}, u32[]{:S(2)}, u32[]{:S(2)}) %collective-permute-start.12) | collective-permute-done | bytes 351264 | tf_op jit(solution)/shard_map/ppermute | solution.py:64
  167.1 4.5 %collective-permute-done.11 = bf16[686,256]{1,0:T(8,128)(2,1)S(1)} collective-permute-done((bf16[686,256]{1,0:T(8,128)(2,1)S(1)}, bf16[686,256]{1,0:T(8,128)(2,1)S(1)}, u32[]{:S(2)}, u32[]{:S(2)}) %collective-permute-start.11) | collective-permute-done | bytes 351264 | tf_op jit(solution)/shard_map/ppermute | solution.py:64
  171.7 2.3 %concatenate.217 = bf16[2744,256]{1,0:T(8,128)(2,1)S(1)} concatenate(bf16[686,256]{1,0:T(8,128)(2,1)S(1)} %get-tuple-element.10, bf16[686,256]{1,0:T(8,128)(2,1)S(1)} %get-tuple-element.9, bf16[686,256]{1,0:T(8,128)(2,1)S(1)} %get-tuple-element.8, bf16[686,256]{1,0:T(8,128)(2,1)S(1)} %get-tuple-element.7), dimensions={0} | concatenate | bytes 2809856 | tf_op jit(solution)/shard_map/concatenate | solution.py:97
  174.1 4.0 %fusion.100 = (bf16[686,256]{1,0:T(8,128)(2,1)}, f32[686,256]{1,0:T(8,128)S(1)}) fusion(bf16[2744,256]{1,0:T(8,128)(2,1)S(1)} %concatenate.217, bf16[686,2744]{1,0:T(8,128)(2,1)} %param.5), kind=kOutput, calls=%fused_computation.162 | convolution fusion | flops 963956224 | bytes 6223392 | tf_op jit(solution)/shard_map/dot_general | solution.py:96
  178.1 3.0 %collective-permute-start.14 = (bf16[686,256]{1,0:T(8,128)(2,1)}, bf16[686,256]{1,0:T(8,128)(2,1)}, u32[]{:S(2)}, u32[]{:S(2)}) collective-permute-start(bf16[686,256]{1,0:T(8,128)(2,1)} %get-tuple-element.77), channel_id=1, source_target_pairs={{0,3},{1,2},{2,1},{3,0},{4,7},{5,6},{6,5},{7,4},{8,11},{9,10},{10,... | collective-permute-start | bytes 1053704 | tf_op jit(solution)/shard_map/ppermute | solution.py:56
  181.1 7.2 %collective-permute-start.13 = (bf16[686,256]{1,0:T(8,128)(2,1)}, bf16[686,256]{1,0:T(8,128)(2,1)}, u32[]{:S(2)}, u32[]{:S(2)}) collective-permute-start(bf16[686,256]{1,0:T(8,128)(2,1)} %get-tuple-element.77), channel_id=1, source_target_pairs={{0,508},{1,509},{2,6},{3,7},{4,0},{5,1},{6,10},{7,11},{8,4},{9,5},... | collective-permute-start | bytes 1053704 | tf_op jit(solution)/shard_map/ppermute | solution.py:51
  193.0 7.2 %collective-permute-done.14 = bf16[686,256]{1,0:T(8,128)(2,1)} collective-permute-done((bf16[686,256]{1,0:T(8,128)(2,1)}, bf16[686,256]{1,0:T(8,128)(2,1)}, u32[]{:S(2)}, u32[]{:S(2)}) %collective-permute-start.14) | collective-permute-done | bytes 351264 | tf_op jit(solution)/shard_map/ppermute | solution.py:56
  200.2 6.4 %rev.16 = bf16[686,256]{1,0:T(8,128)(2,1)} reverse(bf16[686,256]{1,0:T(8,128)(2,1)} %collective-permute-done.14), dimensions={0} | reverse | bytes 702464 | tf_op jit(solution)/shard_map/jit(_flip)/rev | solution.py:70
  206.6 3.6 %fusion.44 = f32[686,1,256]{2,0,1:T(8,128)S(1)} fusion(f32[686,256]{1,0:T(8,128)S(1)} %get-tuple-element.78, bf16[686,256]{1,0:T(8,128)(2,1)} %rev.16, f32[686,240]{1,0:T(8,128)S(1)} %get-tuple-element.24, f32[686,16]{1,0:T(8,128)} %get-tuple-element.26, f32[686,16]{1,0:T(8,128)} %get-tuple-element.25, f32[686,240]{1,0:T(8,128)S(1)} %get-tuple-element.23, ...), kind=kLoop, calls=%fused_computation.66 | loop fusion | flops 4741632 | bytes 6334596 | tf_op jit(solution)/shard_map/broadcast_in_dim | solution.py:100
  (69 shorter events, 36.5 us)
Async XLA Ops:
  0.0 28.1 %copy-start = (f32[686,1,256]{2,1,0:T(1,128)S(1)}, f32[686,1,256]{2,1,0:T(1,128)}, u32[]{:S(2)}) copy-start(f32[686,1,256]{2,1,0:T(1,128)} %param.3) | copy-start | bytes 2107396
  1.9 34.3 %collective-permute-start.2 = (bf16[686,256]{1,0:T(8,128)(2,1)}, bf16[686,256]{1,0:T(8,128)(2,1)}, u32[]{:S(2)}, u32[]{:S(2)}) collective-permute-start(bf16[686,256]{1,0:T(8,128)(2,1)} %bitcast.34), channel_id=1, source_target_pairs={{0,3},{1,2},{2,1},{3,0},{4,7},{5,6},{6,5},{7,4},{8,11},{9,10},{10,... | collective-permute-start | bytes 1053704 | tf_op jit(solution)/shard_map/ppermute | solution.py:56
  5.4 37.3 %collective-permute-start.1 = (bf16[686,256]{1,0:T(8,128)(2,1)}, bf16[686,256]{1,0:T(8,128)(2,1)}, u32[]{:S(2)}, u32[]{:S(2)}) collective-permute-start(bf16[686,256]{1,0:T(8,128)(2,1)} %bitcast.34), channel_id=1, source_target_pairs={{0,508},{1,509},{2,6},{3,7},{4,0},{5,1},{6,10},{7,11},{8,4},{9,5},... | collective-permute-start | bytes 1053704 | tf_op jit(solution)/shard_map/ppermute | solution.py:51
  21.2 13.8 %collective-permute-start = (s32[1,256]{1,0:T(1,128)}, s32[1,256]{1,0:T(1,128)}, u32[]{:S(2)}, u32[]{:S(2)}) collective-permute-start(s32[1,256]{1,0:T(1,128)} %param.4), channel_id=1, source_target_pairs={{0,508},{1,509},{2,6},{3,7},{4,0},{5,1},{6,10},{7,11},{8,4},{9,5},... | collective-permute-start | bytes 3080 | tf_op jit(solution)/shard_map/ppermute | solution.py:51
  31.6 2.0 copy-start.2
  31.6 2.0 copy-start.3
  31.6 2.0 copy-start.4
  31.6 2.0 copy-start.5
  31.6 2.0 copy-start.6
  31.6 2.0 copy-start.7
  47.0 28.4 %collective-permute-start.5 = (bf16[686,256]{1,0:T(8,128)(2,1)}, bf16[686,256]{1,0:T(8,128)(2,1)S(1)}, u32[]{:S(2)}, u32[]{:S(2)}) collective-permute-start(bf16[686,256]{1,0:T(8,128)(2,1)} %fusion.6), channel_id=1, source_target_pairs={{0,3},{1,2},{2,1},{3,0},{4,7},{5,6},{6,5},{7,4},{8,11},{9,10},{10,... | collective-permute-start | bytes 1053704 | tf_op jit(solution)/shard_map/ppermute | solution.py:64
  48.9 30.4 %collective-permute-start.4 = (bf16[686,256]{1,0:T(8,128)(2,1)}, bf16[686,256]{1,0:T(8,128)(2,1)S(1)}, u32[]{:S(2)}, u32[]{:S(2)}) collective-permute-start(bf16[686,256]{1,0:T(8,128)(2,1)} %fusion.6), channel_id=1, source_target_pairs={{0,2},{1,3},{2,0},{3,1},{4,6},{5,7},{6,4},{7,5},{8,10},{9,11},{10,... | collective-permute-start | bytes 1053704 | tf_op jit(solution)/shard_map/ppermute | solution.py:64
  54.8 24.6 %collective-permute-start.3 = (bf16[686,256]{1,0:T(8,128)(2,1)}, bf16[686,256]{1,0:T(8,128)(2,1)S(1)}, u32[]{:S(2)}, u32[]{:S(2)}) collective-permute-start(bf16[686,256]{1,0:T(8,128)(2,1)} %fusion.6), channel_id=1, source_target_pairs={{0,1},{1,0},{2,3},{3,2},{4,5},{5,4},{6,7},{7,6},{8,9},{9,8},{10,11... | collective-permute-start | bytes 1053704 | tf_op jit(solution)/shard_map/ppermute | solution.py:64
  86.9 22.5 %collective-permute-start.7 = (bf16[686,256]{1,0:T(8,128)(2,1)}, bf16[686,256]{1,0:T(8,128)(2,1)S(1)}, u32[]{:S(2)}, u32[]{:S(2)}) collective-permute-start(bf16[686,256]{1,0:T(8,128)(2,1)} %get-tuple-element.75), channel_id=1, source_target_pairs={{0,3},{1,2},{2,1},{3,0},{4,7},{5,6},{6,5},{7,4},{8,11},{9,10},{10,... | collective-permute-start | bytes 1053704 | tf_op jit(solution)/shard_map/ppermute | solution.py:56
  90.5 22.9 %collective-permute-start.6 = (bf16[686,256]{1,0:T(8,128)(2,1)}, bf16[686,256]{1,0:T(8,128)(2,1)S(1)}, u32[]{:S(2)}, u32[]{:S(2)}) collective-permute-start(bf16[686,256]{1,0:T(8,128)(2,1)} %get-tuple-element.75), channel_id=1, source_target_pairs={{0,508},{1,509},{2,6},{3,7},{4,0},{5,1},{6,10},{7,11},{8,4},{9,5},... | collective-permute-start | bytes 1053704 | tf_op jit(solution)/shard_map/ppermute | solution.py:51
  113.4 0.7 copy-start.1
  118.4 18.0 %collective-permute-start.9 = (bf16[686,256]{1,0:T(8,128)(2,1)}, bf16[686,256]{1,0:T(8,128)(2,1)}, u32[]{:S(2)}, u32[]{:S(2)}) collective-permute-start(bf16[686,256]{1,0:T(8,128)(2,1)} %get-tuple-element.5), channel_id=1, source_target_pairs={{0,3},{1,2},{2,1},{3,0},{4,7},{5,6},{6,5},{7,4},{8,11},{9,10},{10,... | collective-permute-start | bytes 1053704 | tf_op jit(solution)/shard_map/ppermute | solution.py:56
  121.8 21.0 %collective-permute-start.8 = (bf16[686,256]{1,0:T(8,128)(2,1)}, bf16[686,256]{1,0:T(8,128)(2,1)}, u32[]{:S(2)}, u32[]{:S(2)}) collective-permute-start(bf16[686,256]{1,0:T(8,128)(2,1)} %get-tuple-element.5), channel_id=1, source_target_pairs={{0,508},{1,509},{2,6},{3,7},{4,0},{5,1},{6,10},{7,11},{8,4},{9,5},... | collective-permute-start | bytes 1053704 | tf_op jit(solution)/shard_map/ppermute | solution.py:51
  146.5 20.6 %collective-permute-start.12 = (bf16[686,256]{1,0:T(8,128)(2,1)S(1)}, bf16[686,256]{1,0:T(8,128)(2,1)S(1)}, u32[]{:S(2)}, u32[]{:S(2)}) collective-permute-start(bf16[686,256]{1,0:T(8,128)(2,1)S(1)} %fusion.31), channel_id=1, source_target_pairs={{0,3},{1,2},{2,1},{3,0},{4,7},{5,6},{6,5},{7,4},{8,11},{9,10},{10,... | collective-permute-start | bytes 1053704 | tf_op jit(solution)/shard_map/ppermute | solution.py:64
  149.4 22.1 %collective-permute-start.11 = (bf16[686,256]{1,0:T(8,128)(2,1)S(1)}, bf16[686,256]{1,0:T(8,128)(2,1)S(1)}, u32[]{:S(2)}, u32[]{:S(2)}) collective-permute-start(bf16[686,256]{1,0:T(8,128)(2,1)S(1)} %fusion.31), channel_id=1, source_target_pairs={{0,2},{1,3},{2,0},{3,1},{4,6},{5,7},{6,4},{7,5},{8,10},{9,11},{10,... | collective-permute-start | bytes 1053704 | tf_op jit(solution)/shard_map/ppermute | solution.py:64
  151.4 20.2 %collective-permute-start.10 = (bf16[686,256]{1,0:T(8,128)(2,1)S(1)}, bf16[686,256]{1,0:T(8,128)(2,1)S(1)}, u32[]{:S(2)}, u32[]{:S(2)}) collective-permute-start(bf16[686,256]{1,0:T(8,128)(2,1)S(1)} %fusion.31), channel_id=1, source_target_pairs={{0,1},{1,0},{2,3},{3,2},{4,5},{5,4},{6,7},{7,6},{8,9},{9,8},{10,11... | collective-permute-start | bytes 1053704 | tf_op jit(solution)/shard_map/ppermute | solution.py:64
  178.1 22.1 %collective-permute-start.14 = (bf16[686,256]{1,0:T(8,128)(2,1)}, bf16[686,256]{1,0:T(8,128)(2,1)}, u32[]{:S(2)}, u32[]{:S(2)}) collective-permute-start(bf16[686,256]{1,0:T(8,128)(2,1)} %get-tuple-element.77), channel_id=1, source_target_pairs={{0,3},{1,2},{2,1},{3,0},{4,7},{5,6},{6,5},{7,4},{8,11},{9,10},{10,... | collective-permute-start | bytes 1053704 | tf_op jit(solution)/shard_map/ppermute | solution.py:56
  181.1 25.5 %collective-permute-start.13 = (bf16[686,256]{1,0:T(8,128)(2,1)}, bf16[686,256]{1,0:T(8,128)(2,1)}, u32[]{:S(2)}, u32[]{:S(2)}) collective-permute-start(bf16[686,256]{1,0:T(8,128)(2,1)} %get-tuple-element.77), channel_id=1, source_target_pairs={{0,508},{1,509},{2,6},{3,7},{4,0},{5,1},{6,10},{7,11},{8,4},{9,5},... | collective-permute-start | bytes 1053704 | tf_op jit(solution)/shard_map/ppermute | solution.py:51

commit v2 on v1

v2 whole, which is shorter than its diff:
```python
import jax
import jax.numpy as jnp
from jax import lax
from jax.experimental import pallas as pl
from jax.experimental.pallas import tpu as pltpu
from jax.sharding import PartitionSpec as P


K = 14
STEPS = 2
NZ = 16
BOTH = ("cells", "vel")
ROWS = 686
PAD = 704
CHUNK = 88
PART = 2 * CHUNK
EDGE = 96
LANES = 128
RING = 16
F32 = jnp.float32
BF16 = jnp.bfloat16
PARAMS = pltpu.CompilerParams(vmem_limit_bytes=40 * 1024 * 1024)


def pairs_of(target):
    pairs = []
    for cell in range(128):
        for part in range(4):
            to_cell, to_part = target(cell, part)
            pairs.append((cell * 4 + part, to_cell * 4 + to_part))
    return pairs


def to_sibling(array):
    return lax.ppermute(array, BOTH, pairs_of(lambda cell, part: (cell ^ 1, part)))


def to_neighbour(array):
    def target(cell, part):
        other = (cell - 1 if cell % 2 == 0 else cell + 1) % 128
        return other, part if (other // RING) % 2 == (cell // RING) % 2 else 3 - part

    return lax.ppermute(array, BOTH, pairs_of(target))


def to_mirror(array):
    return lax.ppermute(array, "vel", [(i, 3 - i) for i in range(4)])


def to_side(array):
    return lax.ppermute(array, "vel", [(i, i ^ 1) for i in range(4)])


def call(kernel, outs, flags, *arrays, flops=0):
    moved = sum(x.size * x.dtype.itemsize for x in arrays)
    moved += sum(s[0] * s[1] * jnp.dtype(d).itemsize for s, d in outs)
    vmem = pl.BlockSpec(memory_space=pltpu.VMEM)
    result = pl.pallas_call(
        kernel,
        out_shape=[jax.ShapeDtypeStruct(shape, dtype) for shape, dtype in outs],
        in_specs=[pl.BlockSpec(memory_space=pltpu.SMEM)] + [vmem] * len(arrays),
        out_specs=[vmem] * len(outs),
        compiler_params=PARAMS,
        cost_estimate=pl.CostEstimate(flops=flops, bytes_accessed=moved, transcendentals=0),
    )(flags, *arrays)
    return result


def roll(values, shift):
    return pltpu.roll(values, shift % values.shape[1], 1)


def order_matrix(low):
    row = lax.broadcasted_iota(jnp.int32, (PAD, PAD), 0)
    column = lax.broadcasted_iota(jnp.int32, (PAD, PAD), 1)
    wanted = jnp.where(low, row, ROWS - 1 - row)
    return jnp.where((column == wanted) & (row < ROWS), 1.0, 0.0).astype(BF16)


def reordered(order, values):
    total = jnp.zeros(values.shape, F32)
    for _ in range(3):
        part = values.astype(BF16)
        total += jnp.dot(order, part, preferred_element_type=F32)
        values = values - part.astype(F32)
    return total


def terms(block, chunk):
    row = CHUNK * chunk + lax.broadcasted_iota(jnp.int32, (CHUNK, LANES), 0)
    ids = ROWS * block + row
    upper = (ids * 4682) >> 16
    k_z = ids - K * upper
    k_x = (upper * 4682) >> 16
    k_y = upper - K * k_x
    centre = (K - 1) / 2.0

    def factor(k):
        return jnp.abs(k.astype(F32) - centre) * (0.3 / centre)

    return (factor(k_x), factor(k_y), factor(k_z)), k_y >= K // 2, k_z >= K // 2


def lanes_of(rows):
    return lax.broadcasted_iota(jnp.int32, (rows, LANES), 1)


def lower_z(values):
    z_place = lax.broadcasted_iota(jnp.int32, values.shape, 1) % NZ
    return jnp.where(z_place == 0, roll(values, 1 - NZ), roll(values, 1))


def upper_z(values):
    z_place = lax.broadcasted_iota(jnp.int32, values.shape, 1) % NZ
    return jnp.where(z_place == NZ - 1, roll(values, NZ - 1), roll(values, -1))


def pack_edge(values, positive, chunk):
    edge = jnp.where(positive, roll(values, NZ), values)
    return jnp.where(lanes_of(CHUNK) // NZ == chunk, roll(edge, NZ * chunk), 0.0)


def edge_block(packed):
    return jnp.concatenate([packed, jnp.zeros((EDGE - CHUNK, LANES), F32)], axis=0).astype(BF16)


def prepare_kernel(flags, populations, solid, own, own_edge, message, masks):
    low, block, half = flags[0] == 1, flags[2], flags[3]
    ordered = reordered(order_matrix(low), populations[...])
    left, right = ordered[:, :LANES], ordered[:, LANES:]
    mine = jnp.where(half == 0, left, right)
    rest = jnp.where(half == 0, right, left)
    own[...] = mine
    edges = jnp.zeros((CHUNK, LANES), F32)
    sent = jnp.zeros((CHUNK, LANES), F32)
    for chunk in range(PAD // CHUNK):
        rows = slice(CHUNK * chunk, CHUNK * (chunk + 1))
        _, positive, _ = terms(block, chunk)
        positive = jnp.where(positive, 1, 0) == flags[0]
        edges += pack_edge(rest[rows], positive, chunk)
        sent += pack_edge(mine[rows], positive, chunk)
    own_edge[...] = edges
    message[:PAD] = rest.astype(BF16)
    message[PAD:] = edge_block(sent)
    fluid = jnp.where(jnp.broadcast_to(solid[...], (8, 2 * LANES)) == 0, 1.0, 0.0)
    place = lax.broadcasted_iota(jnp.int32, (8, 2 * LANES), 0)
    found = jnp.zeros((8, 2 * LANES), F32)
    near = (fluid, roll(fluid, NZ), roll(fluid, -NZ), lower_z(fluid), upper_z(fluid))
    for index, value in enumerate(near):
        found = jnp.where(place == index, value, found)
    masks[...] = jnp.where(half == 0, found[:, :LANES], found[:, LANES:])


def faces_kernel(flags, own, received, masks, sibling, neighbour):
    same = flags[0] == flags[1]
    row = lax.broadcasted_iota(jnp.int32, (16, LANES), 0)
    fluid = jnp.where(row == 0, jnp.broadcast_to(masks[0:1, :], (16, LANES)), 0.0).astype(BF16)
    mine, theirs = own[...], received[:PAD].astype(F32)
    sibling[:PAD] = jnp.where(same, theirs, mine).astype(BF16)
    neighbour[:PAD] = jnp.where(same, mine, theirs).astype(BF16)
    sibling[PAD:] = fluid
    neighbour[PAD:] = fluid


def half_stream(flags, a, b, sibling, neighbour, edge_a, edge_b, masks, emit):
    even = flags[1] == 1
    wide = [jnp.broadcast_to(masks[i : i + 1], (CHUNK, LANES)) for i in range(7)]
    fluid, open_y, open_z, open_x = wide[0], wide[1:3], wide[3:5], wide[5:7]
    lane = lanes_of(CHUNK)
    for part in range(PAD // PART):
        span = slice(PART * part, PART * (part + 1))
        part_a, part_b = a(span), b(span)
        near, far = sibling[span].astype(F32), neighbour[span].astype(F32)
        above, below = jnp.where(even, near, far), jnp.where(even, far, near)
        results = []
        for index in range(2):
            chunk = 2 * part + index
            rows = slice(CHUNK * index, CHUNK * (index + 1))
            factors, up_y, up_z = terms(flags[2], chunk)

            def one(values, mirror, layer, edge, up_y, up_z, open_here):
                put = jnp.where(up_y, roll(edge, -NZ * chunk), roll(edge, -NZ * (chunk + 1)))
                outside = (up_y & (lane < NZ)) | (~up_y & (lane >= LANES - NZ))
                near_y = jnp.where(up_y, roll(values, NZ), roll(values, -NZ))
                near_y = jnp.where(outside, put, near_y)
                near_z = jnp.where(up_z, lower_z(values), upper_z(values))
                upwind_x = jnp.where(open_here > 0, layer, mirror)
                upwind_y = jnp.where(jnp.where(up_y, *open_y) > 0, near_y, mirror)
                upwind_z = jnp.where(jnp.where(up_z, *open_z) > 0, near_z, mirror)
                outflow = factors[0] * (values - upwind_x)
                outflow += factors[1] * (values - upwind_y)
                outflow += factors[2] * (values - upwind_z)
                return (values - outflow) * fluid

            here_a, here_b = part_a[rows], part_b[rows]
            results.append(
                (
                    one(here_a, here_b, above[rows], edge_a, up_y, up_z, open_x[1]),
                    one(here_b, here_a, below[rows], edge_b, ~up_y, ~up_z, open_x[0]),
                    up_y,
                )
            )
        emit(part, results)


def joined(results, index):
    return jnp.concatenate([result[index] for result in results], axis=0)


def first_kernel(flags, own, own_edge, received, sibling, neighbour, masks_in, lowered, masks_out):
    low, even = flags[0] == 1, flags[1] == 1
    near, far = sibling[PAD:].astype(F32)[:1], neighbour[PAD:].astype(F32)[:1]
    place = lax.broadcasted_iota(jnp.int32, (8, LANES), 0)
    masks = masks_in[...]
    masks = jnp.where(place == 5, jnp.where(even, far, near), masks)
    masks = jnp.where(place == 6, jnp.where(even, near, far), masks)
    masks_out[...] = masks
    edge_own, edge_other = own_edge[...], received[PAD:].astype(F32)[:CHUNK]

    def emit(part, results):
        span = PART * part
        lowered[span : span + PART] = joined(results, 0).astype(BF16)
        lowered[PAD + span : PAD + span + PART] = joined(results, 1).astype(BF16)

    half_stream(
        flags,
        lambda span: jnp.where(low, own[span], received[span].astype(F32)),
        lambda span: jnp.where(low, received[span].astype(F32), own[span]),
        sibling,
        neighbour,
        jnp.where(low, edge_own, edge_other),
        jnp.where(low, edge_other, edge_own),
        masks,
        emit,
    )


class Sender:
    def __init__(self, flags, a, b, sibling, neighbour, edges):
        self.even = flags[1] == 1
        self.refs = a, b, sibling, neighbour
        self.edges = edges
        self.packed = [jnp.zeros((CHUNK, LANES), F32)] * 2

    def __call__(self, part, results):
        span = slice(PART * part, PART * (part + 1))
        a, b, sibling, neighbour = self.refs
        rows_a, rows_b = joined(results, 0), joined(results, 1)
        a[span], b[span] = rows_a, rows_b
        sibling[span] = jnp.where(self.even, rows_b, rows_a).astype(BF16)
        neighbour[span] = jnp.where(self.even, rows_a, rows_b).astype(BF16)
        for index, (chunk_a, chunk_b, up_y) in enumerate(results):
            self.packed[0] += pack_edge(chunk_a, up_y, 2 * part + index)
            self.packed[1] += pack_edge(chunk_b, ~up_y, 2 * part + index)
        if part == PAD // PART - 1:
            self.edges[:EDGE] = edge_block(self.packed[0])
            self.edges[EDGE:] = edge_block(self.packed[1])


def received_edges(edges):
    values = edges[...].astype(F32)
    return values[:CHUNK], values[EDGE : EDGE + CHUNK]


def between_kernel(flags, a, b, sibling, neighbour, edges, masks, *outs):
    emit = Sender(flags, *outs)
    half_stream(
        flags, lambda s: a[s], lambda s: b[s], sibling, neighbour, *received_edges(edges), masks[...], emit
    )


def lower_kernel(flags, a, b, sibling, neighbour, edges, masks, lowered):
    def emit(part, results):
        span = PART * part
        lowered[span : span + PART] = joined(results, 0).astype(BF16)
        lowered[PAD + span : PAD + span + PART] = joined(results, 1).astype(BF16)

    half_stream(
        flags, lambda s: a[s], lambda s: b[s], sibling, neighbour, *received_edges(edges), masks[...], emit
    )


def last_kernel(flags, a, b, sibling, neighbour, edges, masks, kept, message):
    low = flags[0] == 1

    def emit(part, results):
        span = slice(PART * part, PART * (part + 1))
        rows_a, rows_b = joined(results, 0), joined(results, 1)
        kept[span] = jnp.where(low, rows_a, rows_b)
        message[span] = jnp.where(low, rows_b, rows_a).astype(BF16)

    half_stream(
        flags, lambda s: a[s], lambda s: b[s], sibling, neighbour, *received_edges(edges), masks[...], emit
    )


def collide_kernel(flags, matrix, lowered, other, rows_out):
    swapped = flags[2] == 1
    first = jnp.where(swapped, other[...], lowered[...])
    second = jnp.where(swapped, lowered[...], other[...])
    for part in range(PAD // PART):
        span = slice(PART * part, PART * (part + 1))
        total = jnp.dot(matrix[span, : 2 * PAD], first, preferred_element_type=F32)
        total += jnp.dot(matrix[span, 2 * PAD :], second, preferred_element_type=F32)
        rows_out[span] = total


def collide_send_kernel(flags, own, mine, theirs, lowered, other, *outs):
    low = flags[0] == 1
    swapped = flags[2] != flags[4]
    first = jnp.where(swapped, other[...], lowered[...])
    second = jnp.where(swapped, lowered[...], other[...])
    emit = Sender(flags, *outs)
    for part in range(PAD // PART):
        span = slice(PART * part, PART * (part + 1))
        total = jnp.dot(mine[span], first, preferred_element_type=F32)
        total += jnp.dot(theirs[span], second, preferred_element_type=F32)
        own_rows = own[span]
        rows_a, rows_b = jnp.where(low, own_rows, total), jnp.where(low, total, own_rows)
        results = []
        for index in range(2):
            rows = slice(CHUNK * index, CHUNK * (index + 1))
            results.append((rows_a[rows], rows_b[rows], terms(flags[2], 2 * part + index)[1]))
        emit(part, results)


def reorder_kernel(flags, kept, ordered):
    ordered[...] = reordered(order_matrix(flags[0] == 1), kept[...])


def finish_kernel(flags, kept, received, evolved):
    order = order_matrix(flags[0] == 1)
    rest = jnp.dot(order, received[...], preferred_element_type=F32)
    mine = kept[...]
    half = flags[3]
    evolved[:, :LANES] = jnp.where(half == 0, mine, rest)[:ROWS]
    evolved[:, LANES:] = jnp.where(half == 0, rest, mine)[:ROWS]


def place(rows, columns, wanted):
    return (lax.broadcasted_iota(jnp.int32, (rows, columns), 0) == wanted[None, :]).astype(BF16)


def chosen(left, right):
    return jnp.dot(left, right, preferred_element_type=BF16)


def column_half(wide, block):
    column = lax.iota(jnp.int32, PAD)
    inside = column < ROWS
    start_a, start_b = 640 * block, jnp.where(block == 1, 1280, 2048)
    part_a = lax.dynamic_slice(wide, (0, start_a), (wide.shape[0], 768))
    part_b = lax.dynamic_slice(wide, (0, start_b), (wide.shape[0], 896))
    wanted_a = jnp.where(inside, ROWS * block + column - start_a, -1)
    wanted_b = jnp.where(inside, 4 * ROWS - 1 - ROWS * block - column - start_b + 768, -1)
    return chosen(
        jnp.concatenate([part_a, part_b], axis=1),
        place(768 + 896, 2 * PAD, jnp.concatenate([wanted_a, wanted_b])),
    )


def padded_columns(matrix):
    return jnp.pad(matrix, ((0, 0), (0, 2944 - matrix.shape[1])))


def per_device(populations, solid_mask, collision):
    cell, vel = lax.axis_index("cells"), lax.axis_index("vel")
    low = (vel < 2).astype(jnp.int32)
    core, z = cell % 2, cell // 2 % 8
    block = jnp.minimum(vel, 3 - vel)
    half = (1 - low) ^ (cell // RING % 2)
    flags = jnp.stack([low, 1 - core, block, half, core]).astype(jnp.int32)

    row = CHUNK * z + lax.iota(jnp.int32, CHUNK)
    wanted = jnp.where(row < ROWS, jnp.where(low == 1, row, ROWS - 1 - row), -1)
    window = chosen(place(ROWS, CHUNK, wanted).T, collision)
    piece = to_mirror(column_half(padded_columns(window), core))
    rings = [
        [(line * 8 + step) * 2 + side for step in range(8)] for line in range(8) for side in range(2)
    ]
    mine = lax.all_gather(piece, "cells", axis=0, tiled=True, axis_index_groups=rings)
    theirs = to_sibling(mine)

    padded = jnp.pad(populations[:, 0, :], ((0, PAD - ROWS), (0, 0)))
    own, own_edge, message, masks = call(
        prepare_kernel,
        [((PAD, LANES), F32), ((CHUNK, LANES), F32), ((PAD + EDGE, LANES), BF16), ((8, LANES), F32)],
        flags, padded, solid_mask, flops=2 * 3 * PAD * PAD * 256,
    )
    received = to_mirror(message)
    faces = [((PAD + 16, LANES), BF16)] * 2
    sibling, neighbour = call(faces_kernel, faces, flags, own, received, masks)
    neighbour, sibling = to_neighbour(neighbour), to_sibling(sibling)

    row = lax.iota(jnp.int32, PAD)
    wanted = jnp.where(row < ROWS, jnp.where(low == 1, row, ROWS - 1 - row), -1)
    ordered = padded_columns(chosen(place(ROWS, PAD, wanted).T, collision))
    matrix = jnp.concatenate([column_half(ordered, 0), column_half(ordered, 1)], axis=1)

    lowered, masks = call(
        first_kernel,
        [((2 * PAD, LANES), BF16), ((8, LANES), F32)],
        flags, own, own_edge, received, sibling, neighbour, masks, flops=100 * PAD * 256,
    )
    sends = [((PAD, LANES), F32)] * 2 + [((PAD, LANES), BF16)] * 2 + [((2 * EDGE, LANES), BF16)]
    multiply = 2 * PAD * 4 * PAD * LANES
    for step in range(STEPS):
        other = to_side(lowered)
        (own,) = call(
            collide_kernel, [((PAD, LANES), F32)], flags, matrix, lowered, other, flops=multiply
        )
        a, b, sibling, neighbour, edges = call(
            collide_send_kernel, sends, flags, own, mine, theirs, lowered, other, flops=multiply
        )
        near = to_neighbour(neighbour), to_mirror(edges), to_sibling(sibling)
        if step == STEPS - 1:
            break
        a, b, sibling, neighbour, edges = call(
            between_kernel, sends, flags, a, b, near[2], near[0], near[1], masks, flops=100 * PAD * 256
        )
        near = to_neighbour(neighbour), to_mirror(edges), to_sibling(sibling)
        (lowered,) = call(
            lower_kernel, [((2 * PAD, LANES), BF16)],
            flags, a, b, near[2], near[0], near[1], masks, flops=100 * PAD * 256,
        )
    kept, message = call(
        last_kernel, [((PAD, LANES), F32), ((PAD, LANES), BF16)],
        flags, a, b, near[2], near[0], near[1], masks, flops=100 * PAD * 256,
    )
    received = to_mirror(message)
    (kept,) = call(
        reorder_kernel, [((PAD, LANES), F32)], flags, kept, flops=2 * 3 * PAD * PAD * LANES
    )
    (evolved,) = call(
        finish_kernel, [((ROWS, 2 * LANES), F32)], flags, kept, received, flops=2 * PAD * PAD * LANES
    )
    return evolved[:, None, :]


def solution(mesh):
    in_specs = (P("vel", "cells", None), P("cells", None), P("vel", None))
    out_specs = P("vel", "cells", None)
    return jax.shard_map(
        per_device, mesh=mesh, in_specs=in_specs, out_specs=out_specs, check_vma=False
    )
```

time: 214 us -> 208 us (0.972)
  local copies, waits for them, and re-layouts: 54.6 us -> 4.22 us
  waiting for transfers between devices: 58.2 us -> 81.5 us
  Pallas kernels: 0 us -> 22.9 us
  other arithmetic: 21.8 us -> 0.53 us
  between operations: 0.35 us -> 13.8 us
  matrix products: 8.01 us -> 19.7 us
  starting transfers between devices: 68.9 us -> 64.2 us
    all_gather x0 -> x1, waiting for transfers between devices: none -> 35.6 us  [per_device(): lax.all_gather(piece, 'cells', axis=0, tiled=True, axis_index_groups=rings)]
    rev x4 -> x0, local copies, waits for them, and re-layouts: 23.1 us -> none  [stream(): mirror = jnp.flip(from_mirror(low), axis=0).astype(jnp.float32)]
    pallas_call x0 -> x12, Pallas kernels: none -> 22.9 us  [call(): pl.pallas_call(kernel, out_shape=[jax.ShapeDtypeStruct(shape, dtype) for...]
    slice x28 -> x0, local copies, waits for them, and re-layouts: 21.7 us -> none  [the longest x6 5.81 us: upper_z(): jnp.roll(values, -1, axis=-1)]
    convert_element_type x4 -> x0, other arithmetic: 13 us -> none  [the longest x2 7.99 us: per_device(): blocks = gathered(read.astype(jnp.bfloat16))]
    ppermute x15 -> x17, waiting for transfers between devices: 58.2 us -> 45.8 us  [the longest x6 25.3 us: to_mirror(): return lax.ppermute(array, 'vel', [(i, 3 - i) for i in range(4)])]
    dot_general x2 -> x5, matrix products: 8.01 us -> 19.7 us  [chosen(): return jnp.dot(left, right, preferred_element_type=BF16)]
    concatenate x4 -> x0, local copies, waits for them, and re-layouts: 5.42 us -> none  [the longest x2 4.7 us: per_device(): jnp.concatenate(blocks, axis=0)]
  transfers between devices with their start and end apart: 15 -> 18, of which waited for: 7 -> 11; matrix products, arithmetic and copies ran while one was open for 24% -> 8% of each run, Pallas kernels for 0% -> 4%
where the time goes in v2:
time: 208 us; the launch traced here: 207 us
  waiting for transfers between devices  81.5 us (39%)
  starting transfers between devices  64.2 us (31%)
  Pallas kernels  22.9 us (11%)
  matrix products  19.7 us (9%)
  between operations  13.8 us (7%)
  local copies, waits for them, and re-layouts  4.22 us (2%)
    all_gather x1, waiting for transfers between devices, per_device(): lax.all_gather(piece, 'cells', axis=0, tiled=True, axis_index_groups=rings)  35.6 us
    ppermute x4, starting transfers between devices, to_neighbour(): return lax.ppermute(array, BOTH, pairs_of(target))  27.7 us
    ppermute x6, waiting for transfers between devices, to_mirror(): return lax.ppermute(array, 'vel', [(i, 3 - i) for i in range(4)])  25.3 us
    pallas_call x12, Pallas kernels, call(): pl.pallas_call(kernel, out_shape=[jax.ShapeDtypeStruct(shape, dtype) for...  22.9 us
    ppermute x6, starting transfers between devices, to_mirror(): return lax.ppermute(array, 'vel', [(i, 3 - i) for i in range(4)])  20.9 us
    dot_general x5, matrix products, chosen(): return jnp.dot(left, right, preferred_element_type=BF16)  19.7 us
    ppermute x2, waiting for transfers between devices, to_side(): return lax.ppermute(array, 'vel', [(i, i ^ 1) for i in range(4)])  15.8 us
    ppermute x5, starting transfers between devices, to_sibling(): lax.ppermute(array, BOTH, pairs_of(lambda cell, part: (cell ^ 1, part)))  10.3 us
  transfers between devices with their start and end apart: 18, of which 11 were waited for; matrix products, arithmetic and copies ran while one was open for 8% of the time, Pallas kernels for 4%

profile of v2, /device:TPU:8, one launch (start us, length us, event | category | flops | bytes accessed | tf_op | source)
XLA Modules:
  0.0 206.9 jit_solution(1278320816085650672)
XLA Ops:
  6.5 2.9 %fusion.14 = bf16[88,2744]{1,0:T(8,128)(2,1)S(1)} fusion(bf16[686,2744]{1,0:T(8,128)(2,1)} %param.5, s32[88]{0:T(128)S(1)} %compare_select_fusion), kind=kOutput, calls=%fused_computation.24 | convolution fusion | flops 331359936 | bytes 4248064 | tf_op jit(solution)/shard_map/dot_general | solution.py:345
  11.6 3.5 %collective-permute-start.4 = (bf16[88,1408]{1,0:T(8,128)(2,1)S(1)}, bf16[88,1408]{1,0:T(8,128)(2,1)S(1)}, u32[]{:S(2)}, u32[]{:S(2)}) collective-permute-start(bf16[88,1408]{1,0:T(8,128)(2,1)S(1)} %fusion.2), channel_id=1, source_target_pairs={{0,3},{1,2},{2,1},{3,0},{4,7},{5,6},{6,5},{7,4},{8,11},{9,10},{10,... | collective-permute-start | bytes 743432 | tf_op jit(solution)/shard_map/ppermute | solution.py:47
  15.1 11.5 %collective-permute-done.4 = bf16[88,1408]{1,0:T(8,128)(2,1)S(1)} collective-permute-done((bf16[88,1408]{1,0:T(8,128)(2,1)S(1)}, bf16[88,1408]{1,0:T(8,128)(2,1)S(1)}, u32[]{:S(2)}, u32[]{:S(2)}) %collective-permute-start.4) | collective-permute-done | bytes 247840 | tf_op jit(solution)/shard_map/ppermute | solution.py:47
  29.4 3.5 %collective-permute-start = (bf16[800,128]{1,0:T(8,128)(2,1)S(1)}, bf16[800,128]{1,0:T(8,128)(2,1)S(1)}, u32[]{:S(2)}, u32[]{:S(2)}) collective-permute-start(bf16[800,128]{1,0:T(8,128)(2,1)S(1)} %get-tuple-element.32), channel_id=1, source_target_pairs={{0,3},{1,2},{2,1},{3,0},{4,7},{5,6},{6,5},{7,4},{8,11},{9,10},{10,... | collective-permute-start | bytes 614408 | tf_op jit(solution)/shard_map/ppermute | solution.py:47
  33.0 5.4 %fusion.12 = bf16[704,2744]{1,0:T(8,128)(2,1)S(1)} fusion(bf16[686,2744]{1,0:T(8,128)(2,1)} %param.5, s32[704]{0:T(1024)S(1)} %select_select_fusion), kind=kOutput, calls=%fused_computation.18 | convolution fusion | flops 2650879488 | bytes 7631136 | tf_op jit(solution)/shard_map/dot_general | solution.py:345
  40.1 35.6 %all-gather.2.cloned.1.call-done.mine = bf16[704,1408]{1,0:T(8,128)(2,1)} async-done(((bf16[88,1408]{1,0:T(8,128)(2,1)}), bf16[704,1408]{1,0:T(8,128)(2,1)}) %all-gather.2.cloned.1.call-update) | async-done | bytes 1982480 | tf_op jit(solution)/shard_map/all_gather | solution.py:381
  75.7 2.1 %collective-permute-start.5 = (bf16[704,1408]{1,0:T(8,128)(2,1)}, bf16[704,1408]{1,0:T(8,128)(2,1)S(1)}, u32[]{:S(2)}, u32[]{:S(2)}) collective-permute-start(bf16[704,1408]{1,0:T(8,128)(2,1)} %all-gather.2.cloned.1.call-done.mine), channel_id=1, source_target_pairs={{0,4},{1,5},{2,6},{3,7},{4,0},{5,1},{6,2},{7,3},{8,12},{9,13},{10,... | collective-permute-start | bytes 5947400 | tf_op jit(solution)/shard_map/ppermute | solution.py:35
  77.8 5.4 %fusion = bf16[704,1408]{1,0:T(8,128)(2,1)S(1)} fusion(s32[1408]{0:T(1024)S(1)} %pad_add_fusion, bf16[704,896]{1,0:T(8,128)(2,1)S(1)} %get-tuple-element.57, bf16[704,768]{1,0:T(8,128)(2,1)} %get-tuple-element.55), kind=kOutput, calls=%fused_computation.3 | convolution fusion | flops 3305848832 | bytes 4331008 | tf_op jit(solution)/shard_map/dot_general | solution.py:345
  83.9 2.4 %collective-permute-start.1 = (bf16[720,128]{1,0:T(8,128)(2,1)S(1)}, bf16[720,128]{1,0:T(8,128)(2,1)S(1)}, u32[]{:S(2)}, u32[]{:S(2)}) collective-permute-start(bf16[720,128]{1,0:T(8,128)(2,1)S(1)} %get-tuple-element.34), channel_id=1, source_target_pairs={{0,4},{1,5},{2,6},{3,7},{4,0},{5,1},{6,2},{7,3},{8,12},{9,13},{10,... | collective-permute-start | bytes 552968 | tf_op jit(solution)/shard_map/ppermute | solution.py:35
  86.3 8.3 %collective-permute-start.2 = (bf16[720,128]{1,0:T(8,128)(2,1)S(1)}, bf16[720,128]{1,0:T(8,128)(2,1)S(1)}, u32[]{:S(2)}, u32[]{:S(2)}) collective-permute-start(bf16[720,128]{1,0:T(8,128)(2,1)S(1)} %get-tuple-element.35), channel_id=1, source_target_pairs={{0,511},{1,510},{2,509},{3,508},{4,8},{5,9},{6,10},{7,11},{8,4},{9... | collective-permute-start | bytes 552968 | tf_op jit(solution)/shard_map/ppermute | solution.py:43
  94.6 4.1 %fusion.1 = bf16[704,1408]{1,0:T(8,128)(2,1)S(1)} fusion(s32[1408]{0:T(1024)S(1)} %pad_add_fusion.1, bf16[704,896]{1,0:T(8,128)(2,1)S(1)} %get-tuple-element.58, bf16[704,768]{1,0:T(8,128)(2,1)S(1)} %copy-done.2), kind=kOutput, calls=%fused_computation.4 | convolution fusion | flops 3305848832 | bytes 4331008 | tf_op jit(solution)/shard_map/dot_general | solution.py:345
  100.5 2.3 %shard_map.39 = (bf16[1408,128]{1,0:T(8,128)(2,1)S(1)}, f32[8,128]{1,0:T(8,128)S(1)}) custom-call(s32[5]{0:T(128)S(1)} %stack.23.flags, f32[704,128]{1,0:T(8,128)S(1)} %get-tuple-element.30.own, f32[88,128]{1,0:T(8,128)S(1)} %get-tuple-element.31.own_edge, bf16[800,128]{1,0:T(8,128)(2,1)S(1)} %collective-permute-done.received, ...), custom_call_target="tpu_custom_call" | custom-call | flops 18022400 | bytes 1347584 | tf_op jit(solution)/shard_map/pallas_call | solution.py:58
  102.7 2.7 %collective-permute-start.3 = (bf16[1408,128]{1,0:T(8,128)(2,1)S(1)}, bf16[1408,128]{1,0:T(8,128)(2,1)S(1)}, u32[]{:S(2)}, u32[]{:S(2)}) collective-permute-start(bf16[1408,128]{1,0:T(8,128)(2,1)S(1)} %get-tuple-element.36.lowered), channel_id=1, source_target_pairs={{0,1},{1,0},{2,3},{3,2},{4,5},{5,4},{6,7},{7,6},{8,9},{9,8},{10,11... | collective-permute-start | bytes 1081352 | tf_op jit(solution)/shard_map/ppermute | solution.py:51
  105.8 6.3 %collective-permute-done.3.other = bf16[1408,128]{1,0:T(8,128)(2,1)S(1)} collective-permute-done((bf16[1408,128]{1,0:T(8,128)(2,1)S(1)}, bf16[1408,128]{1,0:T(8,128)(2,1)S(1)}, u32[]{:S(2)}, u32[]{:S(2)}) %collective-permute-start.3) | collective-permute-done | bytes 360480 | tf_op jit(solution)/shard_map/ppermute | solution.py:51
  114.0 2.0 shard_map.41
  117.9 7.1 %collective-permute-start.7 = (bf16[704,128]{1,0:T(8,128)(2,1)S(1)}, bf16[704,128]{1,0:T(8,128)(2,1)S(1)}, u32[]{:S(2)}, u32[]{:S(2)}) collective-permute-start(bf16[704,128]{1,0:T(8,128)(2,1)S(1)} %get-tuple-element.40), channel_id=1, source_target_pairs={{0,511},{1,510},{2,509},{3,508},{4,8},{5,9},{6,10},{7,11},{8,4},{9... | collective-permute-start | bytes 540680 | tf_op jit(solution)/shard_map/ppermute | solution.py:43
  125.1 3.3 %collective-permute-start.8 = (bf16[192,128]{1,0:T(8,128)(2,1)S(1)}, bf16[192,128]{1,0:T(8,128)(2,1)S(1)}, u32[]{:S(2)}, u32[]{:S(2)}) collective-permute-start(bf16[192,128]{1,0:T(8,128)(2,1)S(1)} %get-tuple-element.41), channel_id=1, source_target_pairs={{0,3},{1,2},{2,1},{3,0},{4,7},{5,6},{6,5},{7,4},{8,11},{9,10},{10,... | collective-permute-start | bytes 147464 | tf_op jit(solution)/shard_map/ppermute | solution.py:47
  128.4 3.2 %collective-permute-done.8.edges = bf16[192,128]{1,0:T(8,128)(2,1)S(1)} collective-permute-done((bf16[192,128]{1,0:T(8,128)(2,1)S(1)}, bf16[192,128]{1,0:T(8,128)(2,1)S(1)}, u32[]{:S(2)}, u32[]{:S(2)}) %collective-permute-start.8) | collective-permute-done | bytes 49184 | tf_op jit(solution)/shard_map/ppermute | solution.py:47
  132.5 3.3 %shard_map.42 = (f32[704,128]{1,0:T(8,128)S(1)}, f32[704,128]{1,0:T(8,128)S(1)}, bf16[704,128]{1,0:T(8,128)(2,1)S(1)}, bf16[704,128]{1,0:T(8,128)(2,1)S(1)}, bf16[192,128]{1,0:T(8,128)(2,1)S(1)}) custom-call(s32[5]{0:T(128)S(1)} %stack.23.flags, f32[704,128]{1,0:T(8,128)S(1)} %get-tuple-element.37.a, f32[704,128]{1,0:T(8,128)S(1)} %get-tuple-element.38.b, ...), custom_call_target="tpu_custom_call" | custom-call | flops 18022400 | bytes 2265088 | tf_op jit(solution)/shard_map/pallas_call | solution.py:58
  135.9 6.7 %collective-permute-start.10 = (bf16[704,128]{1,0:T(8,128)(2,1)S(1)}, bf16[704,128]{1,0:T(8,128)(2,1)S(1)}, u32[]{:S(2)}, u32[]{:S(2)}) collective-permute-start(bf16[704,128]{1,0:T(8,128)(2,1)S(1)} %get-tuple-element.46), channel_id=1, source_target_pairs={{0,511},{1,510},{2,509},{3,508},{4,8},{5,9},{6,10},{7,11},{8,4},{9... | collective-permute-start | bytes 540680 | tf_op jit(solution)/shard_map/ppermute | solution.py:43
  144.5 3.5 %collective-permute-start.11 = (bf16[192,128]{1,0:T(8,128)(2,1)S(1)}, bf16[192,128]{1,0:T(8,128)(2,1)S(1)}, u32[]{:S(2)}, u32[]{:S(2)}) collective-permute-start(bf16[192,128]{1,0:T(8,128)(2,1)S(1)} %get-tuple-element.47), channel_id=1, source_target_pairs={{0,3},{1,2},{2,1},{3,0},{4,7},{5,6},{6,5},{7,4},{8,11},{9,10},{10,... | collective-permute-start | bytes 147464 | tf_op jit(solution)/shard_map/ppermute | solution.py:47
  148.0 3.6 %collective-permute-done.11.edges = bf16[192,128]{1,0:T(8,128)(2,1)S(1)} collective-permute-done((bf16[192,128]{1,0:T(8,128)(2,1)S(1)}, bf16[192,128]{1,0:T(8,128)(2,1)S(1)}, u32[]{:S(2)}, u32[]{:S(2)}) %collective-permute-start.11) | collective-permute-done | bytes 49184 | tf_op jit(solution)/shard_map/ppermute | solution.py:47
  151.6 2.2 %shard_map.43.lowered = bf16[1408,128]{1,0:T(8,128)(2,1)S(1)} custom-call(s32[5]{0:T(128)S(1)} %stack.23.flags, f32[704,128]{1,0:T(8,128)S(1)} %get-tuple-element.43.a, f32[704,128]{1,0:T(8,128)S(1)} %get-tuple-element.44.b, bf16[704,128]{1,0:T(8,128)(2,1)S(1)} %collective-permute-done.9.sibling, bf16[704,128]{1,0:T(8,128)(2,1)S(1)} %collective-permute-done.10.neighbour, ...), custom_call_target="tpu_custom_call" | custom-call | flops 18022400 | bytes 1495040 | tf_op jit(solution)/shard_map/pallas_call | solution.py:58
  153.8 2.5 %collective-permute-start.12 = (bf16[1408,128]{1,0:T(8,128)(2,1)S(1)}, bf16[1408,128]{1,0:T(8,128)(2,1)S(1)}, u32[]{:S(2)}, u32[]{:S(2)}) collective-permute-start(bf16[1408,128]{1,0:T(8,128)(2,1)S(1)} %shard_map.43.lowered), channel_id=1, source_target_pairs={{0,1},{1,0},{2,3},{3,2},{4,5},{5,4},{6,7},{7,6},{8,9},{9,8},{10,11... | collective-permute-start | bytes 1081352 | tf_op jit(solution)/shard_map/ppermute | solution.py:51
  156.4 9.6 %collective-permute-done.12.other = bf16[1408,128]{1,0:T(8,128)(2,1)S(1)} collective-permute-done((bf16[1408,128]{1,0:T(8,128)(2,1)S(1)}, bf16[1408,128]{1,0:T(8,128)(2,1)S(1)}, u32[]{:S(2)}, u32[]{:S(2)}) %collective-permute-start.12) | collective-permute-done | bytes 360480 | tf_op jit(solution)/shard_map/ppermute | solution.py:51
  167.8 2.0 shard_map.45
  171.8 5.7 %collective-permute-start.14 = (bf16[704,128]{1,0:T(8,128)(2,1)S(1)}, bf16[704,128]{1,0:T(8,128)(2,1)S(1)}, u32[]{:S(2)}, u32[]{:S(2)}) collective-permute-start(bf16[704,128]{1,0:T(8,128)(2,1)S(1)} %get-tuple-element.51), channel_id=1, source_target_pairs={{0,511},{1,510},{2,509},{3,508},{4,8},{5,9},{6,10},{7,11},{8,4},{9... | collective-permute-start | bytes 540680 | tf_op jit(solution)/shard_map/ppermute | solution.py:43
  177.5 3.8 %collective-permute-start.15 = (bf16[192,128]{1,0:T(8,128)(2,1)S(1)}, bf16[192,128]{1,0:T(8,128)(2,1)S(1)}, u32[]{:S(2)}, u32[]{:S(2)}) collective-permute-start(bf16[192,128]{1,0:T(8,128)(2,1)S(1)} %get-tuple-element.52), channel_id=1, source_target_pairs={{0,3},{1,2},{2,1},{3,0},{4,7},{5,6},{6,5},{7,4},{8,11},{9,10},{10,... | collective-permute-start | bytes 147464 | tf_op jit(solution)/shard_map/ppermute | solution.py:47
  181.3 2.7 %collective-permute-done.15.edges = bf16[192,128]{1,0:T(8,128)(2,1)S(1)} collective-permute-done((bf16[192,128]{1,0:T(8,128)(2,1)S(1)}, bf16[192,128]{1,0:T(8,128)(2,1)S(1)}, u32[]{:S(2)}, u32[]{:S(2)}) %collective-permute-start.15) | collective-permute-done | bytes 49184 | tf_op jit(solution)/shard_map/ppermute | solution.py:47
  185.8 2.3 %shard_map.46 = (f32[704,128]{1,0:T(8,128)S(1)}, bf16[704,128]{1,0:T(8,128)(2,1)S(1)}) custom-call(s32[5]{0:T(128)S(1)} %stack.23.flags, f32[704,128]{1,0:T(8,128)S(1)} %get-tuple-element.48.a, f32[704,128]{1,0:T(8,128)S(1)} %get-tuple-element.49.b, bf16[704,128]{1,0:T(8,128)(2,1)S(1)} %collective-permute-done.13.sibling, ...), custom_call_target="tpu_custom_call" | custom-call | flops 18022400 | bytes 1675264 | tf_op jit(solution)/shard_map/pallas_call | solution.py:58
  188.1 3.3 %collective-permute-start.16 = (bf16[704,128]{1,0:T(8,128)(2,1)S(1)}, bf16[704,128]{1,0:T(8,128)(2,1)S(1)}, u32[]{:S(2)}, u32[]{:S(2)}) collective-permute-start(bf16[704,128]{1,0:T(8,128)(2,1)S(1)} %get-tuple-element.54), channel_id=1, source_target_pairs={{0,3},{1,2},{2,1},{3,0},{4,7},{5,6},{6,5},{7,4},{8,11},{9,10},{10,... | collective-permute-start | bytes 540680 | tf_op jit(solution)/shard_map/ppermute | solution.py:47
  193.0 4.4 %collective-permute-done.16.received = bf16[704,128]{1,0:T(8,128)(2,1)S(1)} collective-permute-done((bf16[704,128]{1,0:T(8,128)(2,1)S(1)}, bf16[704,128]{1,0:T(8,128)(2,1)S(1)}, u32[]{:S(2)}, u32[]{:S(2)}) %collective-permute-start.16) | collective-permute-done | bytes 180256 | tf_op jit(solution)/shard_map/ppermute | solution.py:47
  (49 shorter events, 25.8 us)
Async XLA Ops:
  6.5 69.1 %all-gather.2.cloned.1.call-start = ((), (), s32[]{:S(2)}) async-start(), calls=%async_computation | async-start | bytes 2230272 | tf_op jit(solution)/shard_map/all_gather | solution.py:381
  9.6 17.8 %copy-start.3 = (f32[686,1,256]{2,1,0:T(1,128)S(1)}, f32[686,1,256]{2,1,0:T(1,128)}, u32[]{:S(2)}) copy-start(f32[686,1,256]{2,1,0:T(1,128)} %param.3) | copy-start | bytes 2107396
  11.6 15.9 %copy-start.1 = (s32[1,256]{1,0:T(1,128)S(1)}, s32[1,256]{1,0:T(1,128)}, u32[]{:S(2)}) copy-start(s32[1,256]{1,0:T(1,128)} %solid.1) | copy-start | bytes 3076
  11.6 14.9 %collective-permute-start.4 = (bf16[88,1408]{1,0:T(8,128)(2,1)S(1)}, bf16[88,1408]{1,0:T(8,128)(2,1)S(1)}, u32[]{:S(2)}, u32[]{:S(2)}) collective-permute-start(bf16[88,1408]{1,0:T(8,128)(2,1)S(1)} %fusion.2), channel_id=1, source_target_pairs={{0,3},{1,2},{2,1},{3,0},{4,7},{5,6},{6,5},{7,4},{8,11},{9,10},{10,... | collective-permute-start | bytes 743432 | tf_op jit(solution)/shard_map/ppermute | solution.py:47
  26.6 0.7 copy-start.4
  29.4 53.9 %collective-permute-start = (bf16[800,128]{1,0:T(8,128)(2,1)S(1)}, bf16[800,128]{1,0:T(8,128)(2,1)S(1)}, u32[]{:S(2)}, u32[]{:S(2)}) collective-permute-start(bf16[800,128]{1,0:T(8,128)(2,1)S(1)} %get-tuple-element.32), channel_id=1, source_target_pairs={{0,3},{1,2},{2,1},{3,0},{4,7},{5,6},{6,5},{7,4},{8,11},{9,10},{10,... | collective-permute-start | bytes 614408 | tf_op jit(solution)/shard_map/ppermute | solution.py:47
  75.7 38.3 %collective-permute-start.5 = (bf16[704,1408]{1,0:T(8,128)(2,1)}, bf16[704,1408]{1,0:T(8,128)(2,1)S(1)}, u32[]{:S(2)}, u32[]{:S(2)}) collective-permute-start(bf16[704,1408]{1,0:T(8,128)(2,1)} %all-gather.2.cloned.1.call-done.mine), channel_id=1, source_target_pairs={{0,4},{1,5},{2,6},{3,7},{4,0},{5,1},{6,2},{7,3},{8,12},{9,13},{10,... | collective-permute-start | bytes 5947400 | tf_op jit(solution)/shard_map/ppermute | solution.py:35
  77.8 16.8 %copy-start.2 = (bf16[704,768]{1,0:T(8,128)(2,1)S(1)}, bf16[704,768]{1,0:T(8,128)(2,1)}, u32[]{:S(2)}) copy-start(bf16[704,768]{1,0:T(8,128)(2,1)} %get-tuple-element.56) | copy-start | bytes 3244036
  83.9 14.8 %collective-permute-start.1 = (bf16[720,128]{1,0:T(8,128)(2,1)S(1)}, bf16[720,128]{1,0:T(8,128)(2,1)S(1)}, u32[]{:S(2)}, u32[]{:S(2)}) collective-permute-start(bf16[720,128]{1,0:T(8,128)(2,1)S(1)} %get-tuple-element.34), channel_id=1, source_target_pairs={{0,4},{1,5},{2,6},{3,7},{4,0},{5,1},{6,2},{7,3},{8,12},{9,13},{10,... | collective-permute-start | bytes 552968 | tf_op jit(solution)/shard_map/ppermute | solution.py:35
  86.3 14.2 %collective-permute-start.2 = (bf16[720,128]{1,0:T(8,128)(2,1)S(1)}, bf16[720,128]{1,0:T(8,128)(2,1)S(1)}, u32[]{:S(2)}, u32[]{:S(2)}) collective-permute-start(bf16[720,128]{1,0:T(8,128)(2,1)S(1)} %get-tuple-element.35), channel_id=1, source_target_pairs={{0,511},{1,510},{2,509},{3,508},{4,8},{5,9},{6,10},{7,11},{8,4},{9... | collective-permute-start | bytes 552968 | tf_op jit(solution)/shard_map/ppermute | solution.py:43
  102.7 9.3 %collective-permute-start.3 = (bf16[1408,128]{1,0:T(8,128)(2,1)S(1)}, bf16[1408,128]{1,0:T(8,128)(2,1)S(1)}, u32[]{:S(2)}, u32[]{:S(2)}) collective-permute-start(bf16[1408,128]{1,0:T(8,128)(2,1)S(1)} %get-tuple-element.36.lowered), channel_id=1, source_target_pairs={{0,1},{1,0},{2,3},{3,2},{4,5},{5,4},{6,7},{7,6},{8,9},{9,8},{10,11... | collective-permute-start | bytes 1081352 | tf_op jit(solution)/shard_map/ppermute | solution.py:51
  105.8 8.2 %copy-start = (bf16[704,1408]{1,0:T(8,128)(2,1)S(1)}, bf16[704,1408]{1,0:T(8,128)(2,1)}, u32[]{:S(2)}) copy-start(bf16[704,1408]{1,0:T(8,128)(2,1)} %all-gather.2.cloned.1.call-done.mine) | copy-start | bytes 5947396
  116.0 15.6 %collective-permute-start.6 = (bf16[704,128]{1,0:T(8,128)(2,1)S(1)}, bf16[704,128]{1,0:T(8,128)(2,1)S(1)}, u32[]{:S(2)}, u32[]{:S(2)}) collective-permute-start(bf16[704,128]{1,0:T(8,128)(2,1)S(1)} %get-tuple-element.39), channel_id=1, source_target_pairs={{0,4},{1,5},{2,6},{3,7},{4,0},{5,1},{6,2},{7,3},{8,12},{9,13},{10,... | collective-permute-start | bytes 540680 | tf_op jit(solution)/shard_map/ppermute | solution.py:35
  117.9 14.6 %collective-permute-start.7 = (bf16[704,128]{1,0:T(8,128)(2,1)S(1)}, bf16[704,128]{1,0:T(8,128)(2,1)S(1)}, u32[]{:S(2)}, u32[]{:S(2)}) collective-permute-start(bf16[704,128]{1,0:T(8,128)(2,1)S(1)} %get-tuple-element.40), channel_id=1, source_target_pairs={{0,511},{1,510},{2,509},{3,508},{4,8},{5,9},{6,10},{7,11},{8,4},{9... | collective-permute-start | bytes 540680 | tf_op jit(solution)/shard_map/ppermute | solution.py:43
  125.1 6.5 %collective-permute-start.8 = (bf16[192,128]{1,0:T(8,128)(2,1)S(1)}, bf16[192,128]{1,0:T(8,128)(2,1)S(1)}, u32[]{:S(2)}, u32[]{:S(2)}) collective-permute-start(bf16[192,128]{1,0:T(8,128)(2,1)S(1)} %get-tuple-element.41), channel_id=1, source_target_pairs={{0,3},{1,2},{2,1},{3,0},{4,7},{5,6},{6,5},{7,4},{8,11},{9,10},{10,... | collective-permute-start | bytes 147464 | tf_op jit(solution)/shard_map/ppermute | solution.py:47
  135.9 15.7 %collective-permute-start.10 = (bf16[704,128]{1,0:T(8,128)(2,1)S(1)}, bf16[704,128]{1,0:T(8,128)(2,1)S(1)}, u32[]{:S(2)}, u32[]{:S(2)}) collective-permute-start(bf16[704,128]{1,0:T(8,128)(2,1)S(1)} %get-tuple-element.46), channel_id=1, source_target_pairs={{0,511},{1,510},{2,509},{3,508},{4,8},{5,9},{6,10},{7,11},{8,4},{9... | collective-permute-start | bytes 540680 | tf_op jit(solution)/shard_map/ppermute | solution.py:43
  142.5 9.0 %collective-permute-start.9 = (bf16[704,128]{1,0:T(8,128)(2,1)S(1)}, bf16[704,128]{1,0:T(8,128)(2,1)S(1)}, u32[]{:S(2)}, u32[]{:S(2)}) collective-permute-start(bf16[704,128]{1,0:T(8,128)(2,1)S(1)} %get-tuple-element.45), channel_id=1, source_target_pairs={{0,4},{1,5},{2,6},{3,7},{4,0},{5,1},{6,2},{7,3},{8,12},{9,13},{10,... | collective-permute-start | bytes 540680 | tf_op jit(solution)/shard_map/ppermute | solution.py:35
  144.5 7.1 %collective-permute-start.11 = (bf16[192,128]{1,0:T(8,128)(2,1)S(1)}, bf16[192,128]{1,0:T(8,128)(2,1)S(1)}, u32[]{:S(2)}, u32[]{:S(2)}) collective-permute-start(bf16[192,128]{1,0:T(8,128)(2,1)S(1)} %get-tuple-element.47), channel_id=1, source_target_pairs={{0,3},{1,2},{2,1},{3,0},{4,7},{5,6},{6,5},{7,4},{8,11},{9,10},{10,... | collective-permute-start | bytes 147464 | tf_op jit(solution)/shard_map/ppermute | solution.py:47
  153.8 12.1 %collective-permute-start.12 = (bf16[1408,128]{1,0:T(8,128)(2,1)S(1)}, bf16[1408,128]{1,0:T(8,128)(2,1)S(1)}, u32[]{:S(2)}, u32[]{:S(2)}) collective-permute-start(bf16[1408,128]{1,0:T(8,128)(2,1)S(1)} %shard_map.43.lowered), channel_id=1, source_target_pairs={{0,1},{1,0},{2,3},{3,2},{4,5},{5,4},{6,7},{7,6},{8,9},{9,8},{10,11... | collective-permute-start | bytes 1081352 | tf_op jit(solution)/shard_map/ppermute | solution.py:51
  169.8 14.2 %collective-permute-start.13 = (bf16[704,128]{1,0:T(8,128)(2,1)S(1)}, bf16[704,128]{1,0:T(8,128)(2,1)S(1)}, u32[]{:S(2)}, u32[]{:S(2)}) collective-permute-start(bf16[704,128]{1,0:T(8,128)(2,1)S(1)} %get-tuple-element.50), channel_id=1, source_target_pairs={{0,4},{1,5},{2,6},{3,7},{4,0},{5,1},{6,2},{7,3},{8,12},{9,13},{10,... | collective-permute-start | bytes 540680 | tf_op jit(solution)/shard_map/ppermute | solution.py:35
  171.8 14.0 %collective-permute-start.14 = (bf16[704,128]{1,0:T(8,128)(2,1)S(1)}, bf16[704,128]{1,0:T(8,128)(2,1)S(1)}, u32[]{:S(2)}, u32[]{:S(2)}) collective-permute-start(bf16[704,128]{1,0:T(8,128)(2,1)S(1)} %get-tuple-element.51), channel_id=1, source_target_pairs={{0,511},{1,510},{2,509},{3,508},{4,8},{5,9},{6,10},{7,11},{8,4},{9... | collective-permute-start | bytes 540680 | tf_op jit(solution)/shard_map/ppermute | solution.py:43
  177.5 6.5 %collective-permute-start.15 = (bf16[192,128]{1,0:T(8,128)(2,1)S(1)}, bf16[192,128]{1,0:T(8,128)(2,1)S(1)}, u32[]{:S(2)}, u32[]{:S(2)}) collective-permute-start(bf16[192,128]{1,0:T(8,128)(2,1)S(1)} %get-tuple-element.52), channel_id=1, source_target_pairs={{0,3},{1,2},{2,1},{3,0},{4,7},{5,6},{6,5},{7,4},{8,11},{9,10},{10,... | collective-permute-start | bytes 147464 | tf_op jit(solution)/shard_map/ppermute | solution.py:47
  188.1 9.3 %collective-permute-start.16 = (bf16[704,128]{1,0:T(8,128)(2,1)S(1)}, bf16[704,128]{1,0:T(8,128)(2,1)S(1)}, u32[]{:S(2)}, u32[]{:S(2)}) collective-permute-start(bf16[704,128]{1,0:T(8,128)(2,1)S(1)} %get-tuple-element.54), channel_id=1, source_target_pairs={{0,3},{1,2},{2,1},{3,0},{4,7},{5,6},{6,5},{7,4},{8,11},{9,10},{10,... | collective-permute-start | bytes 540680 | tf_op jit(solution)/shard_map/ppermute | solution.py:47
Sparse Core Ops, SparseCore 0:
  27.4 48.2 all-gather.1

commit v3 on v2

--- a/solution.py
+++ b/solution.py
@@ -1,3 +1,5 @@
+import math
+
 import jax
 import jax.numpy as jnp
 from jax import lax
@@ -53,7 +55,7 @@
 
 def call(kernel, outs, flags, *arrays, flops=0):
     moved = sum(x.size * x.dtype.itemsize for x in arrays)
-    moved += sum(s[0] * s[1] * jnp.dtype(d).itemsize for s, d in outs)
+    moved += sum(math.prod(shape) * jnp.dtype(dtype).itemsize for shape, dtype in outs)
     vmem = pl.BlockSpec(memory_space=pltpu.VMEM)
     result = pl.pallas_call(
         kernel,
@@ -86,7 +88,7 @@
     return total
 
 
-def terms(block, chunk):
+def signed_factors(block, chunk):
     row = CHUNK * chunk + lax.broadcasted_iota(jnp.int32, (CHUNK, LANES), 0)
     ids = ROWS * block + row
     upper = (ids * 4682) >> 16
@@ -94,11 +96,8 @@
     k_x = (upper * 4682) >> 16
     k_y = upper - K * k_x
     centre = (K - 1) / 2.0
-
-    def factor(k):
-        return jnp.abs(k.astype(F32) - centre) * (0.3 / centre)
-
-    return (factor(k_x), factor(k_y), factor(k_z)), k_y >= K // 2, k_z >= K // 2
+    x, y, z = ((k.astype(F32) - centre) * (0.3 / centre) for k in (k_x, k_y, k_z))
+    return jnp.abs(x), y, z
 
 
 def lanes_of(rows):
@@ -115,16 +114,21 @@
     return jnp.where(z_place == NZ - 1, roll(values, NZ - 1), roll(values, -1))
 
 
-def pack_edge(values, positive, chunk):
-    edge = jnp.where(positive, roll(values, NZ), values)
-    return jnp.where(lanes_of(CHUNK) // NZ == chunk, roll(edge, NZ * chunk), 0.0)
+def picked(values, lanes):
+    return jnp.take_along_axis(values, lanes, axis=1, mode="promise_in_bounds")
+
+
+def pack_edge(packed, values, positive, chunk, lane):
+    place = lane & (NZ - 1)
+    edge = picked(values, jnp.where(positive, place + LANES - NZ, place))
+    return jnp.where((lane >> 4) == chunk, edge, packed)
 
 
 def edge_block(packed):
     return jnp.concatenate([packed, jnp.zeros((EDGE - CHUNK, LANES), F32)], axis=0).astype(BF16)
 
 
-def prepare_kernel(flags, populations, solid, own, own_edge, message, masks):
+def prepare_kernel(flags, populations, solid, own, own_edge, message, masks, factors):
     low, block, half = flags[0] == 1, flags[2], flags[3]
     ordered = reordered(order_matrix(low), populations[...])
     left, right = ordered[:, :LANES], ordered[:, LANES:]
@@ -133,12 +137,14 @@
     own[...] = mine
     edges = jnp.zeros((CHUNK, LANES), F32)
     sent = jnp.zeros((CHUNK, LANES), F32)
+    lane = lanes_of(CHUNK)
     for chunk in range(PAD // CHUNK):
         rows = slice(CHUNK * chunk, CHUNK * (chunk + 1))
-        _, positive, _ = terms(block, chunk)
-        positive = jnp.where(positive, 1, 0) == flags[0]
-        edges += pack_edge(rest[rows], positive, chunk)
-        sent += pack_edge(mine[rows], positive, chunk)
+        x, y, z = signed_factors(block, chunk)
+        factors[0, rows], factors[1, rows], factors[2, rows] = x, y, z
+        positive = jnp.where(low, y, -y) > 0
+        edges = pack_edge(edges, rest[rows], positive, chunk, lane)
+        sent = pack_edge(sent, mine[rows], positive, chunk, lane)
     own_edge[...] = edges
     message[:PAD] = rest.astype(BF16)
     message[PAD:] = edge_block(sent)
@@ -162,11 +168,33 @@
     neighbour[PAD:] = fluid
 
 
-def half_stream(flags, a, b, sibling, neighbour, edge_a, edge_b, masks, emit):
+def half_stream(flags, a, b, sibling, neighbour, edge_a, edge_b, masks, factors, emit):
     even = flags[1] == 1
     wide = [jnp.broadcast_to(masks[i : i + 1], (CHUNK, LANES)) for i in range(7)]
     fluid, open_y, open_z, open_x = wide[0], wide[1:3], wide[3:5], wide[5:7]
     lane = lanes_of(CHUNK)
+    z_place = lane & (NZ - 1)
+    below_z = jnp.where(z_place == 0, lane + NZ - 1, lane - 1)
+    above_z = jnp.where(z_place == NZ - 1, lane + 1 - NZ, lane + 1)
+    below_y, above_y = (lane + LANES - NZ) & (LANES - 1), (lane + NZ) & (LANES - 1)
+    first_y, last_y = lane < NZ, lane >= LANES - NZ
+
+    def one(values, mirror, layer, edge, chunk, up_y, up_z, sizes, open_here):
+        lane_y = jnp.where(up_y, below_y, above_y)
+        lane_z = jnp.where(up_z, below_z, above_z)
+        at_edge = jnp.where(up_y, lane, lane + NZ)
+        put = picked(edge, (at_edge + NZ * chunk) & (LANES - 1))
+        outside = (up_y & first_y) | (~up_y & last_y)
+        near_y = jnp.where(outside, put, picked(values, lane_y))
+        near_z = picked(values, lane_z)
+        upwind_x = jnp.where(open_here > 0, layer, mirror)
+        upwind_y = jnp.where(jnp.where(up_y, *open_y) > 0, near_y, mirror)
+        upwind_z = jnp.where(jnp.where(up_z, *open_z) > 0, near_z, mirror)
+        outflow = sizes[0] * (values - upwind_x)
+        outflow += sizes[1] * (values - upwind_y)
+        outflow += sizes[2] * (values - upwind_z)
+        return (values - outflow) * fluid
+
     for part in range(PAD // PART):
         span = slice(PART * part, PART * (part + 1))
         part_a, part_b = a(span), b(span)
@@ -176,28 +204,14 @@
         for index in range(2):
             chunk = 2 * part + index
             rows = slice(CHUNK * index, CHUNK * (index + 1))
-            factors, up_y, up_z = terms(flags[2], chunk)
-
-            def one(values, mirror, layer, edge, up_y, up_z, open_here):
-                put = jnp.where(up_y, roll(edge, -NZ * chunk), roll(edge, -NZ * (chunk + 1)))
-                outside = (up_y & (lane < NZ)) | (~up_y & (lane >= LANES - NZ))
-                near_y = jnp.where(up_y, roll(values, NZ), roll(values, -NZ))
-                near_y = jnp.where(outside, put, near_y)
-                near_z = jnp.where(up_z, lower_z(values), upper_z(values))
-                upwind_x = jnp.where(open_here > 0, layer, mirror)
-                upwind_y = jnp.where(jnp.where(up_y, *open_y) > 0, near_y, mirror)
-                upwind_z = jnp.where(jnp.where(up_z, *open_z) > 0, near_z, mirror)
-                outflow = factors[0] * (values - upwind_x)
-                outflow += factors[1] * (values - upwind_y)
-                outflow += factors[2] * (values - upwind_z)
-                return (values - outflow) * fluid
-
+            x, y, z = (factors[i, CHUNK * chunk : CHUNK * (chunk + 1)] for i in range(3))
+            sizes = x, jnp.abs(y), jnp.abs(z)
             here_a, here_b = part_a[rows], part_b[rows]
             results.append(
                 (
-                    one(here_a, here_b, above[rows], edge_a, up_y, up_z, open_x[1]),
-                    one(here_b, here_a, below[rows], edge_b, ~up_y, ~up_z, open_x[0]),
-                    up_y,
+                    one(here_a, here_b, above[rows], edge_a, chunk, y > 0, z > 0, sizes, open_x[1]),
+                    one(here_b, here_a, below[rows], edge_b, chunk, y < 0, z < 0, sizes, open_x[0]),
+                    y,
                 )
             )
         emit(part, results)
@@ -207,7 +221,9 @@
     return jnp.concatenate([result[index] for result in results], axis=0)
 
 
-def first_kernel(flags, own, own_edge, received, sibling, neighbour, masks_in, lowered, masks_out):
+def first_kernel(
+    flags, own, own_edge, received, sibling, neighbour, masks_in, factors, lowered, masks_out
+):
     low, even = flags[0] == 1, flags[1] == 1
     near, far = sibling[PAD:].astype(F32)[:1], neighbour[PAD:].astype(F32)[:1]
     place = lax.broadcasted_iota(jnp.int32, (8, LANES), 0)
@@ -231,6 +247,7 @@
         jnp.where(low, edge_own, edge_other),
         jnp.where(low, edge_other, edge_own),
         masks,
+        factors,
         emit,
     )
 
@@ -249,9 +266,11 @@
         a[span], b[span] = rows_a, rows_b
         sibling[span] = jnp.where(self.even, rows_b, rows_a).astype(BF16)
         neighbour[span] = jnp.where(self.even, rows_a, rows_b).astype(BF16)
-        for index, (chunk_a, chunk_b, up_y) in enumerate(results):
-            self.packed[0] += pack_edge(chunk_a, up_y, 2 * part + index)
-            self.packed[1] += pack_edge(chunk_b, ~up_y, 2 * part + index)
+        lane = lanes_of(CHUNK)
+        for index, (chunk_a, chunk_b, y) in enumerate(results):
+            chunk = 2 * part + index
+            self.packed[0] = pack_edge(self.packed[0], chunk_a, y > 0, chunk, lane)
+            self.packed[1] = pack_edge(self.packed[1], chunk_b, y < 0, chunk, lane)
         if part == PAD // PART - 1:
             self.edges[:EDGE] = edge_block(self.packed[0])
             self.edges[EDGE:] = edge_block(self.packed[1])
@@ -262,25 +281,27 @@
     return values[:CHUNK], values[EDGE : EDGE + CHUNK]
 
 
-def between_kernel(flags, a, b, sibling, neighbour, edges, masks, *outs):
+def between_kernel(flags, a, b, sibling, neighbour, edges, masks, factors, *outs):
     emit = Sender(flags, *outs)
     half_stream(
-        flags, lambda s: a[s], lambda s: b[s], sibling, neighbour, *received_edges(edges), masks[...], emit
-    )
-
-
-def lower_kernel(flags, a, b, sibling, neighbour, edges, masks, lowered):
+        flags, lambda s: a[s], lambda s: b[s], sibling, neighbour, *received_edges(edges), masks[...],
+        factors, emit,
+    )
+
+
+def lower_kernel(flags, a, b, sibling, neighbour, edges, masks, factors, lowered):
     def emit(part, results):
         span = PART * part
         lowered[span : span + PART] = joined(results, 0).astype(BF16)
         lowered[PAD + span : PAD + span + PART] = joined(results, 1).astype(BF16)
 
     half_stream(
-        flags, lambda s: a[s], lambda s: b[s], sibling, neighbour, *received_edges(edges), masks[...], emit
-    )
-
-
-def last_kernel(flags, a, b, sibling, neighbour, edges, masks, kept, message):
+        flags, lambda s: a[s], lambda s: b[s], sibling, neighbour, *received_edges(edges), masks[...],
+        factors, emit,
+    )
+
+
+def last_kernel(flags, a, b, sibling, neighbour, edges, masks, factors, kept, message):
     low = flags[0] == 1
 
     def emit(part, results):
@@ -290,7 +311,8 @@
         message[span] = jnp.where(low, rows_b, rows_a).astype(BF16)
 
     half_stream(
-        flags, lambda s: a[s], lambda s: b[s], sibling, neighbour, *received_edges(edges), masks[...], emit
+        flags, lambda s: a[s], lambda s: b[s], sibling, neighbour, *received_edges(edges), masks[...],
+        factors, emit,
     )
 
 
@@ -305,7 +327,7 @@
         rows_out[span] = total
 
 
-def collide_send_kernel(flags, own, mine, theirs, lowered, other, *outs):
+def collide_send_kernel(flags, own, mine, theirs, lowered, other, factors, *outs):
     low = flags[0] == 1
     swapped = flags[2] != flags[4]
     first = jnp.where(swapped, other[...], lowered[...])
@@ -320,7 +342,9 @@
         results = []
         for index in range(2):
             rows = slice(CHUNK * index, CHUNK * (index + 1))
-            results.append((rows_a[rows], rows_b[rows], terms(flags[2], 2 * part + index)[1]))
+            chunk = 2 * part + index
+            y = factors[1, CHUNK * chunk : CHUNK * (chunk + 1)]
+            results.append((rows_a[rows], rows_b[rows], y))
         emit(part, results)
 
 
@@ -352,11 +376,9 @@
     part_a = lax.dynamic_slice(wide, (0, start_a), (wide.shape[0], 768))
     part_b = lax.dynamic_slice(wide, (0, start_b), (wide.shape[0], 896))
     wanted_a = jnp.where(inside, ROWS * block + column - start_a, -1)
-    wanted_b = jnp.where(inside, 4 * ROWS - 1 - ROWS * block - column - start_b + 768, -1)
-    return chosen(
-        jnp.concatenate([part_a, part_b], axis=1),
-        place(768 + 896, 2 * PAD, jnp.concatenate([wanted_a, wanted_b])),
-    )
+    wanted_b = jnp.where(inside, 4 * ROWS - 1 - ROWS * block - column - start_b, -1)
+    halves = chosen(part_a, place(768, PAD, wanted_a)), chosen(part_b, place(896, PAD, wanted_b))
+    return jnp.concatenate(halves, axis=1)
 
 
 def padded_columns(matrix):
@@ -372,19 +394,23 @@
     flags = jnp.stack([low, 1 - core, block, half, core]).astype(jnp.int32)
 
     row = CHUNK * z + lax.iota(jnp.int32, CHUNK)
-    wanted = jnp.where(row < ROWS, jnp.where(low == 1, row, ROWS - 1 - row), -1)
-    window = chosen(place(ROWS, CHUNK, wanted).T, collision)
-    piece = to_mirror(column_half(padded_columns(window), core))
+    start = jnp.clip(jnp.where(low == 1, CHUNK * z, ROWS - CHUNK - CHUNK * z), 0, ROWS - CHUNK)
+    wanted = jnp.where(row < ROWS, jnp.where(low == 1, row, ROWS - 1 - row) - start, -1)
+    window = lax.dynamic_slice(collision, (start, 0), (CHUNK, collision.shape[1]))
+    window = padded_columns(chosen(place(CHUNK, CHUNK, wanted).T, window))
+    piece = column_half(window, core)
+    populations, piece = lax.optimization_barrier((populations, piece))
+    piece = to_mirror(piece)
     rings = [
         [(line * 8 + step) * 2 + side for step in range(8)] for line in range(8) for side in range(2)
     ]
     mine = lax.all_gather(piece, "cells", axis=0, tiled=True, axis_index_groups=rings)
-    theirs = to_sibling(mine)
 
     padded = jnp.pad(populations[:, 0, :], ((0, PAD - ROWS), (0, 0)))
-    own, own_edge, message, masks = call(
+    own, own_edge, message, masks, factors = call(
         prepare_kernel,
-        [((PAD, LANES), F32), ((CHUNK, LANES), F32), ((PAD + EDGE, LANES), BF16), ((8, LANES), F32)],
+        [((PAD, LANES), F32), ((CHUNK, LANES), F32), ((PAD + EDGE, LANES), BF16), ((8, LANES), F32),
+         ((3, PAD, LANES), F32)],
         flags, padded, solid_mask, flops=2 * 3 * PAD * PAD * 256,
     )
     received = to_mirror(message)
@@ -394,14 +420,16 @@
 
     row = lax.iota(jnp.int32, PAD)
     wanted = jnp.where(row < ROWS, jnp.where(low == 1, row, ROWS - 1 - row), -1)
+    received, collision = lax.optimization_barrier((received, collision))
     ordered = padded_columns(chosen(place(ROWS, PAD, wanted).T, collision))
-    matrix = jnp.concatenate([column_half(ordered, 0), column_half(ordered, 1)], axis=1)
 
     lowered, masks = call(
         first_kernel,
         [((2 * PAD, LANES), BF16), ((8, LANES), F32)],
-        flags, own, own_edge, received, sibling, neighbour, masks, flops=100 * PAD * 256,
-    )
+        flags, own, own_edge, received, sibling, neighbour, masks, factors, flops=100 * PAD * 256,
+    )
+    lowered, ordered = lax.optimization_barrier((lowered, ordered))
+    matrix = jnp.concatenate([column_half(ordered, 0), column_half(ordered, 1)], axis=1)
     sends = [((PAD, LANES), F32)] * 2 + [((PAD, LANES), BF16)] * 2 + [((2 * EDGE, LANES), BF16)]
     multiply = 2 * PAD * 4 * PAD * LANES
     for step in range(STEPS):
@@ -409,23 +437,26 @@
         (own,) = call(
             collide_kernel, [((PAD, LANES), F32)], flags, matrix, lowered, other, flops=multiply
         )
+        if step == 0:
+            mine, own = lax.optimization_barrier((mine, own))
+            theirs = to_sibling(mine)
         a, b, sibling, neighbour, edges = call(
-            collide_send_kernel, sends, flags, own, mine, theirs, lowered, other, flops=multiply
+            collide_send_kernel, sends, flags, own, mine, theirs, lowered, other, factors, flops=multiply
         )
         near = to_neighbour(neighbour), to_mirror(edges), to_sibling(sibling)
         if step == STEPS - 1:
             break
         a, b, sibling, neighbour, edges = call(
-            between_kernel, sends, flags, a, b, near[2], near[0], near[1], masks, flops=100 * PAD * 256
+            between_kernel, sends, flags, a, b, near[2], near[0], near[1], masks, factors, flops=100 * PAD * 256
         )
         near = to_neighbour(neighbour), to_mirror(edges), to_sibling(sibling)
         (lowered,) = call(
             lower_kernel, [((2 * PAD, LANES), BF16)],
-            flags, a, b, near[2], near[0], near[1], masks, flops=100 * PAD * 256,
+            flags, a, b, near[2], near[0], near[1], masks, factors, flops=100 * PAD * 256,
         )
     kept, message = call(
         last_kernel, [((PAD, LANES), F32), ((PAD, LANES), BF16)],
-        flags, a, b, near[2], near[0], near[1], masks, flops=100 * PAD * 256,
+        flags, a, b, near[2], near[0], near[1], masks, factors, flops=100 * PAD * 256,
     )
     received = to_mirror(message)
     (kept,) = call(

time: 208 us -> 191 us (0.918)
  the two profiles are of different devices: /device:TPU:8 before, /device:TPU:16 now
where the time goes in v3:
time: 191 us; the launch traced here: 190 us
  starting transfers between devices  70.9 us (37%)
  waiting for transfers between devices  53 us (28%)
  Pallas kernels  22.2 us (12%)
  matrix products  16.1 us (8%)
  between operations  13.9 us (7%)
  local copies, waits for them, and re-layouts  13.6 us (7%)
    ppermute x4, starting transfers between devices, to_neighbour(): return lax.ppermute(array, BOTH, pairs_of(target))  41.6 us
    ppermute x6, waiting for transfers between devices, to_mirror(): return lax.ppermute(array, 'vel', [(i, 3 - i) for i in range(4)])  38.2 us
    pallas_call x12, Pallas kernels, call(): pl.pallas_call(kernel, out_shape=[jax.ShapeDtypeStruct(shape, dtype) for...  22.2 us
    dot_general x8, matrix products, chosen(): return jnp.dot(left, right, preferred_element_type=BF16)  16.1 us
    ppermute x6, starting transfers between devices, to_mirror(): return lax.ppermute(array, 'vel', [(i, 3 - i) for i in range(4)])  12.5 us
    ppermute x5, starting transfers between devices, to_sibling(): lax.ppermute(array, BOTH, pairs_of(lambda cell, part: (cell ^ 1, part)))  9.73 us
    ppermute x2, waiting for transfers between devices, to_side(): return lax.ppermute(array, 'vel', [(i, i ^ 1) for i in range(4)])  8.06 us
    concatenate x1, local copies, waits for them, and re-layouts, per_device(): jnp.concatenate([column_half(ordered, 0), column_half(ordered, 1)], axis=1)  7.19 us
  transfers between devices with their start and end apart: 18, of which 9 were waited for; matrix products, arithmetic and copies ran while one was open for 11% of the time, Pallas kernels for 4%

profile of v3, /device:TPU:16, one launch (start us, length us, event | category | flops | bytes accessed | tf_op | source)
XLA Modules:
  0.0 189.8 jit_solution(8240511499075091936)
XLA Ops:
  9.4 2.4 %collective-permute-start.3 = (bf16[88,1408]{1,0:T(8,128)(2,1)S(1)}, bf16[88,1408]{1,0:T(8,128)(2,1)S(1)}, u32[]{:S(2)}, u32[]{:S(2)}) collective-permute-start(bf16[88,1408]{1,0:T(8,128)(2,1)S(1)} %pad_maximum_fusion), channel_id=1, source_target_pairs={{0,3},{1,2},{2,1},{3,0},{4,7},{5,6},{6,5},{7,4},{8,11},{9,10},{10,... | collective-permute-start | bytes 743432 | tf_op jit(solution)/shard_map/ppermute | solution.py:49
  11.8 12.6 %collective-permute-done.3 = bf16[88,1408]{1,0:T(8,128)(2,1)S(1)} collective-permute-done((bf16[88,1408]{1,0:T(8,128)(2,1)S(1)}, bf16[88,1408]{1,0:T(8,128)(2,1)S(1)}, u32[]{:S(2)}, u32[]{:S(2)}) %collective-permute-start.3) | collective-permute-done | bytes 247840 | tf_op jit(solution)/shard_map/ppermute | solution.py:49
  25.4 1.9 %shard_map.37 = (f32[704,128]{1,0:T(8,128)S(1)}, f32[88,128]{1,0:T(8,128)S(1)}, bf16[800,128]{1,0:T(8,128)(2,1)S(1)}, f32[8,128]{1,0:T(8,128)S(1)}, f32[3,704,128]{2,1,0:T(8,128)S(1)}) custom-call(s32[5]{0:T(128)S(1)} %stack.23.flags, f32[704,256]{1,0:T(8,128)S(1)} %pad.13.populations, s32[1,256]{1,0:T(1,128)S(1)} %copy-done.4), custom_call_target="tpu_custom_call" | custom-call | flops 761266176 | bytes 2417664 | tf_op jit(solution)/shard_map/pallas_call | solution.py:60
  27.3 2.4 %collective-permute-start = (bf16[800,128]{1,0:T(8,128)(2,1)S(1)}, bf16[800,128]{1,0:T(8,128)(2,1)S(1)}, u32[]{:S(2)}, u32[]{:S(2)}) collective-permute-start(bf16[800,128]{1,0:T(8,128)(2,1)S(1)} %get-tuple-element.42), channel_id=1, source_target_pairs={{0,3},{1,2},{2,1},{3,0},{4,7},{5,6},{6,5},{7,4},{8,11},{9,10},{10,... | collective-permute-start | bytes 614408 | tf_op jit(solution)/shard_map/ppermute | solution.py:49
  29.7 7.6 %collective-permute-done.received = bf16[800,128]{1,0:T(8,128)(2,1)S(1)} collective-permute-done((bf16[800,128]{1,0:T(8,128)(2,1)S(1)}, bf16[800,128]{1,0:T(8,128)(2,1)S(1)}, u32[]{:S(2)}, u32[]{:S(2)}) %collective-permute-start) | collective-permute-done | bytes 204832 | tf_op jit(solution)/shard_map/ppermute | solution.py:49
  39.9 17.1 %collective-permute-start.2 = (bf16[720,128]{1,0:T(8,128)(2,1)S(1)}, bf16[720,128]{1,0:T(8,128)(2,1)S(1)}, u32[]{:S(2)}, u32[]{:S(2)}) collective-permute-start(bf16[720,128]{1,0:T(8,128)(2,1)S(1)} %get-tuple-element.46), channel_id=1, source_target_pairs={{0,511},{1,510},{2,509},{3,508},{4,8},{5,9},{6,10},{7,11},{8,4},{9... | collective-permute-start | bytes 552968 | tf_op jit(solution)/shard_map/ppermute | solution.py:45
  57.0 5.4 %fusion.6 = bf16[704,2744]{1,0:T(8,128)(2,1)S(1)} fusion(bf16[686,2744]{1,0:T(8,128)(2,1)} %param.5, s32[704]{0:T(1024)S(1)} %select_select_fusion), kind=kOutput, calls=%fused_computation.13 | convolution fusion | flops 2650879488 | bytes 7631136 | tf_op jit(solution)/shard_map/dot_general | solution.py:369
  62.7 2.2 %shard_map.39 = (bf16[1408,128]{1,0:T(8,128)(2,1)S(1)}, f32[8,128]{1,0:T(8,128)S(1)}) custom-call(s32[5]{0:T(128)S(1)} %stack.23.flags, f32[704,128]{1,0:T(8,128)S(1)} %get-tuple-element.40.own, f32[88,128]{1,0:T(8,128)S(1)} %get-tuple-element.41.own_edge, bf16[800,128]{1,0:T(8,128)(2,1)S(1)} %collective-permute-done.received, ...), custom_call_target="tpu_custom_call" | custom-call | flops 18022400 | bytes 2428928 | tf_op jit(solution)/shard_map/pallas_call | solution.py:60
  64.9 2.1 %collective-permute-start.4 = (bf16[1408,128]{1,0:T(8,128)(2,1)S(1)}, bf16[1408,128]{1,0:T(8,128)(2,1)S(1)}, u32[]{:S(2)}, u32[]{:S(2)}) collective-permute-start(bf16[1408,128]{1,0:T(8,128)(2,1)S(1)} %get-tuple-element.52.lowered), channel_id=1, source_target_pairs={{0,1},{1,0},{2,3},{3,2},{4,5},{5,4},{6,7},{7,6},{8,9},{9,8},{10,11... | collective-permute-start | bytes 1081352 | tf_op jit(solution)/shard_map/ppermute | solution.py:53
  68.1 2.4 %fusion = bf16[704,704]{1,0:T(8,128)(2,1)} fusion(s32[704]{0:T(1024)S(1)} %subtract_select_fusion.1, bf16[704,2944]{1,0:T(8,128)(2,1)S(1)} %pad.14), kind=kOutput, calls=%fused_computation.3 | convolution fusion | flops 888774656 | bytes 2256896 | tf_op jit(solution)/shard_map/dot_general | solution.py:369
  70.5 2.1 %fusion.3 = bf16[704,704]{1,0:T(8,128)(2,1)} fusion(s32[704]{0:T(1024)S(1)} %iota_select_fusion, bf16[704,2944]{1,0:T(8,128)(2,1)S(1)} %pad.14), kind=kOutput, calls=%fused_computation.9 | convolution fusion | flops 761806848 | bytes 2076672 | tf_op jit(solution)/shard_map/dot_general | solution.py:369
  72.6 2.4 %fusion.1 = bf16[704,704]{1,0:T(8,128)(2,1)} fusion(s32[704]{0:T(1024)S(1)} %subtract_select_fusion, bf16[704,2944]{1,0:T(8,128)(2,1)S(1)} %pad.14), kind=kOutput, calls=%fused_computation.4 | convolution fusion | flops 888774656 | bytes 2256896 | tf_op jit(solution)/shard_map/dot_general | solution.py:369
  75.0 7.2 %concatenate.7.matrix = bf16[704,2816]{1,0:T(8,128)(2,1)} concatenate(bf16[704,704]{1,0:T(8,128)(2,1)} %fusion.3, bf16[704,704]{1,0:T(8,128)(2,1)} %fusion, bf16[704,704]{1,0:T(8,128)(2,1)S(1)} %fusion.4, bf16[704,704]{1,0:T(8,128)(2,1)} %fusion.1), dimensions={1} | concatenate | bytes 7929856 | tf_op jit(solution)/shard_map/concatenate | solution.py:432
  82.2 2.1 %copy-done = bf16[704,2816]{1,0:T(8,128)(2,1)S(1)} copy-done((bf16[704,2816]{1,0:T(8,128)(2,1)S(1)}, bf16[704,2816]{1,0:T(8,128)(2,1)}, u32[]{:S(2)}) %copy-start) | copy-done | bytes 3964952
  88.2 4.2 %collective-permute-done.5.theirs = bf16[704,1408]{1,0:T(8,128)(2,1)S(1)} collective-permute-done((bf16[704,1408]{1,0:T(8,128)(2,1)}, bf16[704,1408]{1,0:T(8,128)(2,1)S(1)}, u32[]{:S(2)}, u32[]{:S(2)}) %collective-permute-start.5) | collective-permute-done | bytes 1982496 | tf_op jit(solution)/shard_map/ppermute | solution.py:37
  93.9 2.0 %shard_map.41 = (f32[704,128]{1,0:T(8,128)S(1)}, f32[704,128]{1,0:T(8,128)S(1)}, bf16[704,128]{1,0:T(8,128)(2,1)S(1)}, bf16[704,128]{1,0:T(8,128)(2,1)S(1)}, bf16[192,128]{1,0:T(8,128)(2,1)S(1)}) custom-call(s32[5]{0:T(128)S(1)} %stack.23.flags, f32[704,128]{1,0:T(8,128)S(1)} %shard_map.40.own, bf16[704,1408]{1,0:T(8,128)(2,1)S(1)} %copy-done.2, ...), custom_call_target="tpu_custom_call" | custom-call | flops 507510784 | bytes 7258112 | tf_op jit(solution)/shard_map/pallas_call | solution.py:60
  95.9 2.1 %collective-permute-start.6 = (bf16[704,128]{1,0:T(8,128)(2,1)S(1)}, bf16[704,128]{1,0:T(8,128)(2,1)S(1)}, u32[]{:S(2)}, u32[]{:S(2)}) collective-permute-start(bf16[704,128]{1,0:T(8,128)(2,1)S(1)} %get-tuple-element.57), channel_id=1, source_target_pairs={{0,4},{1,5},{2,6},{3,7},{4,0},{5,1},{6,2},{7,3},{8,12},{9,13},{10,... | collective-permute-start | bytes 540680 | tf_op jit(solution)/shard_map/ppermute | solution.py:37
  98.0 10.4 %collective-permute-start.7 = (bf16[704,128]{1,0:T(8,128)(2,1)S(1)}, bf16[704,128]{1,0:T(8,128)(2,1)S(1)}, u32[]{:S(2)}, u32[]{:S(2)}) collective-permute-start(bf16[704,128]{1,0:T(8,128)(2,1)S(1)} %get-tuple-element.58), channel_id=1, source_target_pairs={{0,511},{1,510},{2,509},{3,508},{4,8},{5,9},{6,10},{7,11},{8,4},{9... | collective-permute-start | bytes 540680 | tf_op jit(solution)/shard_map/ppermute | solution.py:45
  110.3 4.1 %collective-permute-done.8.edges = bf16[192,128]{1,0:T(8,128)(2,1)S(1)} collective-permute-done((bf16[192,128]{1,0:T(8,128)(2,1)S(1)}, bf16[192,128]{1,0:T(8,128)(2,1)S(1)}, u32[]{:S(2)}, u32[]{:S(2)}) %collective-permute-start.8) | collective-permute-done | bytes 49184 | tf_op jit(solution)/shard_map/ppermute | solution.py:49
  114.4 2.6 %shard_map.42 = (f32[704,128]{1,0:T(8,128)S(1)}, f32[704,128]{1,0:T(8,128)S(1)}, bf16[704,128]{1,0:T(8,128)(2,1)S(1)}, bf16[704,128]{1,0:T(8,128)(2,1)S(1)}, bf16[192,128]{1,0:T(8,128)(2,1)S(1)}) custom-call(s32[5]{0:T(128)S(1)} %stack.23.flags, f32[704,128]{1,0:T(8,128)S(1)} %get-tuple-element.55.a, f32[704,128]{1,0:T(8,128)S(1)} %get-tuple-element.56.b, ...), custom_call_target="tpu_custom_call" | custom-call | flops 18022400 | bytes 3346432 | tf_op jit(solution)/shard_map/pallas_call | solution.py:60
  117.0 8.1 %collective-permute-start.10 = (bf16[704,128]{1,0:T(8,128)(2,1)S(1)}, bf16[704,128]{1,0:T(8,128)(2,1)S(1)}, u32[]{:S(2)}, u32[]{:S(2)}) collective-permute-start(bf16[704,128]{1,0:T(8,128)(2,1)S(1)} %get-tuple-element.64), channel_id=1, source_target_pairs={{0,511},{1,510},{2,509},{3,508},{4,8},{5,9},{6,10},{7,11},{8,4},{9... | collective-permute-start | bytes 540680 | tf_op jit(solution)/shard_map/ppermute | solution.py:45
  129.0 4.1 %collective-permute-done.11.edges = bf16[192,128]{1,0:T(8,128)(2,1)S(1)} collective-permute-done((bf16[192,128]{1,0:T(8,128)(2,1)S(1)}, bf16[192,128]{1,0:T(8,128)(2,1)S(1)}, u32[]{:S(2)}, u32[]{:S(2)}) %collective-permute-start.11) | collective-permute-done | bytes 49184 | tf_op jit(solution)/shard_map/ppermute | solution.py:49
  133.1 2.2 %shard_map.43.lowered = bf16[1408,128]{1,0:T(8,128)(2,1)S(1)} custom-call(s32[5]{0:T(128)S(1)} %stack.23.flags, f32[704,128]{1,0:T(8,128)S(1)} %get-tuple-element.61.a, f32[704,128]{1,0:T(8,128)S(1)} %get-tuple-element.62.b, bf16[704,128]{1,0:T(8,128)(2,1)S(1)} %collective-permute-done.9.sibling, bf16[704,128]{1,0:T(8,128)(2,1)S(1)} %collective-permute-done.10.neighbour, ...), custom_call_target="tpu_custom_call" | custom-call | flops 18022400 | bytes 2576384 | tf_op jit(solution)/shard_map/pallas_call | solution.py:60
  135.4 4.9 %collective-permute-start.12 = (bf16[1408,128]{1,0:T(8,128)(2,1)S(1)}, bf16[1408,128]{1,0:T(8,128)(2,1)S(1)}, u32[]{:S(2)}, u32[]{:S(2)}) collective-permute-start(bf16[1408,128]{1,0:T(8,128)(2,1)S(1)} %shard_map.43.lowered), channel_id=1, source_target_pairs={{0,1},{1,0},{2,3},{3,2},{4,5},{5,4},{6,7},{7,6},{8,9},{9,8},{10,11... | collective-permute-start | bytes 1081352 | tf_op jit(solution)/shard_map/ppermute | solution.py:53
  140.3 8.1 %collective-permute-done.12.other = bf16[1408,128]{1,0:T(8,128)(2,1)S(1)} collective-permute-done((bf16[1408,128]{1,0:T(8,128)(2,1)S(1)}, bf16[1408,128]{1,0:T(8,128)(2,1)S(1)}, u32[]{:S(2)}, u32[]{:S(2)}) %collective-permute-start.12) | collective-permute-done | bytes 360480 | tf_op jit(solution)/shard_map/ppermute | solution.py:53
  150.2 2.0 %shard_map.45 = (f32[704,128]{1,0:T(8,128)S(1)}, f32[704,128]{1,0:T(8,128)S(1)}, bf16[704,128]{1,0:T(8,128)(2,1)S(1)}, bf16[704,128]{1,0:T(8,128)(2,1)S(1)}, bf16[192,128]{1,0:T(8,128)(2,1)S(1)}) custom-call(s32[5]{0:T(128)S(1)} %stack.23.flags, f32[704,128]{1,0:T(8,128)S(1)} %shard_map.44.own, bf16[704,1408]{1,0:T(8,128)(2,1)S(1)} %copy-done.3, ...), custom_call_target="tpu_custom_call" | custom-call | flops 507510784 | bytes 7258112 | tf_op jit(solution)/shard_map/pallas_call | solution.py:60
  154.2 6.1 %collective-permute-start.14 = (bf16[704,128]{1,0:T(8,128)(2,1)S(1)}, bf16[704,128]{1,0:T(8,128)(2,1)S(1)}, u32[]{:S(2)}, u32[]{:S(2)}) collective-permute-start(bf16[704,128]{1,0:T(8,128)(2,1)S(1)} %get-tuple-element.69), channel_id=1, source_target_pairs={{0,511},{1,510},{2,509},{3,508},{4,8},{5,9},{6,10},{7,11},{8,4},{9... | collective-permute-start | bytes 540680 | tf_op jit(solution)/shard_map/ppermute | solution.py:45
  162.2 4.1 %collective-permute-done.15.edges = bf16[192,128]{1,0:T(8,128)(2,1)S(1)} collective-permute-done((bf16[192,128]{1,0:T(8,128)(2,1)S(1)}, bf16[192,128]{1,0:T(8,128)(2,1)S(1)}, u32[]{:S(2)}, u32[]{:S(2)}) %collective-permute-start.15) | collective-permute-done | bytes 49184 | tf_op jit(solution)/shard_map/ppermute | solution.py:49
  166.2 2.5 %collective-permute-done.14.neighbour = bf16[704,128]{1,0:T(8,128)(2,1)S(1)} collective-permute-done((bf16[704,128]{1,0:T(8,128)(2,1)S(1)}, bf16[704,128]{1,0:T(8,128)(2,1)S(1)}, u32[]{:S(2)}, u32[]{:S(2)}) %collective-permute-start.14) | collective-permute-done | bytes 180256 | tf_op jit(solution)/shard_map/ppermute | solution.py:45
  168.7 2.3 %shard_map.46 = (f32[704,128]{1,0:T(8,128)S(1)}, bf16[704,128]{1,0:T(8,128)(2,1)S(1)}) custom-call(s32[5]{0:T(128)S(1)} %stack.23.flags, f32[704,128]{1,0:T(8,128)S(1)} %get-tuple-element.66.a, f32[704,128]{1,0:T(8,128)S(1)} %get-tuple-element.67.b, bf16[704,128]{1,0:T(8,128)(2,1)S(1)} %collective-permute-done.13.sibling, ...), custom_call_target="tpu_custom_call" | custom-call | flops 18022400 | bytes 2756608 | tf_op jit(solution)/shard_map/pallas_call | solution.py:60
  171.0 2.0 %collective-permute-start.16 = (bf16[704,128]{1,0:T(8,128)(2,1)S(1)}, bf16[704,128]{1,0:T(8,128)(2,1)S(1)}, u32[]{:S(2)}, u32[]{:S(2)}) collective-permute-start(bf16[704,128]{1,0:T(8,128)(2,1)S(1)} %get-tuple-element.72), channel_id=1, source_target_pairs={{0,3},{1,2},{2,1},{3,0},{4,7},{5,6},{6,5},{7,4},{8,11},{9,10},{10,... | collective-permute-start | bytes 540680 | tf_op jit(solution)/shard_map/ppermute | solution.py:49
  174.6 5.8 %collective-permute-done.16.received = bf16[704,128]{1,0:T(8,128)(2,1)S(1)} collective-permute-done((bf16[704,128]{1,0:T(8,128)(2,1)S(1)}, bf16[704,128]{1,0:T(8,128)(2,1)S(1)}, u32[]{:S(2)}, u32[]{:S(2)}) %collective-permute-start.16) | collective-permute-done | bytes 180256 | tf_op jit(solution)/shard_map/ppermute | solution.py:49
  (54 shorter events, 28.6 us)
Async XLA Ops:
  6.5 18.6 %copy-start.5 = (f32[686,1,256]{2,1,0:T(1,128)S(1)}, f32[686,1,256]{2,1,0:T(1,128)}, u32[]{:S(2)}) copy-start(f32[686,1,256]{2,1,0:T(1,128)} %param.3) | copy-start | bytes 2107396
  6.5 79.7 %all-gather.2.cloned.1.call-start = ((), (), s32[]{:S(2)}) async-start(), calls=%async_computation | async-start | bytes 2230272 | tf_op jit(solution)/shard_map/all_gather | solution.py:407
  8.7 16.6 %copy-start.4 = (s32[1,256]{1,0:T(1,128)S(1)}, s32[1,256]{1,0:T(1,128)}, u32[]{:S(2)}) copy-start(s32[1,256]{1,0:T(1,128)} %solid.1) | copy-start | bytes 3076
  9.4 14.9 %collective-permute-start.3 = (bf16[88,1408]{1,0:T(8,128)(2,1)S(1)}, bf16[88,1408]{1,0:T(8,128)(2,1)S(1)}, u32[]{:S(2)}, u32[]{:S(2)}) collective-permute-start(bf16[88,1408]{1,0:T(8,128)(2,1)S(1)} %pad_maximum_fusion), channel_id=1, source_target_pairs={{0,3},{1,2},{2,1},{3,0},{4,7},{5,6},{6,5},{7,4},{8,11},{9,10},{10,... | collective-permute-start | bytes 743432 | tf_op jit(solution)/shard_map/ppermute | solution.py:49
  24.4 0.7 copy-start.6
  27.3 10.0 %collective-permute-start = (bf16[800,128]{1,0:T(8,128)(2,1)S(1)}, bf16[800,128]{1,0:T(8,128)(2,1)S(1)}, u32[]{:S(2)}, u32[]{:S(2)}) collective-permute-start(bf16[800,128]{1,0:T(8,128)(2,1)S(1)} %get-tuple-element.42), channel_id=1, source_target_pairs={{0,3},{1,2},{2,1},{3,0},{4,7},{5,6},{6,5},{7,4},{8,11},{9,10},{10,... | collective-permute-start | bytes 614408 | tf_op jit(solution)/shard_map/ppermute | solution.py:49
  38.0 24.7 %collective-permute-start.1 = (bf16[720,128]{1,0:T(8,128)(2,1)S(1)}, bf16[720,128]{1,0:T(8,128)(2,1)S(1)}, u32[]{:S(2)}, u32[]{:S(2)}) collective-permute-start(bf16[720,128]{1,0:T(8,128)(2,1)S(1)} %get-tuple-element.45), channel_id=1, source_target_pairs={{0,4},{1,5},{2,6},{3,7},{4,0},{5,1},{6,2},{7,3},{8,12},{9,13},{10,... | collective-permute-start | bytes 552968 | tf_op jit(solution)/shard_map/ppermute | solution.py:37
  39.9 22.8 %collective-permute-start.2 = (bf16[720,128]{1,0:T(8,128)(2,1)S(1)}, bf16[720,128]{1,0:T(8,128)(2,1)S(1)}, u32[]{:S(2)}, u32[]{:S(2)}) collective-permute-start(bf16[720,128]{1,0:T(8,128)(2,1)S(1)} %get-tuple-element.46), channel_id=1, source_target_pairs={{0,511},{1,510},{2,509},{3,508},{4,8},{5,9},{6,10},{7,11},{8,4},{9... | collective-permute-start | bytes 552968 | tf_op jit(solution)/shard_map/ppermute | solution.py:45
  64.9 17.3 %collective-permute-start.4 = (bf16[1408,128]{1,0:T(8,128)(2,1)S(1)}, bf16[1408,128]{1,0:T(8,128)(2,1)S(1)}, u32[]{:S(2)}, u32[]{:S(2)}) collective-permute-start(bf16[1408,128]{1,0:T(8,128)(2,1)S(1)} %get-tuple-element.52.lowered), channel_id=1, source_target_pairs={{0,1},{1,0},{2,3},{3,2},{4,5},{5,4},{6,7},{7,6},{8,9},{9,8},{10,11... | collective-permute-start | bytes 1081352 | tf_op jit(solution)/shard_map/ppermute | solution.py:53
  82.2 2.1 %copy-start = (bf16[704,2816]{1,0:T(8,128)(2,1)S(1)}, bf16[704,2816]{1,0:T(8,128)(2,1)}, u32[]{:S(2)}) copy-start(bf16[704,2816]{1,0:T(8,128)(2,1)} %concatenate.7.matrix) | copy-start | bytes 11894788
  86.3 6.1 %collective-permute-start.5 = (bf16[704,1408]{1,0:T(8,128)(2,1)}, bf16[704,1408]{1,0:T(8,128)(2,1)S(1)}, u32[]{:S(2)}, u32[]{:S(2)}) collective-permute-start(bf16[704,1408]{1,0:T(8,128)(2,1)} %all-gather.2.cloned.1.call-done.mine), channel_id=1, source_target_pairs={{0,4},{1,5},{2,6},{3,7},{4,0},{5,1},{6,2},{7,3},{8,12},{9,13},{10,... | collective-permute-start | bytes 5947400 | tf_op jit(solution)/shard_map/ppermute | solution.py:37
  92.4 1.6 copy-start.2
  95.9 18.4 %collective-permute-start.6 = (bf16[704,128]{1,0:T(8,128)(2,1)S(1)}, bf16[704,128]{1,0:T(8,128)(2,1)S(1)}, u32[]{:S(2)}, u32[]{:S(2)}) collective-permute-start(bf16[704,128]{1,0:T(8,128)(2,1)S(1)} %get-tuple-element.57), channel_id=1, source_target_pairs={{0,4},{1,5},{2,6},{3,7},{4,0},{5,1},{6,2},{7,3},{8,12},{9,13},{10,... | collective-permute-start | bytes 540680 | tf_op jit(solution)/shard_map/ppermute | solution.py:37
  98.0 16.4 %collective-permute-start.7 = (bf16[704,128]{1,0:T(8,128)(2,1)S(1)}, bf16[704,128]{1,0:T(8,128)(2,1)S(1)}, u32[]{:S(2)}, u32[]{:S(2)}) collective-permute-start(bf16[704,128]{1,0:T(8,128)(2,1)S(1)} %get-tuple-element.58), channel_id=1, source_target_pairs={{0,511},{1,510},{2,509},{3,508},{4,8},{5,9},{6,10},{7,11},{8,4},{9... | collective-permute-start | bytes 540680 | tf_op jit(solution)/shard_map/ppermute | solution.py:45
  108.4 6.0 %collective-permute-start.8 = (bf16[192,128]{1,0:T(8,128)(2,1)S(1)}, bf16[192,128]{1,0:T(8,128)(2,1)S(1)}, u32[]{:S(2)}, u32[]{:S(2)}) collective-permute-start(bf16[192,128]{1,0:T(8,128)(2,1)S(1)} %get-tuple-element.59), channel_id=1, source_target_pairs={{0,3},{1,2},{2,1},{3,0},{4,7},{5,6},{6,5},{7,4},{8,11},{9,10},{10,... | collective-permute-start | bytes 147464 | tf_op jit(solution)/shard_map/ppermute | solution.py:49
  114.4 34.0 %copy-start.1 = (bf16[704,2816]{1,0:T(8,128)(2,1)S(1)}, bf16[704,2816]{1,0:T(8,128)(2,1)}, u32[]{:S(2)}) copy-start(bf16[704,2816]{1,0:T(8,128)(2,1)} %concatenate.7.matrix) | copy-start | bytes 11894788
  117.0 16.1 %collective-permute-start.10 = (bf16[704,128]{1,0:T(8,128)(2,1)S(1)}, bf16[704,128]{1,0:T(8,128)(2,1)S(1)}, u32[]{:S(2)}, u32[]{:S(2)}) collective-permute-start(bf16[704,128]{1,0:T(8,128)(2,1)S(1)} %get-tuple-element.64), channel_id=1, source_target_pairs={{0,511},{1,510},{2,509},{3,508},{4,8},{5,9},{6,10},{7,11},{8,4},{9... | collective-permute-start | bytes 540680 | tf_op jit(solution)/shard_map/ppermute | solution.py:45
  125.2 8.0 %collective-permute-start.9 = (bf16[704,128]{1,0:T(8,128)(2,1)S(1)}, bf16[704,128]{1,0:T(8,128)(2,1)S(1)}, u32[]{:S(2)}, u32[]{:S(2)}) collective-permute-start(bf16[704,128]{1,0:T(8,128)(2,1)S(1)} %get-tuple-element.63), channel_id=1, source_target_pairs={{0,4},{1,5},{2,6},{3,7},{4,0},{5,1},{6,2},{7,3},{8,12},{9,13},{10,... | collective-permute-start | bytes 540680 | tf_op jit(solution)/shard_map/ppermute | solution.py:37
  127.1 6.0 %collective-permute-start.11 = (bf16[192,128]{1,0:T(8,128)(2,1)S(1)}, bf16[192,128]{1,0:T(8,128)(2,1)S(1)}, u32[]{:S(2)}, u32[]{:S(2)}) collective-permute-start(bf16[192,128]{1,0:T(8,128)(2,1)S(1)} %get-tuple-element.65), channel_id=1, source_target_pairs={{0,3},{1,2},{2,1},{3,0},{4,7},{5,6},{6,5},{7,4},{8,11},{9,10},{10,... | collective-permute-start | bytes 147464 | tf_op jit(solution)/shard_map/ppermute | solution.py:49
  135.4 14.9 %copy-start.3 = (bf16[704,1408]{1,0:T(8,128)(2,1)S(1)}, bf16[704,1408]{1,0:T(8,128)(2,1)}, u32[]{:S(2)}) copy-start(bf16[704,1408]{1,0:T(8,128)(2,1)} %all-gather.2.cloned.1.call-done.mine) | copy-start | bytes 5947396
  135.4 13.0 %collective-permute-start.12 = (bf16[1408,128]{1,0:T(8,128)(2,1)S(1)}, bf16[1408,128]{1,0:T(8,128)(2,1)S(1)}, u32[]{:S(2)}, u32[]{:S(2)}) collective-permute-start(bf16[1408,128]{1,0:T(8,128)(2,1)S(1)} %shard_map.43.lowered), channel_id=1, source_target_pairs={{0,1},{1,0},{2,3},{3,2},{4,5},{5,4},{6,7},{7,6},{8,9},{9,8},{10,11... | collective-permute-start | bytes 1081352 | tf_op jit(solution)/shard_map/ppermute | solution.py:53
  152.2 14.0 %collective-permute-start.13 = (bf16[704,128]{1,0:T(8,128)(2,1)S(1)}, bf16[704,128]{1,0:T(8,128)(2,1)S(1)}, u32[]{:S(2)}, u32[]{:S(2)}) collective-permute-start(bf16[704,128]{1,0:T(8,128)(2,1)S(1)} %get-tuple-element.68), channel_id=1, source_target_pairs={{0,4},{1,5},{2,6},{3,7},{4,0},{5,1},{6,2},{7,3},{8,12},{9,13},{10,... | collective-permute-start | bytes 540680 | tf_op jit(solution)/shard_map/ppermute | solution.py:37
  154.2 14.6 %collective-permute-start.14 = (bf16[704,128]{1,0:T(8,128)(2,1)S(1)}, bf16[704,128]{1,0:T(8,128)(2,1)S(1)}, u32[]{:S(2)}, u32[]{:S(2)}) collective-permute-start(bf16[704,128]{1,0:T(8,128)(2,1)S(1)} %get-tuple-element.69), channel_id=1, source_target_pairs={{0,511},{1,510},{2,509},{3,508},{4,8},{5,9},{6,10},{7,11},{8,4},{9... | collective-permute-start | bytes 540680 | tf_op jit(solution)/shard_map/ppermute | solution.py:45
  160.3 6.0 %collective-permute-start.15 = (bf16[192,128]{1,0:T(8,128)(2,1)S(1)}, bf16[192,128]{1,0:T(8,128)(2,1)S(1)}, u32[]{:S(2)}, u32[]{:S(2)}) collective-permute-start(bf16[192,128]{1,0:T(8,128)(2,1)S(1)} %get-tuple-element.70), channel_id=1, source_target_pairs={{0,3},{1,2},{2,1},{3,0},{4,7},{5,6},{6,5},{7,4},{8,11},{9,10},{10,... | collective-permute-start | bytes 147464 | tf_op jit(solution)/shard_map/ppermute | solution.py:49
  171.0 9.3 %collective-permute-start.16 = (bf16[704,128]{1,0:T(8,128)(2,1)S(1)}, bf16[704,128]{1,0:T(8,128)(2,1)S(1)}, u32[]{:S(2)}, u32[]{:S(2)}) collective-permute-start(bf16[704,128]{1,0:T(8,128)(2,1)S(1)} %get-tuple-element.72), channel_id=1, source_target_pairs={{0,3},{1,2},{2,1},{3,0},{4,7},{5,6},{6,5},{7,4},{8,11},{9,10},{10,... | collective-permute-start | bytes 540680 | tf_op jit(solution)/shard_map/ppermute | solution.py:49
Sparse Core Ops, SparseCore 0:
  25.2 50.1 all-gather.1

commit v4 on v3

v4 whole, which is shorter than its diff:
```python
import math

import jax
import jax.numpy as jnp
from jax import lax
from jax.experimental import pallas as pl
from jax.experimental.pallas import tpu as pltpu
from jax.sharding import PartitionSpec as P


K = 14
STEPS = 2
NZ = 16
BOTH = ("cells", "vel")
ROWS = 686
PAD = 704
CHUNK = 88
PART = 2 * CHUNK
EDGE = 96
LANES = 128
RING = 16
F32 = jnp.float32
BF16 = jnp.bfloat16
PARAMS = pltpu.CompilerParams(vmem_limit_bytes=40 * 1024 * 1024)


def pairs_of(target):
    pairs = []
    for cell in range(128):
        for part in range(4):
            to_cell, to_part = target(cell, part)
            pairs.append((cell * 4 + part, to_cell * 4 + to_part))
    return pairs


def to_sibling(array):
    return lax.ppermute(array, BOTH, pairs_of(lambda cell, part: (cell ^ 1, part)))


def neighbour_of(cell, part):
    other = (cell - 1 if cell % 2 == 0 else cell + 1) % 128
    return other, part if (other // RING) % 2 == (cell // RING) % 2 else 3 - part


def to_neighbour(array):
    return lax.ppermute(array, BOTH, pairs_of(neighbour_of))


def with_neighbour(array):
    pairs = pairs_of(neighbour_of)
    groups = [list(pair) for pair in pairs if pair[0] // 4 % 2 == 1]
    return lax.all_gather(array, BOTH, axis=0, tiled=True, axis_index_groups=groups)


def to_mirror(array):
    return lax.ppermute(array, "vel", [(i, 3 - i) for i in range(4)])


def to_side(array):
    return lax.ppermute(array, "vel", [(i, i ^ 1) for i in range(4)])


def call(kernel, outs, flags, *arrays, flops=0, scratch=()):
    moved = sum(x.size * x.dtype.itemsize for x in arrays)
    moved += sum(math.prod(shape) * jnp.dtype(dtype).itemsize for shape, dtype in outs)
    vmem = pl.BlockSpec(memory_space=pltpu.VMEM)
    result = pl.pallas_call(
        kernel,
        out_shape=[jax.ShapeDtypeStruct(shape, dtype) for shape, dtype in outs],
        in_specs=[pl.BlockSpec(memory_space=pltpu.SMEM)] + [vmem] * len(arrays),
        out_specs=[vmem] * len(outs),
        scratch_shapes=[pltpu.VMEM(shape, dtype) for shape, dtype in scratch],
        compiler_params=PARAMS,
        cost_estimate=pl.CostEstimate(flops=flops, bytes_accessed=moved, transcendentals=0),
    )(flags, *arrays)
    return result


def roll(values, shift):
    return pltpu.roll(values, shift % values.shape[1], 1)


def order_matrix(low):
    row = lax.broadcasted_iota(jnp.int32, (PAD, PAD), 0)
    column = lax.broadcasted_iota(jnp.int32, (PAD, PAD), 1)
    wanted = jnp.where(low, row, ROWS - 1 - row)
    return jnp.where((column == wanted) & (row < ROWS), 1.0, 0.0).astype(BF16)


def reordered(order, values):
    total = jnp.zeros(values.shape, F32)
    for _ in range(3):
        part = values.astype(BF16)
        total += jnp.dot(order, part, preferred_element_type=F32)
        values = values - part.astype(F32)
    return total


def signed_factors(block, chunk):
    row = CHUNK * chunk + lax.broadcasted_iota(jnp.int32, (CHUNK, LANES), 0)
    ids = ROWS * block + row
    upper = (ids * 4682) >> 16
    k_z = ids - K * upper
    k_x = (upper * 4682) >> 16
    k_y = upper - K * k_x
    centre = (K - 1) / 2.0
    x, y, z = ((k.astype(F32) - centre) * (0.3 / centre) for k in (k_x, k_y, k_z))
    return jnp.abs(x), y, z


def lanes_of(rows):
    return lax.broadcasted_iota(jnp.int32, (rows, LANES), 1)


def lower_z(values):
    z_place = lax.broadcasted_iota(jnp.int32, values.shape, 1) % NZ
    return jnp.where(z_place == 0, roll(values, 1 - NZ), roll(values, 1))


def upper_z(values):
    z_place = lax.broadcasted_iota(jnp.int32, values.shape, 1) % NZ
    return jnp.where(z_place == NZ - 1, roll(values, NZ - 1), roll(values, -1))


def picked(values, lanes):
    return jnp.take_along_axis(values, lanes, axis=1, mode="promise_in_bounds")


def pack_edge(packed, values, positive, chunk, lane):
    place = lane & (NZ - 1)
    edge = picked(values, jnp.where(positive, place + LANES - NZ, place))
    return jnp.where((lane >> 4) == chunk, edge, packed)


def edge_block(packed):
    return jnp.concatenate([packed, jnp.zeros((EDGE - CHUNK, LANES), F32)], axis=0).astype(BF16)


def prepare_kernel(flags, populations, solid, own, own_edge, message, masks, factors):
    low, block, half = flags[0] == 1, flags[2], flags[3]
    ordered = reordered(order_matrix(low), populations[...])
    left, right = ordered[:, :LANES], ordered[:, LANES:]
    mine = jnp.where(half == 0, left, right)
    rest = jnp.where(half == 0, right, left)
    own[...] = mine
    edges = jnp.zeros((CHUNK, LANES), F32)
    sent = jnp.zeros((CHUNK, LANES), F32)
    lane = lanes_of(CHUNK)
    for chunk in range(PAD // CHUNK):
        rows = slice(CHUNK * chunk, CHUNK * (chunk + 1))
        x, y, z = signed_factors(block, chunk)
        factors[0, rows], factors[1, rows], factors[2, rows] = x, y, z
        positive = jnp.where(low, y, -y) > 0
        edges = pack_edge(edges, rest[rows], positive, chunk, lane)
        sent = pack_edge(sent, mine[rows], positive, chunk, lane)
    own_edge[...] = edges
    message[:PAD] = rest.astype(BF16)
    message[PAD:] = edge_block(sent)
    fluid = jnp.where(jnp.broadcast_to(solid[...], (8, 2 * LANES)) == 0, 1.0, 0.0)
    place = lax.broadcasted_iota(jnp.int32, (8, 2 * LANES), 0)
    found = jnp.zeros((8, 2 * LANES), F32)
    near = (fluid, roll(fluid, NZ), roll(fluid, -NZ), lower_z(fluid), upper_z(fluid))
    for index, value in enumerate(near):
        found = jnp.where(place == index, value, found)
    masks[...] = jnp.where(half == 0, found[:, :LANES], found[:, LANES:])


def faces_kernel(flags, own, received, masks, sibling, neighbour):
    same = flags[4] == 1
    row = lax.broadcasted_iota(jnp.int32, (16, LANES), 0)
    fluid = jnp.where(row == 0, jnp.broadcast_to(masks[0:1, :], (16, LANES)), 0.0).astype(BF16)
    mine, theirs = own[...], received[:PAD].astype(F32)
    sibling[:PAD] = jnp.where(same, theirs, mine).astype(BF16)
    neighbour[:PAD] = jnp.where(same, mine, theirs).astype(BF16)
    sibling[PAD:] = fluid
    neighbour[PAD:] = fluid


def rows_of(index, size):
    return slice(size * index, size * (index + 1))


def stream_part(part, sign, values, mirror, layer, edge, masks, open_x, factors):
    fluid, below_open_y, above_open_y, below_open_z, above_open_z = (
        jnp.broadcast_to(masks[i : i + 1], (CHUNK, LANES)) for i in range(5)
    )
    open_x = jnp.broadcast_to(open_x, (CHUNK, LANES))
    lane = lanes_of(CHUNK)
    z_place = lane & (NZ - 1)
    below_z = jnp.where(z_place == 0, lane + NZ - 1, lane - 1)
    above_z = jnp.where(z_place == NZ - 1, lane + 1 - NZ, lane + 1)
    below_y, above_y = (lane + LANES - NZ) & (LANES - 1), (lane + NZ) & (LANES - 1)
    results = []
    for index in range(2):
        chunk = 2 * part + index
        x, y, z = (factors[i, rows_of(chunk, CHUNK)] for i in range(3))
        up_y, up_z = y * sign > 0, z * sign > 0
        here, back = values[rows_of(index, CHUNK)], mirror[rows_of(index, CHUNK)]
        at_edge = jnp.where(up_y, lane, lane + NZ)
        put = picked(edge, (at_edge + NZ * chunk) & (LANES - 1))
        outside = (up_y & (lane < NZ)) | (~up_y & (lane >= LANES - NZ))
        near_y = jnp.where(outside, put, picked(here, jnp.where(up_y, below_y, above_y)))
        near_z = picked(here, jnp.where(up_z, below_z, above_z))
        upwind_x = jnp.where(open_x > 0, layer[rows_of(index, CHUNK)], back)
        upwind_y = jnp.where(jnp.where(up_y, below_open_y, above_open_y) > 0, near_y, back)
        upwind_z = jnp.where(jnp.where(up_z, below_open_z, above_open_z) > 0, near_z, back)
        outflow = x * (here - upwind_x)
        outflow += jnp.abs(y) * (here - upwind_y)
        outflow += jnp.abs(z) * (here - upwind_z)
        results.append((here - outflow) * fluid)
    return jnp.concatenate(results, axis=0)


def pack_part(packed, part, sign, values, factors):
    lane = lanes_of(CHUNK)
    for index in range(2):
        chunk = 2 * part + index
        positive = factors[1, rows_of(chunk, CHUNK)] * sign > 0
        packed = pack_edge(packed, values[rows_of(index, CHUNK)], positive, chunk, lane)
    return packed


def signs(flags):
    near = jnp.where(flags[1] == 1, 1.0, -1.0)
    return near, -near


def place_of_near(flags):
    return pl.multiple_of(PAD * (1 - flags[1]), 16), pl.multiple_of(PAD * flags[1], 16)


def first_kernel(
    flags, own, own_edge, received, sibling, neighbour, masks_in, factors, lowered, masks_out
):
    same = flags[4] == 1
    place = lax.broadcasted_iota(jnp.int32, (8, LANES), 0)
    open_near = sibling[PAD:].astype(F32)[:1]
    open_far = neighbour[PAD:].astype(F32)[:1]
    masks = masks_in[...]
    masks = jnp.where(place == 5, open_near, masks)
    masks = jnp.where(place == 6, open_far, masks)
    masks_out[...] = masks
    edge_own, edge_other = own_edge[...], received[PAD:].astype(F32)[:CHUNK]
    edge_near = jnp.where(same, edge_own, edge_other)
    edge_far = jnp.where(same, edge_other, edge_own)
    sign_near, sign_far = signs(flags)
    at_near, at_far = place_of_near(flags)
    for part in range(PAD // PART):
        span = rows_of(part, PART)
        mine, theirs = own[span], received[span].astype(F32)
        near, far = jnp.where(same, mine, theirs), jnp.where(same, theirs, mine)
        new_near = stream_part(
            part, sign_near, near, far, sibling[span].astype(F32), edge_near, masks, open_near, factors
        )
        new_far = stream_part(
            part, sign_far, far, near, neighbour[span].astype(F32), edge_far, masks, open_far, factors
        )
        lowered[pl.ds(at_near + PART * part, PART)] = new_near.astype(BF16)
        lowered[pl.ds(at_far + PART * part, PART)] = new_far.astype(BF16)


def stream_near(flags, near, far, sibling, edges, masks, factors):
    values = masks[...]
    edge = edges[:EDGE].astype(F32)[:CHUNK]
    for part in range(PAD // PART):
        span = rows_of(part, PART)
        yield part, span, stream_part(
            part, signs(flags)[0], near[span], far[span], sibling[span].astype(F32), edge, values,
            values[5:6], factors,
        )


def stream_far(flags, near, far, neighbour, edges, masks, factors):
    values = masks[...]
    edge = edges[EDGE:].astype(F32)[:CHUNK]
    start = pl.multiple_of(PAD * (1 - flags[1]), 16)
    for part in range(PAD // PART):
        span = rows_of(part, PART)
        layer = neighbour[pl.ds(start + PART * part, PART)].astype(F32)
        yield part, span, stream_part(
            part, signs(flags)[1], far[span], near[span], layer, edge, values, values[6:7], factors
        )


def between_near_kernel(flags, near, far, sibling, edges, masks, factors, rows_out, sent, packed_out):
    packed = jnp.zeros((CHUNK, LANES), F32)
    for part, span, rows in stream_near(flags, near, far, sibling, edges, masks, factors):
        rows_out[span] = rows
        sent[span] = rows.astype(BF16)
        packed = pack_part(packed, part, signs(flags)[0], rows, factors)
    packed_out[...] = edge_block(packed)


def between_far_kernel(
    flags, near, far, neighbour, edges, masks, factors, packed_near, rows_out, sent, packed_out
):
    packed = jnp.zeros((CHUNK, LANES), F32)
    for part, span, rows in stream_far(flags, near, far, neighbour, edges, masks, factors):
        rows_out[span] = rows
        sent[span] = rows.astype(BF16)
        packed = pack_part(packed, part, signs(flags)[1], rows, factors)
    packed_out[:EDGE] = packed_near[...]
    packed_out[EDGE:] = edge_block(packed)


def lower_near_kernel(flags, near, far, sibling, edges, masks, factors, lowered):
    for _, span, rows in stream_near(flags, near, far, sibling, edges, masks, factors):
        lowered[span] = rows.astype(BF16)


def lower_far_kernel(flags, near, far, neighbour, edges, masks, factors, low_near, lowered):
    at_near, at_far = place_of_near(flags)
    for part, span, rows in stream_far(flags, near, far, neighbour, edges, masks, factors):
        lowered[pl.ds(at_far + PART * part, PART)] = rows.astype(BF16)
        lowered[pl.ds(at_near + PART * part, PART)] = low_near[span]


def last_near_kernel(flags, near, far, sibling, edges, masks, factors, rows_out):
    for _, span, rows in stream_near(flags, near, far, sibling, edges, masks, factors):
        rows_out[span] = rows


def last_far_kernel(flags, near, far, neighbour, edges, masks, factors, new_near, kept, message):
    same = flags[4] == 1
    for _, span, rows in stream_far(flags, near, far, neighbour, edges, masks, factors):
        done = new_near[span]
        kept[span] = jnp.where(same, done, rows)
        message[span] = jnp.where(same, rows, done).astype(BF16)


def dot(left, right):
    return jnp.dot(left, right, preferred_element_type=F32)


def own_product(parts, half, values, span):
    return dot(parts[2 * half][span], values[:PAD]) + dot(parts[2 * half + 1][span], values[PAD:])


def collide_kernel(flags, m0, m1, m2, m3, lowered, other, rows_out):
    swapped = flags[2] == 1
    first = jnp.where(swapped, other[...], lowered[...])
    second = jnp.where(swapped, lowered[...], other[...])
    for part in range(PAD // PART):
        span = rows_of(part, PART)
        parts = m0, m1, m2, m3
        rows_out[span] = own_product(parts, 0, first, span) + own_product(parts, 1, second, span)


def give_rows(flags, part, own, partner, factors, packed, outs):
    near, far, to_other_core, to_neighbour_chip = outs
    same = flags[4] == 1
    span = rows_of(part, PART)
    rows_near, rows_far = jnp.where(same, own, partner), jnp.where(same, partner, own)
    near[span], far[span] = rows_near, rows_far
    to_neighbour_chip[span] = rows_near.astype(BF16)
    to_other_core[span] = rows_far.astype(BF16)
    sign_near, sign_far = signs(flags)
    return (
        pack_part(packed[0], part, sign_near, rows_near, factors),
        pack_part(packed[1], part, sign_far, rows_far, factors),
    )


def collide_partner_kernel(flags, own, matrix, lowered, other, factors, *outs):
    swapped = flags[2] == 1
    first = jnp.where(swapped, other[...], lowered[...])
    second = jnp.where(swapped, lowered[...], other[...])
    packed = (jnp.zeros((CHUNK, LANES), F32),) * 2
    for part in range(PAD // PART):
        span = rows_of(part, PART)
        partner = dot(matrix[span], first) + dot(matrix[PAD + PART * part : PAD + PART * (part + 1)], second)
        packed = give_rows(flags, part, own[span], partner, factors, packed, outs[:4])
    outs[4][:EDGE], outs[4][EDGE:] = edge_block(packed[0]), edge_block(packed[1])


def early_kernel(flags, m0, m1, m2, m3, matrix, lowered, own_out, partner_out):
    values = lowered[...]
    for half in range(2):

        @pl.when(flags[2] == half)
        def _():
            for part in range(PAD // PART):
                span = rows_of(part, PART)
                start = PAD * half + PART * part
                own_out[span] = own_product((m0, m1, m2, m3), half, values, span)
                partner_out[span] = dot(matrix[start : start + PART], values)


def late_kernel(flags, m0, m1, m2, m3, matrix, other, own, partner, factors, *outs):
    *outs, total_own, total_partner = outs
    values = other[...]
    for half in range(2):

        @pl.when(flags[2] != half)
        def _():
            for part in range(PAD // PART):
                span = rows_of(part, PART)
                start = PAD * half + PART * part
                total_own[span] = own[span] + own_product((m0, m1, m2, m3), half, values, span)
                total_partner[span] = partner[span] + dot(matrix[start : start + PART], values)

    packed = (jnp.zeros((CHUNK, LANES), F32),) * 2
    for part in range(PAD // PART):
        span = rows_of(part, PART)
        packed = give_rows(flags, part, total_own[span], total_partner[span], factors, packed, outs[:4])
    outs[4][:EDGE], outs[4][EDGE:] = edge_block(packed[0]), edge_block(packed[1])


def reorder_kernel(flags, kept, ordered):
    ordered[...] = reordered(order_matrix(flags[0] == 1), kept[...])


def finish_kernel(flags, kept, received, evolved):
    order = order_matrix(flags[0] == 1)
    rest = jnp.dot(order, received[...], preferred_element_type=F32)
    mine = kept[...]
    half = flags[3]
    evolved[:, :LANES] = jnp.where(half == 0, mine, rest)[:ROWS]
    evolved[:, LANES:] = jnp.where(half == 0, rest, mine)[:ROWS]


def place(rows, columns, wanted):
    return (lax.broadcasted_iota(jnp.int32, (rows, columns), 0) == wanted[None, :]).astype(BF16)


def chosen(left, right):
    return jnp.dot(left, right, preferred_element_type=BF16)


def column_half(wide, block):
    column = lax.iota(jnp.int32, PAD)
    inside = column < ROWS
    start_a, start_b = 640 * block, jnp.where(block == 1, 1280, 2048)
    part_a = lax.dynamic_slice(wide, (0, start_a), (wide.shape[0], 768))
    part_b = lax.dynamic_slice(wide, (0, start_b), (wide.shape[0], 896))
    wanted_a = jnp.where(inside, ROWS * block + column - start_a, -1)
    wanted_b = jnp.where(inside, 4 * ROWS - 1 - ROWS * block - column - start_b, -1)
    halves = chosen(part_a, place(768, PAD, wanted_a)), chosen(part_b, place(896, PAD, wanted_b))
    return halves


def padded_columns(matrix):
    return jnp.pad(matrix, ((0, 0), (0, 2944 - matrix.shape[1])))


def per_device(populations, solid_mask, collision):
    cell, vel = lax.axis_index("cells"), lax.axis_index("vel")
    low = (vel < 2).astype(jnp.int32)
    core, z = cell % 2, cell // 2 % 8
    block = jnp.minimum(vel, 3 - vel)
    half = (1 - low) ^ (cell // RING % 2)
    flags = jnp.stack([low, 1 - core, block, half, (low != core).astype(jnp.int32)])
    flags = flags.astype(jnp.int32)

    row = CHUNK * z + lax.iota(jnp.int32, CHUNK)
    start = jnp.clip(jnp.where(low == 1, CHUNK * z, ROWS - CHUNK - CHUNK * z), 0, ROWS - CHUNK)
    wanted = jnp.where(row < ROWS, jnp.where(low == 1, row, ROWS - 1 - row) - start, -1)
    window = lax.dynamic_slice(collision, (start, 0), (CHUNK, collision.shape[1]))
    window = padded_columns(chosen(place(CHUNK, CHUNK, wanted).T, window))
    piece = jnp.concatenate(column_half(window, core), axis=1)
    populations, piece = lax.optimization_barrier((populations, piece))
    piece = to_mirror(piece)

    padded = jnp.pad(populations[:, 0, :], ((0, PAD - ROWS), (0, 0)))
    rows = (PAD, LANES)
    own, own_edge, message, masks, factors = call(
        prepare_kernel,
        [(rows, F32), ((CHUNK, LANES), F32), ((PAD + EDGE, LANES), BF16), ((8, LANES), F32), ((3, *rows), F32)],
        flags, padded, solid_mask, flops=2 * 3 * PAD * PAD * 256,
    )
    piece, _ = lax.optimization_barrier((piece, message))
    groups = [
        [(line * 8 + step) * 2 + side for side in range(2) for step in range(8)] for line in range(8)
    ]
    partner_matrix = lax.all_gather(piece, "cells", axis=0, tiled=True, axis_index_groups=groups)
    received = to_mirror(message)
    faces = [((PAD + 16, LANES), BF16)] * 2
    sibling, neighbour = call(faces_kernel, faces, flags, own, received, masks)
    neighbour, sibling = to_neighbour(neighbour), to_sibling(sibling)

    row = lax.iota(jnp.int32, PAD)
    wanted = jnp.where(row < ROWS, jnp.where(low == 1, row, ROWS - 1 - row), -1)
    received, collision = lax.optimization_barrier((received, collision))
    ordered = padded_columns(chosen(place(ROWS, PAD, wanted).T, collision))

    lowered, masks = call(
        first_kernel,
        [((2 * PAD, LANES), BF16), ((8, LANES), F32)],
        flags, own, own_edge, received, sibling, neighbour, masks, factors, flops=100 * PAD * 256,
    )
    lowered, ordered = lax.optimization_barrier((lowered, ordered))
    matrix = *column_half(ordered, 0), *column_half(ordered, 1)
    edges_shape = ((2 * EDGE, LANES), BF16)
    sends = [(rows, F32)] * 2 + [(rows, BF16)] * 2 + [edges_shape]
    multiply = 2 * PAD * 4 * PAD * LANES
    work = 60 * PAD * LANES

    other = to_side(lowered)
    (own,) = call(collide_kernel, [(rows, F32)], flags, *matrix, lowered, other, flops=multiply)
    partner_matrix, own = lax.optimization_barrier((partner_matrix, own))
    near, far, for_sibling, for_neighbour, edges = call(
        collide_partner_kernel, sends, flags, own, partner_matrix, lowered, other, factors, flops=multiply
    )

    for step in range(1, STEPS):
        neighbour = with_neighbour(for_neighbour)
        sibling, edges = to_sibling(for_sibling), to_mirror(edges)
        new_near, for_neighbour, packed = call(
            between_near_kernel, [(rows, F32), (rows, BF16), ((EDGE, LANES), BF16)],
            flags, near, far, sibling, edges, masks, factors, flops=work,
        )
        new_far, for_sibling, new_edges = call(
            between_far_kernel, [(rows, F32), (rows, BF16), edges_shape],
            flags, near, far, neighbour, edges, masks, factors, packed, flops=work,
        )
        near, far, edges = new_near, new_far, new_edges
        neighbour = with_neighbour(for_neighbour)
        sibling, edges = to_sibling(for_sibling), to_mirror(edges)
        (low_near,) = call(
            lower_near_kernel, [(rows, BF16)], flags, near, far, sibling, edges, masks, factors, flops=work
        )
        (lowered,) = call(
            lower_far_kernel, [((2 * PAD, LANES), BF16)],
            flags, near, far, neighbour, edges, masks, factors, low_near, flops=work,
        )
        other = to_side(lowered)
        early = call(
            early_kernel, [(rows, F32)] * 2, flags, *matrix, partner_matrix, lowered, flops=multiply
        )
        near, far, for_sibling, for_neighbour, edges = call(
            late_kernel, sends, flags, *matrix, partner_matrix, other, *early, factors,
            flops=multiply, scratch=[(rows, F32)] * 2,
        )

    neighbour = with_neighbour(for_neighbour)
    sibling, edges = to_sibling(for_sibling), to_mirror(edges)
    (new_near,) = call(
        last_near_kernel, [(rows, F32)], flags, near, far, sibling, edges, masks, factors, flops=work
    )
    kept, message = call(
        last_far_kernel, [(rows, F32), (rows, BF16)],
        flags, near, far, neighbour, edges, masks, factors, new_near, flops=work,
    )
    received = to_mirror(message)
    (kept,) = call(reorder_kernel, [(rows, F32)], flags, kept, flops=2 * 3 * PAD * PAD * LANES)
    (evolved,) = call(
        finish_kernel, [((ROWS, 2 * LANES), F32)], flags, kept, received, flops=2 * PAD * PAD * LANES
    )
    return evolved[:, None, :]


def solution(mesh):
    in_specs = (P("vel", "cells", None), P("cells", None), P("vel", None))
    out_specs = P("vel", "cells", None)
    return jax.shard_map(
        per_device, mesh=mesh, in_specs=in_specs, out_specs=out_specs, check_vma=False
    )
```

time: 191 us -> 177 us (0.927)
  the two profiles are of different devices: /device:TPU:16 before, /device:TPU:24 now
where the time goes in v4:
time: 177 us; the launch traced here: 176 us
  starting transfers between devices  61.5 us (35%)
  blocking collectives  38.4 us (22%)
  Pallas kernels  24.7 us (14%)
  waiting for transfers between devices  14.5 us (8%)
  between operations  13.9 us (8%)
  matrix products  12.9 us (7%)
  local copies, waits for them, and re-layouts  10.3 us (6%)
    all_gather x3, blocking collectives, with_neighbour(): lax.all_gather(array, BOTH, axis=0, tiled=True, axis_index_groups=groups)  38.4 us
    ppermute x6, starting transfers between devices, to_mirror(): return lax.ppermute(array, 'vel', [(i, 3 - i) for i in range(4)])  28.5 us
    pallas_call x15, Pallas kernels, call(): pl.pallas_call(kernel, out_shape=[jax.ShapeDtypeStruct(shape, dtype) for...  24.7 us
    ppermute x1, starting transfers between devices, to_neighbour(): return lax.ppermute(array, BOTH, pairs_of(neighbour_of))  15.4 us
    dot_general x8, matrix products, chosen(): return jnp.dot(left, right, preferred_element_type=BF16)  12.9 us
    ppermute x2, starting transfers between devices, to_side(): return lax.ppermute(array, 'vel', [(i, i ^ 1) for i in range(4)])  9.75 us
    ppermute x6, waiting for transfers between devices, to_mirror(): return lax.ppermute(array, 'vel', [(i, 3 - i) for i in range(4)])  8.45 us
    unnamed x31, local copies, waits for them, and re-layouts  8.31 us
  transfers between devices with their start and end apart: 14, of which 6 were waited for; matrix products, arithmetic and copies ran while one was open for 6% of the time, Pallas kernels for 6%

profile of v4, /device:TPU:24, one launch (start us, length us, event | category | flops | bytes accessed | tf_op | source)
XLA Modules:
  0.0 176.4 jit_solution(5155138772700803766)
XLA Ops:
  9.4 7.5 %collective-permute-start.3 = (bf16[88,1408]{1,0:T(8,128)(2,1)S(1)}, bf16[88,1408]{1,0:T(8,128)(2,1)S(1)}, u32[]{:S(2)}, u32[]{:S(2)}) collective-permute-start(bf16[88,1408]{1,0:T(8,128)(2,1)S(1)} %pad_maximum_fusion), channel_id=1, source_target_pairs={{0,3},{1,2},{2,1},{3,0},{4,7},{5,6},{6,5},{7,4},{8,11},{9,10},{10,... | collective-permute-start | bytes 743432 | tf_op jit(solution)/shard_map/ppermute | solution.py:56
  17.2 1.9 %shard_map.37 = (f32[704,128]{1,0:T(8,128)S(1)}, f32[88,128]{1,0:T(8,128)S(1)}, bf16[800,128]{1,0:T(8,128)(2,1)S(1)}, f32[8,128]{1,0:T(8,128)S(1)}, f32[3,704,128]{2,1,0:T(8,128)S(1)}) custom-call(s32[5]{0:T(128)S(1)} %stack.27.flags, f32[704,256]{1,0:T(8,128)S(1)} %pad.13.populations, s32[1,256]{1,0:T(1,128)S(1)} %copy-done.12), custom_call_target="tpu_custom_call" | custom-call | flops 761266176 | bytes 2417664 | tf_op jit(solution)/shard_map/pallas_call | solution.py:67
  19.2 2.0 %collective-permute-done.3 = bf16[88,1408]{1,0:T(8,128)(2,1)S(1)} collective-permute-done((bf16[88,1408]{1,0:T(8,128)(2,1)S(1)}, bf16[88,1408]{1,0:T(8,128)(2,1)S(1)}, u32[]{:S(2)}, u32[]{:S(2)}) %collective-permute-start.3) | collective-permute-done | bytes 247840 | tf_op jit(solution)/shard_map/ppermute | solution.py:56
  21.9 5.8 %collective-permute-start = (bf16[800,128]{1,0:T(8,128)(2,1)S(1)}, bf16[800,128]{1,0:T(8,128)(2,1)S(1)}, u32[]{:S(2)}, u32[]{:S(2)}) collective-permute-start(bf16[800,128]{1,0:T(8,128)(2,1)S(1)} %get-tuple-element.46), channel_id=1, source_target_pairs={{0,3},{1,2},{2,1},{3,0},{4,7},{5,6},{6,5},{7,4},{8,11},{9,10},{10,... | collective-permute-start | bytes 614408 | tf_op jit(solution)/shard_map/ppermute | solution.py:56
  27.7 3.8 %collective-permute-done.received = bf16[800,128]{1,0:T(8,128)(2,1)S(1)} collective-permute-done((bf16[800,128]{1,0:T(8,128)(2,1)S(1)}, bf16[800,128]{1,0:T(8,128)(2,1)S(1)}, u32[]{:S(2)}, u32[]{:S(2)}) %collective-permute-start) | collective-permute-done | bytes 204832 | tf_op jit(solution)/shard_map/ppermute | solution.py:56
  32.1 1.9 %collective-permute-start.1 = (bf16[720,128]{1,0:T(8,128)(2,1)S(1)}, bf16[720,128]{1,0:T(8,128)(2,1)S(1)}, u32[]{:S(2)}, u32[]{:S(2)}) collective-permute-start(bf16[720,128]{1,0:T(8,128)(2,1)S(1)} %get-tuple-element.49), channel_id=1, source_target_pairs={{0,4},{1,5},{2,6},{3,7},{4,0},{5,1},{6,2},{7,3},{8,12},{9,13},{10,... | collective-permute-start | bytes 552968 | tf_op jit(solution)/shard_map/ppermute | solution.py:37
  34.1 15.4 %collective-permute-start.2 = (bf16[720,128]{1,0:T(8,128)(2,1)S(1)}, bf16[720,128]{1,0:T(8,128)(2,1)S(1)}, u32[]{:S(2)}, u32[]{:S(2)}) collective-permute-start(bf16[720,128]{1,0:T(8,128)(2,1)S(1)} %get-tuple-element.50), channel_id=1, source_target_pairs={{0,511},{1,510},{2,509},{3,508},{4,8},{5,9},{6,10},{7,11},{8,4},{9... | collective-permute-start | bytes 552968 | tf_op jit(solution)/shard_map/ppermute | solution.py:46
  49.5 5.4 %fusion.6 = bf16[704,2744]{1,0:T(8,128)(2,1)S(1)} fusion(bf16[686,2744]{1,0:T(8,128)(2,1)} %param.5, s32[704]{0:T(1024)S(1)} %select_select_fusion), kind=kOutput, calls=%fused_computation.13 | convolution fusion | flops 2650879488 | bytes 7631136 | tf_op jit(solution)/shard_map/dot_general | solution.py:427
  55.2 2.2 %shard_map.39 = (bf16[1408,128]{1,0:T(8,128)(2,1)S(1)}, f32[8,128]{1,0:T(8,128)S(1)}) custom-call(s32[5]{0:T(128)S(1)} %stack.27.flags, f32[704,128]{1,0:T(8,128)S(1)} %get-tuple-element.44.own, f32[88,128]{1,0:T(8,128)S(1)} %get-tuple-element.45.own_edge, bf16[800,128]{1,0:T(8,128)(2,1)S(1)} %collective-permute-done.received, ...), custom_call_target="tpu_custom_call" | custom-call | flops 18022400 | bytes 2428928 | tf_op jit(solution)/shard_map/pallas_call | solution.py:67
  57.4 7.8 %collective-permute-start.4 = (bf16[1408,128]{1,0:T(8,128)(2,1)S(1)}, bf16[1408,128]{1,0:T(8,128)(2,1)S(1)}, u32[]{:S(2)}, u32[]{:S(2)}) collective-permute-start(bf16[1408,128]{1,0:T(8,128)(2,1)S(1)} %get-tuple-element.57.lowered), channel_id=1, source_target_pairs={{0,1},{1,0},{2,3},{3,2},{4,5},{5,4},{6,7},{7,6},{8,9},{9,8},{10,11... | collective-permute-start | bytes 1081352 | tf_op jit(solution)/shard_map/ppermute | solution.py:60
  70.5 1.9 %shard_map.40.own = f32[704,128]{1,0:T(8,128)S(1)} custom-call(s32[5]{0:T(128)S(1)} %stack.27.flags, bf16[704,704]{1,0:T(8,128)(2,1)S(1)} %fusion.3.m0, bf16[704,704]{1,0:T(8,128)(2,1)S(1)} %fusion.m1, bf16[704,704]{1,0:T(8,128)(2,1)S(1)} %fusion.4.m2, bf16[704,704]{1,0:T(8,128)(2,1)S(1)} %fusion.1.m3, bf16[1408,128]{1,0:T(8,128)(2,1)S(1)} %get-tuple-element.57.lowered, ...), custom_call_target="tpu_custom_call" | custom-call | flops 507510784 | bytes 5046272 | tf_op jit(solution)/shard_map/pallas_call | solution.py:67
  75.3 2.1 %copy-done = bf16[1408,1408]{1,0:T(8,128)(2,1)S(1)} copy-done((bf16[1408,1408]{1,0:T(8,128)(2,1)S(1)}, bf16[1408,1408]{1,0:T(8,128)(2,1)}, u32[]{:S(2)}) %copy-start) | copy-done | bytes 3964952
  80.4 2.0 %shard_map.41 = (f32[704,128]{1,0:T(8,128)S(1)}, f32[704,128]{1,0:T(8,128)S(1)}, bf16[704,128]{1,0:T(8,128)(2,1)S(1)}, bf16[704,128]{1,0:T(8,128)(2,1)S(1)}, bf16[192,128]{1,0:T(8,128)(2,1)S(1)}) custom-call(s32[5]{0:T(128)S(1)} %stack.27.flags, f32[704,128]{1,0:T(8,128)S(1)} %copy-done.11, bf16[1408,1408]{1,0:T(8,128)(2,1)S(1)} %copy-done, ...), custom_call_target="tpu_custom_call" | custom-call | flops 507510784 | bytes 7258112 | tf_op jit(solution)/shard_map/pallas_call | solution.py:67
  82.4 2.2 %collective-permute-start.5 = (bf16[704,128]{1,0:T(8,128)(2,1)S(1)}, bf16[704,128]{1,0:T(8,128)(2,1)S(1)}, u32[]{:S(2)}, u32[]{:S(2)}) collective-permute-start(bf16[704,128]{1,0:T(8,128)(2,1)S(1)} %get-tuple-element.62), channel_id=1, source_target_pairs={{0,4},{1,5},{2,6},{3,7},{4,0},{5,1},{6,2},{7,3},{8,12},{9,13},{10,... | collective-permute-start | bytes 540680 | tf_op jit(solution)/shard_map/ppermute | solution.py:37
  84.6 2.1 %collective-permute-start.6 = (bf16[192,128]{1,0:T(8,128)(2,1)S(1)}, bf16[192,128]{1,0:T(8,128)(2,1)S(1)}, u32[]{:S(2)}, u32[]{:S(2)}) collective-permute-start(bf16[192,128]{1,0:T(8,128)(2,1)S(1)} %get-tuple-element.63), channel_id=1, source_target_pairs={{0,3},{1,2},{2,1},{3,0},{4,7},{5,6},{6,5},{7,4},{8,11},{9,10},{10,... | collective-permute-start | bytes 147464 | tf_op jit(solution)/shard_map/ppermute | solution.py:56
  86.7 12.5 %all_gather.13.neighbour = bf16[1408,128]{1,0:T(8,128)(2,1)S(1)} all-gather(bf16[704,128]{1,0:T(8,128)(2,1)S(1)} %get-tuple-element.66), channel_id=1, replica_groups={{4,8},{5,9},{6,10},{7,11},{12,16},{13,17},{14,18},{15,19},{20,24},{21,2..., dimensions={0}, use_global_device_ids=true | all-gather | bytes 540672 | tf_op jit(solution)/shard_map/all_gather | solution.py:52
  99.2 1.7 shard_map.42
  100.9 1.7 shard_map.43
  102.6 1.9 %collective-permute-start.8 = (bf16[704,128]{1,0:T(8,128)(2,1)S(1)}, bf16[704,128]{1,0:T(8,128)(2,1)S(1)}, u32[]{:S(2)}, u32[]{:S(2)}) collective-permute-start(bf16[704,128]{1,0:T(8,128)(2,1)S(1)} %get-tuple-element.71), channel_id=1, source_target_pairs={{0,4},{1,5},{2,6},{3,7},{4,0},{5,1},{6,2},{7,3},{8,12},{9,13},{10,... | collective-permute-start | bytes 540680 | tf_op jit(solution)/shard_map/ppermute | solution.py:37
  104.5 6.0 %collective-permute-start.7 = (bf16[192,128]{1,0:T(8,128)(2,1)S(1)}, bf16[192,128]{1,0:T(8,128)(2,1)S(1)}, u32[]{:S(2)}, u32[]{:S(2)}) collective-permute-start(bf16[192,128]{1,0:T(8,128)(2,1)S(1)} %get-tuple-element.70), channel_id=1, source_target_pairs={{0,3},{1,2},{2,1},{3,0},{4,7},{5,6},{6,5},{7,4},{8,11},{9,10},{10,... | collective-permute-start | bytes 147464 | tf_op jit(solution)/shard_map/ppermute | solution.py:56
  110.5 12.9 %all_gather.14.neighbour = bf16[1408,128]{1,0:T(8,128)(2,1)S(1)} all-gather(bf16[704,128]{1,0:T(8,128)(2,1)S(1)} %get-tuple-element.69), channel_id=1, replica_groups={{4,8},{5,9},{6,10},{7,11},{12,16},{13,17},{14,18},{15,19},{20,24},{21,2..., dimensions={0}, use_global_device_ids=true | all-gather | bytes 540672 | tf_op jit(solution)/shard_map/all_gather | solution.py:52
  126.2 1.9 %collective-permute-start.9 = (bf16[1408,128]{1,0:T(8,128)(2,1)S(1)}, bf16[1408,128]{1,0:T(8,128)(2,1)S(1)}, u32[]{:S(2)}, u32[]{:S(2)}) collective-permute-start(bf16[1408,128]{1,0:T(8,128)(2,1)S(1)} %shard_map.45.lowered), channel_id=1, source_target_pairs={{0,1},{1,0},{2,3},{3,2},{4,5},{5,4},{6,7},{7,6},{8,9},{9,8},{10,11... | collective-permute-start | bytes 1081352 | tf_op jit(solution)/shard_map/ppermute | solution.py:60
  128.2 2.1 %shard_map.46 = (f32[704,128]{1,0:T(8,128)S(1)}, f32[704,128]{1,0:T(8,128)S(1)}) custom-call(s32[5]{0:T(128)S(1)} %stack.27.flags, bf16[704,704]{1,0:T(8,128)(2,1)S(1)} %copy-done.3, bf16[704,704]{1,0:T(8,128)(2,1)S(1)} %fusion.m1, bf16[704,704]{1,0:T(8,128)(2,1)S(1)} %fusion.4.m2, bf16[704,704]{1,0:T(8,128)(2,1)S(1)} %copy-done.5, ...), custom_call_target="tpu_custom_call" | custom-call | flops 507510784 | bytes 9011200 | tf_op jit(solution)/shard_map/pallas_call | solution.py:67
  130.3 5.2 %collective-permute-done.9.other = bf16[1408,128]{1,0:T(8,128)(2,1)S(1)} collective-permute-done((bf16[1408,128]{1,0:T(8,128)(2,1)S(1)}, bf16[1408,128]{1,0:T(8,128)(2,1)S(1)}, u32[]{:S(2)}, u32[]{:S(2)}) %collective-permute-start.9) | collective-permute-done | bytes 360480 | tf_op jit(solution)/shard_map/ppermute | solution.py:60
  135.5 2.5 %shard_map.47 = (f32[704,128]{1,0:T(8,128)S(1)}, f32[704,128]{1,0:T(8,128)S(1)}, bf16[704,128]{1,0:T(8,128)(2,1)S(1)}, bf16[704,128]{1,0:T(8,128)(2,1)S(1)}, bf16[192,128]{1,0:T(8,128)(2,1)S(1)}) custom-call(s32[5]{0:T(128)S(1)} %stack.27.flags, bf16[704,704]{1,0:T(8,128)(2,1)S(1)} %copy-done.3, bf16[704,704]{1,0:T(8,128)(2,1)S(1)} %fusion.m1, ...), custom_call_target="tpu_custom_call" | custom-call | flops 507510784 | bytes 11223040 | tf_op jit(solution)/shard_map/pallas_call | solution.py:67
  138.0 1.9 %collective-permute-start.11 = (bf16[704,128]{1,0:T(8,128)(2,1)S(1)}, bf16[704,128]{1,0:T(8,128)(2,1)S(1)}, u32[]{:S(2)}, u32[]{:S(2)}) collective-permute-start(bf16[704,128]{1,0:T(8,128)(2,1)S(1)} %get-tuple-element.78), channel_id=1, source_target_pairs={{0,4},{1,5},{2,6},{3,7},{4,0},{5,1},{6,2},{7,3},{8,12},{9,13},{10,... | collective-permute-start | bytes 540680 | tf_op jit(solution)/shard_map/ppermute | solution.py:37
  139.9 2.1 %collective-permute-start.10 = (bf16[192,128]{1,0:T(8,128)(2,1)S(1)}, bf16[192,128]{1,0:T(8,128)(2,1)S(1)}, u32[]{:S(2)}, u32[]{:S(2)}) collective-permute-start(bf16[192,128]{1,0:T(8,128)(2,1)S(1)} %get-tuple-element.77), channel_id=1, source_target_pairs={{0,3},{1,2},{2,1},{3,0},{4,7},{5,6},{6,5},{7,4},{8,11},{9,10},{10,... | collective-permute-start | bytes 147464 | tf_op jit(solution)/shard_map/ppermute | solution.py:56
  142.0 13.0 %all_gather.15.neighbour = bf16[1408,128]{1,0:T(8,128)(2,1)S(1)} all-gather(bf16[704,128]{1,0:T(8,128)(2,1)S(1)} %get-tuple-element.76), channel_id=1, replica_groups={{4,8},{5,9},{6,10},{7,11},{12,16},{13,17},{14,18},{15,19},{20,24},{21,2..., dimensions={0}, use_global_device_ids=true | all-gather | bytes 540672 | tf_op jit(solution)/shard_map/all_gather | solution.py:52
  157.8 5.0 %collective-permute-start.12 = (bf16[704,128]{1,0:T(8,128)(2,1)S(1)}, bf16[704,128]{1,0:T(8,128)(2,1)S(1)}, u32[]{:S(2)}, u32[]{:S(2)}) collective-permute-start(bf16[704,128]{1,0:T(8,128)(2,1)S(1)} %get-tuple-element.80), channel_id=1, source_target_pairs={{0,3},{1,2},{2,1},{3,0},{4,7},{5,6},{6,5},{7,4},{8,11},{9,10},{10,... | collective-permute-start | bytes 540680 | tf_op jit(solution)/shard_map/ppermute | solution.py:56
  162.8 1.6 shard_map.50.kept
  164.3 2.6 %collective-permute-done.12.received = bf16[704,128]{1,0:T(8,128)(2,1)S(1)} collective-permute-done((bf16[704,128]{1,0:T(8,128)(2,1)S(1)}, bf16[704,128]{1,0:T(8,128)(2,1)S(1)}, u32[]{:S(2)}, u32[]{:S(2)}) %collective-permute-start.12) | collective-permute-done | bytes 180256 | tf_op jit(solution)/shard_map/ppermute | solution.py:56
  167.9 1.6 copy.4
  (67 shorter events, 22.3 us)
Async XLA Ops:
  6.5 10.5 %copy-start.13 = (f32[686,1,256]{2,1,0:T(1,128)S(1)}, f32[686,1,256]{2,1,0:T(1,128)}, u32[]{:S(2)}) copy-start(f32[686,1,256]{2,1,0:T(1,128)} %param.3) | copy-start | bytes 2107396
  6.5 68.8 %all-gather.2.cloned.1.call-start = ((), (), s32[]{:S(2)}) async-start(), calls=%async_computation | async-start | bytes 4212736 | tf_op jit(solution)/shard_map/all_gather | solution.py:475
  8.7 8.5 %copy-start.12 = (s32[1,256]{1,0:T(1,128)S(1)}, s32[1,256]{1,0:T(1,128)}, u32[]{:S(2)}) copy-start(s32[1,256]{1,0:T(1,128)} %solid.1) | copy-start | bytes 3076
  9.4 11.7 %collective-permute-start.3 = (bf16[88,1408]{1,0:T(8,128)(2,1)S(1)}, bf16[88,1408]{1,0:T(8,128)(2,1)S(1)}, u32[]{:S(2)}, u32[]{:S(2)}) collective-permute-start(bf16[88,1408]{1,0:T(8,128)(2,1)S(1)} %pad_maximum_fusion), channel_id=1, source_target_pairs={{0,3},{1,2},{2,1},{3,0},{4,7},{5,6},{6,5},{7,4},{8,11},{9,10},{10,... | collective-permute-start | bytes 743432 | tf_op jit(solution)/shard_map/ppermute | solution.py:56
  21.2 0.7 copy-start.14
  21.9 9.6 %collective-permute-start = (bf16[800,128]{1,0:T(8,128)(2,1)S(1)}, bf16[800,128]{1,0:T(8,128)(2,1)S(1)}, u32[]{:S(2)}, u32[]{:S(2)}) collective-permute-start(bf16[800,128]{1,0:T(8,128)(2,1)S(1)} %get-tuple-element.46), channel_id=1, source_target_pairs={{0,3},{1,2},{2,1},{3,0},{4,7},{5,6},{6,5},{7,4},{8,11},{9,10},{10,... | collective-permute-start | bytes 614408 | tf_op jit(solution)/shard_map/ppermute | solution.py:56
  32.1 23.0 %collective-permute-start.1 = (bf16[720,128]{1,0:T(8,128)(2,1)S(1)}, bf16[720,128]{1,0:T(8,128)(2,1)S(1)}, u32[]{:S(2)}, u32[]{:S(2)}) collective-permute-start(bf16[720,128]{1,0:T(8,128)(2,1)S(1)} %get-tuple-element.49), channel_id=1, source_target_pairs={{0,4},{1,5},{2,6},{3,7},{4,0},{5,1},{6,2},{7,3},{8,12},{9,13},{10,... | collective-permute-start | bytes 552968 | tf_op jit(solution)/shard_map/ppermute | solution.py:37
  34.1 21.1 %collective-permute-start.2 = (bf16[720,128]{1,0:T(8,128)(2,1)S(1)}, bf16[720,128]{1,0:T(8,128)(2,1)S(1)}, u32[]{:S(2)}, u32[]{:S(2)}) collective-permute-start(bf16[720,128]{1,0:T(8,128)(2,1)S(1)} %get-tuple-element.50), channel_id=1, source_target_pairs={{0,511},{1,510},{2,509},{3,508},{4,8},{5,9},{6,10},{7,11},{8,4},{9... | collective-permute-start | bytes 552968 | tf_op jit(solution)/shard_map/ppermute | solution.py:46
  57.4 13.1 %copy-start.6 = (bf16[1408,128]{1,0:T(8,128)(2,1)}, bf16[1408,128]{1,0:T(8,128)(2,1)S(1)}, u32[]{:S(2)}) copy-start(bf16[1408,128]{1,0:T(8,128)(2,1)S(1)} %get-tuple-element.57.lowered) | copy-start | bytes 1081348
  57.4 13.1 %collective-permute-start.4 = (bf16[1408,128]{1,0:T(8,128)(2,1)S(1)}, bf16[1408,128]{1,0:T(8,128)(2,1)S(1)}, u32[]{:S(2)}, u32[]{:S(2)}) collective-permute-start(bf16[1408,128]{1,0:T(8,128)(2,1)S(1)} %get-tuple-element.57.lowered), channel_id=1, source_target_pairs={{0,1},{1,0},{2,3},{3,2},{4,5},{5,4},{6,7},{7,6},{8,9},{9,8},{10,11... | collective-permute-start | bytes 1081352 | tf_op jit(solution)/shard_map/ppermute | solution.py:60
  68.8 1.7 copy-start.2
  72.3 1.0 copy-start.4
  73.3 0.7 copy-start.8
  74.1 0.7 copy-start.10
  75.3 2.1 %copy-start = (bf16[1408,1408]{1,0:T(8,128)(2,1)S(1)}, bf16[1408,1408]{1,0:T(8,128)(2,1)}, u32[]{:S(2)}) copy-start(bf16[1408,1408]{1,0:T(8,128)(2,1)} %all-gather.2.cloned.1.call-done.matrix) | copy-start | bytes 11894788
  77.4 1.0 copy-start.7
  78.4 1.0 copy-start.9
  79.4 1.0 copy-start.11
  82.4 16.8 %collective-permute-start.5 = (bf16[704,128]{1,0:T(8,128)(2,1)S(1)}, bf16[704,128]{1,0:T(8,128)(2,1)S(1)}, u32[]{:S(2)}, u32[]{:S(2)}) collective-permute-start(bf16[704,128]{1,0:T(8,128)(2,1)S(1)} %get-tuple-element.62), channel_id=1, source_target_pairs={{0,4},{1,5},{2,6},{3,7},{4,0},{5,1},{6,2},{7,3},{8,12},{9,13},{10,... | collective-permute-start | bytes 540680 | tf_op jit(solution)/shard_map/ppermute | solution.py:37
  84.6 14.7 %collective-permute-start.6 = (bf16[192,128]{1,0:T(8,128)(2,1)S(1)}, bf16[192,128]{1,0:T(8,128)(2,1)S(1)}, u32[]{:S(2)}, u32[]{:S(2)}) collective-permute-start(bf16[192,128]{1,0:T(8,128)(2,1)S(1)} %get-tuple-element.63), channel_id=1, source_target_pairs={{0,3},{1,2},{2,1},{3,0},{4,7},{5,6},{6,5},{7,4},{8,11},{9,10},{10,... | collective-permute-start | bytes 147464 | tf_op jit(solution)/shard_map/ppermute | solution.py:56
  100.9 27.2 %copy-start.5 = (bf16[704,704]{1,0:T(8,128)(2,1)S(1)}, bf16[704,704]{1,0:T(8,128)(2,1)}, u32[]{:S(2)}) copy-start(bf16[704,704]{1,0:T(8,128)(2,1)} %copy-done.4) | copy-start | bytes 2973700
  102.6 20.8 %collective-permute-start.8 = (bf16[704,128]{1,0:T(8,128)(2,1)S(1)}, bf16[704,128]{1,0:T(8,128)(2,1)S(1)}, u32[]{:S(2)}, u32[]{:S(2)}) collective-permute-start(bf16[704,128]{1,0:T(8,128)(2,1)S(1)} %get-tuple-element.71), channel_id=1, source_target_pairs={{0,4},{1,5},{2,6},{3,7},{4,0},{5,1},{6,2},{7,3},{8,12},{9,13},{10,... | collective-permute-start | bytes 540680 | tf_op jit(solution)/shard_map/ppermute | solution.py:37
  104.5 18.9 %collective-permute-start.7 = (bf16[192,128]{1,0:T(8,128)(2,1)S(1)}, bf16[192,128]{1,0:T(8,128)(2,1)S(1)}, u32[]{:S(2)}, u32[]{:S(2)}) collective-permute-start(bf16[192,128]{1,0:T(8,128)(2,1)S(1)} %get-tuple-element.70), channel_id=1, source_target_pairs={{0,3},{1,2},{2,1},{3,0},{4,7},{5,6},{6,5},{7,4},{8,11},{9,10},{10,... | collective-permute-start | bytes 147464 | tf_op jit(solution)/shard_map/ppermute | solution.py:56
  110.4 17.7 %copy-start.3 = (bf16[704,704]{1,0:T(8,128)(2,1)S(1)}, bf16[704,704]{1,0:T(8,128)(2,1)}, u32[]{:S(2)}) copy-start(bf16[704,704]{1,0:T(8,128)(2,1)} %copy-done.2) | copy-start | bytes 2973700
  123.4 4.8 %copy-start.1 = (bf16[1408,1408]{1,0:T(8,128)(2,1)S(1)}, bf16[1408,1408]{1,0:T(8,128)(2,1)}, u32[]{:S(2)}) copy-start(bf16[1408,1408]{1,0:T(8,128)(2,1)} %all-gather.2.cloned.1.call-done.matrix) | copy-start | bytes 11894788
  126.2 9.3 %collective-permute-start.9 = (bf16[1408,128]{1,0:T(8,128)(2,1)S(1)}, bf16[1408,128]{1,0:T(8,128)(2,1)S(1)}, u32[]{:S(2)}, u32[]{:S(2)}) collective-permute-start(bf16[1408,128]{1,0:T(8,128)(2,1)S(1)} %shard_map.45.lowered), channel_id=1, source_target_pairs={{0,1},{1,0},{2,3},{3,2},{4,5},{5,4},{6,7},{7,6},{8,9},{9,8},{10,11... | collective-permute-start | bytes 1081352 | tf_op jit(solution)/shard_map/ppermute | solution.py:60
  138.0 17.0 %collective-permute-start.11 = (bf16[704,128]{1,0:T(8,128)(2,1)S(1)}, bf16[704,128]{1,0:T(8,128)(2,1)S(1)}, u32[]{:S(2)}, u32[]{:S(2)}) collective-permute-start(bf16[704,128]{1,0:T(8,128)(2,1)S(1)} %get-tuple-element.78), channel_id=1, source_target_pairs={{0,4},{1,5},{2,6},{3,7},{4,0},{5,1},{6,2},{7,3},{8,12},{9,13},{10,... | collective-permute-start | bytes 540680 | tf_op jit(solution)/shard_map/ppermute | solution.py:37
  139.9 15.1 %collective-permute-start.10 = (bf16[192,128]{1,0:T(8,128)(2,1)S(1)}, bf16[192,128]{1,0:T(8,128)(2,1)S(1)}, u32[]{:S(2)}, u32[]{:S(2)}) collective-permute-start(bf16[192,128]{1,0:T(8,128)(2,1)S(1)} %get-tuple-element.77), channel_id=1, source_target_pairs={{0,3},{1,2},{2,1},{3,0},{4,7},{5,6},{6,5},{7,4},{8,11},{9,10},{10,... | collective-permute-start | bytes 147464 | tf_op jit(solution)/shard_map/ppermute | solution.py:56
  157.8 9.2 %collective-permute-start.12 = (bf16[704,128]{1,0:T(8,128)(2,1)S(1)}, bf16[704,128]{1,0:T(8,128)(2,1)S(1)}, u32[]{:S(2)}, u32[]{:S(2)}) collective-permute-start(bf16[704,128]{1,0:T(8,128)(2,1)S(1)} %get-tuple-element.80), channel_id=1, source_target_pairs={{0,3},{1,2},{2,1},{3,0},{4,7},{5,6},{6,5},{7,4},{8,11},{9,10},{10,... | collective-permute-start | bytes 540680 | tf_op jit(solution)/shard_map/ppermute | solution.py:56
Sparse Core Ops, SparseCore 0:
  22.0 53.2 all-gather.1

commit v5 on v4

--- a/solution.py
+++ b/solution.py
@@ -21,7 +21,7 @@
 RING = 16
 F32 = jnp.float32
 BF16 = jnp.bfloat16
-PARAMS = pltpu.CompilerParams(vmem_limit_bytes=40 * 1024 * 1024)
+PARAMS = pltpu.CompilerParams(vmem_limit_bytes=20 * 1024 * 1024)
 
 
 def pairs_of(target):
@@ -33,8 +33,16 @@
     return pairs
 
 
-def to_sibling(array):
-    return lax.ppermute(array, BOTH, pairs_of(lambda cell, part: (cell ^ 1, part)))
+def with_sibling(array):
+    groups = [[cell, cell + 1] for cell in range(0, 128, 2)]
+    return lax.all_gather(array, "cells", axis=0, tiled=True, axis_index_groups=groups)
+
+
+def to_layer(array, turned):
+    def target(cell, part):
+        return (cell - 1 if part < 2 else cell + 1) % 128, 3 - part if turned else part
+
+    return lax.ppermute(array, BOTH, pairs_of(target))
 
 
 def neighbour_of(cell, part):
@@ -44,12 +52,6 @@
 
 def to_neighbour(array):
     return lax.ppermute(array, BOTH, pairs_of(neighbour_of))
-
-
-def with_neighbour(array):
-    pairs = pairs_of(neighbour_of)
-    groups = [list(pair) for pair in pairs if pair[0] // 4 % 2 == 1]
-    return lax.all_gather(array, BOTH, axis=0, tiled=True, axis_index_groups=groups)
 
 
 def to_mirror(array):
@@ -136,7 +138,9 @@
     return jnp.concatenate([packed, jnp.zeros((EDGE - CHUNK, LANES), F32)], axis=0).astype(BF16)
 
 
-def prepare_kernel(flags, populations, solid, own, own_edge, message, masks, factors):
+def prepare_kernel(
+    flags, populations, solid, own, own_edge, message, straight, turned, masks, factors
+):
     low, block, half = flags[0] == 1, flags[2], flags[3]
     ordered = reordered(order_matrix(low), populations[...])
     left, right = ordered[:, :LANES], ordered[:, LANES:]
@@ -163,17 +167,15 @@
     for index, value in enumerate(near):
         found = jnp.where(place == index, value, found)
     masks[...] = jnp.where(half == 0, found[:, :LANES], found[:, LANES:])
-
-
-def faces_kernel(flags, own, received, masks, sibling, neighbour):
-    same = flags[4] == 1
     row = lax.broadcasted_iota(jnp.int32, (16, LANES), 0)
-    fluid = jnp.where(row == 0, jnp.broadcast_to(masks[0:1, :], (16, LANES)), 0.0).astype(BF16)
-    mine, theirs = own[...], received[:PAD].astype(F32)
-    sibling[:PAD] = jnp.where(same, theirs, mine).astype(BF16)
-    neighbour[:PAD] = jnp.where(same, mine, theirs).astype(BF16)
-    sibling[PAD:] = fluid
-    neighbour[PAD:] = fluid
+    halves = []
+    for side in range(2):
+        cells = slice(LANES * side, LANES * (side + 1))
+        open_cells = jnp.where(row == 0, jnp.broadcast_to(fluid[:1, cells], (16, LANES)), 0.0)
+        halves.append((ordered[:, cells].astype(BF16), open_cells.astype(BF16)))
+    for place, target in ((flags[5], straight), (1 - flags[5], turned)):
+        for rows, low_value, high_value in zip((slice(0, PAD), slice(PAD, PAD + 16)), *halves):
+            target[rows] = jnp.where(place == 0, low_value, high_value)
 
 
 def rows_of(index, size):
@@ -230,102 +232,77 @@
 
 
 def first_kernel(
-    flags, own, own_edge, received, sibling, neighbour, masks_in, factors, lowered, masks_out
+    flags, own, own_edge, received, straight, turned, masks_in, factors, lowered, masks_out
 ):
     same = flags[4] == 1
     place = lax.broadcasted_iota(jnp.int32, (8, LANES), 0)
-    open_near = sibling[PAD:].astype(F32)[:1]
-    open_far = neighbour[PAD:].astype(F32)[:1]
+    open_own = straight[PAD:].astype(F32)[:1]
+    open_other = turned[PAD:].astype(F32)[:1]
     masks = masks_in[...]
-    masks = jnp.where(place == 5, open_near, masks)
-    masks = jnp.where(place == 6, open_far, masks)
+    masks = jnp.where(place == 5, jnp.where(same, open_own, open_other), masks)
+    masks = jnp.where(place == 6, jnp.where(same, open_other, open_own), masks)
     masks_out[...] = masks
     edge_own, edge_other = own_edge[...], received[PAD:].astype(F32)[:CHUNK]
-    edge_near = jnp.where(same, edge_own, edge_other)
-    edge_far = jnp.where(same, edge_other, edge_own)
-    sign_near, sign_far = signs(flags)
-    at_near, at_far = place_of_near(flags)
+    sign = jnp.where(flags[0] == 1, 1.0, -1.0)
+    at_own = pl.multiple_of(PAD * (1 - flags[0]), 16)
+    at_other = pl.multiple_of(PAD * flags[0], 16)
     for part in range(PAD // PART):
         span = rows_of(part, PART)
         mine, theirs = own[span], received[span].astype(F32)
-        near, far = jnp.where(same, mine, theirs), jnp.where(same, theirs, mine)
+        new_own = stream_part(
+            part, sign, mine, theirs, straight[span].astype(F32), edge_own, masks, open_own, factors
+        )
+        new_other = stream_part(
+            part, -sign, theirs, mine, turned[span].astype(F32), edge_other, masks, open_other, factors
+        )
+        lowered[pl.ds(at_own + PART * part, PART)] = new_own.astype(BF16)
+        lowered[pl.ds(at_other + PART * part, PART)] = new_other.astype(BF16)
+
+
+def streamed(flags, near, far, sibling, neighbour, edges, masks, factors):
+    values = masks[...]
+    edge_near, edge_far = (edges[rows_of(i, EDGE)].astype(F32)[:CHUNK] for i in range(2))
+    sign_near, sign_far = signs(flags)
+    start = pl.multiple_of(PAD * flags[1], 16)
+    for part in range(PAD // PART):
+        span = rows_of(part, PART)
+        rows_near, rows_far = near[span], far[span]
+        layer = sibling[pl.ds(start + PART * part, PART)].astype(F32)
         new_near = stream_part(
-            part, sign_near, near, far, sibling[span].astype(F32), edge_near, masks, open_near, factors
-        )
+            part, sign_near, rows_near, rows_far, layer, edge_near, values, values[5:6], factors
+        )
+        layer = neighbour[span].astype(F32)
         new_far = stream_part(
-            part, sign_far, far, near, neighbour[span].astype(F32), edge_far, masks, open_far, factors
-        )
+            part, sign_far, rows_far, rows_near, layer, edge_far, values, values[6:7], factors
+        )
+        yield part, span, new_near, new_far
+
+
+def between_kernel(flags, near, far, sibling, neighbour, edges, masks, factors, *outs):
+    packed = (jnp.zeros((CHUNK, LANES), F32),) * 2
+    for part, span, new_near, new_far in streamed(
+        flags, near, far, sibling, neighbour, edges, masks, factors
+    ):
+        packed = give_rows(flags, part, new_near, new_far, factors, packed, outs[:4])
+    outs[4][:EDGE], outs[4][EDGE:] = edge_block(packed[0]), edge_block(packed[1])
+
+
+def lower_kernel(flags, near, far, sibling, neighbour, edges, masks, factors, lowered):
+    at_near, at_far = place_of_near(flags)
+    for part, span, new_near, new_far in streamed(
+        flags, near, far, sibling, neighbour, edges, masks, factors
+    ):
         lowered[pl.ds(at_near + PART * part, PART)] = new_near.astype(BF16)
         lowered[pl.ds(at_far + PART * part, PART)] = new_far.astype(BF16)
 
 
-def stream_near(flags, near, far, sibling, edges, masks, factors):
-    values = masks[...]
-    edge = edges[:EDGE].astype(F32)[:CHUNK]
-    for part in range(PAD // PART):
-        span = rows_of(part, PART)
-        yield part, span, stream_part(
-            part, signs(flags)[0], near[span], far[span], sibling[span].astype(F32), edge, values,
-            values[5:6], factors,
-        )
-
-
-def stream_far(flags, near, far, neighbour, edges, masks, factors):
-    values = masks[...]
-    edge = edges[EDGE:].astype(F32)[:CHUNK]
-    start = pl.multiple_of(PAD * (1 - flags[1]), 16)
-    for part in range(PAD // PART):
-        span = rows_of(part, PART)
-        layer = neighbour[pl.ds(start + PART * part, PART)].astype(F32)
-        yield part, span, stream_part(
-            part, signs(flags)[1], far[span], near[span], layer, edge, values, values[6:7], factors
-        )
-
-
-def between_near_kernel(flags, near, far, sibling, edges, masks, factors, rows_out, sent, packed_out):
-    packed = jnp.zeros((CHUNK, LANES), F32)
-    for part, span, rows in stream_near(flags, near, far, sibling, edges, masks, factors):
-        rows_out[span] = rows
-        sent[span] = rows.astype(BF16)
-        packed = pack_part(packed, part, signs(flags)[0], rows, factors)
-    packed_out[...] = edge_block(packed)
-
-
-def between_far_kernel(
-    flags, near, far, neighbour, edges, masks, factors, packed_near, rows_out, sent, packed_out
-):
-    packed = jnp.zeros((CHUNK, LANES), F32)
-    for part, span, rows in stream_far(flags, near, far, neighbour, edges, masks, factors):
-        rows_out[span] = rows
-        sent[span] = rows.astype(BF16)
-        packed = pack_part(packed, part, signs(flags)[1], rows, factors)
-    packed_out[:EDGE] = packed_near[...]
-    packed_out[EDGE:] = edge_block(packed)
-
-
-def lower_near_kernel(flags, near, far, sibling, edges, masks, factors, lowered):
-    for _, span, rows in stream_near(flags, near, far, sibling, edges, masks, factors):
-        lowered[span] = rows.astype(BF16)
-
-
-def lower_far_kernel(flags, near, far, neighbour, edges, masks, factors, low_near, lowered):
-    at_near, at_far = place_of_near(flags)
-    for part, span, rows in stream_far(flags, near, far, neighbour, edges, masks, factors):
-        lowered[pl.ds(at_far + PART * part, PART)] = rows.astype(BF16)
-        lowered[pl.ds(at_near + PART * part, PART)] = low_near[span]
-
-
-def last_near_kernel(flags, near, far, sibling, edges, masks, factors, rows_out):
-    for _, span, rows in stream_near(flags, near, far, sibling, edges, masks, factors):
-        rows_out[span] = rows
-
-
-def last_far_kernel(flags, near, far, neighbour, edges, masks, factors, new_near, kept, message):
+def last_kernel(flags, near, far, sibling, neighbour, edges, masks, factors, kept, message):
     same = flags[4] == 1
-    for _, span, rows in stream_far(flags, near, far, neighbour, edges, masks, factors):
-        done = new_near[span]
-        kept[span] = jnp.where(same, done, rows)
-        message[span] = jnp.where(same, rows, done).astype(BF16)
+    for part, span, new_near, new_far in streamed(
+        flags, near, far, sibling, neighbour, edges, masks, factors
+    ):
+        kept[span] = jnp.where(same, new_near, new_far)
+        message[span] = jnp.where(same, new_far, new_near).astype(BF16)
 
 
 def dot(left, right):
@@ -346,11 +323,9 @@
         rows_out[span] = own_product(parts, 0, first, span) + own_product(parts, 1, second, span)
 
 
-def give_rows(flags, part, own, partner, factors, packed, outs):
+def give_rows(flags, part, rows_near, rows_far, factors, packed, outs):
     near, far, to_other_core, to_neighbour_chip = outs
-    same = flags[4] == 1
     span = rows_of(part, PART)
-    rows_near, rows_far = jnp.where(same, own, partner), jnp.where(same, partner, own)
     near[span], far[span] = rows_near, rows_far
     to_neighbour_chip[span] = rows_near.astype(BF16)
     to_other_core[span] = rows_far.astype(BF16)
@@ -359,6 +334,12 @@
         pack_part(packed[0], part, sign_near, rows_near, factors),
         pack_part(packed[1], part, sign_far, rows_far, factors),
     )
+
+
+def give_product(flags, part, own, partner, factors, packed, outs):
+    same = flags[4] == 1
+    near, far = jnp.where(same, own, partner), jnp.where(same, partner, own)
+    return give_rows(flags, part, near, far, factors, packed, outs)
 
 
 def collide_partner_kernel(flags, own, matrix, lowered, other, factors, *outs):
@@ -369,7 +350,7 @@
     for part in range(PAD // PART):
         span = rows_of(part, PART)
         partner = dot(matrix[span], first) + dot(matrix[PAD + PART * part : PAD + PART * (part + 1)], second)
-        packed = give_rows(flags, part, own[span], partner, factors, packed, outs[:4])
+        packed = give_product(flags, part, own[span], partner, factors, packed, outs[:4])
     outs[4][:EDGE], outs[4][EDGE:] = edge_block(packed[0]), edge_block(packed[1])
 
 
@@ -402,7 +383,9 @@
     packed = (jnp.zeros((CHUNK, LANES), F32),) * 2
     for part in range(PAD // PART):
         span = rows_of(part, PART)
-        packed = give_rows(flags, part, total_own[span], total_partner[span], factors, packed, outs[:4])
+        packed = give_product(
+            flags, part, total_own[span], total_partner[span], factors, packed, outs[:4]
+        )
     outs[4][:EDGE], outs[4][EDGE:] = edge_block(packed[0]), edge_block(packed[1])
 
 
@@ -449,7 +432,10 @@
     core, z = cell % 2, cell // 2 % 8
     block = jnp.minimum(vel, 3 - vel)
     half = (1 - low) ^ (cell // RING % 2)
-    flags = jnp.stack([low, 1 - core, block, half, (low != core).astype(jnp.int32)])
+    needing = (cell + 1 - 2 * low) % 128
+    straight_half = (1 - low) ^ (needing // RING % 2)
+    same = (low != core).astype(jnp.int32)
+    flags = jnp.stack([low, 1 - core, block, half, same, straight_half])
     flags = flags.astype(jnp.int32)
 
     row = CHUNK * z + lax.iota(jnp.int32, CHUNK)
@@ -463,9 +449,10 @@
 
     padded = jnp.pad(populations[:, 0, :], ((0, PAD - ROWS), (0, 0)))
     rows = (PAD, LANES)
-    own, own_edge, message, masks, factors = call(
+    own, own_edge, message, straight, turned, masks, factors = call(
         prepare_kernel,
-        [(rows, F32), ((CHUNK, LANES), F32), ((PAD + EDGE, LANES), BF16), ((8, LANES), F32), ((3, *rows), F32)],
+        [(rows, F32), ((CHUNK, LANES), F32), ((PAD + EDGE, LANES), BF16),
+         ((PAD + 16, LANES), BF16), ((PAD + 16, LANES), BF16), ((8, LANES), F32), ((3, *rows), F32)],
         flags, padded, solid_mask, flops=2 * 3 * PAD * PAD * 256,
     )
     piece, _ = lax.optimization_barrier((piece, message))
@@ -473,10 +460,8 @@
         [(line * 8 + step) * 2 + side for side in range(2) for step in range(8)] for line in range(8)
     ]
     partner_matrix = lax.all_gather(piece, "cells", axis=0, tiled=True, axis_index_groups=groups)
+    straight, turned = to_layer(straight, False), to_layer(turned, True)
     received = to_mirror(message)
-    faces = [((PAD + 16, LANES), BF16)] * 2
-    sibling, neighbour = call(faces_kernel, faces, flags, own, received, masks)
-    neighbour, sibling = to_neighbour(neighbour), to_sibling(sibling)
 
     row = lax.iota(jnp.int32, PAD)
     wanted = jnp.where(row < ROWS, jnp.where(low == 1, row, ROWS - 1 - row), -1)
@@ -486,14 +471,14 @@
     lowered, masks = call(
         first_kernel,
         [((2 * PAD, LANES), BF16), ((8, LANES), F32)],
-        flags, own, own_edge, received, sibling, neighbour, masks, factors, flops=100 * PAD * 256,
+        flags, own, own_edge, received, straight, turned, masks, factors, flops=100 * PAD * 256,
     )
     lowered, ordered = lax.optimization_barrier((lowered, ordered))
     matrix = *column_half(ordered, 0), *column_half(ordered, 1)
     edges_shape = ((2 * EDGE, LANES), BF16)
     sends = [(rows, F32)] * 2 + [(rows, BF16)] * 2 + [edges_shape]
     multiply = 2 * PAD * 4 * PAD * LANES
-    work = 60 * PAD * LANES
+    work = 100 * PAD * LANES
 
     other = to_side(lowered)
     (own,) = call(collide_kernel, [(rows, F32)], flags, *matrix, lowered, other, flops=multiply)
@@ -503,25 +488,16 @@
     )
 
     for step in range(1, STEPS):
-        neighbour = with_neighbour(for_neighbour)
-        sibling, edges = to_sibling(for_sibling), to_mirror(edges)
-        new_near, for_neighbour, packed = call(
-            between_near_kernel, [(rows, F32), (rows, BF16), ((EDGE, LANES), BF16)],
-            flags, near, far, sibling, edges, masks, factors, flops=work,
-        )
-        new_far, for_sibling, new_edges = call(
-            between_far_kernel, [(rows, F32), (rows, BF16), edges_shape],
-            flags, near, far, neighbour, edges, masks, factors, packed, flops=work,
-        )
-        near, far, edges = new_near, new_far, new_edges
-        neighbour = with_neighbour(for_neighbour)
-        sibling, edges = to_sibling(for_sibling), to_mirror(edges)
-        (low_near,) = call(
-            lower_near_kernel, [(rows, BF16)], flags, near, far, sibling, edges, masks, factors, flops=work
-        )
+        neighbour, edges = to_neighbour(for_neighbour), to_mirror(edges)
+        sibling = with_sibling(for_sibling)
+        near, far, for_sibling, for_neighbour, edges = call(
+            between_kernel, sends, flags, near, far, sibling, neighbour, edges, masks, factors, flops=work
+        )
+        neighbour, edges = to_neighbour(for_neighbour), to_mirror(edges)
+        sibling = with_sibling(for_sibling)
         (lowered,) = call(
-            lower_far_kernel, [((2 * PAD, LANES), BF16)],
-            flags, near, far, neighbour, edges, masks, factors, low_near, flops=work,
+            lower_kernel, [((2 * PAD, LANES), BF16)],
+            flags, near, far, sibling, neighbour, edges, masks, factors, flops=work,
         )
         other = to_side(lowered)
         early = call(
@@ -532,14 +508,11 @@
             flops=multiply, scratch=[(rows, F32)] * 2,
         )
 
-    neighbour = with_neighbour(for_neighbour)
-    sibling, edges = to_sibling(for_sibling), to_mirror(edges)
-    (new_near,) = call(
-        last_near_kernel, [(rows, F32)], flags, near, far, sibling, edges, masks, factors, flops=work
-    )
+    neighbour, edges = to_neighbour(for_neighbour), to_mirror(edges)
+    sibling = with_sibling(for_sibling)
     kept, message = call(
-        last_far_kernel, [(rows, F32), (rows, BF16)],
-        flags, near, far, neighbour, edges, masks, factors, new_near, flops=work,
+        last_kernel, [(rows, F32), (rows, BF16)],
+        flags, near, far, sibling, neighbour, edges, masks, factors, flops=work,
     )
     received = to_mirror(message)
     (kept,) = call(reorder_kernel, [(rows, F32)], flags, kept, flops=2 * 3 * PAD * PAD * LANES)

time: 177 us -> 166 us (0.938)
  the two profiles are of different devices: /device:TPU:24 before, /device:TPU:8 now
where the time goes in v5:
time: 166 us; the launch traced here: 165 us
  starting transfers between devices  60.6 us (37%)
  waiting for transfers between devices  38.4 us (23%)
  Pallas kernels  22.4 us (13%)
  between operations  13.9 us (8%)
  matrix products  13 us (8%)
  local copies, waits for them, and re-layouts  10.3 us (6%)
  blocking collectives  6.32 us (4%)
    pallas_call x11, Pallas kernels, call(): pl.pallas_call(kernel, out_shape=[jax.ShapeDtypeStruct(shape, dtype) for...  22.4 us
    ppermute x3, starting transfers between devices, to_neighbour(): return lax.ppermute(array, BOTH, pairs_of(neighbour_of))  21.8 us
    ppermute x6, waiting for transfers between devices, to_mirror(): return lax.ppermute(array, 'vel', [(i, 3 - i) for i in range(4)])  18.1 us
    ppermute x6, starting transfers between devices, to_mirror(): return lax.ppermute(array, 'vel', [(i, 3 - i) for i in range(4)])  17.8 us
    ppermute x2, starting transfers between devices, to_layer(): return lax.ppermute(array, BOTH, pairs_of(target))  16.2 us
    dot_general x8, matrix products, chosen(): return jnp.dot(left, right, preferred_element_type=BF16)  13 us
    ppermute x2, waiting for transfers between devices, to_side(): return lax.ppermute(array, 'vel', [(i, i ^ 1) for i in range(4)])  9.12 us
    unnamed x31, local copies, waits for them, and re-layouts  8.3 us
  transfers between devices with their start and end apart: 14, of which 11 were waited for; matrix products, arithmetic and copies ran while one was open for 7% of the time, Pallas kernels for 6%

profile of v5, /device:TPU:8, one launch (start us, length us, event | category | flops | bytes accessed | tf_op | source)
XLA Modules:
  0.0 165.1 jit_solution(13137363219693138120)
XLA Ops:
  9.4 3.5 %collective-permute-start.3 = (bf16[88,1408]{1,0:T(8,128)(2,1)S(1)}, bf16[88,1408]{1,0:T(8,128)(2,1)S(1)}, u32[]{:S(2)}, u32[]{:S(2)}) collective-permute-start(bf16[88,1408]{1,0:T(8,128)(2,1)S(1)} %pad_maximum_fusion), channel_id=1, source_target_pairs={{0,3},{1,2},{2,1},{3,0},{4,7},{5,6},{6,5},{7,4},{8,11},{9,10},{10,... | collective-permute-start | bytes 743432 | tf_op jit(solution)/shard_map/ppermute | solution.py:58
  13.3 2.0 %shard_map.37 = (f32[704,128]{1,0:T(8,128)S(1)}, f32[88,128]{1,0:T(8,128)S(1)}, bf16[800,128]{1,0:T(8,128)(2,1)S(1)}, bf16[720,128]{1,0:T(8,128)(2,1)S(1)}, bf16...) custom-call(s32[6]{0:T(128)S(1)} %stack.31.flags, f32[704,256]{1,0:T(8,128)S(1)} %pad.13.populations, ...), custom_call_target="tpu_custom_call" | custom-call | flops 761266176 | bytes 2786304 | tf_op jit(solution)/shard_map/pallas_call | solution.py:69
  15.3 11.3 %collective-permute-done.3 = bf16[88,1408]{1,0:T(8,128)(2,1)S(1)} collective-permute-done((bf16[88,1408]{1,0:T(8,128)(2,1)S(1)}, bf16[88,1408]{1,0:T(8,128)(2,1)S(1)}, u32[]{:S(2)}, u32[]{:S(2)}) %collective-permute-start.3) | collective-permute-done | bytes 247840 | tf_op jit(solution)/shard_map/ppermute | solution.py:58
  29.2 14.3 %collective-permute-start.1 = (bf16[720,128]{1,0:T(8,128)(2,1)S(1)}, bf16[720,128]{1,0:T(8,128)(2,1)S(1)}, u32[]{:S(2)}, u32[]{:S(2)}) collective-permute-start(bf16[720,128]{1,0:T(8,128)(2,1)S(1)} %get-tuple-element.47), channel_id=1, source_target_pairs={{0,508},{1,509},{2,6},{3,7},{4,0},{5,1},{6,10},{7,11},{8,4},{9,5},... | collective-permute-start | bytes 552968 | tf_op jit(solution)/shard_map/ppermute | solution.py:45
  43.5 1.9 %collective-permute-start.2 = (bf16[720,128]{1,0:T(8,128)(2,1)S(1)}, bf16[720,128]{1,0:T(8,128)(2,1)S(1)}, u32[]{:S(2)}, u32[]{:S(2)}) collective-permute-start(bf16[720,128]{1,0:T(8,128)(2,1)S(1)} %get-tuple-element.48), channel_id=1, source_target_pairs={{0,511},{1,510},{2,5},{3,4},{4,3},{5,2},{6,9},{7,8},{8,7},{9,6},{1... | collective-permute-start | bytes 552968 | tf_op jit(solution)/shard_map/ppermute | solution.py:45
  45.5 5.4 %fusion.6 = bf16[704,2744]{1,0:T(8,128)(2,1)S(1)} fusion(bf16[686,2744]{1,0:T(8,128)(2,1)} %param.5, s32[704]{0:T(1024)S(1)} %select_select_fusion), kind=kOutput, calls=%fused_computation.13 | convolution fusion | flops 2650879488 | bytes 7631136 | tf_op jit(solution)/shard_map/dot_general | solution.py:410
  51.3 6.5 %collective-permute-done.2.turned = bf16[720,128]{1,0:T(8,128)(2,1)S(1)} collective-permute-done((bf16[720,128]{1,0:T(8,128)(2,1)S(1)}, bf16[720,128]{1,0:T(8,128)(2,1)S(1)}, u32[]{:S(2)}, u32[]{:S(2)}) %collective-permute-start.2) | collective-permute-done | bytes 184352 | tf_op jit(solution)/shard_map/ppermute | solution.py:45
  57.7 2.2 %shard_map.38 = (bf16[1408,128]{1,0:T(8,128)(2,1)S(1)}, f32[8,128]{1,0:T(8,128)S(1)}) custom-call(s32[6]{0:T(128)S(1)} %stack.31.flags, f32[704,128]{1,0:T(8,128)S(1)} %get-tuple-element.43.own, f32[88,128]{1,0:T(8,128)S(1)} %get-tuple-element.44.own_edge, bf16[800,128]{1,0:T(8,128)(2,1)S(1)} %collective-permute-done.received, ...), custom_call_target="tpu_custom_call" | custom-call | flops 18022400 | bytes 2428928 | tf_op jit(solution)/shard_map/pallas_call | solution.py:69
  60.0 2.1 %collective-permute-start.4 = (bf16[1408,128]{1,0:T(8,128)(2,1)S(1)}, bf16[1408,128]{1,0:T(8,128)(2,1)S(1)}, u32[]{:S(2)}, u32[]{:S(2)}) collective-permute-start(bf16[1408,128]{1,0:T(8,128)(2,1)S(1)} %get-tuple-element.56.lowered), channel_id=1, source_target_pairs={{0,1},{1,0},{2,3},{3,2},{4,5},{5,4},{6,7},{7,6},{8,9},{9,8},{10,11... | collective-permute-start | bytes 1081352 | tf_op jit(solution)/shard_map/ppermute | solution.py:62
  67.0 2.3 %collective-permute-done.4.other = bf16[1408,128]{1,0:T(8,128)(2,1)S(1)} collective-permute-done((bf16[1408,128]{1,0:T(8,128)(2,1)S(1)}, bf16[1408,128]{1,0:T(8,128)(2,1)S(1)}, u32[]{:S(2)}, u32[]{:S(2)}) %collective-permute-start.4) | collective-permute-done | bytes 360480 | tf_op jit(solution)/shard_map/ppermute | solution.py:62
  73.6 2.0 %all-gather.2.cloned.1.call-done.matrix = bf16[1408,1408]{1,0:T(8,128)(2,1)} async-done(((bf16[88,1408]{1,0:T(8,128)(2,1)}), bf16[1408,1408]{1,0:T(8,128)(2,1)}) %all-gather.2.cloned.1.call-update) | async-done | bytes 3964944 | tf_op jit(solution)/shard_map/all_gather | solution.py:462
  75.7 2.1 %copy-done = bf16[1408,1408]{1,0:T(8,128)(2,1)S(1)} copy-done((bf16[1408,1408]{1,0:T(8,128)(2,1)S(1)}, bf16[1408,1408]{1,0:T(8,128)(2,1)}, u32[]{:S(2)}) %copy-start) | copy-done | bytes 3964952
  80.7 2.0 %shard_map.40 = (f32[704,128]{1,0:T(8,128)S(1)}, f32[704,128]{1,0:T(8,128)S(1)}, bf16[704,128]{1,0:T(8,128)(2,1)S(1)}, bf16[704,128]{1,0:T(8,128)(2,1)S(1)}, bf16[192,128]{1,0:T(8,128)(2,1)S(1)}) custom-call(s32[6]{0:T(128)S(1)} %stack.31.flags, f32[704,128]{1,0:T(8,128)S(1)} %copy-done.11, bf16[1408,1408]{1,0:T(8,128)(2,1)S(1)} %copy-done, ...), custom_call_target="tpu_custom_call" | custom-call | flops 507510784 | bytes 7258112 | tf_op jit(solution)/shard_map/pallas_call | solution.py:69
  82.7 8.8 %collective-permute-start.5 = (bf16[704,128]{1,0:T(8,128)(2,1)S(1)}, bf16[704,128]{1,0:T(8,128)(2,1)S(1)}, u32[]{:S(2)}, u32[]{:S(2)}) collective-permute-start(bf16[704,128]{1,0:T(8,128)(2,1)S(1)} %get-tuple-element.62), channel_id=1, source_target_pairs={{0,511},{1,510},{2,509},{3,508},{4,8},{5,9},{6,10},{7,11},{8,4},{9... | collective-permute-start | bytes 540680 | tf_op jit(solution)/shard_map/ppermute | solution.py:54
  91.5 3.3 %collective-permute-start.6 = (bf16[192,128]{1,0:T(8,128)(2,1)S(1)}, bf16[192,128]{1,0:T(8,128)(2,1)S(1)}, u32[]{:S(2)}, u32[]{:S(2)}) collective-permute-start(bf16[192,128]{1,0:T(8,128)(2,1)S(1)} %get-tuple-element.63), channel_id=1, source_target_pairs={{0,3},{1,2},{2,1},{3,0},{4,7},{5,6},{6,5},{7,4},{8,11},{9,10},{10,... | collective-permute-start | bytes 147464 | tf_op jit(solution)/shard_map/ppermute | solution.py:58
  94.8 2.2 %all_gather.13.sibling = bf16[1408,128]{1,0:T(8,128)(2,1)S(1)} all-gather(bf16[704,128]{1,0:T(8,128)(2,1)S(1)} %get-tuple-element.61), channel_id=1, replica_groups={{0,4},{8,12},{16,20},{24,28},{32,36},{40,44},{48,52},{56,60},{64,68},{7..., dimensions={0}, use_global_device_ids=true | all-gather | bytes 540672 | tf_op jit(solution)/shard_map/all_gather | solution.py:38
  97.5 2.6 %shard_map.41 = (f32[704,128]{1,0:T(8,128)S(1)}, f32[704,128]{1,0:T(8,128)S(1)}, bf16[704,128]{1,0:T(8,128)(2,1)S(1)}, bf16[704,128]{1,0:T(8,128)(2,1)S(1)}, bf16[192,128]{1,0:T(8,128)(2,1)S(1)}) custom-call(s32[6]{0:T(128)S(1)} %stack.31.flags, f32[704,128]{1,0:T(8,128)S(1)} %get-tuple-element.59.near, f32[704,128]{1,0:T(8,128)S(1)} %get-tuple-element.60.far, ...), custom_call_target="tpu_custom_call" | custom-call | flops 9011200 | bytes 3526656 | tf_op jit(solution)/shard_map/pallas_call | solution.py:69
  100.1 8.0 %collective-permute-start.7 = (bf16[704,128]{1,0:T(8,128)(2,1)S(1)}, bf16[704,128]{1,0:T(8,128)(2,1)S(1)}, u32[]{:S(2)}, u32[]{:S(2)}) collective-permute-start(bf16[704,128]{1,0:T(8,128)(2,1)S(1)} %get-tuple-element.68), channel_id=1, source_target_pairs={{0,511},{1,510},{2,509},{3,508},{4,8},{5,9},{6,10},{7,11},{8,4},{9... | collective-permute-start | bytes 540680 | tf_op jit(solution)/shard_map/ppermute | solution.py:54
  108.2 3.3 %collective-permute-start.8 = (bf16[192,128]{1,0:T(8,128)(2,1)S(1)}, bf16[192,128]{1,0:T(8,128)(2,1)S(1)}, u32[]{:S(2)}, u32[]{:S(2)}) collective-permute-start(bf16[192,128]{1,0:T(8,128)(2,1)S(1)} %get-tuple-element.69), channel_id=1, source_target_pairs={{0,3},{1,2},{2,1},{3,0},{4,7},{5,6},{6,5},{7,4},{8,11},{9,10},{10,... | collective-permute-start | bytes 147464 | tf_op jit(solution)/shard_map/ppermute | solution.py:58
  111.5 2.1 %all_gather.14.sibling = bf16[1408,128]{1,0:T(8,128)(2,1)S(1)} all-gather(bf16[704,128]{1,0:T(8,128)(2,1)S(1)} %get-tuple-element.67), channel_id=1, replica_groups={{0,4},{8,12},{16,20},{24,28},{32,36},{40,44},{48,52},{56,60},{64,68},{7..., dimensions={0}, use_global_device_ids=true | all-gather | bytes 540672 | tf_op jit(solution)/shard_map/all_gather | solution.py:38
  114.3 2.2 %shard_map.42.lowered = bf16[1408,128]{1,0:T(8,128)(2,1)S(1)} custom-call(s32[6]{0:T(128)S(1)} %stack.31.flags, f32[704,128]{1,0:T(8,128)S(1)} %get-tuple-element.65.near, f32[704,128]{1,0:T(8,128)S(1)} %get-tuple-element.66.far, bf16[1408,128]{1,0:T(8,128)(2,1)S(1)} %all_gather.14.sibling, bf16[704,128]{1,0:T(8,128)(2,1)S(1)} %collective-permute-done.7.neighbour, ...), custom_call_target="tpu_custom_call" | custom-call | flops 9011200 | bytes 2756608 | tf_op jit(solution)/shard_map/pallas_call | solution.py:69
  116.5 2.7 %collective-permute-start.9 = (bf16[1408,128]{1,0:T(8,128)(2,1)S(1)}, bf16[1408,128]{1,0:T(8,128)(2,1)S(1)}, u32[]{:S(2)}, u32[]{:S(2)}) collective-permute-start(bf16[1408,128]{1,0:T(8,128)(2,1)S(1)} %shard_map.42.lowered), channel_id=1, source_target_pairs={{0,1},{1,0},{2,3},{3,2},{4,5},{5,4},{6,7},{7,6},{8,9},{9,8},{10,11... | collective-permute-start | bytes 1081352 | tf_op jit(solution)/shard_map/ppermute | solution.py:62
  119.2 2.1 %shard_map.43 = (f32[704,128]{1,0:T(8,128)S(1)}, f32[704,128]{1,0:T(8,128)S(1)}) custom-call(s32[6]{0:T(128)S(1)} %stack.31.flags, bf16[704,704]{1,0:T(8,128)(2,1)S(1)} %copy-done.3, bf16[704,704]{1,0:T(8,128)(2,1)S(1)} %fusion.m1, bf16[704,704]{1,0:T(8,128)(2,1)S(1)} %fusion.4.m2, bf16[704,704]{1,0:T(8,128)(2,1)S(1)} %copy-done.5, ...), custom_call_target="tpu_custom_call" | custom-call | flops 507510784 | bytes 9011200 | tf_op jit(solution)/shard_map/pallas_call | solution.py:69
  121.4 6.8 %collective-permute-done.9.other = bf16[1408,128]{1,0:T(8,128)(2,1)S(1)} collective-permute-done((bf16[1408,128]{1,0:T(8,128)(2,1)S(1)}, bf16[1408,128]{1,0:T(8,128)(2,1)S(1)}, u32[]{:S(2)}, u32[]{:S(2)}) %collective-permute-start.9) | collective-permute-done | bytes 360480 | tf_op jit(solution)/shard_map/ppermute | solution.py:62
  128.1 2.5 %shard_map.44 = (f32[704,128]{1,0:T(8,128)S(1)}, f32[704,128]{1,0:T(8,128)S(1)}, bf16[704,128]{1,0:T(8,128)(2,1)S(1)}, bf16[704,128]{1,0:T(8,128)(2,1)S(1)}, bf16[192,128]{1,0:T(8,128)(2,1)S(1)}) custom-call(s32[6]{0:T(128)S(1)} %stack.31.flags, bf16[704,704]{1,0:T(8,128)(2,1)S(1)} %copy-done.3, bf16[704,704]{1,0:T(8,128)(2,1)S(1)} %fusion.m1, ...), custom_call_target="tpu_custom_call" | custom-call | flops 507510784 | bytes 11223040 | tf_op jit(solution)/shard_map/pallas_call | solution.py:69
  130.6 5.0 %collective-permute-start.10 = (bf16[704,128]{1,0:T(8,128)(2,1)S(1)}, bf16[704,128]{1,0:T(8,128)(2,1)S(1)}, u32[]{:S(2)}, u32[]{:S(2)}) collective-permute-start(bf16[704,128]{1,0:T(8,128)(2,1)S(1)} %get-tuple-element.75), channel_id=1, source_target_pairs={{0,511},{1,510},{2,509},{3,508},{4,8},{5,9},{6,10},{7,11},{8,4},{9... | collective-permute-start | bytes 540680 | tf_op jit(solution)/shard_map/ppermute | solution.py:54
  135.6 3.3 %collective-permute-start.11 = (bf16[192,128]{1,0:T(8,128)(2,1)S(1)}, bf16[192,128]{1,0:T(8,128)(2,1)S(1)}, u32[]{:S(2)}, u32[]{:S(2)}) collective-permute-start(bf16[192,128]{1,0:T(8,128)(2,1)S(1)} %get-tuple-element.76), channel_id=1, source_target_pairs={{0,3},{1,2},{2,1},{3,0},{4,7},{5,6},{6,5},{7,4},{8,11},{9,10},{10,... | collective-permute-start | bytes 147464 | tf_op jit(solution)/shard_map/ppermute | solution.py:58
  138.9 2.1 %all_gather.15.sibling = bf16[1408,128]{1,0:T(8,128)(2,1)S(1)} all-gather(bf16[704,128]{1,0:T(8,128)(2,1)S(1)} %get-tuple-element.74), channel_id=1, replica_groups={{0,4},{8,12},{16,20},{24,28},{32,36},{40,44},{48,52},{56,60},{64,68},{7..., dimensions={0}, use_global_device_ids=true | all-gather | bytes 540672 | tf_op jit(solution)/shard_map/all_gather | solution.py:38
  142.1 2.5 %collective-permute-done.10.neighbour = bf16[704,128]{1,0:T(8,128)(2,1)S(1)} collective-permute-done((bf16[704,128]{1,0:T(8,128)(2,1)S(1)}, bf16[704,128]{1,0:T(8,128)(2,1)S(1)}, u32[]{:S(2)}, u32[]{:S(2)}) %collective-permute-start.10) | collective-permute-done | bytes 180256 | tf_op jit(solution)/shard_map/ppermute | solution.py:54
  144.7 2.3 %shard_map.45 = (f32[704,128]{1,0:T(8,128)S(1)}, bf16[704,128]{1,0:T(8,128)(2,1)S(1)}) custom-call(s32[6]{0:T(128)S(1)} %stack.31.flags, f32[704,128]{1,0:T(8,128)S(1)} %get-tuple-element.72.near, f32[704,128]{1,0:T(8,128)S(1)} %get-tuple-element.73.far, bf16[1408,128]{1,0:T(8,128)(2,1)S(1)} %all_gather.15.sibling, ...), custom_call_target="tpu_custom_call" | custom-call | flops 9011200 | bytes 2936832 | tf_op jit(solution)/shard_map/pallas_call | solution.py:69
  147.0 2.5 %collective-permute-start.12 = (bf16[704,128]{1,0:T(8,128)(2,1)S(1)}, bf16[704,128]{1,0:T(8,128)(2,1)S(1)}, u32[]{:S(2)}, u32[]{:S(2)}) collective-permute-start(bf16[704,128]{1,0:T(8,128)(2,1)S(1)} %get-tuple-element.78), channel_id=1, source_target_pairs={{0,3},{1,2},{2,1},{3,0},{4,7},{5,6},{6,5},{7,4},{8,11},{9,10},{10,... | collective-permute-start | bytes 540680 | tf_op jit(solution)/shard_map/ppermute | solution.py:58
  151.1 4.6 %collective-permute-done.12.received = bf16[704,128]{1,0:T(8,128)(2,1)S(1)} collective-permute-done((bf16[704,128]{1,0:T(8,128)(2,1)S(1)}, bf16[704,128]{1,0:T(8,128)(2,1)S(1)}, u32[]{:S(2)}, u32[]{:S(2)}) %collective-permute-start.12) | collective-permute-done | bytes 180256 | tf_op jit(solution)/shard_map/ppermute | solution.py:58
  (63 shorter events, 24.6 us)
Async XLA Ops:
  6.5 6.5 %copy-start.13 = (f32[686,1,256]{2,1,0:T(1,128)S(1)}, f32[686,1,256]{2,1,0:T(1,128)}, u32[]{:S(2)}) copy-start(f32[686,1,256]{2,1,0:T(1,128)} %param.3) | copy-start | bytes 2107396
  6.5 69.1 %all-gather.2.cloned.1.call-start = ((), (), s32[]{:S(2)}) async-start(), calls=%async_computation | async-start | bytes 4212736 | tf_op jit(solution)/shard_map/all_gather | solution.py:462
  8.7 4.5 %copy-start.12 = (s32[1,256]{1,0:T(1,128)S(1)}, s32[1,256]{1,0:T(1,128)}, u32[]{:S(2)}) copy-start(s32[1,256]{1,0:T(1,128)} %solid.1) | copy-start | bytes 3076
  9.4 17.1 %collective-permute-start.3 = (bf16[88,1408]{1,0:T(8,128)(2,1)S(1)}, bf16[88,1408]{1,0:T(8,128)(2,1)S(1)}, u32[]{:S(2)}, u32[]{:S(2)}) collective-permute-start(bf16[88,1408]{1,0:T(8,128)(2,1)S(1)} %pad_maximum_fusion), channel_id=1, source_target_pairs={{0,3},{1,2},{2,1},{3,0},{4,7},{5,6},{6,5},{7,4},{8,11},{9,10},{10,... | collective-permute-start | bytes 743432 | tf_op jit(solution)/shard_map/ppermute | solution.py:58
  26.6 0.7 copy-start.14
  27.3 18.2 %collective-permute-start = (bf16[800,128]{1,0:T(8,128)(2,1)S(1)}, bf16[800,128]{1,0:T(8,128)(2,1)S(1)}, u32[]{:S(2)}, u32[]{:S(2)}) collective-permute-start(bf16[800,128]{1,0:T(8,128)(2,1)S(1)} %get-tuple-element.45), channel_id=1, source_target_pairs={{0,3},{1,2},{2,1},{3,0},{4,7},{5,6},{6,5},{7,4},{8,11},{9,10},{10,... | collective-permute-start | bytes 614408 | tf_op jit(solution)/shard_map/ppermute | solution.py:58
  29.2 22.0 %collective-permute-start.1 = (bf16[720,128]{1,0:T(8,128)(2,1)S(1)}, bf16[720,128]{1,0:T(8,128)(2,1)S(1)}, u32[]{:S(2)}, u32[]{:S(2)}) collective-permute-start(bf16[720,128]{1,0:T(8,128)(2,1)S(1)} %get-tuple-element.47), channel_id=1, source_target_pairs={{0,508},{1,509},{2,6},{3,7},{4,0},{5,1},{6,10},{7,11},{8,4},{9,5},... | collective-permute-start | bytes 552968 | tf_op jit(solution)/shard_map/ppermute | solution.py:45
  43.5 14.2 %collective-permute-start.2 = (bf16[720,128]{1,0:T(8,128)(2,1)S(1)}, bf16[720,128]{1,0:T(8,128)(2,1)S(1)}, u32[]{:S(2)}, u32[]{:S(2)}) collective-permute-start(bf16[720,128]{1,0:T(8,128)(2,1)S(1)} %get-tuple-element.48), channel_id=1, source_target_pairs={{0,511},{1,510},{2,5},{3,4},{4,3},{5,2},{6,9},{7,8},{8,7},{9,6},{1... | collective-permute-start | bytes 552968 | tf_op jit(solution)/shard_map/ppermute | solution.py:45
  60.0 9.3 %copy-start.6 = (bf16[1408,128]{1,0:T(8,128)(2,1)}, bf16[1408,128]{1,0:T(8,128)(2,1)S(1)}, u32[]{:S(2)}) copy-start(bf16[1408,128]{1,0:T(8,128)(2,1)S(1)} %get-tuple-element.56.lowered) | copy-start | bytes 1081348
  60.0 9.3 %collective-permute-start.4 = (bf16[1408,128]{1,0:T(8,128)(2,1)S(1)}, bf16[1408,128]{1,0:T(8,128)(2,1)S(1)}, u32[]{:S(2)}, u32[]{:S(2)}) collective-permute-start(bf16[1408,128]{1,0:T(8,128)(2,1)S(1)} %get-tuple-element.56.lowered), channel_id=1, source_target_pairs={{0,1},{1,0},{2,3},{3,2},{4,5},{5,4},{6,7},{7,6},{8,9},{9,8},{10,11... | collective-permute-start | bytes 1081352 | tf_op jit(solution)/shard_map/ppermute | solution.py:62
  65.6 3.7 %copy-start.2 = (bf16[704,704]{1,0:T(8,128)(2,1)}, bf16[704,704]{1,0:T(8,128)(2,1)S(1)}, u32[]{:S(2)}) copy-start(bf16[704,704]{1,0:T(8,128)(2,1)S(1)} %fusion.3.m0) | copy-start | bytes 2973700
  71.2 1.0 copy-start.4
  72.2 0.7 copy-start.8
  72.9 0.7 copy-start.10
  75.7 2.1 %copy-start = (bf16[1408,1408]{1,0:T(8,128)(2,1)S(1)}, bf16[1408,1408]{1,0:T(8,128)(2,1)}, u32[]{:S(2)}) copy-start(bf16[1408,1408]{1,0:T(8,128)(2,1)} %all-gather.2.cloned.1.call-done.matrix) | copy-start | bytes 11894788
  77.8 1.0 copy-start.7
  78.8 1.0 copy-start.9
  79.7 1.0 copy-start.11
  82.7 14.7 %collective-permute-start.5 = (bf16[704,128]{1,0:T(8,128)(2,1)S(1)}, bf16[704,128]{1,0:T(8,128)(2,1)S(1)}, u32[]{:S(2)}, u32[]{:S(2)}) collective-permute-start(bf16[704,128]{1,0:T(8,128)(2,1)S(1)} %get-tuple-element.62), channel_id=1, source_target_pairs={{0,511},{1,510},{2,509},{3,508},{4,8},{5,9},{6,10},{7,11},{8,4},{9... | collective-permute-start | bytes 540680 | tf_op jit(solution)/shard_map/ppermute | solution.py:54
  91.5 6.0 %collective-permute-start.6 = (bf16[192,128]{1,0:T(8,128)(2,1)S(1)}, bf16[192,128]{1,0:T(8,128)(2,1)S(1)}, u32[]{:S(2)}, u32[]{:S(2)}) collective-permute-start(bf16[192,128]{1,0:T(8,128)(2,1)S(1)} %get-tuple-element.63), channel_id=1, source_target_pairs={{0,3},{1,2},{2,1},{3,0},{4,7},{5,6},{6,5},{7,4},{8,11},{9,10},{10,... | collective-permute-start | bytes 147464 | tf_op jit(solution)/shard_map/ppermute | solution.py:58
  94.8 24.4 %copy-start.5 = (bf16[704,704]{1,0:T(8,128)(2,1)S(1)}, bf16[704,704]{1,0:T(8,128)(2,1)}, u32[]{:S(2)}) copy-start(bf16[704,704]{1,0:T(8,128)(2,1)} %copy-done.4) | copy-start | bytes 2973700
  97.5 21.7 %copy-start.1 = (bf16[1408,1408]{1,0:T(8,128)(2,1)S(1)}, bf16[1408,1408]{1,0:T(8,128)(2,1)}, u32[]{:S(2)}) copy-start(bf16[1408,1408]{1,0:T(8,128)(2,1)} %all-gather.2.cloned.1.call-done.matrix) | copy-start | bytes 11894788
  97.5 21.7 %copy-start.3 = (bf16[704,704]{1,0:T(8,128)(2,1)S(1)}, bf16[704,704]{1,0:T(8,128)(2,1)}, u32[]{:S(2)}) copy-start(bf16[704,704]{1,0:T(8,128)(2,1)} %copy-done.2) | copy-start | bytes 2973700
  100.1 14.1 %collective-permute-start.7 = (bf16[704,128]{1,0:T(8,128)(2,1)S(1)}, bf16[704,128]{1,0:T(8,128)(2,1)S(1)}, u32[]{:S(2)}, u32[]{:S(2)}) collective-permute-start(bf16[704,128]{1,0:T(8,128)(2,1)S(1)} %get-tuple-element.68), channel_id=1, source_target_pairs={{0,511},{1,510},{2,509},{3,508},{4,8},{5,9},{6,10},{7,11},{8,4},{9... | collective-permute-start | bytes 540680 | tf_op jit(solution)/shard_map/ppermute | solution.py:54
  108.2 6.0 %collective-permute-start.8 = (bf16[192,128]{1,0:T(8,128)(2,1)S(1)}, bf16[192,128]{1,0:T(8,128)(2,1)S(1)}, u32[]{:S(2)}, u32[]{:S(2)}) collective-permute-start(bf16[192,128]{1,0:T(8,128)(2,1)S(1)} %get-tuple-element.69), channel_id=1, source_target_pairs={{0,3},{1,2},{2,1},{3,0},{4,7},{5,6},{6,5},{7,4},{8,11},{9,10},{10,... | collective-permute-start | bytes 147464 | tf_op jit(solution)/shard_map/ppermute | solution.py:58
  116.5 11.6 %collective-permute-start.9 = (bf16[1408,128]{1,0:T(8,128)(2,1)S(1)}, bf16[1408,128]{1,0:T(8,128)(2,1)S(1)}, u32[]{:S(2)}, u32[]{:S(2)}) collective-permute-start(bf16[1408,128]{1,0:T(8,128)(2,1)S(1)} %shard_map.42.lowered), channel_id=1, source_target_pairs={{0,1},{1,0},{2,3},{3,2},{4,5},{5,4},{6,7},{7,6},{8,9},{9,8},{10,11... | collective-permute-start | bytes 1081352 | tf_op jit(solution)/shard_map/ppermute | solution.py:62
  130.6 14.0 %collective-permute-start.10 = (bf16[704,128]{1,0:T(8,128)(2,1)S(1)}, bf16[704,128]{1,0:T(8,128)(2,1)S(1)}, u32[]{:S(2)}, u32[]{:S(2)}) collective-permute-start(bf16[704,128]{1,0:T(8,128)(2,1)S(1)} %get-tuple-element.75), channel_id=1, source_target_pairs={{0,511},{1,510},{2,509},{3,508},{4,8},{5,9},{6,10},{7,11},{8,4},{9... | collective-permute-start | bytes 540680 | tf_op jit(solution)/shard_map/ppermute | solution.py:54
  135.6 6.5 %collective-permute-start.11 = (bf16[192,128]{1,0:T(8,128)(2,1)S(1)}, bf16[192,128]{1,0:T(8,128)(2,1)S(1)}, u32[]{:S(2)}, u32[]{:S(2)}) collective-permute-start(bf16[192,128]{1,0:T(8,128)(2,1)S(1)} %get-tuple-element.76), channel_id=1, source_target_pairs={{0,3},{1,2},{2,1},{3,0},{4,7},{5,6},{6,5},{7,4},{8,11},{9,10},{10,... | collective-permute-start | bytes 147464 | tf_op jit(solution)/shard_map/ppermute | solution.py:58
  147.0 8.7 %collective-permute-start.12 = (bf16[704,128]{1,0:T(8,128)(2,1)S(1)}, bf16[704,128]{1,0:T(8,128)(2,1)S(1)}, u32[]{:S(2)}, u32[]{:S(2)}) collective-permute-start(bf16[704,128]{1,0:T(8,128)(2,1)S(1)} %get-tuple-element.78), channel_id=1, source_target_pairs={{0,3},{1,2},{2,1},{3,0},{4,7},{5,6},{6,5},{7,4},{8,11},{9,10},{10,... | collective-permute-start | bytes 540680 | tf_op jit(solution)/shard_map/ppermute | solution.py:58
Sparse Core Ops, SparseCore 0:
  27.4 48.1 all-gather.1

commit v6 on v5

--- a/solution.py
+++ b/solution.py
@@ -1,3 +1,4 @@
+import functools
 import math
 
 import jax
@@ -62,20 +63,22 @@
     return lax.ppermute(array, "vel", [(i, i ^ 1) for i in range(4)])
 
 
-def call(kernel, outs, flags, *arrays, flops=0, scratch=()):
+def call(kernel, outs, flags, *arrays, flops=0, stay=0, scratch=()):
     moved = sum(x.size * x.dtype.itemsize for x in arrays)
     moved += sum(math.prod(shape) * jnp.dtype(dtype).itemsize for shape, dtype in outs)
-    vmem = pl.BlockSpec(memory_space=pltpu.VMEM)
-    result = pl.pallas_call(
+    vmem, hbm = (pl.BlockSpec(memory_space=space) for space in (pltpu.VMEM, pltpu.HBM))
+    count = len(arrays) - stay
+    specs = [vmem] * count + [hbm] * stay
+    arrays = *arrays[:count], *(pltpu.with_memory_space_constraint(x, pltpu.HBM) for x in arrays[count:])
+    return pl.pallas_call(
         kernel,
         out_shape=[jax.ShapeDtypeStruct(shape, dtype) for shape, dtype in outs],
-        in_specs=[pl.BlockSpec(memory_space=pltpu.SMEM)] + [vmem] * len(arrays),
+        in_specs=[pl.BlockSpec(memory_space=pltpu.SMEM)] + specs,
         out_specs=[vmem] * len(outs),
-        scratch_shapes=[pltpu.VMEM(shape, dtype) for shape, dtype in scratch],
+        scratch_shapes=scratch,
         compiler_params=PARAMS,
         cost_estimate=pl.CostEstimate(flops=flops, bytes_accessed=moved, transcendentals=0),
     )(flags, *arrays)
-    return result
 
 
 def roll(values, shift):
@@ -296,31 +299,49 @@
         lowered[pl.ds(at_far + PART * part, PART)] = new_far.astype(BF16)
 
 
-def last_kernel(flags, near, far, sibling, neighbour, edges, masks, factors, kept, message):
-    same = flags[4] == 1
-    for part, span, new_near, new_far in streamed(
-        flags, near, far, sibling, neighbour, edges, masks, factors
-    ):
-        kept[span] = jnp.where(same, new_near, new_far)
-        message[span] = jnp.where(same, new_far, new_near).astype(BF16)
+def last_kernel(given, flags, near, far, sibling, neighbour, edges, masks, factors, out):
+    same = (flags[4] == 1) != given
+    values = masks[...]
+    edge_near, edge_far = (edges[rows_of(i, EDGE)].astype(F32)[:CHUNK] for i in range(2))
+    edge, open_x = jnp.where(same, edge_near, edge_far), jnp.where(same, values[5:6], values[6:7])
+    sign = jnp.where((flags[0] == 1) != given, 1.0, -1.0)
+    start = pl.multiple_of(PAD * flags[1], 16)
+    results = []
+    for part in range(PAD // PART):
+        span = rows_of(part, PART)
+        rows_near, rows_far = near[span], far[span]
+        layer_near = sibling[pl.ds(start + PART * part, PART)].astype(F32)
+        layer = jnp.where(same, layer_near, neighbour[span].astype(F32))
+        rows, mirror = jnp.where(same, rows_near, rows_far), jnp.where(same, rows_far, rows_near)
+        results.append(stream_part(part, sign, rows, mirror, layer, edge, values, open_x, factors))
+    results = jnp.concatenate(results, axis=0)
+    if given:
+        out[...] = results.astype(BF16)
+    else:
+        out[...] = reordered(order_matrix(flags[0] == 1), results)
 
 
 def dot(left, right):
     return jnp.dot(left, right, preferred_element_type=F32)
 
 
-def own_product(parts, half, values, span):
-    return dot(parts[2 * half][span], values[:PAD]) + dot(parts[2 * half + 1][span], values[PAD:])
-
-
-def collide_kernel(flags, m0, m1, m2, m3, lowered, other, rows_out):
+def collide_kernel(flags, lowered, other, m0, m1, m2, m3, rows_out, held, done):
+    copies = [
+        pltpu.make_async_copy(source, held.at[index], done.at[index])
+        for index, source in enumerate((m0, m1, m2, m3))
+    ]
+    for copy in copies:
+        copy.start()
     swapped = flags[2] == 1
     first = jnp.where(swapped, other[...], lowered[...])
     second = jnp.where(swapped, lowered[...], other[...])
-    for part in range(PAD // PART):
-        span = rows_of(part, PART)
-        parts = m0, m1, m2, m3
-        rows_out[span] = own_product(parts, 0, first, span) + own_product(parts, 1, second, span)
+    values = first[:PAD], first[PAD:], second[:PAD], second[PAD:]
+    for index, copy in enumerate(copies):
+        copy.wait()
+        for part in range(PAD // PART):
+            span = rows_of(part, PART)
+            total = dot(held[index, span], values[index])
+            rows_out[span] = total if index == 0 else rows_out[span] + total
 
 
 def give_rows(flags, part, rows_near, rows_far, factors, packed, outs):
@@ -342,43 +363,84 @@
     return give_rows(flags, part, near, far, factors, packed, outs)
 
 
-def collide_partner_kernel(flags, own, matrix, lowered, other, factors, *outs):
+def collide_partner_kernel(flags, own, lowered, other, factors, matrix, *refs):
+    *outs, held, done = refs
+    parts = PAD // PART
+    copies = []
+    for part in range(parts):
+        for half in range(2):
+            index = parts * half + part
+            copy = pltpu.make_async_copy(
+                matrix.at[rows_of(index, PART)], held.at[rows_of(index, PART)], done.at[index]
+            )
+            copy.start()
+            copies.append(copy)
     swapped = flags[2] == 1
     first = jnp.where(swapped, other[...], lowered[...])
     second = jnp.where(swapped, lowered[...], other[...])
     packed = (jnp.zeros((CHUNK, LANES), F32),) * 2
-    for part in range(PAD // PART):
+    for part in range(parts):
         span = rows_of(part, PART)
-        partner = dot(matrix[span], first) + dot(matrix[PAD + PART * part : PAD + PART * (part + 1)], second)
+        copies[2 * part].wait()
+        partner = dot(held[span], first)
+        copies[2 * part + 1].wait()
+        partner += dot(held[rows_of(parts + part, PART)], second)
         packed = give_product(flags, part, own[span], partner, factors, packed, outs[:4])
     outs[4][:EDGE], outs[4][EDGE:] = edge_block(packed[0]), edge_block(packed[1])
 
 
-def early_kernel(flags, m0, m1, m2, m3, matrix, lowered, own_out, partner_out):
+def half_products(half, values, parts, matrix, held_own, held_partner, done, give):
+    count = PAD // PART
+    own = [
+        pltpu.make_async_copy(parts[2 * half + i], held_own.at[i], done.at[i]) for i in range(2)
+    ]
+    partner = [
+        pltpu.make_async_copy(
+            matrix.at[rows_of(count * half + i, PART)], held_partner.at[rows_of(i, PART)], done.at[2 + i]
+        )
+        for i in range(count)
+    ]
+    for copy in partner + own:
+        copy.start()
+    totals = []
+    for part in range(count):
+        partner[part].wait()
+        totals.append(dot(held_partner[rows_of(part, PART)], values))
+    for copy in own:
+        copy.wait()
+    for part in range(count):
+        span = rows_of(part, PART)
+        total = dot(held_own[0, span], values[:PAD]) + dot(held_own[1, span], values[PAD:])
+        give(span, total, totals[part])
+
+
+def early_kernel(flags, lowered, m0, m1, m2, m3, matrix, own_out, partner_out, *scratch):
     values = lowered[...]
+
+    def give(span, own, partner):
+        own_out[span] = own
+        partner_out[span] = partner
+
     for half in range(2):
 
         @pl.when(flags[2] == half)
         def _():
-            for part in range(PAD // PART):
-                span = rows_of(part, PART)
-                start = PAD * half + PART * part
-                own_out[span] = own_product((m0, m1, m2, m3), half, values, span)
-                partner_out[span] = dot(matrix[start : start + PART], values)
-
-
-def late_kernel(flags, m0, m1, m2, m3, matrix, other, own, partner, factors, *outs):
-    *outs, total_own, total_partner = outs
+            half_products(half, values, (m0, m1, m2, m3), matrix, *scratch, give)
+
+
+def late_kernel(flags, other, own, partner, factors, m0, m1, m2, m3, matrix, *refs):
+    outs, (total_own, total_partner, *scratch) = refs[:5], refs[5:]
     values = other[...]
+
+    def give(span, more_own, more_partner):
+        total_own[span] = own[span] + more_own
+        total_partner[span] = partner[span] + more_partner
+
     for half in range(2):
 
         @pl.when(flags[2] != half)
         def _():
-            for part in range(PAD // PART):
-                span = rows_of(part, PART)
-                start = PAD * half + PART * part
-                total_own[span] = own[span] + own_product((m0, m1, m2, m3), half, values, span)
-                total_partner[span] = partner[span] + dot(matrix[start : start + PART], values)
+            half_products(half, values, (m0, m1, m2, m3), matrix, *scratch, give)
 
     packed = (jnp.zeros((CHUNK, LANES), F32),) * 2
     for part in range(PAD // PART):
@@ -389,17 +451,13 @@
     outs[4][:EDGE], outs[4][EDGE:] = edge_block(packed[0]), edge_block(packed[1])
 
 
-def reorder_kernel(flags, kept, ordered):
-    ordered[...] = reordered(order_matrix(flags[0] == 1), kept[...])
-
-
 def finish_kernel(flags, kept, received, evolved):
     order = order_matrix(flags[0] == 1)
     rest = jnp.dot(order, received[...], preferred_element_type=F32)
     mine = kept[...]
     half = flags[3]
-    evolved[:, :LANES] = jnp.where(half == 0, mine, rest)[:ROWS]
-    evolved[:, LANES:] = jnp.where(half == 0, rest, mine)[:ROWS]
+    evolved[:, 0, :LANES] = jnp.where(half == 0, mine, rest)[:ROWS]
+    evolved[:, 0, LANES:] = jnp.where(half == 0, rest, mine)[:ROWS]
 
 
 def place(rows, columns, wanted):
@@ -481,11 +539,17 @@
     work = 100 * PAD * LANES
 
     other = to_side(lowered)
-    (own,) = call(collide_kernel, [(rows, F32)], flags, *matrix, lowered, other, flops=multiply)
+    dma = pltpu.SemaphoreType.DMA
+    (own,) = call(
+        collide_kernel, [(rows, F32)], flags, lowered, other, *matrix, flops=multiply, stay=4,
+        scratch=[pltpu.VMEM((4, PAD, PAD), BF16), dma((4,))],
+    )
     partner_matrix, own = lax.optimization_barrier((partner_matrix, own))
     near, far, for_sibling, for_neighbour, edges = call(
-        collide_partner_kernel, sends, flags, own, partner_matrix, lowered, other, factors, flops=multiply
-    )
+        collide_partner_kernel, sends, flags, own, lowered, other, factors, partner_matrix,
+        flops=multiply, stay=1, scratch=[pltpu.VMEM((2 * PAD, 2 * PAD), BF16), dma((8,))],
+    )
+    held = [pltpu.VMEM((2, PAD, PAD), BF16), pltpu.VMEM((PAD, 2 * PAD), BF16), dma((6,))]
 
     for step in range(1, STEPS):
         neighbour, edges = to_neighbour(for_neighbour), to_mirror(edges)
@@ -501,25 +565,24 @@
         )
         other = to_side(lowered)
         early = call(
-            early_kernel, [(rows, F32)] * 2, flags, *matrix, partner_matrix, lowered, flops=multiply
+            early_kernel, [(rows, F32)] * 2, flags, lowered, *matrix, partner_matrix,
+            flops=multiply, stay=5, scratch=held,
         )
         near, far, for_sibling, for_neighbour, edges = call(
-            late_kernel, sends, flags, *matrix, partner_matrix, other, *early, factors,
-            flops=multiply, scratch=[(rows, F32)] * 2,
+            late_kernel, sends, flags, other, *early, factors, *matrix, partner_matrix,
+            flops=multiply, stay=5, scratch=[pltpu.VMEM(rows, F32)] * 2 + held,
         )
 
     neighbour, edges = to_neighbour(for_neighbour), to_mirror(edges)
     sibling = with_sibling(for_sibling)
-    kept, message = call(
-        last_kernel, [(rows, F32), (rows, BF16)],
-        flags, near, far, sibling, neighbour, edges, masks, factors, flops=work,
-    )
+    last = flags, near, far, sibling, neighbour, edges, masks, factors
+    (message,) = call(functools.partial(last_kernel, True), [(rows, BF16)], *last, flops=work)
     received = to_mirror(message)
-    (kept,) = call(reorder_kernel, [(rows, F32)], flags, kept, flops=2 * 3 * PAD * PAD * LANES)
+    (kept,) = call(functools.partial(last_kernel, False), [(rows, F32)], *last, flops=multiply)
     (evolved,) = call(
-        finish_kernel, [((ROWS, 2 * LANES), F32)], flags, kept, received, flops=2 * PAD * PAD * LANES
-    )
-    return evolved[:, None, :]
+        finish_kernel, [((ROWS, 1, 2 * LANES), F32)], flags, kept, received, flops=2 * PAD * PAD * LANES
+    )
+    return evolved
 
 
 def solution(mesh):

time: 166 us -> 163 us (0.982)
  local copies, waits for them, and re-layouts: 10.3 us -> 1.19 us
  Pallas kernels: 22.4 us -> 30.8 us
  waiting for transfers between devices: 38.4 us -> 33 us
  matrix products: 13 us -> 17 us
    pallas_call x11, Pallas kernels: 22.4 us -> 30.8 us  [call(): pl.pallas_call(kernel, out_shape=[jax.ShapeDtypeStruct(shape, dtype) for...]
    unnamed x31 -> x7, local copies, waits for them, and re-layouts: 8.3 us -> 0.75 us
    dot_general x8, matrix products: 13 us -> 17 us  [chosen(): return jnp.dot(left, right, preferred_element_type=BF16)]
    ppermute x2, waiting for transfers between devices: 9.12 us -> 5.19 us  [to_side(): return lax.ppermute(array, 'vel', [(i, i ^ 1) for i in range(4)])]
  transfers between devices with their start and end apart: 14 -> 14, of which waited for: 11 -> 9; matrix products, arithmetic and copies ran while one was open for 7% -> 9% of each run, Pallas kernels for 6% -> 9%
where the time goes in v6:
time: 163 us
  starting transfers between devices  60.4 us (37%)
  waiting for transfers between devices  33 us (20%)
  Pallas kernels  30.8 us (19%)
  matrix products  17 us (10%)
  between operations  13.8 us (8%)
  blocking collectives  6.19 us (4%)
    pallas_call x11, Pallas kernels, call(): pl.pallas_call(kernel, out_shape=[jax.ShapeDtypeStruct(shape, dtype) for...  30.8 us
    ppermute x3, starting transfers between devices, to_neighbour(): return lax.ppermute(array, BOTH, pairs_of(neighbour_of))  23.3 us
    ppermute x6, waiting for transfers between devices, to_mirror(): return lax.ppermute(array, 'vel', [(i, 3 - i) for i in range(4)])  18.2 us
    dot_general x8, matrix products, chosen(): return jnp.dot(left, right, preferred_element_type=BF16)  17 us
    ppermute x6, starting transfers between devices, to_mirror(): return lax.ppermute(array, 'vel', [(i, 3 - i) for i in range(4)])  16.9 us
    ppermute x2, starting transfers between devices, to_layer(): return lax.ppermute(array, BOTH, pairs_of(target))  16.2 us
    ppermute x2, waiting for transfers between devices, to_layer(): return lax.ppermute(array, BOTH, pairs_of(target))  6.46 us
    all_gather x3, blocking collectives, with_sibling(): lax.all_gather(array, 'cells', axis=0, tiled=True, axis_index_groups=groups)  6.19 us
  transfers between devices with their start and end apart: 14, of which 9 were waited for; matrix products, arithmetic and copies ran while one was open for 9% of the time, Pallas kernels for 9%

profile of v6, /device:TPU:8, one launch (start us, length us, event | category | flops | bytes accessed | tf_op | source)
XLA Modules:
  0.0 162.6 jit_solution(17224335068034627727)
XLA Ops:
  9.4 3.5 %collective-permute-start = (bf16[88,1408]{1,0:T(8,128)(2,1)S(1)}, bf16[88,1408]{1,0:T(8,128)(2,1)S(1)}, u32[]{:S(2)}, u32[]{:S(2)}) collective-permute-start(bf16[88,1408]{1,0:T(8,128)(2,1)S(1)} %pad_maximum_fusion), channel_id=1, source_target_pairs={{0,3},{1,2},{2,1},{3,0},{4,7},{5,6},{6,5},{7,4},{8,11},{9,10},{10,... | collective-permute-start | bytes 743432 | tf_op jit(solution)/shard_map/ppermute | solution.py:59
  15.3 11.3 %collective-permute-done = bf16[88,1408]{1,0:T(8,128)(2,1)S(1)} collective-permute-done((bf16[88,1408]{1,0:T(8,128)(2,1)S(1)}, bf16[88,1408]{1,0:T(8,128)(2,1)S(1)}, u32[]{:S(2)}, u32[]{:S(2)}) %collective-permute-start) | collective-permute-done | bytes 247840 | tf_op jit(solution)/shard_map/ppermute | solution.py:59
  29.2 14.3 %collective-permute-start.2 = (bf16[720,128]{1,0:T(8,128)(2,1)S(1)}, bf16[720,128]{1,0:T(8,128)(2,1)S(1)}, u32[]{:S(2)}, u32[]{:S(2)}) collective-permute-start(bf16[720,128]{1,0:T(8,128)(2,1)S(1)} %get-tuple-element.47), channel_id=1, source_target_pairs={{0,508},{1,509},{2,6},{3,7},{4,0},{5,1},{6,10},{7,11},{8,4},{9,5},... | collective-permute-start | bytes 552968 | tf_op jit(solution)/shard_map/ppermute | solution.py:46
  45.5 5.4 %fusion.6 = bf16[704,2744]{1,0:T(8,128)(2,1)S(1)} fusion(bf16[686,2744]{1,0:T(8,128)(2,1)} %param.5, s32[704]{0:T(1024)S(1)} %select_select_fusion), kind=kOutput, calls=%fused_computation.13 | convolution fusion | flops 2650879488 | bytes 7631136 | tf_op jit(solution)/shard_map/dot_general | solution.py:468
  51.3 6.5 %collective-permute-done.3.turned = bf16[720,128]{1,0:T(8,128)(2,1)S(1)} collective-permute-done((bf16[720,128]{1,0:T(8,128)(2,1)S(1)}, bf16[720,128]{1,0:T(8,128)(2,1)S(1)}, u32[]{:S(2)}, u32[]{:S(2)}) %collective-permute-start.3) | collective-permute-done | bytes 184352 | tf_op jit(solution)/shard_map/ppermute | solution.py:46
  57.7 2.2 %shard_map.38 = (bf16[1408,128]{1,0:T(8,128)(2,1)S(1)}, f32[8,128]{1,0:T(8,128)S(1)}) custom-call(s32[6]{0:T(128)S(1)} %stack.31.flags, f32[704,128]{1,0:T(8,128)S(1)} %get-tuple-element.44.own, f32[88,128]{1,0:T(8,128)S(1)} %get-tuple-element.45.own_edge, bf16[800,128]{1,0:T(8,128)(2,1)S(1)} %collective-permute-done.1.received, ...), custom_call_target="tpu_custom_call" | custom-call | flops 18022400 | bytes 2428928 | tf_op jit(solution)/shard_map/pallas_call | solution.py:73
  60.0 2.1 %collective-permute-start.4 = (bf16[1408,128]{1,0:T(8,128)(2,1)S(1)}, bf16[1408,128]{1,0:T(8,128)(2,1)S(1)}, u32[]{:S(2)}, u32[]{:S(2)}) collective-permute-start(bf16[1408,128]{1,0:T(8,128)(2,1)S(1)} %get-tuple-element.53.lowered), channel_id=1, source_target_pairs={{0,1},{1,0},{2,3},{3,2},{4,5},{5,4},{6,7},{7,6},{8,9},{9,8},{10,11... | collective-permute-start | bytes 1081352 | tf_op jit(solution)/shard_map/ppermute | solution.py:63
  62.1 2.1 %fusion.3.m0 = bf16[704,704]{1,0:T(8,128)(2,1)} fusion(s32[704]{0:T(1024)S(1)} %iota_select_fusion, bf16[704,2944]{1,0:T(8,128)(2,1)S(1)} %pad.14), kind=kOutput, calls=%fused_computation.9 | convolution fusion | flops 761806848 | bytes 2076672 | tf_op jit(solution)/shard_map/dot_general | solution.py:468
  64.1 2.4 %fusion.m1 = bf16[704,704]{1,0:T(8,128)(2,1)} fusion(s32[704]{0:T(1024)S(1)} %subtract_select_fusion.1, bf16[704,2944]{1,0:T(8,128)(2,1)S(1)} %pad.14), kind=kOutput, calls=%fused_computation.3 | convolution fusion | flops 888774656 | bytes 2256896 | tf_op jit(solution)/shard_map/dot_general | solution.py:468
  66.5 2.1 %fusion.4.m2 = bf16[704,704]{1,0:T(8,128)(2,1)} fusion(s32[704]{0:T(1024)S(1)} %add_select_fusion, bf16[704,2944]{1,0:T(8,128)(2,1)S(1)} %pad.14), kind=kOutput, calls=%fused_computation.10 | convolution fusion | flops 761806848 | bytes 2076672 | tf_op jit(solution)/shard_map/dot_general | solution.py:468
  68.6 2.4 %fusion.1.m3 = bf16[704,704]{1,0:T(8,128)(2,1)} fusion(s32[704]{0:T(1024)S(1)} %subtract_select_fusion, bf16[704,2944]{1,0:T(8,128)(2,1)S(1)} %pad.14), kind=kOutput, calls=%fused_computation.4 | convolution fusion | flops 888774656 | bytes 2256896 | tf_op jit(solution)/shard_map/dot_general | solution.py:468
  71.0 3.6 %shard_map.39.own = f32[704,128]{1,0:T(8,128)S(1)} custom-call(s32[6]{0:T(128)S(1)} %stack.31.flags, bf16[1408,128]{1,0:T(8,128)(2,1)S(1)} %get-tuple-element.53.lowered, bf16[1408,128]{1,0:T(8,128)(2,1)S(1)} %collective-permute-done.4.other, bf16[704,704]{1,0:T(8,128)(2,1)} %fusion.3.m0, bf16[704,704]{1,0:T(8,128)(2,1)} %fusion.m1, ...), custom_call_target="tpu_custom_call" | custom-call | flops 507510784 | bytes 5046272 | tf_op jit(solution)/shard_map/pallas_call | solution.py:73
  75.7 4.2 %shard_map.40 = (f32[704,128]{1,0:T(8,128)S(1)}, f32[704,128]{1,0:T(8,128)S(1)}, bf16[704,128]{1,0:T(8,128)(2,1)S(1)}, bf16[704,128]{1,0:T(8,128)(2,1)S(1)}, bf16[192,128]{1,0:T(8,128)(2,1)S(1)}) custom-call(s32[6]{0:T(128)S(1)} %stack.31.flags, f32[704,128]{1,0:T(8,128)S(1)} %shard_map.39.own, bf16[1408,128]{1,0:T(8,128)(2,1)S(1)} %get-tuple-element.53.lowered, ...), custom_call_target="tpu_custom_call" | custom-call | flops 507510784 | bytes 7258112 | tf_op jit(solution)/shard_map/pallas_call | solution.py:73
  79.9 9.0 %collective-permute-start.5 = (bf16[704,128]{1,0:T(8,128)(2,1)S(1)}, bf16[704,128]{1,0:T(8,128)(2,1)S(1)}, u32[]{:S(2)}, u32[]{:S(2)}) collective-permute-start(bf16[704,128]{1,0:T(8,128)(2,1)S(1)} %get-tuple-element.60), channel_id=1, source_target_pairs={{0,511},{1,510},{2,509},{3,508},{4,8},{5,9},{6,10},{7,11},{8,4},{9... | collective-permute-start | bytes 540680 | tf_op jit(solution)/shard_map/ppermute | solution.py:55
  88.9 3.1 %collective-permute-start.6 = (bf16[192,128]{1,0:T(8,128)(2,1)S(1)}, bf16[192,128]{1,0:T(8,128)(2,1)S(1)}, u32[]{:S(2)}, u32[]{:S(2)}) collective-permute-start(bf16[192,128]{1,0:T(8,128)(2,1)S(1)} %get-tuple-element.61), channel_id=1, source_target_pairs={{0,3},{1,2},{2,1},{3,0},{4,7},{5,6},{6,5},{7,4},{8,11},{9,10},{10,... | collective-permute-start | bytes 147464 | tf_op jit(solution)/shard_map/ppermute | solution.py:59
  91.9 2.1 %all_gather.13.sibling = bf16[1408,128]{1,0:T(8,128)(2,1)S(1)} all-gather(bf16[704,128]{1,0:T(8,128)(2,1)S(1)} %get-tuple-element.59), channel_id=1, replica_groups={{0,4},{8,12},{16,20},{24,28},{32,36},{40,44},{48,52},{56,60},{64,68},{7..., dimensions={0}, use_global_device_ids=true | all-gather | bytes 540672 | tf_op jit(solution)/shard_map/all_gather | solution.py:39
  94.8 2.7 %shard_map.41 = (f32[704,128]{1,0:T(8,128)S(1)}, f32[704,128]{1,0:T(8,128)S(1)}, bf16[704,128]{1,0:T(8,128)(2,1)S(1)}, bf16[704,128]{1,0:T(8,128)(2,1)S(1)}, bf16[192,128]{1,0:T(8,128)(2,1)S(1)}) custom-call(s32[6]{0:T(128)S(1)} %stack.31.flags, f32[704,128]{1,0:T(8,128)S(1)} %get-tuple-element.57.near, f32[704,128]{1,0:T(8,128)S(1)} %get-tuple-element.58.far, ...), custom_call_target="tpu_custom_call" | custom-call | flops 9011200 | bytes 3526656 | tf_op jit(solution)/shard_map/pallas_call | solution.py:73
  97.5 8.6 %collective-permute-start.7 = (bf16[704,128]{1,0:T(8,128)(2,1)S(1)}, bf16[704,128]{1,0:T(8,128)(2,1)S(1)}, u32[]{:S(2)}, u32[]{:S(2)}) collective-permute-start(bf16[704,128]{1,0:T(8,128)(2,1)S(1)} %get-tuple-element.66), channel_id=1, source_target_pairs={{0,511},{1,510},{2,509},{3,508},{4,8},{5,9},{6,10},{7,11},{8,4},{9... | collective-permute-start | bytes 540680 | tf_op jit(solution)/shard_map/ppermute | solution.py:55
  106.1 2.6 %collective-permute-start.8 = (bf16[192,128]{1,0:T(8,128)(2,1)S(1)}, bf16[192,128]{1,0:T(8,128)(2,1)S(1)}, u32[]{:S(2)}, u32[]{:S(2)}) collective-permute-start(bf16[192,128]{1,0:T(8,128)(2,1)S(1)} %get-tuple-element.67), channel_id=1, source_target_pairs={{0,3},{1,2},{2,1},{3,0},{4,7},{5,6},{6,5},{7,4},{8,11},{9,10},{10,... | collective-permute-start | bytes 147464 | tf_op jit(solution)/shard_map/ppermute | solution.py:59
  108.6 2.1 %all_gather.14.sibling = bf16[1408,128]{1,0:T(8,128)(2,1)S(1)} all-gather(bf16[704,128]{1,0:T(8,128)(2,1)S(1)} %get-tuple-element.65), channel_id=1, replica_groups={{0,4},{8,12},{16,20},{24,28},{32,36},{40,44},{48,52},{56,60},{64,68},{7..., dimensions={0}, use_global_device_ids=true | all-gather | bytes 540672 | tf_op jit(solution)/shard_map/all_gather | solution.py:39
  112.1 2.2 %shard_map.42.lowered = bf16[1408,128]{1,0:T(8,128)(2,1)S(1)} custom-call(s32[6]{0:T(128)S(1)} %stack.31.flags, f32[704,128]{1,0:T(8,128)S(1)} %get-tuple-element.63.near, f32[704,128]{1,0:T(8,128)S(1)} %get-tuple-element.64.far, bf16[1408,128]{1,0:T(8,128)(2,1)S(1)} %all_gather.14.sibling, bf16[704,128]{1,0:T(8,128)(2,1)S(1)} %collective-permute-done.7.neighbour, ...), custom_call_target="tpu_custom_call" | custom-call | flops 9011200 | bytes 2756608 | tf_op jit(solution)/shard_map/pallas_call | solution.py:73
  116.2 3.9 %shard_map.43 = (f32[704,128]{1,0:T(8,128)S(1)}, f32[704,128]{1,0:T(8,128)S(1)}) custom-call(s32[6]{0:T(128)S(1)} %stack.31.flags, bf16[1408,128]{1,0:T(8,128)(2,1)S(1)} %shard_map.42.lowered, bf16[704,704]{1,0:T(8,128)(2,1)} %fusion.3.m0, bf16[704,704]{1,0:T(8,128)(2,1)} %fusion.m1, bf16[704,704]{1,0:T(8,128)(2,1)} %fusion.4.m2, ...), custom_call_target="tpu_custom_call" | custom-call | flops 507510784 | bytes 9011200 | tf_op jit(solution)/shard_map/pallas_call | solution.py:73
  120.1 5.2 %collective-permute-done.9.other = bf16[1408,128]{1,0:T(8,128)(2,1)S(1)} collective-permute-done((bf16[1408,128]{1,0:T(8,128)(2,1)S(1)}, bf16[1408,128]{1,0:T(8,128)(2,1)S(1)}, u32[]{:S(2)}, u32[]{:S(2)}) %collective-permute-start.9) | collective-permute-done | bytes 360480 | tf_op jit(solution)/shard_map/ppermute | solution.py:63
  125.3 4.1 %shard_map.44 = (f32[704,128]{1,0:T(8,128)S(1)}, f32[704,128]{1,0:T(8,128)S(1)}, bf16[704,128]{1,0:T(8,128)(2,1)S(1)}, bf16[704,128]{1,0:T(8,128)(2,1)S(1)}, bf16[192,128]{1,0:T(8,128)(2,1)S(1)}) custom-call(s32[6]{0:T(128)S(1)} %stack.31.flags, bf16[1408,128]{1,0:T(8,128)(2,1)S(1)} %collective-permute-done.9.other, f32[704,128]{1,0:T(8,128)S(1)} %get-tuple-element.68.own, ...), custom_call_target="tpu_custom_call" | custom-call | flops 507510784 | bytes 11223040 | tf_op jit(solution)/shard_map/pallas_call | solution.py:73
  129.5 5.7 %collective-permute-start.10 = (bf16[704,128]{1,0:T(8,128)(2,1)S(1)}, bf16[704,128]{1,0:T(8,128)(2,1)S(1)}, u32[]{:S(2)}, u32[]{:S(2)}) collective-permute-start(bf16[704,128]{1,0:T(8,128)(2,1)S(1)} %get-tuple-element.73), channel_id=1, source_target_pairs={{0,511},{1,510},{2,509},{3,508},{4,8},{5,9},{6,10},{7,11},{8,4},{9... | collective-permute-start | bytes 540680 | tf_op jit(solution)/shard_map/ppermute | solution.py:55
  135.2 2.6 %collective-permute-start.11 = (bf16[192,128]{1,0:T(8,128)(2,1)S(1)}, bf16[192,128]{1,0:T(8,128)(2,1)S(1)}, u32[]{:S(2)}, u32[]{:S(2)}) collective-permute-start(bf16[192,128]{1,0:T(8,128)(2,1)S(1)} %get-tuple-element.74), channel_id=1, source_target_pairs={{0,3},{1,2},{2,1},{3,0},{4,7},{5,6},{6,5},{7,4},{8,11},{9,10},{10,... | collective-permute-start | bytes 147464 | tf_op jit(solution)/shard_map/ppermute | solution.py:59
  137.8 2.1 %all_gather.15.sibling = bf16[1408,128]{1,0:T(8,128)(2,1)S(1)} all-gather(bf16[704,128]{1,0:T(8,128)(2,1)S(1)} %get-tuple-element.72), channel_id=1, replica_groups={{0,4},{8,12},{16,20},{24,28},{32,36},{40,44},{48,52},{56,60},{64,68},{7..., dimensions={0}, use_global_device_ids=true | all-gather | bytes 540672 | tf_op jit(solution)/shard_map/all_gather | solution.py:39
  141.5 2.1 %collective-permute-done.10.neighbour = bf16[704,128]{1,0:T(8,128)(2,1)S(1)} collective-permute-done((bf16[704,128]{1,0:T(8,128)(2,1)S(1)}, bf16[704,128]{1,0:T(8,128)(2,1)S(1)}, u32[]{:S(2)}, u32[]{:S(2)}) %collective-permute-start.10) | collective-permute-done | bytes 180256 | tf_op jit(solution)/shard_map/ppermute | solution.py:55
  145.0 3.3 %collective-permute-start.12 = (bf16[704,128]{1,0:T(8,128)(2,1)S(1)}, bf16[704,128]{1,0:T(8,128)(2,1)S(1)}, u32[]{:S(2)}, u32[]{:S(2)}) collective-permute-start(bf16[704,128]{1,0:T(8,128)(2,1)S(1)} %shard_map.46), channel_id=1, source_target_pairs={{0,3},{1,2},{2,1},{3,0},{4,7},{5,6},{6,5},{7,4},{8,11},{9,10},{10,... | collective-permute-start | bytes 540680 | tf_op jit(solution)/shard_map/ppermute | solution.py:59
  148.2 2.3 %shard_map.45.kept = f32[704,128]{1,0:T(8,128)S(1)} custom-call(s32[6]{0:T(128)S(1)} %stack.31.flags, f32[704,128]{1,0:T(8,128)S(1)} %get-tuple-element.70.near, f32[704,128]{1,0:T(8,128)S(1)} %get-tuple-element.71.far, bf16[1408,128]{1,0:T(8,128)(2,1)S(1)} %all_gather.15.sibling, bf16[704,128]{1,0:T(8,128)(2,1)S(1)} %collective-permute-done.10.neighbour, ...), custom_call_target="tpu_custom_call" | custom-call | flops 507510784 | bytes 2756608 | tf_op jit(solution)/shard_map/pallas_call | solution.py:73
  150.5 3.1 %collective-permute-done.12.received = bf16[704,128]{1,0:T(8,128)(2,1)S(1)} collective-permute-done((bf16[704,128]{1,0:T(8,128)(2,1)S(1)}, bf16[704,128]{1,0:T(8,128)(2,1)S(1)}, u32[]{:S(2)}, u32[]{:S(2)}) %collective-permute-start.12) | collective-permute-done | bytes 180256 | tf_op jit(solution)/shard_map/ppermute | solution.py:59
  153.7 2.1 %shard_map.47 = f32[686,1,256]{2,1,0:T(1,128)} custom-call(s32[6]{0:T(128)S(1)} %stack.31.flags, f32[704,128]{1,0:T(8,128)S(1)} %shard_map.45.kept, bf16[704,128]{1,0:T(8,128)(2,1)S(1)} %collective-permute-done.12.received), custom_call_target="tpu_custom_call" | custom-call | flops 126877696 | bytes 1243136 | tf_op jit(solution)/shard_map/pallas_call | solution.py:73
  (38 shorter events, 18.1 us)
Async XLA Ops:
  6.5 6.5 %copy-start.1 = (f32[686,1,256]{2,1,0:T(1,128)S(1)}, f32[686,1,256]{2,1,0:T(1,128)}, u32[]{:S(2)}) copy-start(f32[686,1,256]{2,1,0:T(1,128)} %param.3) | copy-start | bytes 2107396
  6.5 69.1 %all-gather.2.cloned.1.call-start = ((), (), s32[]{:S(2)}) async-start(), calls=%async_computation | async-start | bytes 4212736 | tf_op jit(solution)/shard_map/all_gather | solution.py:520
  8.7 4.5 %copy-start = (s32[1,256]{1,0:T(1,128)S(1)}, s32[1,256]{1,0:T(1,128)}, u32[]{:S(2)}) copy-start(s32[1,256]{1,0:T(1,128)} %solid.1) | copy-start | bytes 3076
  9.4 17.1 %collective-permute-start = (bf16[88,1408]{1,0:T(8,128)(2,1)S(1)}, bf16[88,1408]{1,0:T(8,128)(2,1)S(1)}, u32[]{:S(2)}, u32[]{:S(2)}) collective-permute-start(bf16[88,1408]{1,0:T(8,128)(2,1)S(1)} %pad_maximum_fusion), channel_id=1, source_target_pairs={{0,3},{1,2},{2,1},{3,0},{4,7},{5,6},{6,5},{7,4},{8,11},{9,10},{10,... | collective-permute-start | bytes 743432 | tf_op jit(solution)/shard_map/ppermute | solution.py:59
  26.6 0.7 copy-start.2
  27.3 18.2 %collective-permute-start.1 = (bf16[800,128]{1,0:T(8,128)(2,1)S(1)}, bf16[800,128]{1,0:T(8,128)(2,1)S(1)}, u32[]{:S(2)}, u32[]{:S(2)}) collective-permute-start(bf16[800,128]{1,0:T(8,128)(2,1)S(1)} %get-tuple-element.42), channel_id=1, source_target_pairs={{0,3},{1,2},{2,1},{3,0},{4,7},{5,6},{6,5},{7,4},{8,11},{9,10},{10,... | collective-permute-start | bytes 614408 | tf_op jit(solution)/shard_map/ppermute | solution.py:59
  29.2 22.0 %collective-permute-start.2 = (bf16[720,128]{1,0:T(8,128)(2,1)S(1)}, bf16[720,128]{1,0:T(8,128)(2,1)S(1)}, u32[]{:S(2)}, u32[]{:S(2)}) collective-permute-start(bf16[720,128]{1,0:T(8,128)(2,1)S(1)} %get-tuple-element.47), channel_id=1, source_target_pairs={{0,508},{1,509},{2,6},{3,7},{4,0},{5,1},{6,10},{7,11},{8,4},{9,5},... | collective-permute-start | bytes 552968 | tf_op jit(solution)/shard_map/ppermute | solution.py:46
  43.5 14.2 %collective-permute-start.3 = (bf16[720,128]{1,0:T(8,128)(2,1)S(1)}, bf16[720,128]{1,0:T(8,128)(2,1)S(1)}, u32[]{:S(2)}, u32[]{:S(2)}) collective-permute-start(bf16[720,128]{1,0:T(8,128)(2,1)S(1)} %get-tuple-element.48), channel_id=1, source_target_pairs={{0,511},{1,510},{2,5},{3,4},{4,3},{5,2},{6,9},{7,8},{8,7},{9,6},{1... | collective-permute-start | bytes 552968 | tf_op jit(solution)/shard_map/ppermute | solution.py:46
  60.0 11.0 %collective-permute-start.4 = (bf16[1408,128]{1,0:T(8,128)(2,1)S(1)}, bf16[1408,128]{1,0:T(8,128)(2,1)S(1)}, u32[]{:S(2)}, u32[]{:S(2)}) collective-permute-start(bf16[1408,128]{1,0:T(8,128)(2,1)S(1)} %get-tuple-element.53.lowered), channel_id=1, source_target_pairs={{0,1},{1,0},{2,3},{3,2},{4,5},{5,4},{6,7},{7,6},{8,9},{9,8},{10,11... | collective-permute-start | bytes 1081352 | tf_op jit(solution)/shard_map/ppermute | solution.py:63
  79.9 15.0 %collective-permute-start.5 = (bf16[704,128]{1,0:T(8,128)(2,1)S(1)}, bf16[704,128]{1,0:T(8,128)(2,1)S(1)}, u32[]{:S(2)}, u32[]{:S(2)}) collective-permute-start(bf16[704,128]{1,0:T(8,128)(2,1)S(1)} %get-tuple-element.60), channel_id=1, source_target_pairs={{0,511},{1,510},{2,509},{3,508},{4,8},{5,9},{6,10},{7,11},{8,4},{9... | collective-permute-start | bytes 540680 | tf_op jit(solution)/shard_map/ppermute | solution.py:55
  88.9 6.0 %collective-permute-start.6 = (bf16[192,128]{1,0:T(8,128)(2,1)S(1)}, bf16[192,128]{1,0:T(8,128)(2,1)S(1)}, u32[]{:S(2)}, u32[]{:S(2)}) collective-permute-start(bf16[192,128]{1,0:T(8,128)(2,1)S(1)} %get-tuple-element.61), channel_id=1, source_target_pairs={{0,3},{1,2},{2,1},{3,0},{4,7},{5,6},{6,5},{7,4},{8,11},{9,10},{10,... | collective-permute-start | bytes 147464 | tf_op jit(solution)/shard_map/ppermute | solution.py:59
  97.5 14.6 %collective-permute-start.7 = (bf16[704,128]{1,0:T(8,128)(2,1)S(1)}, bf16[704,128]{1,0:T(8,128)(2,1)S(1)}, u32[]{:S(2)}, u32[]{:S(2)}) collective-permute-start(bf16[704,128]{1,0:T(8,128)(2,1)S(1)} %get-tuple-element.66), channel_id=1, source_target_pairs={{0,511},{1,510},{2,509},{3,508},{4,8},{5,9},{6,10},{7,11},{8,4},{9... | collective-permute-start | bytes 540680 | tf_op jit(solution)/shard_map/ppermute | solution.py:55
  106.1 6.0 %collective-permute-start.8 = (bf16[192,128]{1,0:T(8,128)(2,1)S(1)}, bf16[192,128]{1,0:T(8,128)(2,1)S(1)}, u32[]{:S(2)}, u32[]{:S(2)}) collective-permute-start(bf16[192,128]{1,0:T(8,128)(2,1)S(1)} %get-tuple-element.67), channel_id=1, source_target_pairs={{0,3},{1,2},{2,1},{3,0},{4,7},{5,6},{6,5},{7,4},{8,11},{9,10},{10,... | collective-permute-start | bytes 147464 | tf_op jit(solution)/shard_map/ppermute | solution.py:59
  114.3 11.0 %collective-permute-start.9 = (bf16[1408,128]{1,0:T(8,128)(2,1)S(1)}, bf16[1408,128]{1,0:T(8,128)(2,1)S(1)}, u32[]{:S(2)}, u32[]{:S(2)}) collective-permute-start(bf16[1408,128]{1,0:T(8,128)(2,1)S(1)} %shard_map.42.lowered), channel_id=1, source_target_pairs={{0,1},{1,0},{2,3},{3,2},{4,5},{5,4},{6,7},{7,6},{8,9},{9,8},{10,11... | collective-permute-start | bytes 1081352 | tf_op jit(solution)/shard_map/ppermute | solution.py:63
  129.5 14.0 %collective-permute-start.10 = (bf16[704,128]{1,0:T(8,128)(2,1)S(1)}, bf16[704,128]{1,0:T(8,128)(2,1)S(1)}, u32[]{:S(2)}, u32[]{:S(2)}) collective-permute-start(bf16[704,128]{1,0:T(8,128)(2,1)S(1)} %get-tuple-element.73), channel_id=1, source_target_pairs={{0,511},{1,510},{2,509},{3,508},{4,8},{5,9},{6,10},{7,11},{8,4},{9... | collective-permute-start | bytes 540680 | tf_op jit(solution)/shard_map/ppermute | solution.py:55
  135.2 6.3 %collective-permute-start.11 = (bf16[192,128]{1,0:T(8,128)(2,1)S(1)}, bf16[192,128]{1,0:T(8,128)(2,1)S(1)}, u32[]{:S(2)}, u32[]{:S(2)}) collective-permute-start(bf16[192,128]{1,0:T(8,128)(2,1)S(1)} %get-tuple-element.74), channel_id=1, source_target_pairs={{0,3},{1,2},{2,1},{3,0},{4,7},{5,6},{6,5},{7,4},{8,11},{9,10},{10,... | collective-permute-start | bytes 147464 | tf_op jit(solution)/shard_map/ppermute | solution.py:59
  145.0 8.7 %collective-permute-start.12 = (bf16[704,128]{1,0:T(8,128)(2,1)S(1)}, bf16[704,128]{1,0:T(8,128)(2,1)S(1)}, u32[]{:S(2)}, u32[]{:S(2)}) collective-permute-start(bf16[704,128]{1,0:T(8,128)(2,1)S(1)} %shard_map.46), channel_id=1, source_target_pairs={{0,3},{1,2},{2,1},{3,0},{4,7},{5,6},{6,5},{7,4},{8,11},{9,10},{10,... | collective-permute-start | bytes 540680 | tf_op jit(solution)/shard_map/ppermute | solution.py:59
Sparse Core Ops, SparseCore 0:
  27.4 48.1 all-gather.1

commit v7 on v6

--- a/solution.py
+++ b/solution.py
@@ -325,23 +325,31 @@
     return jnp.dot(left, right, preferred_element_type=F32)
 
 
-def collide_kernel(flags, lowered, other, m0, m1, m2, m3, rows_out, held, done):
-    copies = [
-        pltpu.make_async_copy(source, held.at[index], done.at[index])
-        for index, source in enumerate((m0, m1, m2, m3))
-    ]
-    for copy in copies:
+AHEAD = 8
+
+
+def in_turn(copies):
+    for copy in copies[:AHEAD]:
         copy.start()
+    waited = iter(range(len(copies)))
+
+    def wait():
+        index = next(waited)
+        copies[index].wait()
+        if index + AHEAD < len(copies):
+            copies[index + AHEAD].start()
+
+    return wait
+
+
+def collide_kernel(flags, lowered, other, m0, m1, m2, m3, rows_out):
     swapped = flags[2] == 1
     first = jnp.where(swapped, other[...], lowered[...])
     second = jnp.where(swapped, lowered[...], other[...])
     values = first[:PAD], first[PAD:], second[:PAD], second[PAD:]
-    for index, copy in enumerate(copies):
-        copy.wait()
-        for part in range(PAD // PART):
-            span = rows_of(part, PART)
-            total = dot(held[index, span], values[index])
-            rows_out[span] = total if index == 0 else rows_out[span] + total
+    for part in range(PAD // PART):
+        span = rows_of(part, PART)
+        rows_out[span] = sum(dot(m[span], v) for m, v in zip((m0, m1, m2, m3), values))
 
 
 def give_rows(flags, part, rows_near, rows_far, factors, packed, outs):
@@ -366,89 +374,82 @@
 def collide_partner_kernel(flags, own, lowered, other, factors, matrix, *refs):
     *outs, held, done = refs
     parts = PAD // PART
-    copies = []
-    for part in range(parts):
-        for half in range(2):
-            index = parts * half + part
-            copy = pltpu.make_async_copy(
-                matrix.at[rows_of(index, PART)], held.at[rows_of(index, PART)], done.at[index]
-            )
-            copy.start()
-            copies.append(copy)
+    order = [parts * half + part for part in range(parts) for half in range(2)]
+    wait = in_turn(
+        [
+            pltpu.make_async_copy(matrix.at[rows_of(i, PART)], held.at[rows_of(i, PART)], done.at[i])
+            for i in order
+        ]
+    )
     swapped = flags[2] == 1
     first = jnp.where(swapped, other[...], lowered[...])
     second = jnp.where(swapped, lowered[...], other[...])
     packed = (jnp.zeros((CHUNK, LANES), F32),) * 2
     for part in range(parts):
         span = rows_of(part, PART)
-        copies[2 * part].wait()
+        wait()
         partner = dot(held[span], first)
-        copies[2 * part + 1].wait()
+        wait()
         partner += dot(held[rows_of(parts + part, PART)], second)
         packed = give_product(flags, part, own[span], partner, factors, packed, outs[:4])
     outs[4][:EDGE], outs[4][EDGE:] = edge_block(packed[0]), edge_block(packed[1])
 
 
-def half_products(half, values, parts, matrix, held_own, held_partner, done, give):
-    count = PAD // PART
-    own = [
-        pltpu.make_async_copy(parts[2 * half + i], held_own.at[i], done.at[i]) for i in range(2)
-    ]
-    partner = [
-        pltpu.make_async_copy(
-            matrix.at[rows_of(count * half + i, PART)], held_partner.at[rows_of(i, PART)], done.at[2 + i]
-        )
-        for i in range(count)
-    ]
-    for copy in partner + own:
-        copy.start()
-    totals = []
-    for part in range(count):
-        partner[part].wait()
-        totals.append(dot(held_partner[rows_of(part, PART)], values))
-    for copy in own:
-        copy.wait()
-    for part in range(count):
-        span = rows_of(part, PART)
-        total = dot(held_own[0, span], values[:PAD]) + dot(held_own[1, span], values[PAD:])
-        give(span, total, totals[part])
-
-
-def early_kernel(flags, lowered, m0, m1, m2, m3, matrix, own_out, partner_out, *scratch):
+def early_kernel(
+    flags, lowered, m0, m1, m2, m3, matrix, own_out, partner_out, next_own, next_partner,
+    held_own, held_partner, done,
+):
     values = lowered[...]
-
-    def give(span, own, partner):
-        own_out[span] = own
-        partner_out[span] = partner
-
+    parts = m0, m1, m2, m3
     for half in range(2):
 
         @pl.when(flags[2] == half)
         def _():
-            half_products(half, values, (m0, m1, m2, m3), matrix, *scratch, give)
-
-
-def late_kernel(flags, other, own, partner, factors, m0, m1, m2, m3, matrix, *refs):
-    outs, (total_own, total_partner, *scratch) = refs[:5], refs[5:]
+            copies = [
+                pltpu.make_async_copy(
+                    matrix.at[rows_of(half, PAD)], held_partner, done.at[0]
+                )
+            ]
+            for i in range(2):
+                copies.append(pltpu.make_async_copy(parts[2 * half + i], held_own.at[i], done.at[1 + i]))
+            copies.append(
+                pltpu.make_async_copy(matrix.at[rows_of(1 - half, PAD)], next_partner, done.at[3])
+            )
+            for i in range(2):
+                source = parts[2 * (1 - half) + i]
+                copies.append(pltpu.make_async_copy(source, next_own.at[i], done.at[4 + i]))
+            wait = in_turn(copies)
+            wait()
+            for part in range(PAD // PART):
+                span = rows_of(part, PART)
+                partner_out[span] = dot(held_partner[span], values)
+            wait()
+            wait()
+            for part in range(PAD // PART):
+                span = rows_of(part, PART)
+                own_out[span] = dot(held_own[0, span], values[:PAD]) + dot(held_own[1, span], values[PAD:])
+            for _ in range(3):
+                wait()
+
+
+def late_kernel(flags, other, own, partner, factors, matrix_own, matrix_partner, *outs):
     values = other[...]
-
-    def give(span, more_own, more_partner):
-        total_own[span] = own[span] + more_own
-        total_partner[span] = partner[span] + more_partner
-
-    for half in range(2):
-
-        @pl.when(flags[2] != half)
-        def _():
-            half_products(half, values, (m0, m1, m2, m3), matrix, *scratch, give)
-
     packed = (jnp.zeros((CHUNK, LANES), F32),) * 2
     for part in range(PAD // PART):
         span = rows_of(part, PART)
+        more_own = dot(matrix_own[0, span], values[:PAD]) + dot(matrix_own[1, span], values[PAD:])
+        more_partner = dot(matrix_partner[span], values)
         packed = give_product(
-            flags, part, total_own[span], total_partner[span], factors, packed, outs[:4]
+            flags, part, own[span] + more_own, partner[span] + more_partner, factors, packed, outs[:4]
         )
     outs[4][:EDGE], outs[4][EDGE:] = edge_block(packed[0]), edge_block(packed[1])
+
+
+ROWS_F32 = ((PAD, LANES), F32)
+PARTNER_SCRATCH = [pltpu.VMEM((2 * PAD, 2 * PAD), BF16), pltpu.SemaphoreType.DMA((8,))]
+HELD = [pltpu.VMEM((2, PAD, PAD), BF16), pltpu.VMEM((PAD, 2 * PAD), BF16)]
+EARLY = [ROWS_F32, ROWS_F32, ((2, PAD, PAD), BF16), ((PAD, 2 * PAD), BF16)]
+EARLY_SCRATCH = HELD + [pltpu.SemaphoreType.DMA((6,))]
 
 
 def finish_kernel(flags, kept, received, evolved):
@@ -487,7 +488,7 @@
 def per_device(populations, solid_mask, collision):
     cell, vel = lax.axis_index("cells"), lax.axis_index("vel")
     low = (vel < 2).astype(jnp.int32)
-    core, z = cell % 2, cell // 2 % 8
+    core, ring_place = cell % 2, cell // 32 + 4 * (cell // 2 % 2)
     block = jnp.minimum(vel, 3 - vel)
     half = (1 - low) ^ (cell // RING % 2)
     needing = (cell + 1 - 2 * low) % 128
@@ -496,8 +497,9 @@
     flags = jnp.stack([low, 1 - core, block, half, same, straight_half])
     flags = flags.astype(jnp.int32)
 
-    row = CHUNK * z + lax.iota(jnp.int32, CHUNK)
-    start = jnp.clip(jnp.where(low == 1, CHUNK * z, ROWS - CHUNK - CHUNK * z), 0, ROWS - CHUNK)
+    first_row = CHUNK * ring_place
+    row = first_row + lax.iota(jnp.int32, CHUNK)
+    start = jnp.clip(jnp.where(low == 1, first_row, ROWS - CHUNK - first_row), 0, ROWS - CHUNK)
     wanted = jnp.where(row < ROWS, jnp.where(low == 1, row, ROWS - 1 - row) - start, -1)
     window = lax.dynamic_slice(collision, (start, 0), (CHUNK, collision.shape[1]))
     window = padded_columns(chosen(place(CHUNK, CHUNK, wanted).T, window))
@@ -515,7 +517,9 @@
     )
     piece, _ = lax.optimization_barrier((piece, message))
     groups = [
-        [(line * 8 + step) * 2 + side for side in range(2) for step in range(8)] for line in range(8)
+        [x * 32 + y * 16 + 4 * pair + 2 * odd + side for side in range(2) for odd in range(2) for x in range(4)]
+        for y in range(2)
+        for pair in range(4)
     ]
     partner_matrix = lax.all_gather(piece, "cells", axis=0, tiled=True, axis_index_groups=groups)
     straight, turned = to_layer(straight, False), to_layer(turned, True)
@@ -539,18 +543,14 @@
     work = 100 * PAD * LANES
 
     other = to_side(lowered)
-    dma = pltpu.SemaphoreType.DMA
     (own,) = call(
-        collide_kernel, [(rows, F32)], flags, lowered, other, *matrix, flops=multiply, stay=4,
-        scratch=[pltpu.VMEM((4, PAD, PAD), BF16), dma((4,))],
+        collide_kernel, [(rows, F32)], flags, lowered, other, *matrix, flops=multiply
     )
     partner_matrix, own = lax.optimization_barrier((partner_matrix, own))
     near, far, for_sibling, for_neighbour, edges = call(
         collide_partner_kernel, sends, flags, own, lowered, other, factors, partner_matrix,
-        flops=multiply, stay=1, scratch=[pltpu.VMEM((2 * PAD, 2 * PAD), BF16), dma((8,))],
-    )
-    held = [pltpu.VMEM((2, PAD, PAD), BF16), pltpu.VMEM((PAD, 2 * PAD), BF16), dma((6,))]
-
+        flops=multiply, stay=1, scratch=PARTNER_SCRATCH,
+    )
     for step in range(1, STEPS):
         neighbour, edges = to_neighbour(for_neighbour), to_mirror(edges)
         sibling = with_sibling(for_sibling)
@@ -565,12 +565,11 @@
         )
         other = to_side(lowered)
         early = call(
-            early_kernel, [(rows, F32)] * 2, flags, lowered, *matrix, partner_matrix,
-            flops=multiply, stay=5, scratch=held,
+            early_kernel, EARLY, flags, lowered, *matrix, partner_matrix,
+            flops=multiply, stay=5, scratch=EARLY_SCRATCH,
         )
         near, far, for_sibling, for_neighbour, edges = call(
-            late_kernel, sends, flags, other, *early, factors, *matrix, partner_matrix,
-            flops=multiply, stay=5, scratch=[pltpu.VMEM(rows, F32)] * 2 + held,
+            late_kernel, sends, flags, other, *early[:2], factors, *early[2:], flops=multiply
         )
 
     neighbour, edges = to_neighbour(for_neighbour), to_mirror(edges)

time: 163 us -> 163 us (level)
  local copies, waits for them, and re-layouts: 1.19 us -> 6.63 us
  matrix products: 17 us -> 13 us
  Pallas kernels: 30.8 us -> 27.2 us
    unnamed x7 -> x27, local copies, waits for them, and re-layouts: 0.75 us -> 6.19 us
    dot_general x8, matrix products: 17 us -> 13 us  [chosen(): return jnp.dot(left, right, preferred_element_type=BF16)]
    pallas_call x11, Pallas kernels: 30.8 us -> 27.2 us  [call(): pl.pallas_call(kernel, out_shape=[jax.ShapeDtypeStruct(shape, dtype) for...]
    ppermute x2, waiting for transfers between devices: 5.19 us -> 8.2 us  [to_side(): return lax.ppermute(array, 'vel', [(i, i ^ 1) for i in range(4)])]
  transfers between devices with their start and end apart: 14 -> 14, of which waited for: 9 -> 9; matrix products, arithmetic and copies ran while one was open for 9% -> 7% of each run, Pallas kernels for 9% -> 8%
where the time goes in v7:
time: 163 us; the launch traced here: 162 us
  starting transfers between devices  60.6 us (37%)
  waiting for transfers between devices  34.3 us (21%)
  Pallas kernels  27.2 us (17%)
  between operations  13.9 us (9%)
  matrix products  13 us (8%)
  local copies, waits for them, and re-layouts  6.63 us (4%)
  blocking collectives  6.19 us (4%)
    pallas_call x11, Pallas kernels, call(): pl.pallas_call(kernel, out_shape=[jax.ShapeDtypeStruct(shape, dtype) for...  27.2 us
    ppermute x3, starting transfers between devices, to_neighbour(): return lax.ppermute(array, BOTH, pairs_of(neighbour_of))  22 us
    ppermute x6, starting transfers between devices, to_mirror(): return lax.ppermute(array, 'vel', [(i, 3 - i) for i in range(4)])  18.5 us
    ppermute x6, waiting for transfers between devices, to_mirror(): return lax.ppermute(array, 'vel', [(i, 3 - i) for i in range(4)])  17 us
    ppermute x2, starting transfers between devices, to_layer(): return lax.ppermute(array, BOTH, pairs_of(target))  16.2 us
    dot_general x8, matrix products, chosen(): return jnp.dot(left, right, preferred_element_type=BF16)  13 us
    ppermute x2, waiting for transfers between devices, to_side(): return lax.ppermute(array, 'vel', [(i, i ^ 1) for i in range(4)])  8.2 us
    ppermute x2, waiting for transfers between devices, to_layer(): return lax.ppermute(array, BOTH, pairs_of(target))  6.36 us
  transfers between devices with their start and end apart: 14, of which 9 were waited for; matrix products, arithmetic and copies ran while one was open for 7% of the time, Pallas kernels for 8%

profile of v7, /device:TPU:8, one launch (start us, length us, event | category | flops | bytes accessed | tf_op | source)
XLA Modules:
  0.0 162.0 jit_solution(15751854658589512709)
XLA Ops:
  9.4 3.5 %collective-permute-start = (bf16[88,1408]{1,0:T(8,128)(2,1)S(1)}, bf16[88,1408]{1,0:T(8,128)(2,1)S(1)}, u32[]{:S(2)}, u32[]{:S(2)}) collective-permute-start(bf16[88,1408]{1,0:T(8,128)(2,1)S(1)} %pad_maximum_fusion), channel_id=1, source_target_pairs={{0,3},{1,2},{2,1},{3,0},{4,7},{5,6},{6,5},{7,4},{8,11},{9,10},{10,... | collective-permute-start | bytes 743432 | tf_op jit(solution)/shard_map/ppermute | solution.py:59
  13.2 2.0 %shard_map.37 = (f32[704,128]{1,0:T(8,128)S(1)}, f32[88,128]{1,0:T(8,128)S(1)}, bf16[800,128]{1,0:T(8,128)(2,1)S(1)}, bf16[720,128]{1,0:T(8,128)(2,1)S(1)}, bf16...) custom-call(s32[6]{0:T(128)S(1)} %stack.31.flags, f32[704,256]{1,0:T(8,128)S(1)} %pad.13.populations, ...), custom_call_target="tpu_custom_call" | custom-call | flops 761266176 | bytes 2786304 | tf_op jit(solution)/shard_map/pallas_call | solution.py:73
  15.2 11.3 %collective-permute-done = bf16[88,1408]{1,0:T(8,128)(2,1)S(1)} collective-permute-done((bf16[88,1408]{1,0:T(8,128)(2,1)S(1)}, bf16[88,1408]{1,0:T(8,128)(2,1)S(1)}, u32[]{:S(2)}, u32[]{:S(2)}) %collective-permute-start) | collective-permute-done | bytes 247840 | tf_op jit(solution)/shard_map/ppermute | solution.py:59
  27.3 1.9 %collective-permute-start.1 = (bf16[800,128]{1,0:T(8,128)(2,1)S(1)}, bf16[800,128]{1,0:T(8,128)(2,1)S(1)}, u32[]{:S(2)}, u32[]{:S(2)}) collective-permute-start(bf16[800,128]{1,0:T(8,128)(2,1)S(1)} %get-tuple-element.44), channel_id=1, source_target_pairs={{0,3},{1,2},{2,1},{3,0},{4,7},{5,6},{6,5},{7,4},{8,11},{9,10},{10,... | collective-permute-start | bytes 614408 | tf_op jit(solution)/shard_map/ppermute | solution.py:59
  29.2 14.3 %collective-permute-start.2 = (bf16[720,128]{1,0:T(8,128)(2,1)S(1)}, bf16[720,128]{1,0:T(8,128)(2,1)S(1)}, u32[]{:S(2)}, u32[]{:S(2)}) collective-permute-start(bf16[720,128]{1,0:T(8,128)(2,1)S(1)} %get-tuple-element.49), channel_id=1, source_target_pairs={{0,508},{1,509},{2,6},{3,7},{4,0},{5,1},{6,10},{7,11},{8,4},{9,5},... | collective-permute-start | bytes 552968 | tf_op jit(solution)/shard_map/ppermute | solution.py:46
  43.5 1.9 %collective-permute-start.3 = (bf16[720,128]{1,0:T(8,128)(2,1)S(1)}, bf16[720,128]{1,0:T(8,128)(2,1)S(1)}, u32[]{:S(2)}, u32[]{:S(2)}) collective-permute-start(bf16[720,128]{1,0:T(8,128)(2,1)S(1)} %get-tuple-element.50), channel_id=1, source_target_pairs={{0,511},{1,510},{2,5},{3,4},{4,3},{5,2},{6,9},{7,8},{8,7},{9,6},{1... | collective-permute-start | bytes 552968 | tf_op jit(solution)/shard_map/ppermute | solution.py:46
  45.5 5.4 %fusion.6 = bf16[704,2744]{1,0:T(8,128)(2,1)S(1)} fusion(bf16[686,2744]{1,0:T(8,128)(2,1)} %param.5, s32[704]{0:T(1024)S(1)} %select_select_fusion), kind=kOutput, calls=%fused_computation.13 | convolution fusion | flops 2650879488 | bytes 7631136 | tf_op jit(solution)/shard_map/dot_general | solution.py:469
  51.2 6.4 %collective-permute-done.3.turned = bf16[720,128]{1,0:T(8,128)(2,1)S(1)} collective-permute-done((bf16[720,128]{1,0:T(8,128)(2,1)S(1)}, bf16[720,128]{1,0:T(8,128)(2,1)S(1)}, u32[]{:S(2)}, u32[]{:S(2)}) %collective-permute-start.3) | collective-permute-done | bytes 184352 | tf_op jit(solution)/shard_map/ppermute | solution.py:46
  57.6 2.2 %shard_map.38 = (bf16[1408,128]{1,0:T(8,128)(2,1)S(1)}, f32[8,128]{1,0:T(8,128)S(1)}) custom-call(s32[6]{0:T(128)S(1)} %stack.31.flags, f32[704,128]{1,0:T(8,128)S(1)} %get-tuple-element.46.own, f32[88,128]{1,0:T(8,128)S(1)} %get-tuple-element.47.own_edge, bf16[800,128]{1,0:T(8,128)(2,1)S(1)} %collective-permute-done.1.received, ...), custom_call_target="tpu_custom_call" | custom-call | flops 18022400 | bytes 2428928 | tf_op jit(solution)/shard_map/pallas_call | solution.py:73
  59.8 2.1 %collective-permute-start.4 = (bf16[1408,128]{1,0:T(8,128)(2,1)S(1)}, bf16[1408,128]{1,0:T(8,128)(2,1)S(1)}, u32[]{:S(2)}, u32[]{:S(2)}) collective-permute-start(bf16[1408,128]{1,0:T(8,128)(2,1)S(1)} %get-tuple-element.55.lowered), channel_id=1, source_target_pairs={{0,1},{1,0},{2,3},{3,2},{4,5},{5,4},{6,7},{7,6},{8,9},{9,8},{10,11... | collective-permute-start | bytes 1081352 | tf_op jit(solution)/shard_map/ppermute | solution.py:63
  66.8 2.3 %collective-permute-done.4.other = bf16[1408,128]{1,0:T(8,128)(2,1)S(1)} collective-permute-done((bf16[1408,128]{1,0:T(8,128)(2,1)S(1)}, bf16[1408,128]{1,0:T(8,128)(2,1)S(1)}, u32[]{:S(2)}, u32[]{:S(2)}) %collective-permute-start.4) | collective-permute-done | bytes 360480 | tf_op jit(solution)/shard_map/ppermute | solution.py:63
  76.5 4.2 %shard_map.40 = (f32[704,128]{1,0:T(8,128)S(1)}, f32[704,128]{1,0:T(8,128)S(1)}, bf16[704,128]{1,0:T(8,128)(2,1)S(1)}, bf16[704,128]{1,0:T(8,128)(2,1)S(1)}, bf16[192,128]{1,0:T(8,128)(2,1)S(1)}) custom-call(s32[6]{0:T(128)S(1)} %stack.31.flags, f32[704,128]{1,0:T(8,128)S(1)} %copy-done.9, bf16[1408,128]{1,0:T(8,128)(2,1)S(1)} %copy-done.5, ...), custom_call_target="tpu_custom_call" | custom-call | flops 507510784 | bytes 7258112 | tf_op jit(solution)/shard_map/pallas_call | solution.py:73
  80.7 9.2 %collective-permute-start.5 = (bf16[704,128]{1,0:T(8,128)(2,1)S(1)}, bf16[704,128]{1,0:T(8,128)(2,1)S(1)}, u32[]{:S(2)}, u32[]{:S(2)}) collective-permute-start(bf16[704,128]{1,0:T(8,128)(2,1)S(1)} %get-tuple-element.62), channel_id=1, source_target_pairs={{0,511},{1,510},{2,509},{3,508},{4,8},{5,9},{6,10},{7,11},{8,4},{9... | collective-permute-start | bytes 540680 | tf_op jit(solution)/shard_map/ppermute | solution.py:55
  89.9 3.6 %collective-permute-start.6 = (bf16[192,128]{1,0:T(8,128)(2,1)S(1)}, bf16[192,128]{1,0:T(8,128)(2,1)S(1)}, u32[]{:S(2)}, u32[]{:S(2)}) collective-permute-start(bf16[192,128]{1,0:T(8,128)(2,1)S(1)} %get-tuple-element.63), channel_id=1, source_target_pairs={{0,3},{1,2},{2,1},{3,0},{4,7},{5,6},{6,5},{7,4},{8,11},{9,10},{10,... | collective-permute-start | bytes 147464 | tf_op jit(solution)/shard_map/ppermute | solution.py:59
  93.5 2.1 %all_gather.13.sibling = bf16[1408,128]{1,0:T(8,128)(2,1)S(1)} all-gather(bf16[704,128]{1,0:T(8,128)(2,1)S(1)} %get-tuple-element.61), channel_id=1, replica_groups={{0,4},{8,12},{16,20},{24,28},{32,36},{40,44},{48,52},{56,60},{64,68},{7..., dimensions={0}, use_global_device_ids=true | all-gather | bytes 540672 | tf_op jit(solution)/shard_map/all_gather | solution.py:39
  95.8 2.6 %shard_map.41 = (f32[704,128]{1,0:T(8,128)S(1)}, f32[704,128]{1,0:T(8,128)S(1)}, bf16[704,128]{1,0:T(8,128)(2,1)S(1)}, bf16[704,128]{1,0:T(8,128)(2,1)S(1)}, bf16[192,128]{1,0:T(8,128)(2,1)S(1)}) custom-call(s32[6]{0:T(128)S(1)} %stack.31.flags, f32[704,128]{1,0:T(8,128)S(1)} %get-tuple-element.59.near, f32[704,128]{1,0:T(8,128)S(1)} %get-tuple-element.60.far, ...), custom_call_target="tpu_custom_call" | custom-call | flops 9011200 | bytes 3526656 | tf_op jit(solution)/shard_map/pallas_call | solution.py:73
  98.5 8.1 %collective-permute-start.7 = (bf16[704,128]{1,0:T(8,128)(2,1)S(1)}, bf16[704,128]{1,0:T(8,128)(2,1)S(1)}, u32[]{:S(2)}, u32[]{:S(2)}) collective-permute-start(bf16[704,128]{1,0:T(8,128)(2,1)S(1)} %get-tuple-element.68), channel_id=1, source_target_pairs={{0,511},{1,510},{2,509},{3,508},{4,8},{5,9},{6,10},{7,11},{8,4},{9... | collective-permute-start | bytes 540680 | tf_op jit(solution)/shard_map/ppermute | solution.py:55
  106.6 3.6 %collective-permute-start.8 = (bf16[192,128]{1,0:T(8,128)(2,1)S(1)}, bf16[192,128]{1,0:T(8,128)(2,1)S(1)}, u32[]{:S(2)}, u32[]{:S(2)}) collective-permute-start(bf16[192,128]{1,0:T(8,128)(2,1)S(1)} %get-tuple-element.69), channel_id=1, source_target_pairs={{0,3},{1,2},{2,1},{3,0},{4,7},{5,6},{6,5},{7,4},{8,11},{9,10},{10,... | collective-permute-start | bytes 147464 | tf_op jit(solution)/shard_map/ppermute | solution.py:59
  110.2 2.1 %all_gather.14.sibling = bf16[1408,128]{1,0:T(8,128)(2,1)S(1)} all-gather(bf16[704,128]{1,0:T(8,128)(2,1)S(1)} %get-tuple-element.67), channel_id=1, replica_groups={{0,4},{8,12},{16,20},{24,28},{32,36},{40,44},{48,52},{56,60},{64,68},{7..., dimensions={0}, use_global_device_ids=true | all-gather | bytes 540672 | tf_op jit(solution)/shard_map/all_gather | solution.py:39
  112.5 2.2 %shard_map.42.lowered = bf16[1408,128]{1,0:T(8,128)(2,1)S(1)} custom-call(s32[6]{0:T(128)S(1)} %stack.31.flags, f32[704,128]{1,0:T(8,128)S(1)} %get-tuple-element.65.near, f32[704,128]{1,0:T(8,128)S(1)} %get-tuple-element.66.far, bf16[1408,128]{1,0:T(8,128)(2,1)S(1)} %all_gather.14.sibling, bf16[704,128]{1,0:T(8,128)(2,1)S(1)} %collective-permute-done.7.neighbour, ...), custom_call_target="tpu_custom_call" | custom-call | flops 9011200 | bytes 2756608 | tf_op jit(solution)/shard_map/pallas_call | solution.py:73
  114.8 1.9 %collective-permute-start.9 = (bf16[1408,128]{1,0:T(8,128)(2,1)S(1)}, bf16[1408,128]{1,0:T(8,128)(2,1)S(1)}, u32[]{:S(2)}, u32[]{:S(2)}) collective-permute-start(bf16[1408,128]{1,0:T(8,128)(2,1)S(1)} %shard_map.42.lowered), channel_id=1, source_target_pairs={{0,1},{1,0},{2,3},{3,2},{4,5},{5,4},{6,7},{7,6},{8,9},{9,8},{10,11... | collective-permute-start | bytes 1081352 | tf_op jit(solution)/shard_map/ppermute | solution.py:63
  116.7 4.2 %shard_map.43 = (f32[704,128]{1,0:T(8,128)S(1)}, f32[704,128]{1,0:T(8,128)S(1)}, bf16[2,704,704]{2,1,0:T(8,128)(2,1)S(1)}, bf16[704,1408]{1,0:T(8,128)(2,1)S(1)}) custom-call(s32[6]{0:T(128)S(1)} %stack.31.flags, bf16[1408,128]{1,0:T(8,128)(2,1)S(1)} %shard_map.42.lowered, bf16[704,704]{1,0:T(8,128)(2,1)} %copy-done.2, bf16[704,704]{1,0:T(8,128)(2,1)} %copy-done.3, ...), custom_call_target="tpu_custom_call" | custom-call | flops 507510784 | bytes 12976128 | tf_op jit(solution)/shard_map/pallas_call | solution.py:73
  121.0 5.9 %collective-permute-done.9.other = bf16[1408,128]{1,0:T(8,128)(2,1)S(1)} collective-permute-done((bf16[1408,128]{1,0:T(8,128)(2,1)S(1)}, bf16[1408,128]{1,0:T(8,128)(2,1)S(1)}, u32[]{:S(2)}, u32[]{:S(2)}) %collective-permute-start.9) | collective-permute-done | bytes 360480 | tf_op jit(solution)/shard_map/ppermute | solution.py:63
  126.9 2.0 %shard_map.44 = (f32[704,128]{1,0:T(8,128)S(1)}, f32[704,128]{1,0:T(8,128)S(1)}, bf16[704,128]{1,0:T(8,128)(2,1)S(1)}, bf16[704,128]{1,0:T(8,128)(2,1)S(1)}, bf16[192,128]{1,0:T(8,128)(2,1)S(1)}) custom-call(s32[6]{0:T(128)S(1)} %stack.31.flags, bf16[1408,128]{1,0:T(8,128)(2,1)S(1)} %collective-permute-done.9.other, f32[704,128]{1,0:T(8,128)S(1)} %get-tuple-element.70.own, ...), custom_call_target="tpu_custom_call" | custom-call | flops 507510784 | bytes 7258112 | tf_op jit(solution)/shard_map/pallas_call | solution.py:73
  128.8 4.7 %collective-permute-start.10 = (bf16[704,128]{1,0:T(8,128)(2,1)S(1)}, bf16[704,128]{1,0:T(8,128)(2,1)S(1)}, u32[]{:S(2)}, u32[]{:S(2)}) collective-permute-start(bf16[704,128]{1,0:T(8,128)(2,1)S(1)} %get-tuple-element.77), channel_id=1, source_target_pairs={{0,511},{1,510},{2,509},{3,508},{4,8},{5,9},{6,10},{7,11},{8,4},{9... | collective-permute-start | bytes 540680 | tf_op jit(solution)/shard_map/ppermute | solution.py:55
  133.6 3.6 %collective-permute-start.11 = (bf16[192,128]{1,0:T(8,128)(2,1)S(1)}, bf16[192,128]{1,0:T(8,128)(2,1)S(1)}, u32[]{:S(2)}, u32[]{:S(2)}) collective-permute-start(bf16[192,128]{1,0:T(8,128)(2,1)S(1)} %get-tuple-element.78), channel_id=1, source_target_pairs={{0,3},{1,2},{2,1},{3,0},{4,7},{5,6},{6,5},{7,4},{8,11},{9,10},{10,... | collective-permute-start | bytes 147464 | tf_op jit(solution)/shard_map/ppermute | solution.py:59
  137.2 2.1 %all_gather.15.sibling = bf16[1408,128]{1,0:T(8,128)(2,1)S(1)} all-gather(bf16[704,128]{1,0:T(8,128)(2,1)S(1)} %get-tuple-element.76), channel_id=1, replica_groups={{0,4},{8,12},{16,20},{24,28},{32,36},{40,44},{48,52},{56,60},{64,68},{7..., dimensions={0}, use_global_device_ids=true | all-gather | bytes 540672 | tf_op jit(solution)/shard_map/all_gather | solution.py:39
  140.1 2.8 %collective-permute-done.10.neighbour = bf16[704,128]{1,0:T(8,128)(2,1)S(1)} collective-permute-done((bf16[704,128]{1,0:T(8,128)(2,1)S(1)}, bf16[704,128]{1,0:T(8,128)(2,1)S(1)}, u32[]{:S(2)}, u32[]{:S(2)}) %collective-permute-start.10) | collective-permute-done | bytes 180256 | tf_op jit(solution)/shard_map/ppermute | solution.py:55
  144.3 2.2 %collective-permute-start.12 = (bf16[704,128]{1,0:T(8,128)(2,1)S(1)}, bf16[704,128]{1,0:T(8,128)(2,1)S(1)}, u32[]{:S(2)}, u32[]{:S(2)}) collective-permute-start(bf16[704,128]{1,0:T(8,128)(2,1)S(1)} %shard_map.46), channel_id=1, source_target_pairs={{0,3},{1,2},{2,1},{3,0},{4,7},{5,6},{6,5},{7,4},{8,11},{9,10},{10,... | collective-permute-start | bytes 540680 | tf_op jit(solution)/shard_map/ppermute | solution.py:59
  146.5 2.3 %shard_map.45.kept = f32[704,128]{1,0:T(8,128)S(1)} custom-call(s32[6]{0:T(128)S(1)} %stack.31.flags, f32[704,128]{1,0:T(8,128)S(1)} %get-tuple-element.74.near, f32[704,128]{1,0:T(8,128)S(1)} %get-tuple-element.75.far, bf16[1408,128]{1,0:T(8,128)(2,1)S(1)} %all_gather.15.sibling, bf16[704,128]{1,0:T(8,128)(2,1)S(1)} %collective-permute-done.10.neighbour, ...), custom_call_target="tpu_custom_call" | custom-call | flops 507510784 | bytes 2756608 | tf_op jit(solution)/shard_map/pallas_call | solution.py:73
  148.8 4.2 %collective-permute-done.12.received = bf16[704,128]{1,0:T(8,128)(2,1)S(1)} collective-permute-done((bf16[704,128]{1,0:T(8,128)(2,1)S(1)}, bf16[704,128]{1,0:T(8,128)(2,1)S(1)}, u32[]{:S(2)}, u32[]{:S(2)}) %collective-permute-start.12) | collective-permute-done | bytes 180256 | tf_op jit(solution)/shard_map/ppermute | solution.py:59
  153.0 2.1 %shard_map.47 = f32[686,1,256]{2,1,0:T(1,128)} custom-call(s32[6]{0:T(128)S(1)} %stack.31.flags, f32[704,128]{1,0:T(8,128)S(1)} %shard_map.45.kept, bf16[704,128]{1,0:T(8,128)(2,1)S(1)} %collective-permute-done.12.received), custom_call_target="tpu_custom_call" | custom-call | flops 126877696 | bytes 1243136 | tf_op jit(solution)/shard_map/pallas_call | solution.py:73
  (58 shorter events, 19.1 us)
Async XLA Ops:
  6.5 6.5 %copy-start.11 = (f32[686,1,256]{2,1,0:T(1,128)S(1)}, f32[686,1,256]{2,1,0:T(1,128)}, u32[]{:S(2)}) copy-start(f32[686,1,256]{2,1,0:T(1,128)} %param.3) | copy-start | bytes 2107396
  6.5 67.0 %all-gather.2.cloned.1.call-start = ((), (), s32[]{:S(2)}) async-start(), calls=%async_computation | async-start | bytes 4212736 | tf_op jit(solution)/shard_map/all_gather | solution.py:524
  8.7 4.5 %copy-start.10 = (s32[1,256]{1,0:T(1,128)S(1)}, s32[1,256]{1,0:T(1,128)}, u32[]{:S(2)}) copy-start(s32[1,256]{1,0:T(1,128)} %solid.1) | copy-start | bytes 3076
  9.4 17.1 %collective-permute-start = (bf16[88,1408]{1,0:T(8,128)(2,1)S(1)}, bf16[88,1408]{1,0:T(8,128)(2,1)S(1)}, u32[]{:S(2)}, u32[]{:S(2)}) collective-permute-start(bf16[88,1408]{1,0:T(8,128)(2,1)S(1)} %pad_maximum_fusion), channel_id=1, source_target_pairs={{0,3},{1,2},{2,1},{3,0},{4,7},{5,6},{6,5},{7,4},{8,11},{9,10},{10,... | collective-permute-start | bytes 743432 | tf_op jit(solution)/shard_map/ppermute | solution.py:59
  26.6 0.7 copy-start.12
  27.3 18.2 %collective-permute-start.1 = (bf16[800,128]{1,0:T(8,128)(2,1)S(1)}, bf16[800,128]{1,0:T(8,128)(2,1)S(1)}, u32[]{:S(2)}, u32[]{:S(2)}) collective-permute-start(bf16[800,128]{1,0:T(8,128)(2,1)S(1)} %get-tuple-element.44), channel_id=1, source_target_pairs={{0,3},{1,2},{2,1},{3,0},{4,7},{5,6},{6,5},{7,4},{8,11},{9,10},{10,... | collective-permute-start | bytes 614408 | tf_op jit(solution)/shard_map/ppermute | solution.py:59
  29.2 22.0 %collective-permute-start.2 = (bf16[720,128]{1,0:T(8,128)(2,1)S(1)}, bf16[720,128]{1,0:T(8,128)(2,1)S(1)}, u32[]{:S(2)}, u32[]{:S(2)}) collective-permute-start(bf16[720,128]{1,0:T(8,128)(2,1)S(1)} %get-tuple-element.49), channel_id=1, source_target_pairs={{0,508},{1,509},{2,6},{3,7},{4,0},{5,1},{6,10},{7,11},{8,4},{9,5},... | collective-permute-start | bytes 552968 | tf_op jit(solution)/shard_map/ppermute | solution.py:46
  43.5 14.1 %collective-permute-start.3 = (bf16[720,128]{1,0:T(8,128)(2,1)S(1)}, bf16[720,128]{1,0:T(8,128)(2,1)S(1)}, u32[]{:S(2)}, u32[]{:S(2)}) collective-permute-start(bf16[720,128]{1,0:T(8,128)(2,1)S(1)} %get-tuple-element.50), channel_id=1, source_target_pairs={{0,511},{1,510},{2,5},{3,4},{4,3},{5,2},{6,9},{7,8},{8,7},{9,6},{1... | collective-permute-start | bytes 552968 | tf_op jit(solution)/shard_map/ppermute | solution.py:46
  59.8 9.3 %copy-start.4 = (bf16[1408,128]{1,0:T(8,128)(2,1)}, bf16[1408,128]{1,0:T(8,128)(2,1)S(1)}, u32[]{:S(2)}) copy-start(bf16[1408,128]{1,0:T(8,128)(2,1)S(1)} %get-tuple-element.55.lowered) | copy-start | bytes 1081348
  59.8 9.3 %collective-permute-start.4 = (bf16[1408,128]{1,0:T(8,128)(2,1)S(1)}, bf16[1408,128]{1,0:T(8,128)(2,1)S(1)}, u32[]{:S(2)}, u32[]{:S(2)}) collective-permute-start(bf16[1408,128]{1,0:T(8,128)(2,1)S(1)} %get-tuple-element.55.lowered), channel_id=1, source_target_pairs={{0,1},{1,0},{2,3},{3,2},{4,5},{5,4},{6,7},{7,6},{8,9},{9,8},{10,11... | collective-permute-start | bytes 1081352 | tf_op jit(solution)/shard_map/ppermute | solution.py:63
  63.0 6.1 %copy-start = (bf16[704,704]{1,0:T(8,128)(2,1)}, bf16[704,704]{1,0:T(8,128)(2,1)S(1)}, u32[]{:S(2)}) copy-start(bf16[704,704]{1,0:T(8,128)(2,1)S(1)} %fusion.4.m2) | copy-start | bytes 2973700
  64.4 4.8 %copy-start.1 = (bf16[704,704]{1,0:T(8,128)(2,1)}, bf16[704,704]{1,0:T(8,128)(2,1)S(1)}, u32[]{:S(2)}) copy-start(bf16[704,704]{1,0:T(8,128)(2,1)S(1)} %fusion.1.m3) | copy-start | bytes 2973700
  65.5 3.7 %copy-start.2 = (bf16[704,704]{1,0:T(8,128)(2,1)}, bf16[704,704]{1,0:T(8,128)(2,1)S(1)}, u32[]{:S(2)}) copy-start(bf16[704,704]{1,0:T(8,128)(2,1)S(1)} %fusion.3.m0) | copy-start | bytes 2973700
  71.0 1.0 copy-start.3
  72.0 0.8 copy-start.6
  72.8 0.7 copy-start.8
  73.5 1.0 copy-start.5
  74.5 1.0 copy-start.7
  75.5 1.0 copy-start.9
  80.7 15.2 %collective-permute-start.5 = (bf16[704,128]{1,0:T(8,128)(2,1)S(1)}, bf16[704,128]{1,0:T(8,128)(2,1)S(1)}, u32[]{:S(2)}, u32[]{:S(2)}) collective-permute-start(bf16[704,128]{1,0:T(8,128)(2,1)S(1)} %get-tuple-element.62), channel_id=1, source_target_pairs={{0,511},{1,510},{2,509},{3,508},{4,8},{5,9},{6,10},{7,11},{8,4},{9... | collective-permute-start | bytes 540680 | tf_op jit(solution)/shard_map/ppermute | solution.py:55
  89.9 6.0 %collective-permute-start.6 = (bf16[192,128]{1,0:T(8,128)(2,1)S(1)}, bf16[192,128]{1,0:T(8,128)(2,1)S(1)}, u32[]{:S(2)}, u32[]{:S(2)}) collective-permute-start(bf16[192,128]{1,0:T(8,128)(2,1)S(1)} %get-tuple-element.63), channel_id=1, source_target_pairs={{0,3},{1,2},{2,1},{3,0},{4,7},{5,6},{6,5},{7,4},{8,11},{9,10},{10,... | collective-permute-start | bytes 147464 | tf_op jit(solution)/shard_map/ppermute | solution.py:59
  98.5 14.0 %collective-permute-start.7 = (bf16[704,128]{1,0:T(8,128)(2,1)S(1)}, bf16[704,128]{1,0:T(8,128)(2,1)S(1)}, u32[]{:S(2)}, u32[]{:S(2)}) collective-permute-start(bf16[704,128]{1,0:T(8,128)(2,1)S(1)} %get-tuple-element.68), channel_id=1, source_target_pairs={{0,511},{1,510},{2,509},{3,508},{4,8},{5,9},{6,10},{7,11},{8,4},{9... | collective-permute-start | bytes 540680 | tf_op jit(solution)/shard_map/ppermute | solution.py:55
  106.6 6.0 %collective-permute-start.8 = (bf16[192,128]{1,0:T(8,128)(2,1)S(1)}, bf16[192,128]{1,0:T(8,128)(2,1)S(1)}, u32[]{:S(2)}, u32[]{:S(2)}) collective-permute-start(bf16[192,128]{1,0:T(8,128)(2,1)S(1)} %get-tuple-element.69), channel_id=1, source_target_pairs={{0,3},{1,2},{2,1},{3,0},{4,7},{5,6},{6,5},{7,4},{8,11},{9,10},{10,... | collective-permute-start | bytes 147464 | tf_op jit(solution)/shard_map/ppermute | solution.py:59
  114.8 12.1 %collective-permute-start.9 = (bf16[1408,128]{1,0:T(8,128)(2,1)S(1)}, bf16[1408,128]{1,0:T(8,128)(2,1)S(1)}, u32[]{:S(2)}, u32[]{:S(2)}) collective-permute-start(bf16[1408,128]{1,0:T(8,128)(2,1)S(1)} %shard_map.42.lowered), channel_id=1, source_target_pairs={{0,1},{1,0},{2,3},{3,2},{4,5},{5,4},{6,7},{7,6},{8,9},{9,8},{10,11... | collective-permute-start | bytes 1081352 | tf_op jit(solution)/shard_map/ppermute | solution.py:63
  128.8 14.0 %collective-permute-start.10 = (bf16[704,128]{1,0:T(8,128)(2,1)S(1)}, bf16[704,128]{1,0:T(8,128)(2,1)S(1)}, u32[]{:S(2)}, u32[]{:S(2)}) collective-permute-start(bf16[704,128]{1,0:T(8,128)(2,1)S(1)} %get-tuple-element.77), channel_id=1, source_target_pairs={{0,511},{1,510},{2,509},{3,508},{4,8},{5,9},{6,10},{7,11},{8,4},{9... | collective-permute-start | bytes 540680 | tf_op jit(solution)/shard_map/ppermute | solution.py:55
  133.6 6.5 %collective-permute-start.11 = (bf16[192,128]{1,0:T(8,128)(2,1)S(1)}, bf16[192,128]{1,0:T(8,128)(2,1)S(1)}, u32[]{:S(2)}, u32[]{:S(2)}) collective-permute-start(bf16[192,128]{1,0:T(8,128)(2,1)S(1)} %get-tuple-element.78), channel_id=1, source_target_pairs={{0,3},{1,2},{2,1},{3,0},{4,7},{5,6},{6,5},{7,4},{8,11},{9,10},{10,... | collective-permute-start | bytes 147464 | tf_op jit(solution)/shard_map/ppermute | solution.py:59
  144.3 8.7 %collective-permute-start.12 = (bf16[704,128]{1,0:T(8,128)(2,1)S(1)}, bf16[704,128]{1,0:T(8,128)(2,1)S(1)}, u32[]{:S(2)}, u32[]{:S(2)}) collective-permute-start(bf16[704,128]{1,0:T(8,128)(2,1)S(1)} %shard_map.46), channel_id=1, source_target_pairs={{0,3},{1,2},{2,1},{3,0},{4,7},{5,6},{6,5},{7,4},{8,11},{9,10},{10,... | collective-permute-start | bytes 540680 | tf_op jit(solution)/shard_map/ppermute | solution.py:59
Sparse Core Ops, SparseCore 0:
  27.4 44.9 all-gather.1

commit v8 on v7

--- a/solution.py
+++ b/solution.py
@@ -19,6 +19,7 @@
 PART = 2 * CHUNK
 EDGE = 96
 LANES = 128
+BAND = 4 * CHUNK
 RING = 16
 F32 = jnp.float32
 BF16 = jnp.bfloat16
@@ -57,6 +58,10 @@
 
 def to_mirror(array):
     return lax.ppermute(array, "vel", [(i, 3 - i) for i in range(4)])
+
+
+def to_opposite(array):
+    return lax.ppermute(array, "vel", [(i, i ^ 2) for i in range(4)])
 
 
 def to_side(array):
@@ -235,7 +240,7 @@
 
 
 def first_kernel(
-    flags, own, own_edge, received, straight, turned, masks_in, factors, lowered, masks_out
+    flags, own, own_edge, received, straight, turned, masks_in, factors, lowered, masks_out, bands
 ):
     same = flags[4] == 1
     place = lax.broadcasted_iota(jnp.int32, (8, LANES), 0)
@@ -247,8 +252,9 @@
     masks_out[...] = masks
     edge_own, edge_other = own_edge[...], received[PAD:].astype(F32)[:CHUNK]
     sign = jnp.where(flags[0] == 1, 1.0, -1.0)
-    at_own = pl.multiple_of(PAD * (1 - flags[0]), 16)
-    at_other = pl.multiple_of(PAD * flags[0], 16)
+    low = flags[0] == 1
+    group = lanes_of(PART) >> 5
+    packed = [jnp.zeros((PART, LANES), F32)] * 2
     for part in range(PAD // PART):
         span = rows_of(part, PART)
         mine, theirs = own[span], received[span].astype(F32)
@@ -258,8 +264,14 @@
         new_other = stream_part(
             part, -sign, theirs, mine, turned[span].astype(F32), edge_other, masks, open_other, factors
         )
-        lowered[pl.ds(at_own + PART * part, PART)] = new_own.astype(BF16)
-        lowered[pl.ds(at_other + PART * part, PART)] = new_other.astype(BF16)
+        rows_a, rows_b = jnp.where(low, new_own, new_other), jnp.where(low, new_other, new_own)
+        for index, rows in enumerate((rows_a, rows_b)):
+            lowered[PAD * index + PART * part : PAD * index + PART * (part + 1)] = rows.astype(BF16)
+            place = 2 * index + part // 2
+            edge = roll(rows, NZ + 2 * NZ * place)
+            packed[part % 2] = jnp.where(group == place, edge, packed[part % 2])
+    for index in range(2):
+        bands[rows_of(index, PART)] = packed[index].astype(BF16)
 
 
 def streamed(flags, near, far, sibling, neighbour, edges, masks, factors):
@@ -281,13 +293,42 @@
         yield part, span, new_near, new_far
 
 
-def between_kernel(flags, near, far, sibling, neighbour, edges, masks, factors, *outs):
-    packed = (jnp.zeros((CHUNK, LANES), F32),) * 2
-    for part, span, new_near, new_far in streamed(
-        flags, near, far, sibling, neighbour, edges, masks, factors
-    ):
-        packed = give_rows(flags, part, new_near, new_far, factors, packed, outs[:4])
-    outs[4][:EDGE], outs[4][EDGE:] = edge_block(packed[0]), edge_block(packed[1])
+def between_near_kernel(flags, near, far, sibling, edges, masks, factors, rows_out, sent, packed_out):
+    values = masks[...]
+    sign = signs(flags)[0]
+    start = pl.multiple_of(PAD * flags[1], 16)
+    edge = edges[:EDGE].astype(F32)[:CHUNK]
+    packed = jnp.zeros((CHUNK, LANES), F32)
+    for part in range(PAD // PART):
+        span = rows_of(part, PART)
+        layer = sibling[pl.ds(start + PART * part, PART)].astype(F32)
+        rows = stream_part(
+            part, sign, near[span], far[span], layer, edge, values, values[5:6], factors
+        )
+        rows_out[span] = rows
+        sent[span] = rows.astype(BF16)
+        packed = pack_part(packed, part, sign, rows, factors)
+    packed_out[...] = edge_block(packed)
+
+
+def between_far_kernel(
+    flags, near, far, neighbour, edges, masks, factors, packed_near, rows_out, sent, packed_out
+):
+    values = masks[...]
+    sign = signs(flags)[1]
+    edge = edges[EDGE:].astype(F32)[:CHUNK]
+    packed = jnp.zeros((CHUNK, LANES), F32)
+    for part in range(PAD // PART):
+        span = rows_of(part, PART)
+        layer = neighbour[span].astype(F32)
+        rows = stream_part(
+            part, sign, far[span], near[span], layer, edge, values, values[6:7], factors
+        )
+        rows_out[span] = rows
+        sent[span] = rows.astype(BF16)
+        packed = pack_part(packed, part, sign, rows, factors)
+    packed_out[:EDGE] = packed_near[...]
+    packed_out[EDGE:] = edge_block(packed)
 
 
 def lower_kernel(flags, near, far, sibling, neighbour, edges, masks, factors, lowered):
@@ -325,31 +366,43 @@
     return jnp.dot(left, right, preferred_element_type=F32)
 
 
-AHEAD = 8
-
-
-def in_turn(copies):
-    for copy in copies[:AHEAD]:
-        copy.start()
-    waited = iter(range(len(copies)))
-
-    def wait():
-        index = next(waited)
-        copies[index].wait()
-        if index + AHEAD < len(copies):
-            copies[index + AHEAD].start()
-
-    return wait
-
-
-def collide_kernel(flags, lowered, other, m0, m1, m2, m3, rows_out):
+def pack_other(packed, part, sign, values, factors):
+    lane = lanes_of(CHUNK)
+    place = lane & (NZ - 1)
+    for index in range(2):
+        chunk = 2 * part + index
+        positive = factors[1, rows_of(chunk, CHUNK)] * sign > 0
+        edge = picked(values[rows_of(index, CHUNK)], jnp.where(positive, place, place + NZ))
+        packed = jnp.where((lane >> 4) == chunk, edge, packed)
+    return packed
+
+
+def unpacked(bands):
+    values = bands.astype(F32)
+    return jnp.concatenate([roll(values, -2 * NZ * group) for group in range(4)], axis=0).astype(BF16)
+
+
+def collide_kernel(
+    flags, lowered, other, bands, other_bands, factors, m0, m1, m2, m3, rows_out, packed_out, all_rows, all_bands
+):
     swapped = flags[2] == 1
-    first = jnp.where(swapped, other[...], lowered[...])
-    second = jnp.where(swapped, lowered[...], other[...])
-    values = first[:PAD], first[PAD:], second[:PAD], second[PAD:]
+    for index, right in enumerate((swapped, ~swapped)):
+        all_rows[rows_of(index, 2 * PAD)] = jnp.where(right, other[...], lowered[...])
+        all_bands[rows_of(index, BAND)] = jnp.where(right, other_bands[...], bands[...])
+    values = []
+    for index in range(2):
+        rows, band = all_rows[rows_of(index, 2 * PAD)], unpacked(all_bands[rows_of(index, BAND)])
+        for side in range(2):
+            span = rows_of(side, PAD)
+            values.append(jnp.concatenate([rows[span], band[span]], axis=1))
+    sign = jnp.where(flags[0] == 1, 1.0, -1.0)
+    packed = jnp.zeros((CHUNK, LANES), F32)
     for part in range(PAD // PART):
         span = rows_of(part, PART)
-        rows_out[span] = sum(dot(m[span], v) for m, v in zip((m0, m1, m2, m3), values))
+        total = sum(dot(m[span], v) for m, v in zip((m0, m1, m2, m3), values))
+        rows_out[span] = total[:, :LANES]
+        packed = pack_other(packed, part, sign, total[:, LANES:], factors)
+    packed_out[...] = edge_block(packed)
 
 
 def give_rows(flags, part, rows_near, rows_far, factors, packed, outs):
@@ -371,28 +424,55 @@
     return give_rows(flags, part, near, far, factors, packed, outs)
 
 
-def collide_partner_kernel(flags, own, lowered, other, factors, matrix, *refs):
-    *outs, held, done = refs
+def collide_partner_kernel(
+    flags, own_packed, factors, all_rows, all_bands, own, matrix,
+    near, far, for_sibling, for_neighbour, edges,
+    held, held_rows, held_bands, held_own, done,
+):
+    small = [
+        pltpu.make_async_copy(source, target, done.at[index])
+        for index, (source, target) in enumerate(
+            ((all_rows, held_rows), (all_bands, held_bands), (own, held_own))
+        )
+    ]
     parts = PAD // PART
-    order = [parts * half + part for part in range(parts) for half in range(2)]
-    wait = in_turn(
+    pieces = [
         [
-            pltpu.make_async_copy(matrix.at[rows_of(i, PART)], held.at[rows_of(i, PART)], done.at[i])
-            for i in order
+            pltpu.make_async_copy(
+                matrix.at[rows_of(parts * half + part, PART)],
+                held.at[rows_of(parts * half + part, PART)],
+                done.at[3 + parts * half + part],
+            )
+            for half in range(2)
         ]
-    )
-    swapped = flags[2] == 1
-    first = jnp.where(swapped, other[...], lowered[...])
-    second = jnp.where(swapped, lowered[...], other[...])
-    packed = (jnp.zeros((CHUNK, LANES), F32),) * 2
+        for part in range(parts)
+    ]
+    for copy in small + sum(pieces, []):
+        copy.start()
+    for copy in small:
+        copy.wait()
+    low, same = flags[0] == 1, flags[4] == 1
+    values = []
+    for index in range(2):
+        band = unpacked(held_bands[rows_of(index, BAND)])
+        values.append(jnp.concatenate([held_rows[rows_of(index, 2 * PAD)], band], axis=1))
+    sign = jnp.where(low, -1.0, 1.0)
+    packed = jnp.zeros((CHUNK, LANES), F32)
     for part in range(parts):
         span = rows_of(part, PART)
-        wait()
-        partner = dot(held[span], first)
-        wait()
-        partner += dot(held[rows_of(parts + part, PART)], second)
-        packed = give_product(flags, part, own[span], partner, factors, packed, outs[:4])
-    outs[4][:EDGE], outs[4][EDGE:] = edge_block(packed[0]), edge_block(packed[1])
+        total = 0.0
+        for half in range(2):
+            pieces[part][half].wait()
+            total += dot(held[rows_of(parts * half + part, PART)], values[half])
+        mine, theirs = held_own[span], total[:, :LANES]
+        rows_near, rows_far = jnp.where(same, mine, theirs), jnp.where(same, theirs, mine)
+        near[span], far[span] = rows_near, rows_far
+        for_neighbour[span] = rows_near.astype(BF16)
+        for_sibling[span] = rows_far.astype(BF16)
+        packed = pack_other(packed, part, sign, total[:, LANES:], factors)
+    mine, theirs = own_packed[...], edge_block(packed)
+    edges[:EDGE] = jnp.where(same, mine, theirs)
+    edges[EDGE:] = jnp.where(same, theirs, mine)
 
 
 def early_kernel(
@@ -418,18 +498,19 @@
             for i in range(2):
                 source = parts[2 * (1 - half) + i]
                 copies.append(pltpu.make_async_copy(source, next_own.at[i], done.at[4 + i]))
-            wait = in_turn(copies)
-            wait()
+            for copy in copies:
+                copy.start()
+            copies[0].wait()
             for part in range(PAD // PART):
                 span = rows_of(part, PART)
                 partner_out[span] = dot(held_partner[span], values)
-            wait()
-            wait()
+            copies[1].wait()
+            copies[2].wait()
             for part in range(PAD // PART):
                 span = rows_of(part, PART)
                 own_out[span] = dot(held_own[0, span], values[:PAD]) + dot(held_own[1, span], values[PAD:])
-            for _ in range(3):
-                wait()
+            for copy in copies[3:]:
+                copy.wait()
 
 
 def late_kernel(flags, other, own, partner, factors, matrix_own, matrix_partner, *outs):
@@ -446,7 +527,13 @@
 
 
 ROWS_F32 = ((PAD, LANES), F32)
-PARTNER_SCRATCH = [pltpu.VMEM((2 * PAD, 2 * PAD), BF16), pltpu.SemaphoreType.DMA((8,))]
+PARTNER_SCRATCH = [
+    pltpu.VMEM((2 * PAD, 2 * PAD), BF16),
+    pltpu.VMEM((4 * PAD, LANES), BF16),
+    pltpu.VMEM((2 * BAND, LANES), BF16),
+    pltpu.VMEM((PAD, LANES), F32),
+    pltpu.SemaphoreType.DMA((11,)),
+]
 HELD = [pltpu.VMEM((2, PAD, PAD), BF16), pltpu.VMEM((PAD, 2 * PAD), BF16)]
 EARLY = [ROWS_F32, ROWS_F32, ((2, PAD, PAD), BF16), ((PAD, 2 * PAD), BF16)]
 EARLY_SCRATCH = HELD + [pltpu.SemaphoreType.DMA((6,))]
@@ -530,9 +617,9 @@
     received, collision = lax.optimization_barrier((received, collision))
     ordered = padded_columns(chosen(place(ROWS, PAD, wanted).T, collision))
 
-    lowered, masks = call(
+    lowered, masks, bands = call(
         first_kernel,
-        [((2 * PAD, LANES), BF16), ((8, LANES), F32)],
+        [((2 * PAD, LANES), BF16), ((8, LANES), F32), ((BAND, LANES), BF16)],
         flags, own, own_edge, received, straight, turned, masks, factors, flops=100 * PAD * 256,
     )
     lowered, ordered = lax.optimization_barrier((lowered, ordered))
@@ -543,20 +630,29 @@
     work = 100 * PAD * LANES
 
     other = to_side(lowered)
-    (own,) = call(
-        collide_kernel, [(rows, F32)], flags, lowered, other, *matrix, flops=multiply
+    bands = to_mirror(bands), to_opposite(bands)
+    own, own_packed, all_rows, all_bands = call(
+        collide_kernel,
+        [(rows, F32), ((EDGE, LANES), BF16), ((4 * PAD, LANES), BF16), ((2 * BAND, LANES), BF16)],
+        flags, lowered, other, *bands, factors, *matrix, flops=2 * multiply,
     )
     partner_matrix, own = lax.optimization_barrier((partner_matrix, own))
     near, far, for_sibling, for_neighbour, edges = call(
-        collide_partner_kernel, sends, flags, own, lowered, other, factors, partner_matrix,
-        flops=multiply, stay=1, scratch=PARTNER_SCRATCH,
-    )
+        collide_partner_kernel, sends, flags, own_packed, factors, all_rows, all_bands, own, partner_matrix,
+        flops=2 * multiply, stay=4, scratch=PARTNER_SCRATCH,
+    )
+
     for step in range(1, STEPS):
-        neighbour, edges = to_neighbour(for_neighbour), to_mirror(edges)
-        sibling = with_sibling(for_sibling)
-        near, far, for_sibling, for_neighbour, edges = call(
-            between_kernel, sends, flags, near, far, sibling, neighbour, edges, masks, factors, flops=work
-        )
+        neighbour, sibling = to_neighbour(for_neighbour), with_sibling(for_sibling)
+        new_near, for_neighbour, packed = call(
+            between_near_kernel, [(rows, F32), (rows, BF16), ((EDGE, LANES), BF16)],
+            flags, near, far, sibling, edges, masks, factors, flops=work,
+        )
+        new_far, for_sibling, edges = call(
+            between_far_kernel, [(rows, F32), (rows, BF16), edges_shape],
+            flags, near, far, neighbour, edges, masks, factors, packed, flops=work,
+        )
+        near, far = new_near, new_far
         neighbour, edges = to_neighbour(for_neighbour), to_mirror(edges)
         sibling = with_sibling(for_sibling)
         (lowered,) = call(

time: 163 us -> 166 us (1.018)
  Pallas kernels: 27.2 us -> 29.6 us
  local copies, waits for them, and re-layouts: 6.63 us -> 4.54 us
    ppermute x2, starting transfers between devices: 4.02 us -> 10.3 us  [to_side(): return lax.ppermute(array, 'vel', [(i, i ^ 1) for i in range(4)])]
    ppermute x2, waiting for transfers between devices: 6.36 us -> 12.1 us  [to_layer(): return lax.ppermute(array, BOTH, pairs_of(target))]
    ppermute x2, waiting for transfers between devices: 8.2 us -> 2.48 us  [to_side(): return lax.ppermute(array, 'vel', [(i, i ^ 1) for i in range(4)])]
    ppermute x3, starting transfers between devices: 22 us -> 18.3 us  [to_neighbour(): return lax.ppermute(array, BOTH, pairs_of(neighbour_of))]
    ppermute x6, starting transfers between devices: 18.5 us -> 15.1 us  [to_mirror(): return lax.ppermute(array, 'vel', [(i, 3 - i) for i in range(4)])]
    pallas_call x11 -> x12, Pallas kernels: 27.2 us -> 29.6 us  [call(): pl.pallas_call(kernel, out_shape=[jax.ShapeDtypeStruct(shape, dtype) for...]
    unnamed x27 -> x21, local copies, waits for them, and re-layouts: 6.19 us -> 4.1 us
    ppermute x0 -> x1, starting transfers between devices: none -> 1.92 us  [to_opposite(): return lax.ppermute(array, 'vel', [(i, i ^ 2) for i in range(4)])]
  transfers between devices with their start and end apart: 14 -> 15, of which waited for: 9 -> 9; matrix products, arithmetic and copies ran while one was open for 7% -> 7% of each run, Pallas kernels for 8% -> 10%
where the time goes in v8:
time: 166 us; the launch traced here: 165 us
  starting transfers between devices  61.8 us (37%)
  waiting for transfers between devices  35.7 us (22%)
  Pallas kernels  29.6 us (18%)
  between operations  13.9 us (8%)
  matrix products  13 us (8%)
  blocking collectives  6.19 us (4%)
  local copies, waits for them, and re-layouts  4.54 us (3%)
    pallas_call x12, Pallas kernels, call(): pl.pallas_call(kernel, out_shape=[jax.ShapeDtypeStruct(shape, dtype) for...  29.6 us
    ppermute x6, waiting for transfers between devices, to_mirror(): return lax.ppermute(array, 'vel', [(i, 3 - i) for i in range(4)])  18.4 us
    ppermute x3, starting transfers between devices, to_neighbour(): return lax.ppermute(array, BOTH, pairs_of(neighbour_of))  18.3 us
    ppermute x2, starting transfers between devices, to_layer(): return lax.ppermute(array, BOTH, pairs_of(target))  16.2 us
    ppermute x6, starting transfers between devices, to_mirror(): return lax.ppermute(array, 'vel', [(i, 3 - i) for i in range(4)])  15.1 us
    dot_general x8, matrix products, chosen(): return jnp.dot(left, right, preferred_element_type=BF16)  13 us
    ppermute x2, waiting for transfers between devices, to_layer(): return lax.ppermute(array, BOTH, pairs_of(target))  12.1 us
    ppermute x2, starting transfers between devices, to_side(): return lax.ppermute(array, 'vel', [(i, i ^ 1) for i in range(4)])  10.3 us
  transfers between devices with their start and end apart: 15, of which 9 were waited for; matrix products, arithmetic and copies ran while one was open for 7% of the time, Pallas kernels for 10%

profile of v8, /device:TPU:8, one launch (start us, length us, event | category | flops | bytes accessed | tf_op | source)
XLA Modules:
  0.0 164.9 jit_solution(10404912360882590086)
XLA Ops:
  9.4 3.5 %collective-permute-start.6 = (bf16[88,1408]{1,0:T(8,128)(2,1)S(1)}, bf16[88,1408]{1,0:T(8,128)(2,1)S(1)}, u32[]{:S(2)}, u32[]{:S(2)}) collective-permute-start(bf16[88,1408]{1,0:T(8,128)(2,1)S(1)} %pad_maximum_fusion), channel_id=1, source_target_pairs={{0,3},{1,2},{2,1},{3,0},{4,7},{5,6},{6,5},{7,4},{8,11},{9,10},{10,... | collective-permute-start | bytes 743432 | tf_op jit(solution)/shard_map/ppermute | solution.py:60
  13.2 2.0 %shard_map.37 = (f32[704,128]{1,0:T(8,128)S(1)}, f32[88,128]{1,0:T(8,128)S(1)}, bf16[800,128]{1,0:T(8,128)(2,1)S(1)}, bf16[720,128]{1,0:T(8,128)(2,1)S(1)}, bf16...) custom-call(s32[6]{0:T(128)S(1)} %stack.31.flags, f32[704,256]{1,0:T(8,128)S(1)} %pad.13.populations, ...), custom_call_target="tpu_custom_call" | custom-call | flops 761266176 | bytes 2786304 | tf_op jit(solution)/shard_map/pallas_call | solution.py:78
  15.2 11.3 %collective-permute-done.6 = bf16[88,1408]{1,0:T(8,128)(2,1)S(1)} collective-permute-done((bf16[88,1408]{1,0:T(8,128)(2,1)S(1)}, bf16[88,1408]{1,0:T(8,128)(2,1)S(1)}, u32[]{:S(2)}, u32[]{:S(2)}) %collective-permute-start.6) | collective-permute-done | bytes 247840 | tf_op jit(solution)/shard_map/ppermute | solution.py:60
  27.3 1.9 %collective-permute-start = (bf16[800,128]{1,0:T(8,128)(2,1)S(1)}, bf16[800,128]{1,0:T(8,128)(2,1)S(1)}, u32[]{:S(2)}, u32[]{:S(2)}) collective-permute-start(bf16[800,128]{1,0:T(8,128)(2,1)S(1)} %get-tuple-element.51), channel_id=1, source_target_pairs={{0,3},{1,2},{2,1},{3,0},{4,7},{5,6},{6,5},{7,4},{8,11},{9,10},{10,... | collective-permute-start | bytes 614408 | tf_op jit(solution)/shard_map/ppermute | solution.py:60
  29.2 14.3 %collective-permute-start.1 = (bf16[720,128]{1,0:T(8,128)(2,1)S(1)}, bf16[720,128]{1,0:T(8,128)(2,1)S(1)}, u32[]{:S(2)}, u32[]{:S(2)}) collective-permute-start(bf16[720,128]{1,0:T(8,128)(2,1)S(1)} %get-tuple-element.53), channel_id=1, source_target_pairs={{0,508},{1,509},{2,6},{3,7},{4,0},{5,1},{6,10},{7,11},{8,4},{9,5},... | collective-permute-start | bytes 552968 | tf_op jit(solution)/shard_map/ppermute | solution.py:47
  43.5 1.9 %collective-permute-start.2 = (bf16[720,128]{1,0:T(8,128)(2,1)S(1)}, bf16[720,128]{1,0:T(8,128)(2,1)S(1)}, u32[]{:S(2)}, u32[]{:S(2)}) collective-permute-start(bf16[720,128]{1,0:T(8,128)(2,1)S(1)} %get-tuple-element.54), channel_id=1, source_target_pairs={{0,511},{1,510},{2,5},{3,4},{4,3},{5,2},{6,9},{7,8},{8,7},{9,6},{1... | collective-permute-start | bytes 552968 | tf_op jit(solution)/shard_map/ppermute | solution.py:47
  46.6 11.0 %collective-permute-done.2.turned = bf16[720,128]{1,0:T(8,128)(2,1)S(1)} collective-permute-done((bf16[720,128]{1,0:T(8,128)(2,1)S(1)}, bf16[720,128]{1,0:T(8,128)(2,1)S(1)}, u32[]{:S(2)}, u32[]{:S(2)}) %collective-permute-start.2) | collective-permute-done | bytes 184352 | tf_op jit(solution)/shard_map/ppermute | solution.py:47
  57.6 2.6 %shard_map.38 = (bf16[1408,128]{1,0:T(8,128)(2,1)S(1)}, f32[8,128]{1,0:T(8,128)S(1)}, bf16[352,128]{1,0:T(8,128)(2,1)S(1)}) custom-call(s32[6]{0:T(128)S(1)} %stack.31.flags, f32[704,128]{1,0:T(8,128)S(1)} %get-tuple-element.49.own, f32[88,128]{1,0:T(8,128)S(1)} %get-tuple-element.50.own_edge, bf16[800,128]{1,0:T(8,128)(2,1)S(1)} %collective-permute-done.received, ...), custom_call_target="tpu_custom_call" | custom-call | flops 18022400 | bytes 2519040 | tf_op jit(solution)/shard_map/pallas_call | solution.py:78
  60.2 1.9 %collective-permute-start.5 = (bf16[352,128]{1,0:T(8,128)(2,1)S(1)}, bf16[352,128]{1,0:T(8,128)(2,1)S(1)}, u32[]{:S(2)}, u32[]{:S(2)}) collective-permute-start(bf16[352,128]{1,0:T(8,128)(2,1)S(1)} %get-tuple-element.60), channel_id=1, source_target_pairs={{0,2},{1,3},{2,0},{3,1},{4,6},{5,7},{6,4},{7,5},{8,10},{9,11},{10,... | collective-permute-start | bytes 270344 | tf_op jit(solution)/shard_map/ppermute | solution.py:64
  62.1 1.9 %collective-permute-start.4 = (bf16[352,128]{1,0:T(8,128)(2,1)S(1)}, bf16[352,128]{1,0:T(8,128)(2,1)S(1)}, u32[]{:S(2)}, u32[]{:S(2)}) collective-permute-start(bf16[352,128]{1,0:T(8,128)(2,1)S(1)} %get-tuple-element.60), channel_id=1, source_target_pairs={{0,3},{1,2},{2,1},{3,0},{4,7},{5,6},{6,5},{7,4},{8,11},{9,10},{10,... | collective-permute-start | bytes 270344 | tf_op jit(solution)/shard_map/ppermute | solution.py:60
  64.0 5.5 %fusion.6 = bf16[704,2744]{1,0:T(8,128)(2,1)S(1)} fusion(bf16[686,2744]{1,0:T(8,128)(2,1)} %param.5, s32[704]{0:T(1024)S(1)} %select_select_fusion), kind=kOutput, calls=%fused_computation.13 | convolution fusion | flops 2650879488 | bytes 7631136 | tf_op jit(solution)/shard_map/dot_general | solution.py:556
  69.8 6.4 %collective-permute-start.3 = (bf16[1408,128]{1,0:T(8,128)(2,1)S(1)}, bf16[1408,128]{1,0:T(8,128)(2,1)S(1)}, u32[]{:S(2)}, u32[]{:S(2)}) collective-permute-start(bf16[1408,128]{1,0:T(8,128)(2,1)S(1)} %get-tuple-element.59.lowered), channel_id=1, source_target_pairs={{0,1},{1,0},{2,3},{3,2},{4,5},{5,4},{6,7},{7,6},{8,9},{9,8},{10,11... | collective-permute-start | bytes 1081352 | tf_op jit(solution)/shard_map/ppermute | solution.py:68
  81.4 2.1 %shard_map.39 = (f32[704,128]{1,0:T(8,128)S(1)}, bf16[96,128]{1,0:T(8,128)(2,1)S(1)}, bf16[2816,128]{1,0:T(8,128)(2,1)S(1)}, bf16[704,128]{1,0:T(8,128)(2,1)S(1)}) custom-call(s32[6]{0:T(128)S(1)} %stack.31.flags, bf16[1408,128]{1,0:T(8,128)(2,1)S(1)} %get-tuple-element.59.lowered, bf16[1408,128]{1,0:T(8,128)(2,1)S(1)} %collective-permute-done.3.other, ...), custom_call_target="tpu_custom_call" | custom-call | flops 1015021568 | bytes 7233536 | tf_op jit(solution)/shard_map/pallas_call | solution.py:78
  86.9 5.5 %shard_map.40 = (f32[704,128]{1,0:T(8,128)S(1)}, f32[704,128]{1,0:T(8,128)S(1)}, bf16[704,128]{1,0:T(8,128)(2,1)S(1)}, bf16[704,128]{1,0:T(8,128)(2,1)S(1)}, bf16[192,128]{1,0:T(8,128)(2,1)S(1)}) custom-call(s32[6]{0:T(128)S(1)} %stack.31.flags, bf16[96,128]{1,0:T(8,128)(2,1)S(1)} %get-tuple-element.62.own_packed, ...), custom_call_target="tpu_custom_call" | custom-call | flops 1015021568 | bytes 7462912 | tf_op jit(solution)/shard_map/pallas_call | solution.py:78
  92.4 2.3 %collective-permute-start.7 = (bf16[704,128]{1,0:T(8,128)(2,1)S(1)}, bf16[704,128]{1,0:T(8,128)(2,1)S(1)}, u32[]{:S(2)}, u32[]{:S(2)}) collective-permute-start(bf16[704,128]{1,0:T(8,128)(2,1)S(1)} %get-tuple-element.76), channel_id=1, source_target_pairs={{0,511},{1,510},{2,509},{3,508},{4,8},{5,9},{6,10},{7,11},{8,4},{9... | collective-permute-start | bytes 540680 | tf_op jit(solution)/shard_map/ppermute | solution.py:56
  94.7 2.1 %all_gather.13.sibling = bf16[1408,128]{1,0:T(8,128)(2,1)S(1)} all-gather(bf16[704,128]{1,0:T(8,128)(2,1)S(1)} %get-tuple-element.72), channel_id=1, replica_groups={{0,4},{8,12},{16,20},{24,28},{32,36},{40,44},{48,52},{56,60},{64,68},{7..., dimensions={0}, use_global_device_ids=true | all-gather | bytes 540672 | tf_op jit(solution)/shard_map/all_gather | solution.py:40
  98.4 10.5 %collective-permute-start.8 = (bf16[704,128]{1,0:T(8,128)(2,1)S(1)}, bf16[704,128]{1,0:T(8,128)(2,1)S(1)}, u32[]{:S(2)}, u32[]{:S(2)}) collective-permute-start(bf16[704,128]{1,0:T(8,128)(2,1)S(1)} %get-tuple-element.80), channel_id=1, source_target_pairs={{0,511},{1,510},{2,509},{3,508},{4,8},{5,9},{6,10},{7,11},{8,4},{9... | collective-permute-start | bytes 540680 | tf_op jit(solution)/shard_map/ppermute | solution.py:56
  112.5 2.1 %all_gather.14.sibling = bf16[1408,128]{1,0:T(8,128)(2,1)S(1)} all-gather(bf16[704,128]{1,0:T(8,128)(2,1)S(1)} %get-tuple-element.79), channel_id=1, replica_groups={{0,4},{8,12},{16,20},{24,28},{32,36},{40,44},{48,52},{56,60},{64,68},{7..., dimensions={0}, use_global_device_ids=true | all-gather | bytes 540672 | tf_op jit(solution)/shard_map/all_gather | solution.py:40
  114.6 2.0 %collective-permute-done.9.edges = bf16[192,128]{1,0:T(8,128)(2,1)S(1)} collective-permute-done((bf16[192,128]{1,0:T(8,128)(2,1)S(1)}, bf16[192,128]{1,0:T(8,128)(2,1)S(1)}, u32[]{:S(2)}, u32[]{:S(2)}) %collective-permute-start.9) | collective-permute-done | bytes 49184 | tf_op jit(solution)/shard_map/ppermute | solution.py:60
  116.5 2.2 %shard_map.43.lowered = bf16[1408,128]{1,0:T(8,128)(2,1)S(1)} custom-call(s32[6]{0:T(128)S(1)} %stack.31.flags, f32[704,128]{1,0:T(8,128)S(1)} %get-tuple-element.75.near, f32[704,128]{1,0:T(8,128)S(1)} %get-tuple-element.78.far, bf16[1408,128]{1,0:T(8,128)(2,1)S(1)} %all_gather.14.sibling, bf16[704,128]{1,0:T(8,128)(2,1)S(1)} %collective-permute-done.8.neighbour, ...), custom_call_target="tpu_custom_call" | custom-call | flops 9011200 | bytes 2756608 | tf_op jit(solution)/shard_map/pallas_call | solution.py:78
  118.7 3.9 %collective-permute-start.10 = (bf16[1408,128]{1,0:T(8,128)(2,1)S(1)}, bf16[1408,128]{1,0:T(8,128)(2,1)S(1)}, u32[]{:S(2)}, u32[]{:S(2)}) collective-permute-start(bf16[1408,128]{1,0:T(8,128)(2,1)S(1)} %shard_map.43.lowered), channel_id=1, source_target_pairs={{0,1},{1,0},{2,3},{3,2},{4,5},{5,4},{6,7},{7,6},{8,9},{9,8},{10,11... | collective-permute-start | bytes 1081352 | tf_op jit(solution)/shard_map/ppermute | solution.py:68
  122.7 4.2 %shard_map.44 = (f32[704,128]{1,0:T(8,128)S(1)}, f32[704,128]{1,0:T(8,128)S(1)}, bf16[2,704,704]{2,1,0:T(8,128)(2,1)S(1)}, bf16[704,1408]{1,0:T(8,128)(2,1)S(1)}) custom-call(s32[6]{0:T(128)S(1)} %stack.31.flags, bf16[1408,128]{1,0:T(8,128)(2,1)S(1)} %shard_map.43.lowered, bf16[704,704]{1,0:T(8,128)(2,1)} %copy-done.3, bf16[704,704]{1,0:T(8,128)(2,1)} %copy-done.1, ...), custom_call_target="tpu_custom_call" | custom-call | flops 507510784 | bytes 12976128 | tf_op jit(solution)/shard_map/pallas_call | solution.py:78
  126.9 2.2 %collective-permute-done.10.other = bf16[1408,128]{1,0:T(8,128)(2,1)S(1)} collective-permute-done((bf16[1408,128]{1,0:T(8,128)(2,1)S(1)}, bf16[1408,128]{1,0:T(8,128)(2,1)S(1)}, u32[]{:S(2)}, u32[]{:S(2)}) %collective-permute-start.10) | collective-permute-done | bytes 360480 | tf_op jit(solution)/shard_map/ppermute | solution.py:68
  129.1 2.0 %shard_map.45 = (f32[704,128]{1,0:T(8,128)S(1)}, f32[704,128]{1,0:T(8,128)S(1)}, bf16[704,128]{1,0:T(8,128)(2,1)S(1)}, bf16[704,128]{1,0:T(8,128)(2,1)S(1)}, bf16[192,128]{1,0:T(8,128)(2,1)S(1)}) custom-call(s32[6]{0:T(128)S(1)} %stack.31.flags, bf16[1408,128]{1,0:T(8,128)(2,1)S(1)} %collective-permute-done.10.other, f32[704,128]{1,0:T(8,128)S(1)} %get-tuple-element.82.own, ...), custom_call_target="tpu_custom_call" | custom-call | flops 507510784 | bytes 7258112 | tf_op jit(solution)/shard_map/pallas_call | solution.py:78
  131.1 5.5 %collective-permute-start.11 = (bf16[704,128]{1,0:T(8,128)(2,1)S(1)}, bf16[704,128]{1,0:T(8,128)(2,1)S(1)}, u32[]{:S(2)}, u32[]{:S(2)}) collective-permute-start(bf16[704,128]{1,0:T(8,128)(2,1)S(1)} %get-tuple-element.89), channel_id=1, source_target_pairs={{0,511},{1,510},{2,509},{3,508},{4,8},{5,9},{6,10},{7,11},{8,4},{9... | collective-permute-start | bytes 540680 | tf_op jit(solution)/shard_map/ppermute | solution.py:56
  138.5 2.1 %all_gather.15.sibling = bf16[1408,128]{1,0:T(8,128)(2,1)S(1)} all-gather(bf16[704,128]{1,0:T(8,128)(2,1)S(1)} %get-tuple-element.88), channel_id=1, replica_groups={{0,4},{8,12},{16,20},{24,28},{32,36},{40,44},{48,52},{56,60},{64,68},{7..., dimensions={0}, use_global_device_ids=true | all-gather | bytes 540672 | tf_op jit(solution)/shard_map/all_gather | solution.py:40
  140.6 2.0 %collective-permute-done.12.edges = bf16[192,128]{1,0:T(8,128)(2,1)S(1)} collective-permute-done((bf16[192,128]{1,0:T(8,128)(2,1)S(1)}, bf16[192,128]{1,0:T(8,128)(2,1)S(1)}, u32[]{:S(2)}, u32[]{:S(2)}) %collective-permute-start.12) | collective-permute-done | bytes 49184 | tf_op jit(solution)/shard_map/ppermute | solution.py:60
  142.5 2.7 %collective-permute-done.11.neighbour = bf16[704,128]{1,0:T(8,128)(2,1)S(1)} collective-permute-done((bf16[704,128]{1,0:T(8,128)(2,1)S(1)}, bf16[704,128]{1,0:T(8,128)(2,1)S(1)}, u32[]{:S(2)}, u32[]{:S(2)}) %collective-permute-start.11) | collective-permute-done | bytes 180256 | tf_op jit(solution)/shard_map/ppermute | solution.py:56
  146.6 3.9 %collective-permute-start.13 = (bf16[704,128]{1,0:T(8,128)(2,1)S(1)}, bf16[704,128]{1,0:T(8,128)(2,1)S(1)}, u32[]{:S(2)}, u32[]{:S(2)}) collective-permute-start(bf16[704,128]{1,0:T(8,128)(2,1)S(1)} %shard_map.47), channel_id=1, source_target_pairs={{0,3},{1,2},{2,1},{3,0},{4,7},{5,6},{6,5},{7,4},{8,11},{9,10},{10,... | collective-permute-start | bytes 540680 | tf_op jit(solution)/shard_map/ppermute | solution.py:60
  150.6 2.3 %shard_map.46.kept = f32[704,128]{1,0:T(8,128)S(1)} custom-call(s32[6]{0:T(128)S(1)} %stack.31.flags, f32[704,128]{1,0:T(8,128)S(1)} %get-tuple-element.86.near, f32[704,128]{1,0:T(8,128)S(1)} %get-tuple-element.87.far, bf16[1408,128]{1,0:T(8,128)(2,1)S(1)} %all_gather.15.sibling, bf16[704,128]{1,0:T(8,128)(2,1)S(1)} %collective-permute-done.11.neighbour, ...), custom_call_target="tpu_custom_call" | custom-call | flops 507510784 | bytes 2756608 | tf_op jit(solution)/shard_map/pallas_call | solution.py:78
  152.8 3.1 %collective-permute-done.13.received = bf16[704,128]{1,0:T(8,128)(2,1)S(1)} collective-permute-done((bf16[704,128]{1,0:T(8,128)(2,1)S(1)}, bf16[704,128]{1,0:T(8,128)(2,1)S(1)}, u32[]{:S(2)}, u32[]{:S(2)}) %collective-permute-start.13) | collective-permute-done | bytes 180256 | tf_op jit(solution)/shard_map/ppermute | solution.py:60
  156.0 2.1 %shard_map.48 = f32[686,1,256]{2,1,0:T(1,128)} custom-call(s32[6]{0:T(128)S(1)} %stack.31.flags, f32[704,128]{1,0:T(8,128)S(1)} %shard_map.46.kept, bf16[704,128]{1,0:T(8,128)(2,1)S(1)} %collective-permute-done.13.received), custom_call_target="tpu_custom_call" | custom-call | flops 126877696 | bytes 1243136 | tf_op jit(solution)/shard_map/pallas_call | solution.py:78
  (55 shorter events, 22.2 us)
Async XLA Ops:
  6.5 6.5 %copy-start.8 = (f32[686,1,256]{2,1,0:T(1,128)S(1)}, f32[686,1,256]{2,1,0:T(1,128)}, u32[]{:S(2)}) copy-start(f32[686,1,256]{2,1,0:T(1,128)} %param.3) | copy-start | bytes 2107396
  6.5 80.4 %all-gather.2.cloned.1.call-start = ((), (), s32[]{:S(2)}) async-start(), calls=%async_computation | async-start | bytes 4212736 | tf_op jit(solution)/shard_map/all_gather | solution.py:611
  8.7 4.5 %copy-start.7 = (s32[1,256]{1,0:T(1,128)S(1)}, s32[1,256]{1,0:T(1,128)}, u32[]{:S(2)}) copy-start(s32[1,256]{1,0:T(1,128)} %solid.1) | copy-start | bytes 3076
  9.4 17.1 %collective-permute-start.6 = (bf16[88,1408]{1,0:T(8,128)(2,1)S(1)}, bf16[88,1408]{1,0:T(8,128)(2,1)S(1)}, u32[]{:S(2)}, u32[]{:S(2)}) collective-permute-start(bf16[88,1408]{1,0:T(8,128)(2,1)S(1)} %pad_maximum_fusion), channel_id=1, source_target_pairs={{0,3},{1,2},{2,1},{3,0},{4,7},{5,6},{6,5},{7,4},{8,11},{9,10},{10,... | collective-permute-start | bytes 743432 | tf_op jit(solution)/shard_map/ppermute | solution.py:60
  26.6 0.7 copy-start.9
  27.3 18.2 %collective-permute-start = (bf16[800,128]{1,0:T(8,128)(2,1)S(1)}, bf16[800,128]{1,0:T(8,128)(2,1)S(1)}, u32[]{:S(2)}, u32[]{:S(2)}) collective-permute-start(bf16[800,128]{1,0:T(8,128)(2,1)S(1)} %get-tuple-element.51), channel_id=1, source_target_pairs={{0,3},{1,2},{2,1},{3,0},{4,7},{5,6},{6,5},{7,4},{8,11},{9,10},{10,... | collective-permute-start | bytes 614408 | tf_op jit(solution)/shard_map/ppermute | solution.py:60
  29.2 17.4 %collective-permute-start.1 = (bf16[720,128]{1,0:T(8,128)(2,1)S(1)}, bf16[720,128]{1,0:T(8,128)(2,1)S(1)}, u32[]{:S(2)}, u32[]{:S(2)}) collective-permute-start(bf16[720,128]{1,0:T(8,128)(2,1)S(1)} %get-tuple-element.53), channel_id=1, source_target_pairs={{0,508},{1,509},{2,6},{3,7},{4,0},{5,1},{6,10},{7,11},{8,4},{9,5},... | collective-permute-start | bytes 552968 | tf_op jit(solution)/shard_map/ppermute | solution.py:47
  43.5 14.1 %collective-permute-start.2 = (bf16[720,128]{1,0:T(8,128)(2,1)S(1)}, bf16[720,128]{1,0:T(8,128)(2,1)S(1)}, u32[]{:S(2)}, u32[]{:S(2)}) collective-permute-start(bf16[720,128]{1,0:T(8,128)(2,1)S(1)} %get-tuple-element.54), channel_id=1, source_target_pairs={{0,511},{1,510},{2,5},{3,4},{4,3},{5,2},{6,9},{7,8},{8,7},{9,6},{1... | collective-permute-start | bytes 552968 | tf_op jit(solution)/shard_map/ppermute | solution.py:47
  60.2 20.9 %collective-permute-start.5 = (bf16[352,128]{1,0:T(8,128)(2,1)S(1)}, bf16[352,128]{1,0:T(8,128)(2,1)S(1)}, u32[]{:S(2)}, u32[]{:S(2)}) collective-permute-start(bf16[352,128]{1,0:T(8,128)(2,1)S(1)} %get-tuple-element.60), channel_id=1, source_target_pairs={{0,2},{1,3},{2,0},{3,1},{4,6},{5,7},{6,4},{7,5},{8,10},{9,11},{10,... | collective-permute-start | bytes 270344 | tf_op jit(solution)/shard_map/ppermute | solution.py:64
  62.1 19.0 %collective-permute-start.4 = (bf16[352,128]{1,0:T(8,128)(2,1)S(1)}, bf16[352,128]{1,0:T(8,128)(2,1)S(1)}, u32[]{:S(2)}, u32[]{:S(2)}) collective-permute-start(bf16[352,128]{1,0:T(8,128)(2,1)S(1)} %get-tuple-element.60), channel_id=1, source_target_pairs={{0,3},{1,2},{2,1},{3,0},{4,7},{5,6},{6,5},{7,4},{8,11},{9,10},{10,... | collective-permute-start | bytes 270344 | tf_op jit(solution)/shard_map/ppermute | solution.py:60
  69.8 11.6 %collective-permute-start.3 = (bf16[1408,128]{1,0:T(8,128)(2,1)S(1)}, bf16[1408,128]{1,0:T(8,128)(2,1)S(1)}, u32[]{:S(2)}, u32[]{:S(2)}) collective-permute-start(bf16[1408,128]{1,0:T(8,128)(2,1)S(1)} %get-tuple-element.59.lowered), channel_id=1, source_target_pairs={{0,1},{1,0},{2,3},{3,2},{4,5},{5,4},{6,7},{7,6},{8,9},{9,8},{10,11... | collective-permute-start | bytes 1081352 | tf_op jit(solution)/shard_map/ppermute | solution.py:68
  77.6 3.9 %copy-start = (bf16[704,704]{1,0:T(8,128)(2,1)}, bf16[704,704]{1,0:T(8,128)(2,1)S(1)}, u32[]{:S(2)}) copy-start(bf16[704,704]{1,0:T(8,128)(2,1)S(1)} %fusion.1.m3) | copy-start | bytes 2973700
  78.9 2.5 %copy-start.1 = (bf16[704,704]{1,0:T(8,128)(2,1)}, bf16[704,704]{1,0:T(8,128)(2,1)S(1)}, u32[]{:S(2)}) copy-start(bf16[704,704]{1,0:T(8,128)(2,1)S(1)} %fusion.m1) | copy-start | bytes 2973700
  80.0 1.4 copy-start.2
  83.5 1.0 copy-start.3
  84.5 1.0 copy-start.4
  85.5 0.7 copy-start.5
  86.2 0.7 copy-start.6
  92.4 16.5 %collective-permute-start.7 = (bf16[704,128]{1,0:T(8,128)(2,1)S(1)}, bf16[704,128]{1,0:T(8,128)(2,1)S(1)}, u32[]{:S(2)}, u32[]{:S(2)}) collective-permute-start(bf16[704,128]{1,0:T(8,128)(2,1)S(1)} %get-tuple-element.76), channel_id=1, source_target_pairs={{0,511},{1,510},{2,509},{3,508},{4,8},{5,9},{6,10},{7,11},{8,4},{9... | collective-permute-start | bytes 540680 | tf_op jit(solution)/shard_map/ppermute | solution.py:56
  98.4 16.2 %collective-permute-start.8 = (bf16[704,128]{1,0:T(8,128)(2,1)S(1)}, bf16[704,128]{1,0:T(8,128)(2,1)S(1)}, u32[]{:S(2)}, u32[]{:S(2)}) collective-permute-start(bf16[704,128]{1,0:T(8,128)(2,1)S(1)} %get-tuple-element.80), channel_id=1, source_target_pairs={{0,511},{1,510},{2,509},{3,508},{4,8},{5,9},{6,10},{7,11},{8,4},{9... | collective-permute-start | bytes 540680 | tf_op jit(solution)/shard_map/ppermute | solution.py:56
  110.6 6.0 %collective-permute-start.9 = (bf16[192,128]{1,0:T(8,128)(2,1)S(1)}, bf16[192,128]{1,0:T(8,128)(2,1)S(1)}, u32[]{:S(2)}, u32[]{:S(2)}) collective-permute-start(bf16[192,128]{1,0:T(8,128)(2,1)S(1)} %get-tuple-element.81), channel_id=1, source_target_pairs={{0,3},{1,2},{2,1},{3,0},{4,7},{5,6},{6,5},{7,4},{8,11},{9,10},{10,... | collective-permute-start | bytes 147464 | tf_op jit(solution)/shard_map/ppermute | solution.py:60
  118.7 10.4 %collective-permute-start.10 = (bf16[1408,128]{1,0:T(8,128)(2,1)S(1)}, bf16[1408,128]{1,0:T(8,128)(2,1)S(1)}, u32[]{:S(2)}, u32[]{:S(2)}) collective-permute-start(bf16[1408,128]{1,0:T(8,128)(2,1)S(1)} %shard_map.43.lowered), channel_id=1, source_target_pairs={{0,1},{1,0},{2,3},{3,2},{4,5},{5,4},{6,7},{7,6},{8,9},{9,8},{10,11... | collective-permute-start | bytes 1081352 | tf_op jit(solution)/shard_map/ppermute | solution.py:68
  131.1 14.1 %collective-permute-start.11 = (bf16[704,128]{1,0:T(8,128)(2,1)S(1)}, bf16[704,128]{1,0:T(8,128)(2,1)S(1)}, u32[]{:S(2)}, u32[]{:S(2)}) collective-permute-start(bf16[704,128]{1,0:T(8,128)(2,1)S(1)} %get-tuple-element.89), channel_id=1, source_target_pairs={{0,511},{1,510},{2,509},{3,508},{4,8},{5,9},{6,10},{7,11},{8,4},{9... | collective-permute-start | bytes 540680 | tf_op jit(solution)/shard_map/ppermute | solution.py:56
  136.6 6.0 %collective-permute-start.12 = (bf16[192,128]{1,0:T(8,128)(2,1)S(1)}, bf16[192,128]{1,0:T(8,128)(2,1)S(1)}, u32[]{:S(2)}, u32[]{:S(2)}) collective-permute-start(bf16[192,128]{1,0:T(8,128)(2,1)S(1)} %get-tuple-element.90), channel_id=1, source_target_pairs={{0,3},{1,2},{2,1},{3,0},{4,7},{5,6},{6,5},{7,4},{8,11},{9,10},{10,... | collective-permute-start | bytes 147464 | tf_op jit(solution)/shard_map/ppermute | solution.py:60
  146.6 9.3 %collective-permute-start.13 = (bf16[704,128]{1,0:T(8,128)(2,1)S(1)}, bf16[704,128]{1,0:T(8,128)(2,1)S(1)}, u32[]{:S(2)}, u32[]{:S(2)}) collective-permute-start(bf16[704,128]{1,0:T(8,128)(2,1)S(1)} %shard_map.47), channel_id=1, source_target_pairs={{0,3},{1,2},{2,1},{3,0},{4,7},{5,6},{6,5},{7,4},{8,11},{9,10},{10,... | collective-permute-start | bytes 540680 | tf_op jit(solution)/shard_map/ppermute | solution.py:60
Sparse Core Ops, SparseCore 0:
  27.4 44.8 all-gather.1

commit v9 on v8

--- a/solution.py
+++ b/solution.py
@@ -68,7 +68,7 @@
     return lax.ppermute(array, "vel", [(i, i ^ 1) for i in range(4)])
 
 
-def call(kernel, outs, flags, *arrays, flops=0, stay=0, scratch=()):
+def call(kernel, outs, flags, *arrays, flops=0, stay=0, scratch=(), leave=False):
     moved = sum(x.size * x.dtype.itemsize for x in arrays)
     moved += sum(math.prod(shape) * jnp.dtype(dtype).itemsize for shape, dtype in outs)
     vmem, hbm = (pl.BlockSpec(memory_space=space) for space in (pltpu.VMEM, pltpu.HBM))
@@ -77,7 +77,7 @@
     arrays = *arrays[:count], *(pltpu.with_memory_space_constraint(x, pltpu.HBM) for x in arrays[count:])
     return pl.pallas_call(
         kernel,
-        out_shape=[jax.ShapeDtypeStruct(shape, dtype) for shape, dtype in outs],
+        out_shape=[(pltpu.HBM if leave else jax.ShapeDtypeStruct)(shape, dtype) for shape, dtype in outs],
         in_specs=[pl.BlockSpec(memory_space=pltpu.SMEM)] + specs,
         out_specs=[vmem] * len(outs),
         scratch_shapes=scratch,
@@ -425,14 +425,14 @@
 
 
 def collide_partner_kernel(
-    flags, own_packed, factors, all_rows, all_bands, own, matrix,
+    flags, factors, own_packed, all_rows, all_bands, own, matrix,
     near, far, for_sibling, for_neighbour, edges,
-    held, held_rows, held_bands, held_own, done,
+    held, held_rows, held_bands, held_own, held_packed, done,
 ):
     small = [
         pltpu.make_async_copy(source, target, done.at[index])
         for index, (source, target) in enumerate(
-            ((all_rows, held_rows), (all_bands, held_bands), (own, held_own))
+            ((all_rows, held_rows), (all_bands, held_bands), (own, held_own), (own_packed, held_packed))
         )
     ]
     parts = PAD // PART
@@ -441,7 +441,7 @@
             pltpu.make_async_copy(
                 matrix.at[rows_of(parts * half + part, PART)],
                 held.at[rows_of(parts * half + part, PART)],
-                done.at[3 + parts * half + part],
+                done.at[4 + parts * half + part],
             )
             for half in range(2)
         ]
@@ -470,7 +470,7 @@
         for_neighbour[span] = rows_near.astype(BF16)
         for_sibling[span] = rows_far.astype(BF16)
         packed = pack_other(packed, part, sign, total[:, LANES:], factors)
-    mine, theirs = own_packed[...], edge_block(packed)
+    mine, theirs = held_packed[...], edge_block(packed)
     edges[:EDGE] = jnp.where(same, mine, theirs)
     edges[EDGE:] = jnp.where(same, theirs, mine)
 
@@ -532,7 +532,8 @@
     pltpu.VMEM((4 * PAD, LANES), BF16),
     pltpu.VMEM((2 * BAND, LANES), BF16),
     pltpu.VMEM((PAD, LANES), F32),
-    pltpu.SemaphoreType.DMA((11,)),
+    pltpu.VMEM((EDGE, LANES), BF16),
+    pltpu.SemaphoreType.DMA((12,)),
 ]
 HELD = [pltpu.VMEM((2, PAD, PAD), BF16), pltpu.VMEM((PAD, 2 * PAD), BF16)]
 EARLY = [ROWS_F32, ROWS_F32, ((2, PAD, PAD), BF16), ((PAD, 2 * PAD), BF16)]
@@ -617,13 +618,13 @@
     received, collision = lax.optimization_barrier((received, collision))
     ordered = padded_columns(chosen(place(ROWS, PAD, wanted).T, collision))
 
+    matrix = *column_half(ordered, 0), *column_half(ordered, 1)
+    turned, *matrix = lax.optimization_barrier((turned, *matrix))
     lowered, masks, bands = call(
         first_kernel,
         [((2 * PAD, LANES), BF16), ((8, LANES), F32), ((BAND, LANES), BF16)],
         flags, own, own_edge, received, straight, turned, masks, factors, flops=100 * PAD * 256,
     )
-    lowered, ordered = lax.optimization_barrier((lowered, ordered))
-    matrix = *column_half(ordered, 0), *column_half(ordered, 1)
     edges_shape = ((2 * EDGE, LANES), BF16)
     sends = [(rows, F32)] * 2 + [(rows, BF16)] * 2 + [edges_shape]
     multiply = 2 * PAD * 4 * PAD * LANES
@@ -634,12 +635,12 @@
     own, own_packed, all_rows, all_bands = call(
         collide_kernel,
         [(rows, F32), ((EDGE, LANES), BF16), ((4 * PAD, LANES), BF16), ((2 * BAND, LANES), BF16)],
-        flags, lowered, other, *bands, factors, *matrix, flops=2 * multiply,
+        flags, lowered, other, *bands, factors, *matrix, flops=2 * multiply, leave=True,
     )
     partner_matrix, own = lax.optimization_barrier((partner_matrix, own))
     near, far, for_sibling, for_neighbour, edges = call(
-        collide_partner_kernel, sends, flags, own_packed, factors, all_rows, all_bands, own, partner_matrix,
-        flops=2 * multiply, stay=4, scratch=PARTNER_SCRATCH,
+        collide_partner_kernel, sends, flags, factors, own_packed, all_rows, all_bands, own, partner_matrix,
+        flops=2 * multiply, stay=5, scratch=PARTNER_SCRATCH,
     )
 
     for step in range(1, STEPS):

time: 166 us -> 161 us (0.970)
  waiting for transfers between devices: 35.7 us -> 27 us
  starting transfers between devices: 61.8 us -> 67.3 us
  local copies, waits for them, and re-layouts: 4.54 us -> 1.63 us
    ppermute x2, waiting for transfers between devices: 12.1 us -> 1.79 us  [to_layer(): return lax.ppermute(array, BOTH, pairs_of(target))]
    ppermute x3, starting transfers between devices: 18.3 us -> 23.6 us  [to_neighbour(): return lax.ppermute(array, BOTH, pairs_of(neighbour_of))]
    ppermute x2, starting transfers between devices: 10.3 us -> 6.22 us  [to_side(): return lax.ppermute(array, 'vel', [(i, i ^ 1) for i in range(4)])]
    ppermute x6, starting transfers between devices: 15.1 us -> 19.2 us  [to_mirror(): return lax.ppermute(array, 'vel', [(i, 3 - i) for i in range(4)])]
    unnamed x21 -> x19, local copies, waits for them, and re-layouts: 4.1 us -> 1.5 us
    ppermute x6, waiting for transfers between devices: 18.4 us -> 20.4 us  [to_mirror(): return lax.ppermute(array, 'vel', [(i, 3 - i) for i in range(4)])]
  transfers between devices with their start and end apart: 15 -> 15, of which waited for: 9 -> 7; matrix products, arithmetic and copies ran while one was open for 7% -> 7% of each run, Pallas kernels for 10% -> 11%
where the time goes in v9:
time: 161 us; the launch traced here: 160 us
  starting transfers between devices  67.3 us (42%)
  Pallas kernels  30.8 us (19%)
  waiting for transfers between devices  27 us (17%)
  between operations  13.9 us (9%)
  matrix products  13 us (8%)
  blocking collectives  6.45 us (4%)
  local copies, waits for them, and re-layouts  1.63 us (1%)
    pallas_call x12, Pallas kernels, call(): pl.pallas_call(kernel, out_shape=[(pltpu.HBM if leave else jax.ShapeDtype...  30.8 us
    ppermute x3, starting transfers between devices, to_neighbour(): return lax.ppermute(array, BOTH, pairs_of(neighbour_of))  23.6 us
    ppermute x6, waiting for transfers between devices, to_mirror(): return lax.ppermute(array, 'vel', [(i, 3 - i) for i in range(4)])  20.4 us
    ppermute x6, starting transfers between devices, to_mirror(): return lax.ppermute(array, 'vel', [(i, 3 - i) for i in range(4)])  19.2 us
    ppermute x2, starting transfers between devices, to_layer(): return lax.ppermute(array, BOTH, pairs_of(target))  16.4 us
    dot_general x8, matrix products, chosen(): return jnp.dot(left, right, preferred_element_type=BF16)  13 us
    all_gather x3, blocking collectives, with_sibling(): lax.all_gather(array, 'cells', axis=0, tiled=True, axis_index_groups=groups)  6.45 us
    ppermute x2, starting transfers between devices, to_side(): return lax.ppermute(array, 'vel', [(i, i ^ 1) for i in range(4)])  6.22 us
  transfers between devices with their start and end apart: 15, of which 7 were waited for; matrix products, arithmetic and copies ran while one was open for 7% of the time, Pallas kernels for 11%

profile of v9, /device:TPU:8, one launch (start us, length us, event | category | flops | bytes accessed | tf_op | source)
XLA Modules:
  0.0 160.1 jit_solution(8344684236577327164)
XLA Ops:
  9.4 3.5 %collective-permute-start.6 = (bf16[88,1408]{1,0:T(8,128)(2,1)S(1)}, bf16[88,1408]{1,0:T(8,128)(2,1)S(1)}, u32[]{:S(2)}, u32[]{:S(2)}) collective-permute-start(bf16[88,1408]{1,0:T(8,128)(2,1)S(1)} %pad_maximum_fusion), channel_id=1, source_target_pairs={{0,3},{1,2},{2,1},{3,0},{4,7},{5,6},{6,5},{7,4},{8,11},{9,10},{10,... | collective-permute-start | bytes 743432 | tf_op jit(solution)/shard_map/ppermute | solution.py:60
  13.2 2.3 %shard_map.37 = (f32[704,128]{1,0:T(8,128)S(1)}, f32[88,128]{1,0:T(8,128)S(1)}, bf16[800,128]{1,0:T(8,128)(2,1)S(1)}, bf16[720,128]{1,0:T(8,128)(2,1)S(1)}, bf16...) custom-call(s32[6]{0:T(128)S(1)} %stack.31.flags, f32[704,256]{1,0:T(8,128)S(1)} %pad.13.populations, ...), custom_call_target="tpu_custom_call" | custom-call | flops 761266176 | bytes 2786304 | tf_op jit(solution)/shard_map/pallas_call | solution.py:78
  16.3 10.3 %collective-permute-done.6 = bf16[88,1408]{1,0:T(8,128)(2,1)S(1)} collective-permute-done((bf16[88,1408]{1,0:T(8,128)(2,1)S(1)}, bf16[88,1408]{1,0:T(8,128)(2,1)S(1)}, u32[]{:S(2)}, u32[]{:S(2)}) %collective-permute-start.6) | collective-permute-done | bytes 247840 | tf_op jit(solution)/shard_map/ppermute | solution.py:60
  27.3 1.9 %collective-permute-start = (bf16[800,128]{1,0:T(8,128)(2,1)S(1)}, bf16[800,128]{1,0:T(8,128)(2,1)S(1)}, u32[]{:S(2)}, u32[]{:S(2)}) collective-permute-start(bf16[800,128]{1,0:T(8,128)(2,1)S(1)} %get-tuple-element.55), channel_id=1, source_target_pairs={{0,3},{1,2},{2,1},{3,0},{4,7},{5,6},{6,5},{7,4},{8,11},{9,10},{10,... | collective-permute-start | bytes 614408 | tf_op jit(solution)/shard_map/ppermute | solution.py:60
  29.2 14.3 %collective-permute-start.1 = (bf16[720,128]{1,0:T(8,128)(2,1)S(1)}, bf16[720,128]{1,0:T(8,128)(2,1)S(1)}, u32[]{:S(2)}, u32[]{:S(2)}) collective-permute-start(bf16[720,128]{1,0:T(8,128)(2,1)S(1)} %get-tuple-element.57), channel_id=1, source_target_pairs={{0,508},{1,509},{2,6},{3,7},{4,0},{5,1},{6,10},{7,11},{8,4},{9,5},... | collective-permute-start | bytes 552968 | tf_op jit(solution)/shard_map/ppermute | solution.py:47
  43.5 2.1 %collective-permute-start.2 = (bf16[720,128]{1,0:T(8,128)(2,1)}, bf16[720,128]{1,0:T(8,128)(2,1)S(1)}, u32[]{:S(2)}, u32[]{:S(2)}) collective-permute-start(bf16[720,128]{1,0:T(8,128)(2,1)} %get-tuple-element.58), channel_id=1, source_target_pairs={{0,511},{1,510},{2,5},{3,4},{4,3},{5,2},{6,9},{7,8},{8,7},{9,6},{1... | collective-permute-start | bytes 552968 | tf_op jit(solution)/shard_map/ppermute | solution.py:47
  45.7 5.4 %fusion.6 = bf16[704,2744]{1,0:T(8,128)(2,1)S(1)} fusion(bf16[686,2744]{1,0:T(8,128)(2,1)} %param.5, s32[704]{0:T(1024)S(1)} %select_select_fusion), kind=kOutput, calls=%fused_computation.14 | convolution fusion | flops 2650879488 | bytes 7631136 | tf_op jit(solution)/shard_map/dot_general | solution.py:557
  57.8 2.6 %shard_map.38 = (bf16[1408,128]{1,0:T(8,128)(2,1)S(1)}, f32[8,128]{1,0:T(8,128)S(1)}, bf16[352,128]{1,0:T(8,128)(2,1)S(1)}) custom-call(s32[6]{0:T(128)S(1)} %stack.31.flags, f32[704,128]{1,0:T(8,128)S(1)} %copy-done.5, f32[88,128]{1,0:T(8,128)S(1)} %get-tuple-element.54.own_edge, bf16[800,128]{1,0:T(8,128)(2,1)S(1)} %collective-permute-done.received, ...), custom_call_target="tpu_custom_call" | custom-call | flops 18022400 | bytes 2519040 | tf_op jit(solution)/shard_map/pallas_call | solution.py:78
  60.4 1.9 %collective-permute-start.3 = (bf16[1408,128]{1,0:T(8,128)(2,1)S(1)}, bf16[1408,128]{1,0:T(8,128)(2,1)S(1)}, u32[]{:S(2)}, u32[]{:S(2)}) collective-permute-start(bf16[1408,128]{1,0:T(8,128)(2,1)S(1)} %get-tuple-element.62.lowered), channel_id=1, source_target_pairs={{0,1},{1,0},{2,3},{3,2},{4,5},{5,4},{6,7},{7,6},{8,9},{9,8},{10,11... | collective-permute-start | bytes 1081352 | tf_op jit(solution)/shard_map/ppermute | solution.py:68
  62.3 1.9 %collective-permute-start.5 = (bf16[352,128]{1,0:T(8,128)(2,1)S(1)}, bf16[352,128]{1,0:T(8,128)(2,1)S(1)}, u32[]{:S(2)}, u32[]{:S(2)}) collective-permute-start(bf16[352,128]{1,0:T(8,128)(2,1)S(1)} %get-tuple-element.63), channel_id=1, source_target_pairs={{0,2},{1,3},{2,0},{3,1},{4,6},{5,7},{6,4},{7,5},{8,10},{9,11},{10,... | collective-permute-start | bytes 270344 | tf_op jit(solution)/shard_map/ppermute | solution.py:64
  64.2 5.6 %collective-permute-start.4 = (bf16[352,128]{1,0:T(8,128)(2,1)S(1)}, bf16[352,128]{1,0:T(8,128)(2,1)S(1)}, u32[]{:S(2)}, u32[]{:S(2)}) collective-permute-start(bf16[352,128]{1,0:T(8,128)(2,1)S(1)} %get-tuple-element.63), channel_id=1, source_target_pairs={{0,3},{1,2},{2,1},{3,0},{4,7},{5,6},{6,5},{7,4},{8,11},{9,10},{10,... | collective-permute-start | bytes 270344 | tf_op jit(solution)/shard_map/ppermute | solution.py:60
  69.9 2.8 %collective-permute-done.4.bands = bf16[352,128]{1,0:T(8,128)(2,1)S(1)} collective-permute-done((bf16[352,128]{1,0:T(8,128)(2,1)S(1)}, bf16[352,128]{1,0:T(8,128)(2,1)S(1)}, u32[]{:S(2)}, u32[]{:S(2)}) %collective-permute-start.4) | collective-permute-done | bytes 90144 | tf_op jit(solution)/shard_map/ppermute | solution.py:60
  72.7 3.1 %shard_map.39 = (f32[704,128]{1,0:T(8,128)}, bf16[96,128]{1,0:T(8,128)(2,1)}, bf16[2816,128]{1,0:T(8,128)(2,1)}, bf16[704,128]{1,0:T(8,128)(2,1)}) custom-call(s32[6]{0:T(128)S(1)} %stack.31.flags, bf16[1408,128]{1,0:T(8,128)(2,1)S(1)} %get-tuple-element.62.lowered, bf16[1408,128]{1,0:T(8,128)(2,1)S(1)} %collective-permute-done.3.other, ...), custom_call_target="tpu_custom_call" | custom-call | flops 1015021568 | bytes 7233536 | tf_op jit(solution)/shard_map/pallas_call | solution.py:78
  75.8 5.5 %shard_map.40 = (f32[704,128]{1,0:T(8,128)S(1)}, f32[704,128]{1,0:T(8,128)S(1)}, bf16[704,128]{1,0:T(8,128)(2,1)S(1)}, bf16[704,128]{1,0:T(8,128)(2,1)S(1)}, bf16[192,128]{1,0:T(8,128)(2,1)S(1)}) custom-call(s32[6]{0:T(128)S(1)} %stack.31.flags, f32[3,704,128]{2,1,0:T(8,128)S(1)} %get-tuple-element.52.factors, bf16[96,128]{1,0:T(8,128)(2,1)} %get-tuple-element.68.own_packed, ...), custom_call_target="tpu_custom_call" | custom-call | flops 1015021568 | bytes 7462912 | tf_op jit(solution)/shard_map/pallas_call | solution.py:78
  81.3 10.3 %collective-permute-start.7 = (bf16[704,128]{1,0:T(8,128)(2,1)S(1)}, bf16[704,128]{1,0:T(8,128)(2,1)S(1)}, u32[]{:S(2)}, u32[]{:S(2)}) collective-permute-start(bf16[704,128]{1,0:T(8,128)(2,1)S(1)} %get-tuple-element.82), channel_id=1, source_target_pairs={{0,511},{1,510},{2,509},{3,508},{4,8},{5,9},{6,10},{7,11},{8,4},{9... | collective-permute-start | bytes 540680 | tf_op jit(solution)/shard_map/ppermute | solution.py:56
  91.5 2.1 %all_gather.13.sibling = bf16[1408,128]{1,0:T(8,128)(2,1)S(1)} all-gather(bf16[704,128]{1,0:T(8,128)(2,1)S(1)} %get-tuple-element.78), channel_id=1, replica_groups={{0,4},{8,12},{16,20},{24,28},{32,36},{40,44},{48,52},{56,60},{64,68},{7..., dimensions={0}, use_global_device_ids=true | all-gather | bytes 540672 | tf_op jit(solution)/shard_map/all_gather | solution.py:40
  95.3 5.0 %collective-permute-start.8 = (bf16[704,128]{1,0:T(8,128)(2,1)S(1)}, bf16[704,128]{1,0:T(8,128)(2,1)S(1)}, u32[]{:S(2)}, u32[]{:S(2)}) collective-permute-start(bf16[704,128]{1,0:T(8,128)(2,1)S(1)} %get-tuple-element.86), channel_id=1, source_target_pairs={{0,511},{1,510},{2,509},{3,508},{4,8},{5,9},{6,10},{7,11},{8,4},{9... | collective-permute-start | bytes 540680 | tf_op jit(solution)/shard_map/ppermute | solution.py:56
  101.9 2.9 %collective-permute-start.9 = (bf16[192,128]{1,0:T(8,128)(2,1)S(1)}, bf16[192,128]{1,0:T(8,128)(2,1)S(1)}, u32[]{:S(2)}, u32[]{:S(2)}) collective-permute-start(bf16[192,128]{1,0:T(8,128)(2,1)S(1)} %get-tuple-element.87), channel_id=1, source_target_pairs={{0,3},{1,2},{2,1},{3,0},{4,7},{5,6},{6,5},{7,4},{8,11},{9,10},{10,... | collective-permute-start | bytes 147464 | tf_op jit(solution)/shard_map/ppermute | solution.py:60
  104.9 2.1 %all_gather.14.sibling = bf16[1408,128]{1,0:T(8,128)(2,1)S(1)} all-gather(bf16[704,128]{1,0:T(8,128)(2,1)S(1)} %get-tuple-element.85), channel_id=1, replica_groups={{0,4},{8,12},{16,20},{24,28},{32,36},{40,44},{48,52},{56,60},{64,68},{7..., dimensions={0}, use_global_device_ids=true | all-gather | bytes 540672 | tf_op jit(solution)/shard_map/all_gather | solution.py:40
  106.9 2.5 %collective-permute-done.8.neighbour = bf16[704,128]{1,0:T(8,128)(2,1)S(1)} collective-permute-done((bf16[704,128]{1,0:T(8,128)(2,1)S(1)}, bf16[704,128]{1,0:T(8,128)(2,1)S(1)}, u32[]{:S(2)}, u32[]{:S(2)}) %collective-permute-start.8) | collective-permute-done | bytes 180256 | tf_op jit(solution)/shard_map/ppermute | solution.py:56
  109.4 2.2 %shard_map.43.lowered = bf16[1408,128]{1,0:T(8,128)(2,1)S(1)} custom-call(s32[6]{0:T(128)S(1)} %stack.31.flags, f32[704,128]{1,0:T(8,128)S(1)} %get-tuple-element.81.near, f32[704,128]{1,0:T(8,128)S(1)} %get-tuple-element.84.far, bf16[1408,128]{1,0:T(8,128)(2,1)S(1)} %all_gather.14.sibling, bf16[704,128]{1,0:T(8,128)(2,1)S(1)} %collective-permute-done.8.neighbour, ...), custom_call_target="tpu_custom_call" | custom-call | flops 9011200 | bytes 2756608 | tf_op jit(solution)/shard_map/pallas_call | solution.py:78
  111.6 4.3 %collective-permute-start.10 = (bf16[1408,128]{1,0:T(8,128)(2,1)S(1)}, bf16[1408,128]{1,0:T(8,128)(2,1)S(1)}, u32[]{:S(2)}, u32[]{:S(2)}) collective-permute-start(bf16[1408,128]{1,0:T(8,128)(2,1)S(1)} %shard_map.43.lowered), channel_id=1, source_target_pairs={{0,1},{1,0},{2,3},{3,2},{4,5},{5,4},{6,7},{7,6},{8,9},{9,8},{10,11... | collective-permute-start | bytes 1081352 | tf_op jit(solution)/shard_map/ppermute | solution.py:68
  115.9 4.0 %shard_map.44 = (f32[704,128]{1,0:T(8,128)S(1)}, f32[704,128]{1,0:T(8,128)S(1)}, bf16[2,704,704]{2,1,0:T(8,128)(2,1)S(1)}, bf16[704,1408]{1,0:T(8,128)(2,1)S(1)}) custom-call(s32[6]{0:T(128)S(1)} %stack.31.flags, bf16[1408,128]{1,0:T(8,128)(2,1)S(1)} %shard_map.43.lowered, bf16[704,704]{1,0:T(8,128)(2,1)} %copy-done.1, bf16[704,704]{1,0:T(8,128)(2,1)} %copy-done.3, ...), custom_call_target="tpu_custom_call" | custom-call | flops 507510784 | bytes 12976128 | tf_op jit(solution)/shard_map/pallas_call | solution.py:78
  120.0 2.3 %collective-permute-done.10.other = bf16[1408,128]{1,0:T(8,128)(2,1)S(1)} collective-permute-done((bf16[1408,128]{1,0:T(8,128)(2,1)S(1)}, bf16[1408,128]{1,0:T(8,128)(2,1)S(1)}, u32[]{:S(2)}, u32[]{:S(2)}) %collective-permute-start.10) | collective-permute-done | bytes 360480 | tf_op jit(solution)/shard_map/ppermute | solution.py:68
  122.2 2.0 %shard_map.45 = (f32[704,128]{1,0:T(8,128)S(1)}, f32[704,128]{1,0:T(8,128)S(1)}, bf16[704,128]{1,0:T(8,128)(2,1)S(1)}, bf16[704,128]{1,0:T(8,128)(2,1)S(1)}, bf16[192,128]{1,0:T(8,128)(2,1)S(1)}) custom-call(s32[6]{0:T(128)S(1)} %stack.31.flags, bf16[1408,128]{1,0:T(8,128)(2,1)S(1)} %collective-permute-done.10.other, f32[704,128]{1,0:T(8,128)S(1)} %get-tuple-element.88.own, ...), custom_call_target="tpu_custom_call" | custom-call | flops 507510784 | bytes 7258112 | tf_op jit(solution)/shard_map/pallas_call | solution.py:78
  124.2 8.3 %collective-permute-start.11 = (bf16[704,128]{1,0:T(8,128)(2,1)S(1)}, bf16[704,128]{1,0:T(8,128)(2,1)S(1)}, u32[]{:S(2)}, u32[]{:S(2)}) collective-permute-start(bf16[704,128]{1,0:T(8,128)(2,1)S(1)} %get-tuple-element.95), channel_id=1, source_target_pairs={{0,511},{1,510},{2,509},{3,508},{4,8},{5,9},{6,10},{7,11},{8,4},{9... | collective-permute-start | bytes 540680 | tf_op jit(solution)/shard_map/ppermute | solution.py:56
  132.5 2.2 %collective-permute-start.12 = (bf16[192,128]{1,0:T(8,128)(2,1)S(1)}, bf16[192,128]{1,0:T(8,128)(2,1)S(1)}, u32[]{:S(2)}, u32[]{:S(2)}) collective-permute-start(bf16[192,128]{1,0:T(8,128)(2,1)S(1)} %get-tuple-element.96), channel_id=1, source_target_pairs={{0,3},{1,2},{2,1},{3,0},{4,7},{5,6},{6,5},{7,4},{8,11},{9,10},{10,... | collective-permute-start | bytes 147464 | tf_op jit(solution)/shard_map/ppermute | solution.py:60
  134.7 2.3 %all_gather.15.sibling = bf16[1408,128]{1,0:T(8,128)(2,1)S(1)} all-gather(bf16[704,128]{1,0:T(8,128)(2,1)S(1)} %get-tuple-element.94), channel_id=1, replica_groups={{0,4},{8,12},{16,20},{24,28},{32,36},{40,44},{48,52},{56,60},{64,68},{7..., dimensions={0}, use_global_device_ids=true | all-gather | bytes 540672 | tf_op jit(solution)/shard_map/all_gather | solution.py:40
  139.9 3.1 %collective-permute-start.13 = (bf16[704,128]{1,0:T(8,128)(2,1)S(1)}, bf16[704,128]{1,0:T(8,128)(2,1)S(1)}, u32[]{:S(2)}, u32[]{:S(2)}) collective-permute-start(bf16[704,128]{1,0:T(8,128)(2,1)S(1)} %shard_map.47), channel_id=1, source_target_pairs={{0,3},{1,2},{2,1},{3,0},{4,7},{5,6},{6,5},{7,4},{8,11},{9,10},{10,... | collective-permute-start | bytes 540680 | tf_op jit(solution)/shard_map/ppermute | solution.py:60
  143.0 2.3 %shard_map.46.kept = f32[704,128]{1,0:T(8,128)S(1)} custom-call(s32[6]{0:T(128)S(1)} %stack.31.flags, f32[704,128]{1,0:T(8,128)S(1)} %get-tuple-element.92.near, f32[704,128]{1,0:T(8,128)S(1)} %get-tuple-element.93.far, bf16[1408,128]{1,0:T(8,128)(2,1)S(1)} %all_gather.15.sibling, bf16[704,128]{1,0:T(8,128)(2,1)S(1)} %collective-permute-done.11.neighbour, ...), custom_call_target="tpu_custom_call" | custom-call | flops 507510784 | bytes 2756608 | tf_op jit(solution)/shard_map/pallas_call | solution.py:78
  145.3 5.9 %collective-permute-done.13.received = bf16[704,128]{1,0:T(8,128)(2,1)S(1)} collective-permute-done((bf16[704,128]{1,0:T(8,128)(2,1)S(1)}, bf16[704,128]{1,0:T(8,128)(2,1)S(1)}, u32[]{:S(2)}, u32[]{:S(2)}) %collective-permute-start.13) | collective-permute-done | bytes 180256 | tf_op jit(solution)/shard_map/ppermute | solution.py:60
  151.2 2.1 %shard_map.48 = f32[686,1,256]{2,1,0:T(1,128)} custom-call(s32[6]{0:T(128)S(1)} %stack.31.flags, f32[704,128]{1,0:T(8,128)S(1)} %shard_map.46.kept, bf16[704,128]{1,0:T(8,128)(2,1)S(1)} %collective-permute-done.13.received), custom_call_target="tpu_custom_call" | custom-call | flops 126877696 | bytes 1243136 | tf_op jit(solution)/shard_map/pallas_call | solution.py:78
  (52 shorter events, 17.3 us)
Async XLA Ops:
  6.5 6.5 %copy-start.7 = (f32[686,1,256]{2,1,0:T(1,128)S(1)}, f32[686,1,256]{2,1,0:T(1,128)}, u32[]{:S(2)}) copy-start(f32[686,1,256]{2,1,0:T(1,128)} %param.3) | copy-start | bytes 2107396
  6.5 69.2 %all-gather.2.cloned.1.call-start = ((), (), s32[]{:S(2)}) async-start(), calls=%async_computation | async-start | bytes 4212736 | tf_op jit(solution)/shard_map/all_gather | solution.py:612
  8.7 4.5 %copy-start.6 = (s32[1,256]{1,0:T(1,128)S(1)}, s32[1,256]{1,0:T(1,128)}, u32[]{:S(2)}) copy-start(s32[1,256]{1,0:T(1,128)} %solid.1) | copy-start | bytes 3076
  9.4 17.1 %collective-permute-start.6 = (bf16[88,1408]{1,0:T(8,128)(2,1)S(1)}, bf16[88,1408]{1,0:T(8,128)(2,1)S(1)}, u32[]{:S(2)}, u32[]{:S(2)}) collective-permute-start(bf16[88,1408]{1,0:T(8,128)(2,1)S(1)} %pad_maximum_fusion), channel_id=1, source_target_pairs={{0,3},{1,2},{2,1},{3,0},{4,7},{5,6},{6,5},{7,4},{8,11},{9,10},{10,... | collective-permute-start | bytes 743432 | tf_op jit(solution)/shard_map/ppermute | solution.py:60
  15.6 0.7 copy-start.4
  26.6 0.7 copy-start.8
  27.3 18.4 %collective-permute-start = (bf16[800,128]{1,0:T(8,128)(2,1)S(1)}, bf16[800,128]{1,0:T(8,128)(2,1)S(1)}, u32[]{:S(2)}, u32[]{:S(2)}) collective-permute-start(bf16[800,128]{1,0:T(8,128)(2,1)S(1)} %get-tuple-element.55), channel_id=1, source_target_pairs={{0,3},{1,2},{2,1},{3,0},{4,7},{5,6},{6,5},{7,4},{8,11},{9,10},{10,... | collective-permute-start | bytes 614408 | tf_op jit(solution)/shard_map/ppermute | solution.py:60
  29.2 28.6 %collective-permute-start.1 = (bf16[720,128]{1,0:T(8,128)(2,1)S(1)}, bf16[720,128]{1,0:T(8,128)(2,1)S(1)}, u32[]{:S(2)}, u32[]{:S(2)}) collective-permute-start(bf16[720,128]{1,0:T(8,128)(2,1)S(1)} %get-tuple-element.57), channel_id=1, source_target_pairs={{0,508},{1,509},{2,6},{3,7},{4,0},{5,1},{6,10},{7,11},{8,4},{9,5},... | collective-permute-start | bytes 552968 | tf_op jit(solution)/shard_map/ppermute | solution.py:47
  43.5 14.3 %collective-permute-start.2 = (bf16[720,128]{1,0:T(8,128)(2,1)}, bf16[720,128]{1,0:T(8,128)(2,1)S(1)}, u32[]{:S(2)}, u32[]{:S(2)}) collective-permute-start(bf16[720,128]{1,0:T(8,128)(2,1)} %get-tuple-element.58), channel_id=1, source_target_pairs={{0,511},{1,510},{2,5},{3,4},{4,3},{5,2},{6,9},{7,8},{8,7},{9,6},{1... | collective-permute-start | bytes 552968 | tf_op jit(solution)/shard_map/ppermute | solution.py:47
  52.2 20.5 %copy-start = (bf16[704,704]{1,0:T(8,128)(2,1)}, bf16[704,704]{1,0:T(8,128)(2,1)S(1)}, u32[]{:S(2)}) copy-start(bf16[704,704]{1,0:T(8,128)(2,1)S(1)} %fusion.4.m2) | copy-start | bytes 2973700
  53.3 19.4 %copy-start.1 = (bf16[704,704]{1,0:T(8,128)(2,1)}, bf16[704,704]{1,0:T(8,128)(2,1)S(1)}, u32[]{:S(2)}) copy-start(bf16[704,704]{1,0:T(8,128)(2,1)S(1)} %fusion.3.m0) | copy-start | bytes 2973700
  54.6 18.0 %copy-start.2 = (bf16[704,704]{1,0:T(8,128)(2,1)}, bf16[704,704]{1,0:T(8,128)(2,1)S(1)}, u32[]{:S(2)}) copy-start(bf16[704,704]{1,0:T(8,128)(2,1)S(1)} %fusion.1.m3) | copy-start | bytes 2973700
  54.6 3.2 %copy-start.5 = (f32[704,128]{1,0:T(8,128)S(1)}, f32[704,128]{1,0:T(8,128)}, u32[]{:S(2)}) copy-start(f32[704,128]{1,0:T(8,128)} %copy-done.4) | copy-start | bytes 1081348
  56.0 16.7 %copy-start.3 = (bf16[704,704]{1,0:T(8,128)(2,1)}, bf16[704,704]{1,0:T(8,128)(2,1)S(1)}, u32[]{:S(2)}) copy-start(bf16[704,704]{1,0:T(8,128)(2,1)S(1)} %fusion.m1) | copy-start | bytes 2973700
  60.4 12.3 %collective-permute-start.3 = (bf16[1408,128]{1,0:T(8,128)(2,1)S(1)}, bf16[1408,128]{1,0:T(8,128)(2,1)S(1)}, u32[]{:S(2)}, u32[]{:S(2)}) collective-permute-start(bf16[1408,128]{1,0:T(8,128)(2,1)S(1)} %get-tuple-element.62.lowered), channel_id=1, source_target_pairs={{0,1},{1,0},{2,3},{3,2},{4,5},{5,4},{6,7},{7,6},{8,9},{9,8},{10,11... | collective-permute-start | bytes 1081352 | tf_op jit(solution)/shard_map/ppermute | solution.py:68
  62.3 7.5 %collective-permute-start.5 = (bf16[352,128]{1,0:T(8,128)(2,1)S(1)}, bf16[352,128]{1,0:T(8,128)(2,1)S(1)}, u32[]{:S(2)}, u32[]{:S(2)}) collective-permute-start(bf16[352,128]{1,0:T(8,128)(2,1)S(1)} %get-tuple-element.63), channel_id=1, source_target_pairs={{0,2},{1,3},{2,0},{3,1},{4,6},{5,7},{6,4},{7,5},{8,10},{9,11},{10,... | collective-permute-start | bytes 270344 | tf_op jit(solution)/shard_map/ppermute | solution.py:64
  64.2 8.4 %collective-permute-start.4 = (bf16[352,128]{1,0:T(8,128)(2,1)S(1)}, bf16[352,128]{1,0:T(8,128)(2,1)S(1)}, u32[]{:S(2)}, u32[]{:S(2)}) collective-permute-start(bf16[352,128]{1,0:T(8,128)(2,1)S(1)} %get-tuple-element.63), channel_id=1, source_target_pairs={{0,3},{1,2},{2,1},{3,0},{4,7},{5,6},{6,5},{7,4},{8,11},{9,10},{10,... | collective-permute-start | bytes 270344 | tf_op jit(solution)/shard_map/ppermute | solution.py:60
  81.3 19.0 %collective-permute-start.7 = (bf16[704,128]{1,0:T(8,128)(2,1)S(1)}, bf16[704,128]{1,0:T(8,128)(2,1)S(1)}, u32[]{:S(2)}, u32[]{:S(2)}) collective-permute-start(bf16[704,128]{1,0:T(8,128)(2,1)S(1)} %get-tuple-element.82), channel_id=1, source_target_pairs={{0,511},{1,510},{2,509},{3,508},{4,8},{5,9},{6,10},{7,11},{8,4},{9... | collective-permute-start | bytes 540680 | tf_op jit(solution)/shard_map/ppermute | solution.py:56
  95.3 14.1 %collective-permute-start.8 = (bf16[704,128]{1,0:T(8,128)(2,1)S(1)}, bf16[704,128]{1,0:T(8,128)(2,1)S(1)}, u32[]{:S(2)}, u32[]{:S(2)}) collective-permute-start(bf16[704,128]{1,0:T(8,128)(2,1)S(1)} %get-tuple-element.86), channel_id=1, source_target_pairs={{0,511},{1,510},{2,509},{3,508},{4,8},{5,9},{6,10},{7,11},{8,4},{9... | collective-permute-start | bytes 540680 | tf_op jit(solution)/shard_map/ppermute | solution.py:56
  101.9 7.5 %collective-permute-start.9 = (bf16[192,128]{1,0:T(8,128)(2,1)S(1)}, bf16[192,128]{1,0:T(8,128)(2,1)S(1)}, u32[]{:S(2)}, u32[]{:S(2)}) collective-permute-start(bf16[192,128]{1,0:T(8,128)(2,1)S(1)} %get-tuple-element.87), channel_id=1, source_target_pairs={{0,3},{1,2},{2,1},{3,0},{4,7},{5,6},{6,5},{7,4},{8,11},{9,10},{10,... | collective-permute-start | bytes 147464 | tf_op jit(solution)/shard_map/ppermute | solution.py:60
  111.6 10.6 %collective-permute-start.10 = (bf16[1408,128]{1,0:T(8,128)(2,1)S(1)}, bf16[1408,128]{1,0:T(8,128)(2,1)S(1)}, u32[]{:S(2)}, u32[]{:S(2)}) collective-permute-start(bf16[1408,128]{1,0:T(8,128)(2,1)S(1)} %shard_map.43.lowered), channel_id=1, source_target_pairs={{0,1},{1,0},{2,3},{3,2},{4,5},{5,4},{6,7},{7,6},{8,9},{9,8},{10,11... | collective-permute-start | bytes 1081352 | tf_op jit(solution)/shard_map/ppermute | solution.py:68
  124.2 14.3 %collective-permute-start.11 = (bf16[704,128]{1,0:T(8,128)(2,1)S(1)}, bf16[704,128]{1,0:T(8,128)(2,1)S(1)}, u32[]{:S(2)}, u32[]{:S(2)}) collective-permute-start(bf16[704,128]{1,0:T(8,128)(2,1)S(1)} %get-tuple-element.95), channel_id=1, source_target_pairs={{0,511},{1,510},{2,509},{3,508},{4,8},{5,9},{6,10},{7,11},{8,4},{9... | collective-permute-start | bytes 540680 | tf_op jit(solution)/shard_map/ppermute | solution.py:56
  132.5 6.0 %collective-permute-start.12 = (bf16[192,128]{1,0:T(8,128)(2,1)S(1)}, bf16[192,128]{1,0:T(8,128)(2,1)S(1)}, u32[]{:S(2)}, u32[]{:S(2)}) collective-permute-start(bf16[192,128]{1,0:T(8,128)(2,1)S(1)} %get-tuple-element.96), channel_id=1, source_target_pairs={{0,3},{1,2},{2,1},{3,0},{4,7},{5,6},{6,5},{7,4},{8,11},{9,10},{10,... | collective-permute-start | bytes 147464 | tf_op jit(solution)/shard_map/ppermute | solution.py:60
  139.9 11.3 %collective-permute-start.13 = (bf16[704,128]{1,0:T(8,128)(2,1)S(1)}, bf16[704,128]{1,0:T(8,128)(2,1)S(1)}, u32[]{:S(2)}, u32[]{:S(2)}) collective-permute-start(bf16[704,128]{1,0:T(8,128)(2,1)S(1)} %shard_map.47), channel_id=1, source_target_pairs={{0,3},{1,2},{2,1},{3,0},{4,7},{5,6},{6,5},{7,4},{8,11},{9,10},{10,... | collective-permute-start | bytes 540680 | tf_op jit(solution)/shard_map/ppermute | solution.py:60
Sparse Core Ops, SparseCore 0:
  27.4 45.0 all-gather.1

commit v10 on v8

--- a/solution.py
+++ b/solution.py
@@ -20,6 +20,8 @@
 EDGE = 96
 LANES = 128
 BAND = 4 * CHUNK
+PIECE = 96
+PIECES = 8
 RING = 16
 F32 = jnp.float32
 BF16 = jnp.bfloat16
@@ -35,6 +37,10 @@
     return pairs
 
 
+def to_sibling(array):
+    return lax.ppermute(array, "cells", [(cell, cell ^ 1) for cell in range(128)])
+
+
 def with_sibling(array):
     groups = [[cell, cell + 1] for cell in range(0, 128, 2)]
     return lax.all_gather(array, "cells", axis=0, tiled=True, axis_index_groups=groups)
@@ -56,6 +62,14 @@
     return lax.ppermute(array, BOTH, pairs_of(neighbour_of))
 
 
+def to_next_z(array):
+    return lax.ppermute(array, "cells", [(cell, cell ^ 2) for cell in range(128)])
+
+
+def along_x(array, step):
+    return lax.ppermute(array, "cells", [(cell, (cell + 32 * step) % 128) for cell in range(128)])
+
+
 def to_mirror(array):
     return lax.ppermute(array, "vel", [(i, 3 - i) for i in range(4)])
 
@@ -68,19 +82,16 @@
     return lax.ppermute(array, "vel", [(i, i ^ 1) for i in range(4)])
 
 
-def call(kernel, outs, flags, *arrays, flops=0, stay=0, scratch=()):
+def call(kernel, outs, flags, *arrays, flops=0, scratch=()):
     moved = sum(x.size * x.dtype.itemsize for x in arrays)
     moved += sum(math.prod(shape) * jnp.dtype(dtype).itemsize for shape, dtype in outs)
-    vmem, hbm = (pl.BlockSpec(memory_space=space) for space in (pltpu.VMEM, pltpu.HBM))
-    count = len(arrays) - stay
-    specs = [vmem] * count + [hbm] * stay
-    arrays = *arrays[:count], *(pltpu.with_memory_space_constraint(x, pltpu.HBM) for x in arrays[count:])
+    vmem = pl.BlockSpec(memory_space=pltpu.VMEM)
     return pl.pallas_call(
         kernel,
         out_shape=[jax.ShapeDtypeStruct(shape, dtype) for shape, dtype in outs],
-        in_specs=[pl.BlockSpec(memory_space=pltpu.SMEM)] + specs,
+        in_specs=[pl.BlockSpec(memory_space=pltpu.SMEM)] + [vmem] * len(arrays),
         out_specs=[vmem] * len(outs),
-        scratch_shapes=scratch,
+        scratch_shapes=[pltpu.VMEM(shape, dtype) for shape, dtype in scratch],
         compiler_params=PARAMS,
         cost_estimate=pl.CostEstimate(flops=flops, bytes_accessed=moved, transcendentals=0),
     )(flags, *arrays)
@@ -386,12 +397,13 @@
     flags, lowered, other, bands, other_bands, factors, m0, m1, m2, m3, rows_out, packed_out, all_rows, all_bands
 ):
     swapped = flags[2] == 1
+    values = []
     for index, right in enumerate((swapped, ~swapped)):
-        all_rows[rows_of(index, 2 * PAD)] = jnp.where(right, other[...], lowered[...])
-        all_bands[rows_of(index, BAND)] = jnp.where(right, other_bands[...], bands[...])
-    values = []
-    for index in range(2):
-        rows, band = all_rows[rows_of(index, 2 * PAD)], unpacked(all_bands[rows_of(index, BAND)])
+        slot = jnp.where(flags[1] == 1, index, 1 - index)
+        rows = jnp.where(right, other[...], lowered[...])
+        all_rows[pl.ds(pl.multiple_of(2 * PAD * slot, 16), 2 * PAD)] = rows
+        band = unpacked(jnp.where(right, other_bands[...], bands[...]))
+        all_bands[pl.ds(pl.multiple_of(2 * PAD * slot, 16), 2 * PAD)] = band
         for side in range(2):
             span = rows_of(side, PAD)
             values.append(jnp.concatenate([rows[span], band[span]], axis=1))
@@ -424,119 +436,91 @@
     return give_rows(flags, part, near, far, factors, packed, outs)
 
 
+def partner_product(flags, matrix, values, give):
+    for index in range(PIECES):
+        start = pl.multiple_of(PIECE * flags[6 + index], 8)
+        give(pl.ds(start, PIECE), dot(matrix[rows_of(index, PIECE)], values))
+
+
 def collide_partner_kernel(
-    flags, own_packed, factors, all_rows, all_bands, own, matrix,
-    near, far, for_sibling, for_neighbour, edges,
-    held, held_rows, held_bands, held_own, done,
+    flags, own, own_packed, all_rows, all_bands, factors, mine, theirs,
+    near, far, for_sibling, for_neighbour, edges, total,
 ):
-    small = [
-        pltpu.make_async_copy(source, target, done.at[index])
-        for index, (source, target) in enumerate(
-            ((all_rows, held_rows), (all_bands, held_bands), (own, held_own))
-        )
+    values = [
+        jnp.concatenate([all_rows[rows_of(i, 2 * PAD)], all_bands[rows_of(i, 2 * PAD)]], axis=1)
+        for i in range(2)
     ]
-    parts = PAD // PART
-    pieces = [
-        [
-            pltpu.make_async_copy(
-                matrix.at[rows_of(parts * half + part, PART)],
-                held.at[rows_of(parts * half + part, PART)],
-                done.at[3 + parts * half + part],
-            )
-            for half in range(2)
-        ]
-        for part in range(parts)
-    ]
-    for copy in small + sum(pieces, []):
-        copy.start()
-    for copy in small:
-        copy.wait()
+    for index in range(PIECES):
+        start = pl.multiple_of(PIECE * flags[6 + index], 8)
+        span = rows_of(index, PIECE)
+        total[pl.ds(start, PIECE)] = dot(mine[span], values[0]) + dot(theirs[span], values[1])
     low, same = flags[0] == 1, flags[4] == 1
-    values = []
-    for index in range(2):
-        band = unpacked(held_bands[rows_of(index, BAND)])
-        values.append(jnp.concatenate([held_rows[rows_of(index, 2 * PAD)], band], axis=1))
     sign = jnp.where(low, -1.0, 1.0)
     packed = jnp.zeros((CHUNK, LANES), F32)
-    for part in range(parts):
-        span = rows_of(part, PART)
-        total = 0.0
-        for half in range(2):
-            pieces[part][half].wait()
-            total += dot(held[rows_of(parts * half + part, PART)], values[half])
-        mine, theirs = held_own[span], total[:, :LANES]
-        rows_near, rows_far = jnp.where(same, mine, theirs), jnp.where(same, theirs, mine)
+    for part in range(PAD // PART):
+        span = rows_of(part, PART)
+        rows_own, rows_partner = own[span], total[span, :LANES]
+        rows_near = jnp.where(same, rows_own, rows_partner)
+        rows_far = jnp.where(same, rows_partner, rows_own)
         near[span], far[span] = rows_near, rows_far
         for_neighbour[span] = rows_near.astype(BF16)
         for_sibling[span] = rows_far.astype(BF16)
-        packed = pack_other(packed, part, sign, total[:, LANES:], factors)
-    mine, theirs = own_packed[...], edge_block(packed)
-    edges[:EDGE] = jnp.where(same, mine, theirs)
-    edges[EDGE:] = jnp.where(same, theirs, mine)
-
-
-def early_kernel(
-    flags, lowered, m0, m1, m2, m3, matrix, own_out, partner_out, next_own, next_partner,
-    held_own, held_partner, done,
-):
+        packed = pack_other(packed, part, sign, total[span, LANES:], factors)
+    packed_own, packed_partner = own_packed[...], edge_block(packed)
+    edges[:EDGE] = jnp.where(same, packed_own, packed_partner)
+    edges[EDGE:] = jnp.where(same, packed_partner, packed_own)
+
+
+def half_products(flags, half_wanted, lowered, parts, mine, theirs, give_own, give_partner):
     values = lowered[...]
-    parts = m0, m1, m2, m3
     for half in range(2):
 
-        @pl.when(flags[2] == half)
+        @pl.when(half_wanted == half)
         def _():
-            copies = [
-                pltpu.make_async_copy(
-                    matrix.at[rows_of(half, PAD)], held_partner, done.at[0]
-                )
-            ]
-            for i in range(2):
-                copies.append(pltpu.make_async_copy(parts[2 * half + i], held_own.at[i], done.at[1 + i]))
-            copies.append(
-                pltpu.make_async_copy(matrix.at[rows_of(1 - half, PAD)], next_partner, done.at[3])
-            )
-            for i in range(2):
-                source = parts[2 * (1 - half) + i]
-                copies.append(pltpu.make_async_copy(source, next_own.at[i], done.at[4 + i]))
-            for copy in copies:
-                copy.start()
-            copies[0].wait()
             for part in range(PAD // PART):
                 span = rows_of(part, PART)
-                partner_out[span] = dot(held_partner[span], values)
-            copies[1].wait()
-            copies[2].wait()
-            for part in range(PAD // PART):
-                span = rows_of(part, PART)
-                own_out[span] = dot(held_own[0, span], values[:PAD]) + dot(held_own[1, span], values[PAD:])
-            for copy in copies[3:]:
-                copy.wait()
-
-
-def late_kernel(flags, other, own, partner, factors, matrix_own, matrix_partner, *outs):
-    values = other[...]
+                total = dot(parts[2 * half][span], values[:PAD])
+                give_own(span, total + dot(parts[2 * half + 1][span], values[PAD:]))
+
+    core = 1 - flags[1]
+    for held, here in ((mine, half_wanted == core), (theirs, half_wanted != core)):
+
+        @pl.when(here)
+        def _():
+            partner_product(flags, held, values, give_partner)
+
+
+def early_kernel(flags, lowered, m0, m1, m2, m3, mine, theirs, own_out, partner_out):
+    def give_own(span, rows):
+        own_out[span] = rows
+
+    def give_partner(span, rows):
+        partner_out[span] = rows
+
+    half_products(flags, flags[2], lowered, (m0, m1, m2, m3), mine, theirs, give_own, give_partner)
+
+
+def late_kernel(flags, other, own, partner, factors, m0, m1, m2, m3, mine, theirs, *refs):
+    outs, (total_own, total_partner) = refs[:5], refs[5:]
+
+    def give_own(span, rows):
+        total_own[span] = own[span] + rows
+
+    def give_partner(span, rows):
+        total_partner[span] = partner[span] + rows
+
+    half_products(flags, 1 - flags[2], other, (m0, m1, m2, m3), mine, theirs, give_own, give_partner)
     packed = (jnp.zeros((CHUNK, LANES), F32),) * 2
     for part in range(PAD // PART):
         span = rows_of(part, PART)
-        more_own = dot(matrix_own[0, span], values[:PAD]) + dot(matrix_own[1, span], values[PAD:])
-        more_partner = dot(matrix_partner[span], values)
         packed = give_product(
-            flags, part, own[span] + more_own, partner[span] + more_partner, factors, packed, outs[:4]
+            flags, part, total_own[span], total_partner[span], factors, packed, outs[:4]
         )
     outs[4][:EDGE], outs[4][EDGE:] = edge_block(packed[0]), edge_block(packed[1])
 
 
 ROWS_F32 = ((PAD, LANES), F32)
-PARTNER_SCRATCH = [
-    pltpu.VMEM((2 * PAD, 2 * PAD), BF16),
-    pltpu.VMEM((4 * PAD, LANES), BF16),
-    pltpu.VMEM((2 * BAND, LANES), BF16),
-    pltpu.VMEM((PAD, LANES), F32),
-    pltpu.SemaphoreType.DMA((11,)),
-]
-HELD = [pltpu.VMEM((2, PAD, PAD), BF16), pltpu.VMEM((PAD, 2 * PAD), BF16)]
-EARLY = [ROWS_F32, ROWS_F32, ((2, PAD, PAD), BF16), ((PAD, 2 * PAD), BF16)]
-EARLY_SCRATCH = HELD + [pltpu.SemaphoreType.DMA((6,))]
+PIECES_F32 = ((PIECES * PIECE, LANES), F32)
 
 
 def finish_kernel(flags, kept, received, evolved):
@@ -575,24 +559,30 @@
 def per_device(populations, solid_mask, collision):
     cell, vel = lax.axis_index("cells"), lax.axis_index("vel")
     low = (vel < 2).astype(jnp.int32)
-    core, ring_place = cell % 2, cell // 32 + 4 * (cell // 2 % 2)
+    core, line, odd = cell % 2, cell // 32, cell // 2 % 2
+    pieces = [2 * ((line + step) % 4) + (odd ^ other) for step in (0, 3, 1, 2) for other in range(2)]
     block = jnp.minimum(vel, 3 - vel)
     half = (1 - low) ^ (cell // RING % 2)
     needing = (cell + 1 - 2 * low) % 128
     straight_half = (1 - low) ^ (needing // RING % 2)
     same = (low != core).astype(jnp.int32)
-    flags = jnp.stack([low, 1 - core, block, half, same, straight_half])
+    flags = jnp.stack([low, 1 - core, block, half, same, straight_half, *pieces])
     flags = flags.astype(jnp.int32)
 
-    first_row = CHUNK * ring_place
-    row = first_row + lax.iota(jnp.int32, CHUNK)
-    start = jnp.clip(jnp.where(low == 1, first_row, ROWS - CHUNK - first_row), 0, ROWS - CHUNK)
+    first_row = PIECE * pieces[0]
+    row = first_row + lax.iota(jnp.int32, PIECE)
+    start = jnp.clip(jnp.where(low == 1, first_row, ROWS - PIECE - first_row), 0, ROWS - PIECE)
     wanted = jnp.where(row < ROWS, jnp.where(low == 1, row, ROWS - 1 - row) - start, -1)
-    window = lax.dynamic_slice(collision, (start, 0), (CHUNK, collision.shape[1]))
-    window = padded_columns(chosen(place(CHUNK, CHUNK, wanted).T, window))
+    window = lax.dynamic_slice(collision, (start, 0), (PIECE, collision.shape[1]))
+    window = padded_columns(chosen(place(PIECE, PIECE, wanted).T, window))
     piece = jnp.concatenate(column_half(window, core), axis=1)
     populations, piece = lax.optimization_barrier((populations, piece))
     piece = to_mirror(piece)
+    pair = jnp.concatenate([piece, to_next_z(piece)], axis=0)
+    below, above = along_x(pair, 1), along_x(pair, -1)
+    beyond = along_x(below[:PIECE], 1), along_x(above[PIECE:], -1)
+    mine = jnp.concatenate([pair, below, above, *beyond], axis=0)
+    theirs = to_sibling(mine)
 
     padded = jnp.pad(populations[:, 0, :], ((0, PAD - ROWS), (0, 0)))
     rows = (PAD, LANES)
@@ -602,13 +592,6 @@
          ((PAD + 16, LANES), BF16), ((PAD + 16, LANES), BF16), ((8, LANES), F32), ((3, *rows), F32)],
         flags, padded, solid_mask, flops=2 * 3 * PAD * PAD * 256,
     )
-    piece, _ = lax.optimization_barrier((piece, message))
-    groups = [
-        [x * 32 + y * 16 + 4 * pair + 2 * odd + side for side in range(2) for odd in range(2) for x in range(4)]
-        for y in range(2)
-        for pair in range(4)
-    ]
-    partner_matrix = lax.all_gather(piece, "cells", axis=0, tiled=True, axis_index_groups=groups)
     straight, turned = to_layer(straight, False), to_layer(turned, True)
     received = to_mirror(message)
 
@@ -617,13 +600,13 @@
     received, collision = lax.optimization_barrier((received, collision))
     ordered = padded_columns(chosen(place(ROWS, PAD, wanted).T, collision))
 
+    matrix = *column_half(ordered, 0), *column_half(ordered, 1)
+    turned, *matrix = lax.optimization_barrier((turned, *matrix))
     lowered, masks, bands = call(
         first_kernel,
         [((2 * PAD, LANES), BF16), ((8, LANES), F32), ((BAND, LANES), BF16)],
         flags, own, own_edge, received, straight, turned, masks, factors, flops=100 * PAD * 256,
     )
-    lowered, ordered = lax.optimization_barrier((lowered, ordered))
-    matrix = *column_half(ordered, 0), *column_half(ordered, 1)
     edges_shape = ((2 * EDGE, LANES), BF16)
     sends = [(rows, F32)] * 2 + [(rows, BF16)] * 2 + [edges_shape]
     multiply = 2 * PAD * 4 * PAD * LANES
@@ -631,15 +614,15 @@
 
     other = to_side(lowered)
     bands = to_mirror(bands), to_opposite(bands)
+    wide = ((4 * PAD, LANES), BF16)
     own, own_packed, all_rows, all_bands = call(
-        collide_kernel,
-        [(rows, F32), ((EDGE, LANES), BF16), ((4 * PAD, LANES), BF16), ((2 * BAND, LANES), BF16)],
+        collide_kernel, [(rows, F32), ((EDGE, LANES), BF16), wide, wide],
         flags, lowered, other, *bands, factors, *matrix, flops=2 * multiply,
     )
-    partner_matrix, own = lax.optimization_barrier((partner_matrix, own))
     near, far, for_sibling, for_neighbour, edges = call(
-        collide_partner_kernel, sends, flags, own_packed, factors, all_rows, all_bands, own, partner_matrix,
-        flops=2 * multiply, stay=4, scratch=PARTNER_SCRATCH,
+        collide_partner_kernel, sends,
+        flags, own, own_packed, all_rows, all_bands, factors, mine, theirs,
+        flops=2 * multiply, scratch=[((PIECES * PIECE, 2 * LANES), F32)],
     )
 
     for step in range(1, STEPS):
@@ -661,11 +644,11 @@
         )
         other = to_side(lowered)
         early = call(
-            early_kernel, EARLY, flags, lowered, *matrix, partner_matrix,
-            flops=multiply, stay=5, scratch=EARLY_SCRATCH,
+            early_kernel, [ROWS_F32, PIECES_F32], flags, lowered, *matrix, mine, theirs, flops=multiply
         )
         near, far, for_sibling, for_neighbour, edges = call(
-            late_kernel, sends, flags, other, *early[:2], factors, *early[2:], flops=multiply
+            late_kernel, sends, flags, other, *early, factors, *matrix, mine, theirs,
+            flops=multiply, scratch=[ROWS_F32, PIECES_F32],
         )
 
     neighbour, edges = to_neighbour(for_neighbour), to_mirror(edges)

time: 166 us -> 176 us (1.060)
  starting transfers between devices: 61.8 us -> 81.7 us
  between operations: 13.9 us -> 0.68 us
  waiting for transfers between devices: 35.7 us -> 48.7 us
  local copies, waits for them, and re-layouts: 4.54 us -> 0.52 us
  Pallas kernels: 29.6 us -> 25.6 us
    ppermute x0 -> x6, starting transfers between devices: none -> 20.5 us  [the longest x4 14.1 us: along_x(): lax.ppermute(array, 'cells', [(cell, (cell + 32 * step) % 128) for cell i...]
    ppermute x0 -> x6, waiting for transfers between devices: none -> 14 us  [the longest x4 14 us: along_x(): lax.ppermute(array, 'cells', [(cell, (cell + 32 * step) % 128) for cell i...]
    ppermute x2, waiting for transfers between devices: 12.1 us -> 0.01 us  [to_layer(): return lax.ppermute(array, BOTH, pairs_of(target))]
    ppermute x2, starting transfers between devices: 10.3 us -> 4.38 us  [to_side(): return lax.ppermute(array, 'vel', [(i, i ^ 1) for i in range(4)])]
    ppermute x1, waiting for transfers between devices: 0.01 us -> 5.91 us  [to_opposite(): return lax.ppermute(array, 'vel', [(i, i ^ 2) for i in range(4)])]
    ppermute x2, waiting for transfers between devices: 2.48 us -> 7.43 us  [to_side(): return lax.ppermute(array, 'vel', [(i, i ^ 1) for i in range(4)])]
    ppermute x1, starting transfers between devices: 1.92 us -> 6.27 us  [to_opposite(): return lax.ppermute(array, 'vel', [(i, i ^ 2) for i in range(4)])]
    pallas_call x12, Pallas kernels: 29.6 us -> 25.6 us  [call(): pl.pallas_call(kernel, out_shape=[jax.ShapeDtypeStruct(shape, dtype) for...]
  transfers between devices with their start and end apart: 15 -> 20, of which waited for: 9 -> 10; matrix products, arithmetic and copies ran while one was open for 7% -> 5% of each run, Pallas kernels for 10% -> 8%
where the time goes in v10:
time: 176 us; the launch traced here: 175 us
  starting transfers between devices  81.7 us (46%)
  waiting for transfers between devices  48.7 us (28%)
  Pallas kernels  25.6 us (15%)
  matrix products  11.4 us (6%)
  blocking collectives  6.41 us (4%)
    pallas_call x12, Pallas kernels, call(): pl.pallas_call(kernel, out_shape=[jax.ShapeDtypeStruct(shape, dtype) for...  25.6 us
    ppermute x6, starting transfers between devices, to_mirror(): return lax.ppermute(array, 'vel', [(i, 3 - i) for i in range(4)])  18.4 us
    ppermute x6, waiting for transfers between devices, to_mirror(): return lax.ppermute(array, 'vel', [(i, 3 - i) for i in range(4)])  17.4 us
    ppermute x3, starting transfers between devices, to_neighbour(): return lax.ppermute(array, BOTH, pairs_of(neighbour_of))  17.4 us
    ppermute x2, starting transfers between devices, to_layer(): return lax.ppermute(array, BOTH, pairs_of(target))  14.7 us
    ppermute x4, starting transfers between devices, along_x(): lax.ppermute(array, 'cells', [(cell, (cell + 32 * step) % 128) for cell i...  14.1 us
    ppermute x4, waiting for transfers between devices, along_x(): lax.ppermute(array, 'cells', [(cell, (cell + 32 * step) % 128) for cell i...  14 us
    dot_general x8, matrix products, chosen(): return jnp.dot(left, right, preferred_element_type=BF16)  11.4 us
  transfers between devices with their start and end apart: 20, of which 10 were waited for; matrix products, arithmetic and copies ran while one was open for 5% of the time, Pallas kernels for 8%

profile of v10, /device:TPU:8, one launch (start us, length us, event | category | flops | bytes accessed | tf_op | source)
XLA Modules:
  0.0 175.1 jit_solution(16443196629441932123)
XLA Ops:
  2.9 3.5 %collective-permute-start.6 = (bf16[96,1408]{1,0:T(8,128)(2,1)S(1)}, bf16[96,1408]{1,0:T(8,128)(2,1)S(1)}, u32[]{:S(2)}, u32[]{:S(2)}) collective-permute-start(bf16[96,1408]{1,0:T(8,128)(2,1)S(1)} %pad_maximum_fusion), channel_id=1, source_target_pairs={{0,3},{1,2},{2,1},{3,0},{4,7},{5,6},{6,5},{7,4},{8,11},{9,10},{10,... | collective-permute-start | bytes 811016 | tf_op jit(solution)/shard_map/ppermute | solution.py:74
  6.8 12.0 %collective-permute-done.6 = bf16[96,1408]{1,0:T(8,128)(2,1)S(1)} collective-permute-done((bf16[96,1408]{1,0:T(8,128)(2,1)S(1)}, bf16[96,1408]{1,0:T(8,128)(2,1)S(1)}, u32[]{:S(2)}, u32[]{:S(2)}) %collective-permute-start.6) | collective-permute-done | bytes 270368 | tf_op jit(solution)/shard_map/ppermute | solution.py:74
  18.8 4.3 %collective-permute-start.7 = (bf16[96,1408]{1,0:T(8,128)(2,1)S(1)}, bf16[96,1408]{1,0:T(8,128)(2,1)S(1)}, u32[]{:S(2)}, u32[]{:S(2)}) collective-permute-start(bf16[96,1408]{1,0:T(8,128)(2,1)S(1)} %collective-permute-done.6), channel_id=1, source_target_pairs={{0,8},{4,12},{8,0},{12,4},{16,24},{20,28},{24,16},{28,20},{32,40},... | collective-permute-start | bytes 811016 | tf_op jit(solution)/shard_map/ppermute | solution.py:66
  25.1 3.5 %collective-permute-start = (bf16[800,128]{1,0:T(8,128)(2,1)S(1)}, bf16[800,128]{1,0:T(8,128)(2,1)S(1)}, u32[]{:S(2)}, u32[]{:S(2)}) collective-permute-start(bf16[800,128]{1,0:T(8,128)(2,1)S(1)} %get-tuple-element.49), channel_id=1, source_target_pairs={{0,3},{1,2},{2,1},{3,0},{4,7},{5,6},{6,5},{7,4},{8,11},{9,10},{10,... | collective-permute-start | bytes 614408 | tf_op jit(solution)/shard_map/ppermute | solution.py:74
  28.6 12.8 %collective-permute-start.1 = (bf16[720,128]{1,0:T(8,128)(2,1)S(1)}, bf16[720,128]{1,0:T(8,128)(2,1)S(1)}, u32[]{:S(2)}, u32[]{:S(2)}) collective-permute-start(bf16[720,128]{1,0:T(8,128)(2,1)S(1)} %get-tuple-element.51), channel_id=1, source_target_pairs={{0,508},{1,509},{2,6},{3,7},{4,0},{5,1},{6,10},{7,11},{8,4},{9,5},... | collective-permute-start | bytes 552968 | tf_op jit(solution)/shard_map/ppermute | solution.py:53
  45.4 5.1 %collective-permute-start.9 = (bf16[192,1408]{1,0:T(8,128)(2,1)S(1)}, bf16[192,1408]{1,0:T(8,128)(2,1)S(1)}, u32[]{:S(2)}, u32[]{:S(2)}) collective-permute-start(bf16[192,1408]{1,0:T(8,128)(2,1)S(1)} %get-tuple-element.87), channel_id=1, source_target_pairs={{0,384},{4,388},{8,392},{12,396},{16,400},{20,404},{24,408},{28,41... | collective-permute-start | bytes 1622024 | tf_op jit(solution)/shard_map/ppermute | solution.py:70
  50.6 10.2 %collective-permute-done.8 = bf16[192,1408]{1,0:T(8,128)(2,1)S(1)} collective-permute-done((bf16[192,1408]{1,0:T(8,128)(2,1)S(1)}, bf16[192,1408]{1,0:T(8,128)(2,1)S(1)}, u32[]{:S(2)}, u32[]{:S(2)}) %collective-permute-start.8) | collective-permute-done | bytes 540704 | tf_op jit(solution)/shard_map/ppermute | solution.py:70
  62.8 5.1 %collective-permute-start.11 = (bf16[96,1408]{1,0:T(8,128)(2,1)S(1)}, bf16[96,1408]{1,0:T(8,128)(2,1)S(1)}, u32[]{:S(2)}, u32[]{:S(2)}) collective-permute-start(bf16[96,1408]{1,0:T(8,128)(2,1)S(1)} %slice.14), channel_id=1, source_target_pairs={{0,384},{4,388},{8,392},{12,396},{16,400},{20,404},{24,408},{28,41... | collective-permute-start | bytes 811016 | tf_op jit(solution)/shard_map/ppermute | solution.py:70
  68.1 2.3 %collective-permute-done.10 = bf16[96,1408]{1,0:T(8,128)(2,1)S(1)} collective-permute-done((bf16[96,1408]{1,0:T(8,128)(2,1)S(1)}, bf16[96,1408]{1,0:T(8,128)(2,1)S(1)}, u32[]{:S(2)}, u32[]{:S(2)}) %collective-permute-start.10) | collective-permute-done | bytes 270368 | tf_op jit(solution)/shard_map/ppermute | solution.py:70
  71.9 2.1 %collective-permute-start.12 = (bf16[768,1408]{1,0:T(8,128)(2,1)S(1)}, bf16[768,1408]{1,0:T(8,128)(2,1)S(1)}, u32[]{:S(2)}, u32[]{:S(2)}) collective-permute-start(bf16[768,1408]{1,0:T(8,128)(2,1)S(1)} %constant_dynamic-update-slice_fusion.2.mine), channel_id=1, source_target_pairs={{0,4},{4,0},{8,12},{12,8},{16,20},{20,16},{24,28},{28,24},{32,36},... | collective-permute-start | bytes 6488072 | tf_op jit(solution)/shard_map/ppermute | solution.py:41
  74.0 3.9 %fusion.6 = bf16[704,2744]{1,0:T(8,128)(2,1)S(1)} fusion(bf16[686,2744]{1,0:T(8,128)(2,1)S(1)} %copy-done.2, s32[704]{0:T(1024)S(1)} %select_select_fusion), kind=kOutput, calls=%fused_computation.14 | convolution fusion | flops 2650879488 | bytes 7631136 | tf_op jit(solution)/shard_map/dot_general | solution.py:540
  82.8 2.6 %shard_map.38 = (bf16[1408,128]{1,0:T(8,128)(2,1)S(1)}, f32[8,128]{1,0:T(8,128)S(1)}, bf16[352,128]{1,0:T(8,128)(2,1)S(1)}) custom-call(s32[14]{0:T(128)S(1)} %stack.63.flags, f32[704,128]{1,0:T(8,128)S(1)} %get-tuple-element.47.own, f32[88,128]{1,0:T(8,128)S(1)} %get-tuple-element.48.own_edge, bf16[800,128]{1,0:T(8,128)(2,1)S(1)} %collective-permute-done.received, ...), custom_call_target="tpu_custom_call" | custom-call | flops 18022400 | bytes 2519040 | tf_op jit(solution)/shard_map/pallas_call | solution.py:89
  89.2 6.3 %collective-permute-start.5 = (bf16[352,128]{1,0:T(8,128)(2,1)S(1)}, bf16[352,128]{1,0:T(8,128)(2,1)S(1)}, u32[]{:S(2)}, u32[]{:S(2)}) collective-permute-start(bf16[352,128]{1,0:T(8,128)(2,1)S(1)} %get-tuple-element.58), channel_id=1, source_target_pairs={{0,2},{1,3},{2,0},{3,1},{4,6},{5,7},{6,4},{7,5},{8,10},{9,11},{10,... | collective-permute-start | bytes 270344 | tf_op jit(solution)/shard_map/ppermute | solution.py:78
  95.5 5.9 %collective-permute-done.5.other_bands = bf16[352,128]{1,0:T(8,128)(2,1)S(1)} collective-permute-done((bf16[352,128]{1,0:T(8,128)(2,1)S(1)}, bf16[352,128]{1,0:T(8,128)(2,1)S(1)}, u32[]{:S(2)}, u32[]{:S(2)}) %collective-permute-start.5) | collective-permute-done | bytes 90144 | tf_op jit(solution)/shard_map/ppermute | solution.py:78
  101.4 2.1 %shard_map.39 = (f32[704,128]{1,0:T(8,128)S(1)}, bf16[96,128]{1,0:T(8,128)(2,1)S(1)}, bf16[2816,128]{1,0:T(8,128)(2,1)S(1)}, bf16[2816,128]{1,0:T(8,128)(2,1)S(1)}) custom-call(s32[14]{0:T(128)S(1)} %stack.63.flags, bf16[1408,128]{1,0:T(8,128)(2,1)S(1)} %get-tuple-element.57.lowered, bf16[1408,128]{1,0:T(8,128)(2,1)S(1)} %collective-permute-done.3.other, ...), custom_call_target="tpu_custom_call" | custom-call | flops 1015021568 | bytes 7774208 | tf_op jit(solution)/shard_map/pallas_call | solution.py:89
  103.5 2.9 %shard_map.40 = (f32[704,128]{1,0:T(8,128)S(1)}, f32[704,128]{1,0:T(8,128)S(1)}, bf16[704,128]{1,0:T(8,128)(2,1)S(1)}, bf16[704,128]{1,0:T(8,128)(2,1)S(1)}, bf16[192,128]{1,0:T(8,128)(2,1)S(1)}) custom-call(s32[14]{0:T(128)S(1)} %stack.63.flags, f32[704,128]{1,0:T(8,128)S(1)} %get-tuple-element.63.own, bf16[96,128]{1,0:T(8,128)(2,1)S(1)} %get-tuple-element.64.own_packed, ...), custom_call_target="tpu_custom_call" | custom-call | flops 1015021568 | bytes 8364032 | tf_op jit(solution)/shard_map/pallas_call | solution.py:89
  106.4 6.4 %collective-permute-start.13 = (bf16[704,128]{1,0:T(8,128)(2,1)S(1)}, bf16[704,128]{1,0:T(8,128)(2,1)S(1)}, u32[]{:S(2)}, u32[]{:S(2)}) collective-permute-start(bf16[704,128]{1,0:T(8,128)(2,1)S(1)} %get-tuple-element.74), channel_id=1, source_target_pairs={{0,511},{1,510},{2,509},{3,508},{4,8},{5,9},{6,10},{7,11},{8,4},{9... | collective-permute-start | bytes 540680 | tf_op jit(solution)/shard_map/ppermute | solution.py:62
  112.8 2.3 %all_gather.9.sibling = bf16[1408,128]{1,0:T(8,128)(2,1)S(1)} all-gather(bf16[704,128]{1,0:T(8,128)(2,1)S(1)} %get-tuple-element.70), channel_id=1, replica_groups={{0,4},{8,12},{16,20},{24,28},{32,36},{40,44},{48,52},{56,60},{64,68},{7..., dimensions={0}, use_global_device_ids=true | all-gather | bytes 540672 | tf_op jit(solution)/shard_map/all_gather | solution.py:46
  116.7 6.4 %collective-permute-start.14 = (bf16[704,128]{1,0:T(8,128)(2,1)S(1)}, bf16[704,128]{1,0:T(8,128)(2,1)S(1)}, u32[]{:S(2)}, u32[]{:S(2)}) collective-permute-start(bf16[704,128]{1,0:T(8,128)(2,1)S(1)} %get-tuple-element.78), channel_id=1, source_target_pairs={{0,511},{1,510},{2,509},{3,508},{4,8},{5,9},{6,10},{7,11},{8,4},{9... | collective-permute-start | bytes 540680 | tf_op jit(solution)/shard_map/ppermute | solution.py:62
  124.9 4.0 %collective-permute-start.15 = (bf16[192,128]{1,0:T(8,128)(2,1)S(1)}, bf16[192,128]{1,0:T(8,128)(2,1)S(1)}, u32[]{:S(2)}, u32[]{:S(2)}) collective-permute-start(bf16[192,128]{1,0:T(8,128)(2,1)S(1)} %get-tuple-element.79), channel_id=1, source_target_pairs={{0,3},{1,2},{2,1},{3,0},{4,7},{5,6},{6,5},{7,4},{8,11},{9,10},{10,... | collective-permute-start | bytes 147464 | tf_op jit(solution)/shard_map/ppermute | solution.py:74
  128.8 2.1 %all_gather.10.sibling = bf16[1408,128]{1,0:T(8,128)(2,1)S(1)} all-gather(bf16[704,128]{1,0:T(8,128)(2,1)S(1)} %get-tuple-element.77), channel_id=1, replica_groups={{0,4},{8,12},{16,20},{24,28},{32,36},{40,44},{48,52},{56,60},{64,68},{7..., dimensions={0}, use_global_device_ids=true | all-gather | bytes 540672 | tf_op jit(solution)/shard_map/all_gather | solution.py:46
  131.3 2.2 %shard_map.43.lowered = bf16[1408,128]{1,0:T(8,128)(2,1)S(1)} custom-call(s32[14]{0:T(128)S(1)} %stack.63.flags, f32[704,128]{1,0:T(8,128)S(1)} %get-tuple-element.73.near, f32[704,128]{1,0:T(8,128)S(1)} %get-tuple-element.76.far, bf16[1408,128]{1,0:T(8,128)(2,1)S(1)} %all_gather.10.sibling, bf16[704,128]{1,0:T(8,128)(2,1)S(1)} %collective-permute-done.14.neighbour, ...), custom_call_target="tpu_custom_call" | custom-call | flops 9011200 | bytes 2756608 | tf_op jit(solution)/shard_map/pallas_call | solution.py:89
  133.5 2.5 %collective-permute-start.16 = (bf16[1408,128]{1,0:T(8,128)(2,1)S(1)}, bf16[1408,128]{1,0:T(8,128)(2,1)S(1)}, u32[]{:S(2)}, u32[]{:S(2)}) collective-permute-start(bf16[1408,128]{1,0:T(8,128)(2,1)S(1)} %shard_map.43.lowered), channel_id=1, source_target_pairs={{0,1},{1,0},{2,3},{3,2},{4,5},{5,4},{6,7},{7,6},{8,9},{9,8},{10,11... | collective-permute-start | bytes 1081352 | tf_op jit(solution)/shard_map/ppermute | solution.py:82
  138.1 7.4 %collective-permute-done.16.other = bf16[1408,128]{1,0:T(8,128)(2,1)S(1)} collective-permute-done((bf16[1408,128]{1,0:T(8,128)(2,1)S(1)}, bf16[1408,128]{1,0:T(8,128)(2,1)S(1)}, u32[]{:S(2)}, u32[]{:S(2)}) %collective-permute-start.16) | collective-permute-done | bytes 360480 | tf_op jit(solution)/shard_map/ppermute | solution.py:82
  145.5 2.6 %shard_map.45 = (f32[704,128]{1,0:T(8,128)S(1)}, f32[704,128]{1,0:T(8,128)S(1)}, bf16[704,128]{1,0:T(8,128)(2,1)S(1)}, bf16[704,128]{1,0:T(8,128)(2,1)S(1)}, bf16[192,128]{1,0:T(8,128)(2,1)S(1)}) custom-call(s32[14]{0:T(128)S(1)} %stack.63.flags, bf16[1408,128]{1,0:T(8,128)(2,1)S(1)} %collective-permute-done.16.other, f32[704,128]{1,0:T(8,128)S(1)} %get-tuple-element.80.own, ...), custom_call_target="tpu_custom_call" | custom-call | flops 507510784 | bytes 11616256 | tf_op jit(solution)/shard_map/pallas_call | solution.py:89
  148.1 4.6 %collective-permute-start.17 = (bf16[704,128]{1,0:T(8,128)(2,1)S(1)}, bf16[704,128]{1,0:T(8,128)(2,1)S(1)}, u32[]{:S(2)}, u32[]{:S(2)}) collective-permute-start(bf16[704,128]{1,0:T(8,128)(2,1)S(1)} %get-tuple-element.85), channel_id=1, source_target_pairs={{0,511},{1,510},{2,509},{3,508},{4,8},{5,9},{6,10},{7,11},{8,4},{9... | collective-permute-start | bytes 540680 | tf_op jit(solution)/shard_map/ppermute | solution.py:62
  152.7 3.6 %collective-permute-start.18 = (bf16[192,128]{1,0:T(8,128)(2,1)S(1)}, bf16[192,128]{1,0:T(8,128)(2,1)S(1)}, u32[]{:S(2)}, u32[]{:S(2)}) collective-permute-start(bf16[192,128]{1,0:T(8,128)(2,1)S(1)} %get-tuple-element.86), channel_id=1, source_target_pairs={{0,3},{1,2},{2,1},{3,0},{4,7},{5,6},{6,5},{7,4},{8,11},{9,10},{10,... | collective-permute-start | bytes 147464 | tf_op jit(solution)/shard_map/ppermute | solution.py:74
  156.4 2.1 %all_gather.11.sibling = bf16[1408,128]{1,0:T(8,128)(2,1)S(1)} all-gather(bf16[704,128]{1,0:T(8,128)(2,1)S(1)} %get-tuple-element.84), channel_id=1, replica_groups={{0,4},{8,12},{16,20},{24,28},{32,36},{40,44},{48,52},{56,60},{64,68},{7..., dimensions={0}, use_global_device_ids=true | all-gather | bytes 540672 | tf_op jit(solution)/shard_map/all_gather | solution.py:46
  158.7 3.6 %collective-permute-done.17.neighbour = bf16[704,128]{1,0:T(8,128)(2,1)S(1)} collective-permute-done((bf16[704,128]{1,0:T(8,128)(2,1)S(1)}, bf16[704,128]{1,0:T(8,128)(2,1)S(1)}, u32[]{:S(2)}, u32[]{:S(2)}) %collective-permute-start.17) | collective-permute-done | bytes 180256 | tf_op jit(solution)/shard_map/ppermute | solution.py:62
  165.6 2.3 %shard_map.46.kept = f32[704,128]{1,0:T(8,128)S(1)} custom-call(s32[14]{0:T(128)S(1)} %stack.63.flags, f32[704,128]{1,0:T(8,128)S(1)} %get-tuple-element.82.near, f32[704,128]{1,0:T(8,128)S(1)} %get-tuple-element.83.far, bf16[1408,128]{1,0:T(8,128)(2,1)S(1)} %all_gather.11.sibling, bf16[704,128]{1,0:T(8,128)(2,1)S(1)} %collective-permute-done.17.neighbour, ...), custom_call_target="tpu_custom_call" | custom-call | flops 507510784 | bytes 2756608 | tf_op jit(solution)/shard_map/pallas_call | solution.py:89
  167.9 5.1 %collective-permute-done.19.received = bf16[704,128]{1,0:T(8,128)(2,1)S(1)} collective-permute-done((bf16[704,128]{1,0:T(8,128)(2,1)S(1)}, bf16[704,128]{1,0:T(8,128)(2,1)S(1)}, u32[]{:S(2)}, u32[]{:S(2)}) %collective-permute-start.19) | collective-permute-done | bytes 180256 | tf_op jit(solution)/shard_map/ppermute | solution.py:74
  173.0 2.1 %shard_map.48 = f32[686,1,256]{2,1,0:T(1,128)} custom-call(s32[14]{0:T(128)S(1)} %stack.63.flags, f32[704,128]{1,0:T(8,128)S(1)} %shard_map.46.kept, bf16[704,128]{1,0:T(8,128)(2,1)S(1)} %collective-permute-done.19.received), custom_call_target="tpu_custom_call" | custom-call | flops 126877696 | bytes 1243136 | tf_op jit(solution)/shard_map/pallas_call | solution.py:89
  (57 shorter events, 30.7 us)
Async XLA Ops:
  0.0 6.6 %copy-start.1 = (f32[686,1,256]{2,1,0:T(1,128)S(1)}, f32[686,1,256]{2,1,0:T(1,128)}, u32[]{:S(2)}) copy-start(f32[686,1,256]{2,1,0:T(1,128)} %param.3) | copy-start | bytes 2107396
  2.2 20.9 %copy-start = (s32[1,256]{1,0:T(1,128)S(1)}, s32[1,256]{1,0:T(1,128)}, u32[]{:S(2)}) copy-start(s32[1,256]{1,0:T(1,128)} %solid.1) | copy-start | bytes 3076
  2.9 15.9 %collective-permute-start.6 = (bf16[96,1408]{1,0:T(8,128)(2,1)S(1)}, bf16[96,1408]{1,0:T(8,128)(2,1)S(1)}, u32[]{:S(2)}, u32[]{:S(2)}) collective-permute-start(bf16[96,1408]{1,0:T(8,128)(2,1)S(1)} %pad_maximum_fusion), channel_id=1, source_target_pairs={{0,3},{1,2},{2,1},{3,0},{4,7},{5,6},{6,5},{7,4},{8,11},{9,10},{10,... | collective-permute-start | bytes 811016 | tf_op jit(solution)/shard_map/ppermute | solution.py:74
  18.8 24.6 %collective-permute-start.7 = (bf16[96,1408]{1,0:T(8,128)(2,1)S(1)}, bf16[96,1408]{1,0:T(8,128)(2,1)S(1)}, u32[]{:S(2)}, u32[]{:S(2)}) collective-permute-start(bf16[96,1408]{1,0:T(8,128)(2,1)S(1)} %collective-permute-done.6), channel_id=1, source_target_pairs={{0,8},{4,12},{8,0},{12,4},{16,24},{20,28},{24,16},{28,20},{32,40},... | collective-permute-start | bytes 811016 | tf_op jit(solution)/shard_map/ppermute | solution.py:66
  25.1 25.5 %collective-permute-start = (bf16[800,128]{1,0:T(8,128)(2,1)S(1)}, bf16[800,128]{1,0:T(8,128)(2,1)S(1)}, u32[]{:S(2)}, u32[]{:S(2)}) collective-permute-start(bf16[800,128]{1,0:T(8,128)(2,1)S(1)} %get-tuple-element.49), channel_id=1, source_target_pairs={{0,3},{1,2},{2,1},{3,0},{4,7},{5,6},{6,5},{7,4},{8,11},{9,10},{10,... | collective-permute-start | bytes 614408 | tf_op jit(solution)/shard_map/ppermute | solution.py:74
  28.6 54.2 %collective-permute-start.1 = (bf16[720,128]{1,0:T(8,128)(2,1)S(1)}, bf16[720,128]{1,0:T(8,128)(2,1)S(1)}, u32[]{:S(2)}, u32[]{:S(2)}) collective-permute-start(bf16[720,128]{1,0:T(8,128)(2,1)S(1)} %get-tuple-element.51), channel_id=1, source_target_pairs={{0,508},{1,509},{2,6},{3,7},{4,0},{5,1},{6,10},{7,11},{8,4},{9,5},... | collective-permute-start | bytes 552968 | tf_op jit(solution)/shard_map/ppermute | solution.py:53
  41.4 41.4 %collective-permute-start.2 = (bf16[720,128]{1,0:T(8,128)(2,1)S(1)}, bf16[720,128]{1,0:T(8,128)(2,1)S(1)}, u32[]{:S(2)}, u32[]{:S(2)}) collective-permute-start(bf16[720,128]{1,0:T(8,128)(2,1)S(1)} %get-tuple-element.52), channel_id=1, source_target_pairs={{0,511},{1,510},{2,5},{3,4},{4,3},{5,2},{6,9},{7,8},{8,7},{9,6},{1... | collective-permute-start | bytes 552968 | tf_op jit(solution)/shard_map/ppermute | solution.py:53
  43.5 17.3 %collective-permute-start.8 = (bf16[192,1408]{1,0:T(8,128)(2,1)S(1)}, bf16[192,1408]{1,0:T(8,128)(2,1)S(1)}, u32[]{:S(2)}, u32[]{:S(2)}) collective-permute-start(bf16[192,1408]{1,0:T(8,128)(2,1)S(1)} %get-tuple-element.87), channel_id=1, source_target_pairs={{0,128},{4,132},{8,136},{12,140},{16,144},{20,148},{24,152},{28,15... | collective-permute-start | bytes 1622024 | tf_op jit(solution)/shard_map/ppermute | solution.py:70
  45.4 17.4 %collective-permute-start.9 = (bf16[192,1408]{1,0:T(8,128)(2,1)S(1)}, bf16[192,1408]{1,0:T(8,128)(2,1)S(1)}, u32[]{:S(2)}, u32[]{:S(2)}) collective-permute-start(bf16[192,1408]{1,0:T(8,128)(2,1)S(1)} %get-tuple-element.87), channel_id=1, source_target_pairs={{0,384},{4,388},{8,392},{12,396},{16,400},{20,404},{24,408},{28,41... | collective-permute-start | bytes 1622024 | tf_op jit(solution)/shard_map/ppermute | solution.py:70
  50.6 23.4 %copy-start.2 = (bf16[686,2744]{1,0:T(8,128)(2,1)S(1)}, bf16[686,2744]{1,0:T(8,128)(2,1)}, u32[]{:S(2)}) copy-start(bf16[686,2744]{1,0:T(8,128)(2,1)} %param.5) | copy-start | bytes 11294308
  60.8 9.6 %collective-permute-start.10 = (bf16[96,1408]{1,0:T(8,128)(2,1)S(1)}, bf16[96,1408]{1,0:T(8,128)(2,1)S(1)}, u32[]{:S(2)}, u32[]{:S(2)}) collective-permute-start(bf16[96,1408]{1,0:T(8,128)(2,1)S(1)} %slice.13), channel_id=1, source_target_pairs={{0,128},{4,132},{8,136},{12,140},{16,144},{20,148},{24,152},{28,15... | collective-permute-start | bytes 811016 | tf_op jit(solution)/shard_map/ppermute | solution.py:70
  62.8 9.1 %collective-permute-start.11 = (bf16[96,1408]{1,0:T(8,128)(2,1)S(1)}, bf16[96,1408]{1,0:T(8,128)(2,1)S(1)}, u32[]{:S(2)}, u32[]{:S(2)}) collective-permute-start(bf16[96,1408]{1,0:T(8,128)(2,1)S(1)} %slice.14), channel_id=1, source_target_pairs={{0,384},{4,388},{8,392},{12,396},{16,400},{20,404},{24,408},{28,41... | collective-permute-start | bytes 811016 | tf_op jit(solution)/shard_map/ppermute | solution.py:70
  71.9 31.6 %collective-permute-start.12 = (bf16[768,1408]{1,0:T(8,128)(2,1)S(1)}, bf16[768,1408]{1,0:T(8,128)(2,1)S(1)}, u32[]{:S(2)}, u32[]{:S(2)}) collective-permute-start(bf16[768,1408]{1,0:T(8,128)(2,1)S(1)} %constant_dynamic-update-slice_fusion.2.mine), channel_id=1, source_target_pairs={{0,4},{4,0},{8,12},{12,8},{16,20},{20,16},{24,28},{28,24},{32,36},... | collective-permute-start | bytes 6488072 | tf_op jit(solution)/shard_map/ppermute | solution.py:41
  85.4 16.1 %collective-permute-start.3 = (bf16[1408,128]{1,0:T(8,128)(2,1)S(1)}, bf16[1408,128]{1,0:T(8,128)(2,1)S(1)}, u32[]{:S(2)}, u32[]{:S(2)}) collective-permute-start(bf16[1408,128]{1,0:T(8,128)(2,1)S(1)} %get-tuple-element.57.lowered), channel_id=1, source_target_pairs={{0,1},{1,0},{2,3},{3,2},{4,5},{5,4},{6,7},{7,6},{8,9},{9,8},{10,11... | collective-permute-start | bytes 1081352 | tf_op jit(solution)/shard_map/ppermute | solution.py:82
  87.3 8.2 %collective-permute-start.4 = (bf16[352,128]{1,0:T(8,128)(2,1)S(1)}, bf16[352,128]{1,0:T(8,128)(2,1)S(1)}, u32[]{:S(2)}, u32[]{:S(2)}) collective-permute-start(bf16[352,128]{1,0:T(8,128)(2,1)S(1)} %get-tuple-element.58), channel_id=1, source_target_pairs={{0,3},{1,2},{2,1},{3,0},{4,7},{5,6},{6,5},{7,4},{8,11},{9,10},{10,... | collective-permute-start | bytes 270344 | tf_op jit(solution)/shard_map/ppermute | solution.py:74
  89.2 12.2 %collective-permute-start.5 = (bf16[352,128]{1,0:T(8,128)(2,1)S(1)}, bf16[352,128]{1,0:T(8,128)(2,1)S(1)}, u32[]{:S(2)}, u32[]{:S(2)}) collective-permute-start(bf16[352,128]{1,0:T(8,128)(2,1)S(1)} %get-tuple-element.58), channel_id=1, source_target_pairs={{0,2},{1,3},{2,0},{3,1},{4,6},{5,7},{6,4},{7,5},{8,10},{9,11},{10,... | collective-permute-start | bytes 270344 | tf_op jit(solution)/shard_map/ppermute | solution.py:78
  106.4 16.7 %collective-permute-start.13 = (bf16[704,128]{1,0:T(8,128)(2,1)S(1)}, bf16[704,128]{1,0:T(8,128)(2,1)S(1)}, u32[]{:S(2)}, u32[]{:S(2)}) collective-permute-start(bf16[704,128]{1,0:T(8,128)(2,1)S(1)} %get-tuple-element.74), channel_id=1, source_target_pairs={{0,511},{1,510},{2,509},{3,508},{4,8},{5,9},{6,10},{7,11},{8,4},{9... | collective-permute-start | bytes 540680 | tf_op jit(solution)/shard_map/ppermute | solution.py:62
  116.7 14.6 %collective-permute-start.14 = (bf16[704,128]{1,0:T(8,128)(2,1)S(1)}, bf16[704,128]{1,0:T(8,128)(2,1)S(1)}, u32[]{:S(2)}, u32[]{:S(2)}) collective-permute-start(bf16[704,128]{1,0:T(8,128)(2,1)S(1)} %get-tuple-element.78), channel_id=1, source_target_pairs={{0,511},{1,510},{2,509},{3,508},{4,8},{5,9},{6,10},{7,11},{8,4},{9... | collective-permute-start | bytes 540680 | tf_op jit(solution)/shard_map/ppermute | solution.py:62
  124.9 6.5 %collective-permute-start.15 = (bf16[192,128]{1,0:T(8,128)(2,1)S(1)}, bf16[192,128]{1,0:T(8,128)(2,1)S(1)}, u32[]{:S(2)}, u32[]{:S(2)}) collective-permute-start(bf16[192,128]{1,0:T(8,128)(2,1)S(1)} %get-tuple-element.79), channel_id=1, source_target_pairs={{0,3},{1,2},{2,1},{3,0},{4,7},{5,6},{6,5},{7,4},{8,11},{9,10},{10,... | collective-permute-start | bytes 147464 | tf_op jit(solution)/shard_map/ppermute | solution.py:74
  133.5 12.0 %collective-permute-start.16 = (bf16[1408,128]{1,0:T(8,128)(2,1)S(1)}, bf16[1408,128]{1,0:T(8,128)(2,1)S(1)}, u32[]{:S(2)}, u32[]{:S(2)}) collective-permute-start(bf16[1408,128]{1,0:T(8,128)(2,1)S(1)} %shard_map.43.lowered), channel_id=1, source_target_pairs={{0,1},{1,0},{2,3},{3,2},{4,5},{5,4},{6,7},{7,6},{8,9},{9,8},{10,11... | collective-permute-start | bytes 1081352 | tf_op jit(solution)/shard_map/ppermute | solution.py:82
  148.1 14.1 %collective-permute-start.17 = (bf16[704,128]{1,0:T(8,128)(2,1)S(1)}, bf16[704,128]{1,0:T(8,128)(2,1)S(1)}, u32[]{:S(2)}, u32[]{:S(2)}) collective-permute-start(bf16[704,128]{1,0:T(8,128)(2,1)S(1)} %get-tuple-element.85), channel_id=1, source_target_pairs={{0,511},{1,510},{2,509},{3,508},{4,8},{5,9},{6,10},{7,11},{8,4},{9... | collective-permute-start | bytes 540680 | tf_op jit(solution)/shard_map/ppermute | solution.py:62
  152.7 6.0 %collective-permute-start.18 = (bf16[192,128]{1,0:T(8,128)(2,1)S(1)}, bf16[192,128]{1,0:T(8,128)(2,1)S(1)}, u32[]{:S(2)}, u32[]{:S(2)}) collective-permute-start(bf16[192,128]{1,0:T(8,128)(2,1)S(1)} %get-tuple-element.86), channel_id=1, source_target_pairs={{0,3},{1,2},{2,1},{3,0},{4,7},{5,6},{6,5},{7,4},{8,11},{9,10},{10,... | collective-permute-start | bytes 147464 | tf_op jit(solution)/shard_map/ppermute | solution.py:74
  163.7 9.3 %collective-permute-start.19 = (bf16[704,128]{1,0:T(8,128)(2,1)S(1)}, bf16[704,128]{1,0:T(8,128)(2,1)S(1)}, u32[]{:S(2)}, u32[]{:S(2)}) collective-permute-start(bf16[704,128]{1,0:T(8,128)(2,1)S(1)} %shard_map.47), channel_id=1, source_target_pairs={{0,3},{1,2},{2,1},{3,0},{4,7},{5,6},{6,5},{7,4},{8,11},{9,10},{10,... | collective-permute-start | bytes 540680 | tf_op jit(solution)/shard_map/ppermute | solution.py:74

commit v11 on v10

--- a/solution.py
+++ b/solution.py
@@ -578,12 +578,6 @@
     piece = jnp.concatenate(column_half(window, core), axis=1)
     populations, piece = lax.optimization_barrier((populations, piece))
     piece = to_mirror(piece)
-    pair = jnp.concatenate([piece, to_next_z(piece)], axis=0)
-    below, above = along_x(pair, 1), along_x(pair, -1)
-    beyond = along_x(below[:PIECE], 1), along_x(above[PIECE:], -1)
-    mine = jnp.concatenate([pair, below, above, *beyond], axis=0)
-    theirs = to_sibling(mine)
-
     padded = jnp.pad(populations[:, 0, :], ((0, PAD - ROWS), (0, 0)))
     rows = (PAD, LANES)
     own, own_edge, message, straight, turned, masks, factors = call(
@@ -592,14 +586,18 @@
          ((PAD + 16, LANES), BF16), ((PAD + 16, LANES), BF16), ((8, LANES), F32), ((3, *rows), F32)],
         flags, padded, solid_mask, flops=2 * 3 * PAD * PAD * 256,
     )
+    received = to_mirror(message)
+    piece, straight, turned = lax.optimization_barrier((piece, straight, turned))
+    pair = jnp.concatenate([piece, to_next_z(piece)], axis=0)
     straight, turned = to_layer(straight, False), to_layer(turned, True)
-    received = to_mirror(message)
 
     row = lax.iota(jnp.int32, PAD)
     wanted = jnp.where(row < ROWS, jnp.where(low == 1, row, ROWS - 1 - row), -1)
-    received, collision = lax.optimization_barrier((received, collision))
+    piece, collision = lax.optimization_barrier((piece, collision))
     ordered = padded_columns(chosen(place(ROWS, PAD, wanted).T, collision))
 
+    pair, ordered = lax.optimization_barrier((pair, ordered))
+    below, above = along_x(pair, 1), along_x(pair, -1)
     matrix = *column_half(ordered, 0), *column_half(ordered, 1)
     turned, *matrix = lax.optimization_barrier((turned, *matrix))
     lowered, masks, bands = call(
@@ -612,6 +610,8 @@
     multiply = 2 * PAD * 4 * PAD * LANES
     work = 100 * PAD * LANES
 
+    below, above, lowered = lax.optimization_barrier((below, above, lowered))
+    beyond = along_x(below[:PIECE], 1), along_x(above[PIECE:], -1)
     other = to_side(lowered)
     bands = to_mirror(bands), to_opposite(bands)
     wide = ((4 * PAD, LANES), BF16)
@@ -619,6 +619,9 @@
         collide_kernel, [(rows, F32), ((EDGE, LANES), BF16), wide, wide],
         flags, lowered, other, *bands, factors, *matrix, flops=2 * multiply,
     )
+    *beyond, own = lax.optimization_barrier((*beyond, own))
+    mine = jnp.concatenate([pair, below, above, *beyond], axis=0)
+    theirs = to_sibling(mine)
     near, far, for_sibling, for_neighbour, edges = call(
         collide_partner_kernel, sends,
         flags, own, own_packed, all_rows, all_bands, factors, mine, theirs,

time: 176 us -> 167 us (0.949)
  the two profiles are of different devices: /device:TPU:8 before, /device:TPU:16 now
where the time goes in v11:
time: 167 us
  starting transfers between devices  83.9 us (50%)
  waiting for transfers between devices  36.1 us (22%)
  Pallas kernels  25.7 us (15%)
  matrix products  12.9 us (8%)
  blocking collectives  6.19 us (4%)
    ppermute x6, starting transfers between devices, to_mirror(): return lax.ppermute(array, 'vel', [(i, 3 - i) for i in range(4)])  32.2 us
    pallas_call x12, Pallas kernels, call(): pl.pallas_call(kernel, out_shape=[jax.ShapeDtypeStruct(shape, dtype) for...  25.7 us
    ppermute x6, waiting for transfers between devices, to_mirror(): return lax.ppermute(array, 'vel', [(i, 3 - i) for i in range(4)])  17.8 us
    ppermute x3, starting transfers between devices, to_neighbour(): return lax.ppermute(array, BOTH, pairs_of(neighbour_of))  16.2 us
    ppermute x4, starting transfers between devices, along_x(): lax.ppermute(array, 'cells', [(cell, (cell + 32 * step) % 128) for cell i...  16 us
    dot_general x8, matrix products, chosen(): return jnp.dot(left, right, preferred_element_type=BF16)  12.9 us
    ppermute x2, waiting for transfers between devices, to_side(): return lax.ppermute(array, 'vel', [(i, i ^ 1) for i in range(4)])  7.83 us
    all_gather x3, blocking collectives, with_sibling(): lax.all_gather(array, 'cells', axis=0, tiled=True, axis_index_groups=groups)  6.19 us
  transfers between devices with their start and end apart: 20, of which 8 were waited for; matrix products, arithmetic and copies ran while one was open for 7% of the time, Pallas kernels for 9%

profile of v11, /device:TPU:16, one launch (start us, length us, event | category | flops | bytes accessed | tf_op | source)
XLA Modules:
  0.0 166.6 jit_solution(4936713936392582588)
XLA Ops:
  2.9 2.4 %collective-permute-start = (bf16[96,1408]{1,0:T(8,128)(2,1)S(1)}, bf16[96,1408]{1,0:T(8,128)(2,1)S(1)}, u32[]{:S(2)}, u32[]{:S(2)}) collective-permute-start(bf16[96,1408]{1,0:T(8,128)(2,1)S(1)} %pad_maximum_fusion.1), channel_id=1, source_target_pairs={{0,3},{1,2},{2,1},{3,0},{4,7},{5,6},{6,5},{7,4},{8,11},{9,10},{10,... | collective-permute-start | bytes 811016 | tf_op jit(solution)/shard_map/ppermute | solution.py:74
  7.7 3.5 %collective-permute-start.4 = (bf16[800,128]{1,0:T(8,128)(2,1)S(1)}, bf16[800,128]{1,0:T(8,128)(2,1)S(1)}, u32[]{:S(2)}, u32[]{:S(2)}) collective-permute-start(bf16[800,128]{1,0:T(8,128)(2,1)S(1)} %get-tuple-element.65), channel_id=1, source_target_pairs={{0,3},{1,2},{2,1},{3,0},{4,7},{5,6},{6,5},{7,4},{8,11},{9,10},{10,... | collective-permute-start | bytes 614408 | tf_op jit(solution)/shard_map/ppermute | solution.py:74
  11.2 13.1 %collective-permute-done = bf16[96,1408]{1,0:T(8,128)(2,1)S(1)} collective-permute-done((bf16[96,1408]{1,0:T(8,128)(2,1)S(1)}, bf16[96,1408]{1,0:T(8,128)(2,1)S(1)}, u32[]{:S(2)}, u32[]{:S(2)}) %collective-permute-start) | collective-permute-done | bytes 270368 | tf_op jit(solution)/shard_map/ppermute | solution.py:74
  24.4 4.3 %collective-permute-start.1 = (bf16[96,1408]{1,0:T(8,128)(2,1)S(1)}, bf16[96,1408]{1,0:T(8,128)(2,1)S(1)}, u32[]{:S(2)}, u32[]{:S(2)}) collective-permute-start(bf16[96,1408]{1,0:T(8,128)(2,1)S(1)} %collective-permute-done), channel_id=1, source_target_pairs={{0,8},{4,12},{8,0},{12,4},{16,24},{20,28},{24,16},{28,20},{32,40},... | collective-permute-start | bytes 811016 | tf_op jit(solution)/shard_map/ppermute | solution.py:66
  30.6 3.7 %collective-permute-start.5 = (bf16[720,128]{1,0:T(8,128)(2,1)S(1)}, bf16[720,128]{1,0:T(8,128)(2,1)S(1)}, u32[]{:S(2)}, u32[]{:S(2)}) collective-permute-start(bf16[720,128]{1,0:T(8,128)(2,1)S(1)} %get-tuple-element.66), channel_id=1, source_target_pairs={{0,508},{1,509},{2,6},{3,7},{4,0},{5,1},{6,10},{7,11},{8,4},{9,5},... | collective-permute-start | bytes 552968 | tf_op jit(solution)/shard_map/ppermute | solution.py:53
  34.3 5.4 %fusion.6 = bf16[704,2744]{1,0:T(8,128)(2,1)S(1)} fusion(bf16[686,2744]{1,0:T(8,128)(2,1)} %param.5, s32[704]{0:T(1024)S(1)} %select_select_fusion), kind=kOutput, calls=%fused_computation.13 | convolution fusion | flops 2650879488 | bytes 7631136 | tf_op jit(solution)/shard_map/dot_general | solution.py:540
  40.1 5.6 %collective-permute-start.2 = (bf16[192,1408]{1,0:T(8,128)(2,1)S(1)}, bf16[192,1408]{1,0:T(8,128)(2,1)S(1)}, u32[]{:S(2)}, u32[]{:S(2)}) collective-permute-start(bf16[192,1408]{1,0:T(8,128)(2,1)S(1)} %pad_maximum_fusion), channel_id=1, source_target_pairs={{0,128},{4,132},{8,136},{12,140},{16,144},{20,148},{24,152},{28,15... | collective-permute-start | bytes 1622024 | tf_op jit(solution)/shard_map/ppermute | solution.py:70
  45.6 3.4 %collective-permute-start.3 = (bf16[192,1408]{1,0:T(8,128)(2,1)S(1)}, bf16[192,1408]{1,0:T(8,128)(2,1)S(1)}, u32[]{:S(2)}, u32[]{:S(2)}) collective-permute-start(bf16[192,1408]{1,0:T(8,128)(2,1)S(1)} %pad_maximum_fusion), channel_id=1, source_target_pairs={{0,384},{4,388},{8,392},{12,396},{16,400},{20,404},{24,408},{28,41... | collective-permute-start | bytes 1622024 | tf_op jit(solution)/shard_map/ppermute | solution.py:70
  53.9 2.6 %shard_map.38 = (bf16[1408,128]{1,0:T(8,128)(2,1)S(1)}, f32[8,128]{1,0:T(8,128)S(1)}, bf16[352,128]{1,0:T(8,128)(2,1)S(1)}) custom-call(s32[14]{0:T(128)S(1)} %stack.63.flags, f32[704,128]{1,0:T(8,128)S(1)} %get-tuple-element.63.own, f32[88,128]{1,0:T(8,128)S(1)} %get-tuple-element.64.own_edge, bf16[800,128]{1,0:T(8,128)(2,1)S(1)} %collective-permute-done.4.received, ...), custom_call_target="tpu_custom_call" | custom-call | flops 18022400 | bytes 2519040 | tf_op jit(solution)/shard_map/pallas_call | solution.py:89
  56.5 17.0 %collective-permute-start.10 = (bf16[352,128]{1,0:T(8,128)(2,1)S(1)}, bf16[352,128]{1,0:T(8,128)(2,1)S(1)}, u32[]{:S(2)}, u32[]{:S(2)}) collective-permute-start(bf16[352,128]{1,0:T(8,128)(2,1)S(1)} %get-tuple-element.76), channel_id=1, source_target_pairs={{0,3},{1,2},{2,1},{3,0},{4,7},{5,6},{6,5},{7,4},{8,11},{9,10},{10,... | collective-permute-start | bytes 270344 | tf_op jit(solution)/shard_map/ppermute | solution.py:74
  75.5 3.4 %collective-permute-start.9 = (bf16[1408,128]{1,0:T(8,128)(2,1)S(1)}, bf16[1408,128]{1,0:T(8,128)(2,1)S(1)}, u32[]{:S(2)}, u32[]{:S(2)}) collective-permute-start(bf16[1408,128]{1,0:T(8,128)(2,1)S(1)} %get-tuple-element.75.lowered), channel_id=1, source_target_pairs={{0,1},{1,0},{2,3},{3,2},{4,5},{5,4},{6,7},{7,6},{8,9},{9,8},{10,11... | collective-permute-start | bytes 1081352 | tf_op jit(solution)/shard_map/ppermute | solution.py:82
  80.9 5.1 %collective-permute-start.8 = (bf16[96,1408]{1,0:T(8,128)(2,1)S(1)}, bf16[96,1408]{1,0:T(8,128)(2,1)S(1)}, u32[]{:S(2)}, u32[]{:S(2)}) collective-permute-start(bf16[96,1408]{1,0:T(8,128)(2,1)S(1)} %slice.9), channel_id=1, source_target_pairs={{0,384},{4,388},{8,392},{12,396},{16,400},{20,404},{24,408},{28,41... | collective-permute-start | bytes 811016 | tf_op jit(solution)/shard_map/ppermute | solution.py:70
  86.2 2.1 %shard_map.39 = (f32[704,128]{1,0:T(8,128)S(1)}, bf16[96,128]{1,0:T(8,128)(2,1)S(1)}, bf16[2816,128]{1,0:T(8,128)(2,1)S(1)}, bf16[2816,128]{1,0:T(8,128)(2,1)S(1)}) custom-call(s32[14]{0:T(128)S(1)} %stack.63.flags, bf16[1408,128]{1,0:T(8,128)(2,1)S(1)} %get-tuple-element.75.lowered, bf16[1408,128]{1,0:T(8,128)(2,1)S(1)} %collective-permute-done.9.other, ...), custom_call_target="tpu_custom_call" | custom-call | flops 1015021568 | bytes 7774208 | tf_op jit(solution)/shard_map/pallas_call | solution.py:89
  92.0 4.2 %collective-permute-done.12.theirs = bf16[768,1408]{1,0:T(8,128)(2,1)S(1)} collective-permute-done((bf16[768,1408]{1,0:T(8,128)(2,1)S(1)}, bf16[768,1408]{1,0:T(8,128)(2,1)S(1)}, u32[]{:S(2)}, u32[]{:S(2)}) %collective-permute-start.12) | collective-permute-done | bytes 2162720 | tf_op jit(solution)/shard_map/ppermute | solution.py:41
  96.2 2.9 %shard_map.40 = (f32[704,128]{1,0:T(8,128)S(1)}, f32[704,128]{1,0:T(8,128)S(1)}, bf16[704,128]{1,0:T(8,128)(2,1)S(1)}, bf16[704,128]{1,0:T(8,128)(2,1)S(1)}, bf16[192,128]{1,0:T(8,128)(2,1)S(1)}) custom-call(s32[14]{0:T(128)S(1)} %stack.63.flags, f32[704,128]{1,0:T(8,128)S(1)} %get-tuple-element.82.own, bf16[96,128]{1,0:T(8,128)(2,1)S(1)} %get-tuple-element.83.own_packed, ...), custom_call_target="tpu_custom_call" | custom-call | flops 1015021568 | bytes 8364032 | tf_op jit(solution)/shard_map/pallas_call | solution.py:89
  99.1 4.6 %collective-permute-start.13 = (bf16[704,128]{1,0:T(8,128)(2,1)S(1)}, bf16[704,128]{1,0:T(8,128)(2,1)S(1)}, u32[]{:S(2)}, u32[]{:S(2)}) collective-permute-start(bf16[704,128]{1,0:T(8,128)(2,1)S(1)} %get-tuple-element.94), channel_id=1, source_target_pairs={{0,511},{1,510},{2,509},{3,508},{4,8},{5,9},{6,10},{7,11},{8,4},{9... | collective-permute-start | bytes 540680 | tf_op jit(solution)/shard_map/ppermute | solution.py:62
  103.7 2.1 %all_gather.9.sibling = bf16[1408,128]{1,0:T(8,128)(2,1)S(1)} all-gather(bf16[704,128]{1,0:T(8,128)(2,1)S(1)} %get-tuple-element.90), channel_id=1, replica_groups={{0,4},{8,12},{16,20},{24,28},{32,36},{40,44},{48,52},{56,60},{64,68},{7..., dimensions={0}, use_global_device_ids=true | all-gather | bytes 540672 | tf_op jit(solution)/shard_map/all_gather | solution.py:46
  107.4 8.4 %collective-permute-start.14 = (bf16[704,128]{1,0:T(8,128)(2,1)S(1)}, bf16[704,128]{1,0:T(8,128)(2,1)S(1)}, u32[]{:S(2)}, u32[]{:S(2)}) collective-permute-start(bf16[704,128]{1,0:T(8,128)(2,1)S(1)} %get-tuple-element.98), channel_id=1, source_target_pairs={{0,511},{1,510},{2,509},{3,508},{4,8},{5,9},{6,10},{7,11},{8,4},{9... | collective-permute-start | bytes 540680 | tf_op jit(solution)/shard_map/ppermute | solution.py:62
  117.5 3.9 %collective-permute-start.15 = (bf16[192,128]{1,0:T(8,128)(2,1)S(1)}, bf16[192,128]{1,0:T(8,128)(2,1)S(1)}, u32[]{:S(2)}, u32[]{:S(2)}) collective-permute-start(bf16[192,128]{1,0:T(8,128)(2,1)S(1)} %get-tuple-element.99), channel_id=1, source_target_pairs={{0,3},{1,2},{2,1},{3,0},{4,7},{5,6},{6,5},{7,4},{8,11},{9,10},{10,... | collective-permute-start | bytes 147464 | tf_op jit(solution)/shard_map/ppermute | solution.py:74
  121.5 2.1 %all_gather.10.sibling = bf16[1408,128]{1,0:T(8,128)(2,1)S(1)} all-gather(bf16[704,128]{1,0:T(8,128)(2,1)S(1)} %get-tuple-element.97), channel_id=1, replica_groups={{0,4},{8,12},{16,20},{24,28},{32,36},{40,44},{48,52},{56,60},{64,68},{7..., dimensions={0}, use_global_device_ids=true | all-gather | bytes 540672 | tf_op jit(solution)/shard_map/all_gather | solution.py:46
  123.6 2.3 %shard_map.43.lowered = bf16[1408,128]{1,0:T(8,128)(2,1)S(1)} custom-call(s32[14]{0:T(128)S(1)} %stack.63.flags, f32[704,128]{1,0:T(8,128)S(1)} %get-tuple-element.93.near, f32[704,128]{1,0:T(8,128)S(1)} %get-tuple-element.96.far, bf16[1408,128]{1,0:T(8,128)(2,1)S(1)} %all_gather.10.sibling, bf16[704,128]{1,0:T(8,128)(2,1)S(1)} %collective-permute-done.14.neighbour, ...), custom_call_target="tpu_custom_call" | custom-call | flops 9011200 | bytes 2756608 | tf_op jit(solution)/shard_map/pallas_call | solution.py:89
  125.8 2.4 %collective-permute-start.16 = (bf16[1408,128]{1,0:T(8,128)(2,1)S(1)}, bf16[1408,128]{1,0:T(8,128)(2,1)S(1)}, u32[]{:S(2)}, u32[]{:S(2)}) collective-permute-start(bf16[1408,128]{1,0:T(8,128)(2,1)S(1)} %shard_map.43.lowered), channel_id=1, source_target_pairs={{0,1},{1,0},{2,3},{3,2},{4,5},{5,4},{6,7},{7,6},{8,9},{9,8},{10,11... | collective-permute-start | bytes 1081352 | tf_op jit(solution)/shard_map/ppermute | solution.py:82
  128.3 2.1 %shard_map.44 = (f32[704,128]{1,0:T(8,128)S(1)}, f32[768,128]{1,0:T(8,128)S(1)}) custom-call(s32[14]{0:T(128)S(1)} %stack.63.flags, bf16[1408,128]{1,0:T(8,128)(2,1)S(1)} %shard_map.43.lowered, bf16[704,704]{1,0:T(8,128)(2,1)S(1)} %fusion.3.m0, bf16[704,704]{1,0:T(8,128)(2,1)S(1)} %fusion.m1, bf16[704,704]{1,0:T(8,128)(2,1)S(1)} %fusion.4.m2, ...), custom_call_target="tpu_custom_call" | custom-call | flops 507510784 | bytes 9404416 | tf_op jit(solution)/shard_map/pallas_call | solution.py:89
  130.4 7.8 %collective-permute-done.16.other = bf16[1408,128]{1,0:T(8,128)(2,1)S(1)} collective-permute-done((bf16[1408,128]{1,0:T(8,128)(2,1)S(1)}, bf16[1408,128]{1,0:T(8,128)(2,1)S(1)}, u32[]{:S(2)}, u32[]{:S(2)}) %collective-permute-start.16) | collective-permute-done | bytes 360480 | tf_op jit(solution)/shard_map/ppermute | solution.py:82
  138.2 2.7 %shard_map.45 = (f32[704,128]{1,0:T(8,128)S(1)}, f32[704,128]{1,0:T(8,128)S(1)}, bf16[704,128]{1,0:T(8,128)(2,1)S(1)}, bf16[704,128]{1,0:T(8,128)(2,1)S(1)}, bf16[192,128]{1,0:T(8,128)(2,1)S(1)}) custom-call(s32[14]{0:T(128)S(1)} %stack.63.flags, bf16[1408,128]{1,0:T(8,128)(2,1)S(1)} %collective-permute-done.16.other, ...), custom_call_target="tpu_custom_call" | custom-call | flops 507510784 | bytes 11616256 | tf_op jit(solution)/shard_map/pallas_call | solution.py:89
  140.8 3.2 %collective-permute-start.17 = (bf16[704,128]{1,0:T(8,128)(2,1)S(1)}, bf16[704,128]{1,0:T(8,128)(2,1)S(1)}, u32[]{:S(2)}, u32[]{:S(2)}) collective-permute-start(bf16[704,128]{1,0:T(8,128)(2,1)S(1)} %get-tuple-element.105), channel_id=1, source_target_pairs={{0,511},{1,510},{2,509},{3,508},{4,8},{5,9},{6,10},{7,11},{8,4},{9... | collective-permute-start | bytes 540680 | tf_op jit(solution)/shard_map/ppermute | solution.py:62
  144.1 3.5 %collective-permute-start.18 = (bf16[192,128]{1,0:T(8,128)(2,1)S(1)}, bf16[192,128]{1,0:T(8,128)(2,1)S(1)}, u32[]{:S(2)}, u32[]{:S(2)}) collective-permute-start(bf16[192,128]{1,0:T(8,128)(2,1)S(1)} %get-tuple-element.106), channel_id=1, source_target_pairs={{0,3},{1,2},{2,1},{3,0},{4,7},{5,6},{6,5},{7,4},{8,11},{9,10},{10,... | collective-permute-start | bytes 147464 | tf_op jit(solution)/shard_map/ppermute | solution.py:74
  147.6 2.1 %all_gather.11.sibling = bf16[1408,128]{1,0:T(8,128)(2,1)S(1)} all-gather(bf16[704,128]{1,0:T(8,128)(2,1)S(1)} %get-tuple-element.104), channel_id=1, replica_groups={{0,4},{8,12},{16,20},{24,28},{32,36},{40,44},{48,52},{56,60},{64,68},{7..., dimensions={0}, use_global_device_ids=true | all-gather | bytes 540672 | tf_op jit(solution)/shard_map/all_gather | solution.py:46
  150.5 4.4 %collective-permute-done.17.neighbour = bf16[704,128]{1,0:T(8,128)(2,1)S(1)} collective-permute-done((bf16[704,128]{1,0:T(8,128)(2,1)S(1)}, bf16[704,128]{1,0:T(8,128)(2,1)S(1)}, u32[]{:S(2)}, u32[]{:S(2)}) %collective-permute-start.17) | collective-permute-done | bytes 180256 | tf_op jit(solution)/shard_map/ppermute | solution.py:62
  158.3 2.3 %shard_map.46.kept = f32[704,128]{1,0:T(8,128)S(1)} custom-call(s32[14]{0:T(128)S(1)} %stack.63.flags, f32[704,128]{1,0:T(8,128)S(1)} %get-tuple-element.102.near, f32[704,128]{1,0:T(8,128)S(1)} %get-tuple-element.103.far, bf16[1408,128]{1,0:T(8,128)(2,1)S(1)} %all_gather.11.sibling, bf16[704,128]{1,0:T(8,128)(2,1)S(1)} %collective-permute-done.17.neighbour, ...), custom_call_target="tpu_custom_call" | custom-call | flops 507510784 | bytes 2756608 | tf_op jit(solution)/shard_map/pallas_call | solution.py:89
  160.6 3.9 %collective-permute-done.19.received = bf16[704,128]{1,0:T(8,128)(2,1)S(1)} collective-permute-done((bf16[704,128]{1,0:T(8,128)(2,1)S(1)}, bf16[704,128]{1,0:T(8,128)(2,1)S(1)}, u32[]{:S(2)}, u32[]{:S(2)}) %collective-permute-start.19) | collective-permute-done | bytes 180256 | tf_op jit(solution)/shard_map/ppermute | solution.py:74
  164.5 2.1 %shard_map.48 = f32[686,1,256]{2,1,0:T(1,128)} custom-call(s32[14]{0:T(128)S(1)} %stack.63.flags, f32[704,128]{1,0:T(8,128)S(1)} %shard_map.46.kept, bf16[704,128]{1,0:T(8,128)(2,1)S(1)} %collective-permute-done.19.received), custom_call_target="tpu_custom_call" | custom-call | flops 126877696 | bytes 1243136 | tf_op jit(solution)/shard_map/pallas_call | solution.py:89
  (56 shorter events, 27.5 us)
Async XLA Ops:
  0.0 5.4 %copy-start.1 = (f32[686,1,256]{2,1,0:T(1,128)S(1)}, f32[686,1,256]{2,1,0:T(1,128)}, u32[]{:S(2)}) copy-start(f32[686,1,256]{2,1,0:T(1,128)} %param.3) | copy-start | bytes 2107396
  2.2 3.5 %copy-start = (s32[1,256]{1,0:T(1,128)S(1)}, s32[1,256]{1,0:T(1,128)}, u32[]{:S(2)}) copy-start(s32[1,256]{1,0:T(1,128)} %solid.1) | copy-start | bytes 3076
  2.9 21.4 %collective-permute-start = (bf16[96,1408]{1,0:T(8,128)(2,1)S(1)}, bf16[96,1408]{1,0:T(8,128)(2,1)S(1)}, u32[]{:S(2)}, u32[]{:S(2)}) collective-permute-start(bf16[96,1408]{1,0:T(8,128)(2,1)S(1)} %pad_maximum_fusion.1), channel_id=1, source_target_pairs={{0,3},{1,2},{2,1},{3,0},{4,7},{5,6},{6,5},{7,4},{8,11},{9,10},{10,... | collective-permute-start | bytes 811016 | tf_op jit(solution)/shard_map/ppermute | solution.py:74
  7.7 46.2 %collective-permute-start.4 = (bf16[800,128]{1,0:T(8,128)(2,1)S(1)}, bf16[800,128]{1,0:T(8,128)(2,1)S(1)}, u32[]{:S(2)}, u32[]{:S(2)}) collective-permute-start(bf16[800,128]{1,0:T(8,128)(2,1)S(1)} %get-tuple-element.65), channel_id=1, source_target_pairs={{0,3},{1,2},{2,1},{3,0},{4,7},{5,6},{6,5},{7,4},{8,11},{9,10},{10,... | collective-permute-start | bytes 614408 | tf_op jit(solution)/shard_map/ppermute | solution.py:74
  24.4 15.6 %collective-permute-start.1 = (bf16[96,1408]{1,0:T(8,128)(2,1)S(1)}, bf16[96,1408]{1,0:T(8,128)(2,1)S(1)}, u32[]{:S(2)}, u32[]{:S(2)}) collective-permute-start(bf16[96,1408]{1,0:T(8,128)(2,1)S(1)} %collective-permute-done), channel_id=1, source_target_pairs={{0,8},{4,12},{8,0},{12,4},{16,24},{20,28},{24,16},{28,20},{32,40},... | collective-permute-start | bytes 811016 | tf_op jit(solution)/shard_map/ppermute | solution.py:66
  28.6 25.2 %collective-permute-start.6 = (bf16[720,128]{1,0:T(8,128)(2,1)S(1)}, bf16[720,128]{1,0:T(8,128)(2,1)S(1)}, u32[]{:S(2)}, u32[]{:S(2)}) collective-permute-start(bf16[720,128]{1,0:T(8,128)(2,1)S(1)} %get-tuple-element.67), channel_id=1, source_target_pairs={{0,511},{1,510},{2,5},{3,4},{4,3},{5,2},{6,9},{7,8},{8,7},{9,6},{1... | collective-permute-start | bytes 552968 | tf_op jit(solution)/shard_map/ppermute | solution.py:53
  30.6 23.3 %collective-permute-start.5 = (bf16[720,128]{1,0:T(8,128)(2,1)S(1)}, bf16[720,128]{1,0:T(8,128)(2,1)S(1)}, u32[]{:S(2)}, u32[]{:S(2)}) collective-permute-start(bf16[720,128]{1,0:T(8,128)(2,1)S(1)} %get-tuple-element.66), channel_id=1, source_target_pairs={{0,508},{1,509},{2,6},{3,7},{4,0},{5,1},{6,10},{7,11},{8,4},{9,5},... | collective-permute-start | bytes 552968 | tf_op jit(solution)/shard_map/ppermute | solution.py:53
  40.1 35.4 %collective-permute-start.2 = (bf16[192,1408]{1,0:T(8,128)(2,1)S(1)}, bf16[192,1408]{1,0:T(8,128)(2,1)S(1)}, u32[]{:S(2)}, u32[]{:S(2)}) collective-permute-start(bf16[192,1408]{1,0:T(8,128)(2,1)S(1)} %pad_maximum_fusion), channel_id=1, source_target_pairs={{0,128},{4,132},{8,136},{12,140},{16,144},{20,148},{24,152},{28,15... | collective-permute-start | bytes 1622024 | tf_op jit(solution)/shard_map/ppermute | solution.py:70
  45.6 29.8 %collective-permute-start.3 = (bf16[192,1408]{1,0:T(8,128)(2,1)S(1)}, bf16[192,1408]{1,0:T(8,128)(2,1)S(1)}, u32[]{:S(2)}, u32[]{:S(2)}) collective-permute-start(bf16[192,1408]{1,0:T(8,128)(2,1)S(1)} %pad_maximum_fusion), channel_id=1, source_target_pairs={{0,384},{4,388},{8,392},{12,396},{16,400},{20,404},{24,408},{28,41... | collective-permute-start | bytes 1622024 | tf_op jit(solution)/shard_map/ppermute | solution.py:70
  56.5 29.6 %collective-permute-start.10 = (bf16[352,128]{1,0:T(8,128)(2,1)S(1)}, bf16[352,128]{1,0:T(8,128)(2,1)S(1)}, u32[]{:S(2)}, u32[]{:S(2)}) collective-permute-start(bf16[352,128]{1,0:T(8,128)(2,1)S(1)} %get-tuple-element.76), channel_id=1, source_target_pairs={{0,3},{1,2},{2,1},{3,0},{4,7},{5,6},{6,5},{7,4},{8,11},{9,10},{10,... | collective-permute-start | bytes 270344 | tf_op jit(solution)/shard_map/ppermute | solution.py:74
  73.5 12.7 %collective-permute-start.11 = (bf16[352,128]{1,0:T(8,128)(2,1)S(1)}, bf16[352,128]{1,0:T(8,128)(2,1)S(1)}, u32[]{:S(2)}, u32[]{:S(2)}) collective-permute-start(bf16[352,128]{1,0:T(8,128)(2,1)S(1)} %get-tuple-element.76), channel_id=1, source_target_pairs={{0,2},{1,3},{2,0},{3,1},{4,6},{5,7},{6,4},{7,5},{8,10},{9,11},{10,... | collective-permute-start | bytes 270344 | tf_op jit(solution)/shard_map/ppermute | solution.py:78
  75.5 10.7 %collective-permute-start.9 = (bf16[1408,128]{1,0:T(8,128)(2,1)S(1)}, bf16[1408,128]{1,0:T(8,128)(2,1)S(1)}, u32[]{:S(2)}, u32[]{:S(2)}) collective-permute-start(bf16[1408,128]{1,0:T(8,128)(2,1)S(1)} %get-tuple-element.75.lowered), channel_id=1, source_target_pairs={{0,1},{1,0},{2,3},{3,2},{4,5},{5,4},{6,7},{7,6},{8,9},{9,8},{10,11... | collective-permute-start | bytes 1081352 | tf_op jit(solution)/shard_map/ppermute | solution.py:82
  79.0 9.6 %collective-permute-start.7 = (bf16[96,1408]{1,0:T(8,128)(2,1)S(1)}, bf16[96,1408]{1,0:T(8,128)(2,1)S(1)}, u32[]{:S(2)}, u32[]{:S(2)}) collective-permute-start(bf16[96,1408]{1,0:T(8,128)(2,1)S(1)} %slice.8), channel_id=1, source_target_pairs={{0,128},{4,132},{8,136},{12,140},{16,144},{20,148},{24,152},{28,15... | collective-permute-start | bytes 811016 | tf_op jit(solution)/shard_map/ppermute | solution.py:70
  80.9 9.1 %collective-permute-start.8 = (bf16[96,1408]{1,0:T(8,128)(2,1)S(1)}, bf16[96,1408]{1,0:T(8,128)(2,1)S(1)}, u32[]{:S(2)}, u32[]{:S(2)}) collective-permute-start(bf16[96,1408]{1,0:T(8,128)(2,1)S(1)} %slice.9), channel_id=1, source_target_pairs={{0,384},{4,388},{8,392},{12,396},{16,400},{20,404},{24,408},{28,41... | collective-permute-start | bytes 811016 | tf_op jit(solution)/shard_map/ppermute | solution.py:70
  90.1 6.1 %collective-permute-start.12 = (bf16[768,1408]{1,0:T(8,128)(2,1)S(1)}, bf16[768,1408]{1,0:T(8,128)(2,1)S(1)}, u32[]{:S(2)}, u32[]{:S(2)}) collective-permute-start(bf16[768,1408]{1,0:T(8,128)(2,1)S(1)} %constant_dynamic-update-slice_fusion.mine), channel_id=1, source_target_pairs={{0,4},{4,0},{8,12},{12,8},{16,20},{20,16},{24,28},{28,24},{32,36},... | collective-permute-start | bytes 6488072 | tf_op jit(solution)/shard_map/ppermute | solution.py:41
  99.1 16.8 %collective-permute-start.13 = (bf16[704,128]{1,0:T(8,128)(2,1)S(1)}, bf16[704,128]{1,0:T(8,128)(2,1)S(1)}, u32[]{:S(2)}, u32[]{:S(2)}) collective-permute-start(bf16[704,128]{1,0:T(8,128)(2,1)S(1)} %get-tuple-element.94), channel_id=1, source_target_pairs={{0,511},{1,510},{2,509},{3,508},{4,8},{5,9},{6,10},{7,11},{8,4},{9... | collective-permute-start | bytes 540680 | tf_op jit(solution)/shard_map/ppermute | solution.py:62
  107.4 16.1 %collective-permute-start.14 = (bf16[704,128]{1,0:T(8,128)(2,1)S(1)}, bf16[704,128]{1,0:T(8,128)(2,1)S(1)}, u32[]{:S(2)}, u32[]{:S(2)}) collective-permute-start(bf16[704,128]{1,0:T(8,128)(2,1)S(1)} %get-tuple-element.98), channel_id=1, source_target_pairs={{0,511},{1,510},{2,509},{3,508},{4,8},{5,9},{6,10},{7,11},{8,4},{9... | collective-permute-start | bytes 540680 | tf_op jit(solution)/shard_map/ppermute | solution.py:62
  117.5 6.0 %collective-permute-start.15 = (bf16[192,128]{1,0:T(8,128)(2,1)S(1)}, bf16[192,128]{1,0:T(8,128)(2,1)S(1)}, u32[]{:S(2)}, u32[]{:S(2)}) collective-permute-start(bf16[192,128]{1,0:T(8,128)(2,1)S(1)} %get-tuple-element.99), channel_id=1, source_target_pairs={{0,3},{1,2},{2,1},{3,0},{4,7},{5,6},{6,5},{7,4},{8,11},{9,10},{10,... | collective-permute-start | bytes 147464 | tf_op jit(solution)/shard_map/ppermute | solution.py:74
  125.8 12.4 %collective-permute-start.16 = (bf16[1408,128]{1,0:T(8,128)(2,1)S(1)}, bf16[1408,128]{1,0:T(8,128)(2,1)S(1)}, u32[]{:S(2)}, u32[]{:S(2)}) collective-permute-start(bf16[1408,128]{1,0:T(8,128)(2,1)S(1)} %shard_map.43.lowered), channel_id=1, source_target_pairs={{0,1},{1,0},{2,3},{3,2},{4,5},{5,4},{6,7},{7,6},{8,9},{9,8},{10,11... | collective-permute-start | bytes 1081352 | tf_op jit(solution)/shard_map/ppermute | solution.py:82
  140.8 14.0 %collective-permute-start.17 = (bf16[704,128]{1,0:T(8,128)(2,1)S(1)}, bf16[704,128]{1,0:T(8,128)(2,1)S(1)}, u32[]{:S(2)}, u32[]{:S(2)}) collective-permute-start(bf16[704,128]{1,0:T(8,128)(2,1)S(1)} %get-tuple-element.105), channel_id=1, source_target_pairs={{0,511},{1,510},{2,509},{3,508},{4,8},{5,9},{6,10},{7,11},{8,4},{9... | collective-permute-start | bytes 540680 | tf_op jit(solution)/shard_map/ppermute | solution.py:62
  144.1 6.4 %collective-permute-start.18 = (bf16[192,128]{1,0:T(8,128)(2,1)S(1)}, bf16[192,128]{1,0:T(8,128)(2,1)S(1)}, u32[]{:S(2)}, u32[]{:S(2)}) collective-permute-start(bf16[192,128]{1,0:T(8,128)(2,1)S(1)} %get-tuple-element.106), channel_id=1, source_target_pairs={{0,3},{1,2},{2,1},{3,0},{4,7},{5,6},{6,5},{7,4},{8,11},{9,10},{10,... | collective-permute-start | bytes 147464 | tf_op jit(solution)/shard_map/ppermute | solution.py:74
  156.3 8.2 %collective-permute-start.19 = (bf16[704,128]{1,0:T(8,128)(2,1)S(1)}, bf16[704,128]{1,0:T(8,128)(2,1)S(1)}, u32[]{:S(2)}, u32[]{:S(2)}) collective-permute-start(bf16[704,128]{1,0:T(8,128)(2,1)S(1)} %shard_map.47), channel_id=1, source_target_pairs={{0,3},{1,2},{2,1},{3,0},{4,7},{5,6},{6,5},{7,4},{8,11},{9,10},{10,... | collective-permute-start | bytes 540680 | tf_op jit(solution)/shard_map/ppermute | solution.py:74

commit v12 on v9

--- a/solution.py
+++ b/solution.py
@@ -447,9 +447,9 @@
         ]
         for part in range(parts)
     ]
-    for copy in small + sum(pieces, []):
+    for copy in small[:2] + sum(pieces, []) + small[2:]:
         copy.start()
-    for copy in small:
+    for copy in small[:2]:
         copy.wait()
     low, same = flags[0] == 1, flags[4] == 1
     values = []
@@ -464,6 +464,9 @@
         for half in range(2):
             pieces[part][half].wait()
             total += dot(held[rows_of(parts * half + part, PART)], values[half])
+        if part == 0:
+            for copy in small[2:]:
+                copy.wait()
         mine, theirs = held_own[span], total[:, :LANES]
         rows_near, rows_far = jnp.where(same, mine, theirs), jnp.where(same, theirs, mine)
         near[span], far[span] = rows_near, rows_far
@@ -610,14 +613,16 @@
         for pair in range(4)
     ]
     partner_matrix = lax.all_gather(piece, "cells", axis=0, tiled=True, axis_index_groups=groups)
-    straight, turned = to_layer(straight, False), to_layer(turned, True)
+    turned = to_layer(turned, True)
     received = to_mirror(message)
 
     row = lax.iota(jnp.int32, PAD)
     wanted = jnp.where(row < ROWS, jnp.where(low == 1, row, ROWS - 1 - row), -1)
-    received, collision = lax.optimization_barrier((received, collision))
+    message, collision = lax.optimization_barrier((message, collision))
     ordered = padded_columns(chosen(place(ROWS, PAD, wanted).T, collision))
 
+    straight, ordered = lax.optimization_barrier((straight, ordered))
+    straight = to_layer(straight, False)
     matrix = *column_half(ordered, 0), *column_half(ordered, 1)
     turned, *matrix = lax.optimization_barrier((turned, *matrix))
     lowered, masks, bands = call(

time: 161 us -> 161 us (level)
  starting transfers between devices: 67.3 us -> 65.3 us
  waiting for transfers between devices: 27 us -> 28.7 us
    ppermute x3, starting transfers between devices: 23.6 us -> 19.6 us  [to_neighbour(): return lax.ppermute(array, BOTH, pairs_of(neighbour_of))]
    ppermute x2, starting transfers between devices: 16.4 us -> 19.1 us  [to_layer(): return lax.ppermute(array, BOTH, pairs_of(target))]
    ppermute x2, starting transfers between devices: 6.22 us -> 3.84 us  [to_side(): return lax.ppermute(array, 'vel', [(i, i ^ 1) for i in range(4)])]
    ppermute x2, waiting for transfers between devices: 2.27 us -> 4.52 us  [to_side(): return lax.ppermute(array, 'vel', [(i, i ^ 1) for i in range(4)])]
    ppermute x2, waiting for transfers between devices: 1.79 us -> 0.01 us  [to_layer(): return lax.ppermute(array, BOTH, pairs_of(target))]
    ppermute x6, starting transfers between devices: 19.2 us -> 20.8 us  [to_mirror(): return lax.ppermute(array, 'vel', [(i, 3 - i) for i in range(4)])]
  transfers between devices with their start and end apart: 15 -> 15, of which waited for: 7 -> 8; matrix products, arithmetic and copies ran while one was open for 7% -> 7% of each run, Pallas kernels for 11% -> 11%
where the time goes in v12:
time: 161 us
  starting transfers between devices  65.3 us (41%)
  Pallas kernels  31.1 us (19%)
  waiting for transfers between devices  28.7 us (18%)
  between operations  13.9 us (9%)
  matrix products  13 us (8%)
  blocking collectives  6.41 us (4%)
  local copies, waits for them, and re-layouts  2.05 us (1%)
    pallas_call x12, Pallas kernels, call(): pl.pallas_call(kernel, out_shape=[(pltpu.HBM if leave else jax.ShapeDtype...  31.1 us
    ppermute x6, starting transfers between devices, to_mirror(): return lax.ppermute(array, 'vel', [(i, 3 - i) for i in range(4)])  20.8 us
    ppermute x6, waiting for transfers between devices, to_mirror(): return lax.ppermute(array, 'vel', [(i, 3 - i) for i in range(4)])  19.7 us
    ppermute x3, starting transfers between devices, to_neighbour(): return lax.ppermute(array, BOTH, pairs_of(neighbour_of))  19.6 us
    ppermute x2, starting transfers between devices, to_layer(): return lax.ppermute(array, BOTH, pairs_of(target))  19.1 us
    dot_general x8, matrix products, chosen(): return jnp.dot(left, right, preferred_element_type=BF16)  13 us
    all_gather x3, blocking collectives, with_sibling(): lax.all_gather(array, 'cells', axis=0, tiled=True, axis_index_groups=groups)  6.41 us
    ppermute x2, waiting for transfers between devices, to_side(): return lax.ppermute(array, 'vel', [(i, i ^ 1) for i in range(4)])  4.52 us
  transfers between devices with their start and end apart: 15, of which 8 were waited for; matrix products, arithmetic and copies ran while one was open for 7% of the time, Pallas kernels for 11%

profile of v12, /device:TPU:8, one launch (start us, length us, event | category | flops | bytes accessed | tf_op | source)
XLA Modules:
  0.0 160.6 jit_solution(13272827290965534234)
XLA Ops:
  9.4 3.5 %collective-permute-start.6 = (bf16[88,1408]{1,0:T(8,128)(2,1)S(1)}, bf16[88,1408]{1,0:T(8,128)(2,1)S(1)}, u32[]{:S(2)}, u32[]{:S(2)}) collective-permute-start(bf16[88,1408]{1,0:T(8,128)(2,1)S(1)} %pad_maximum_fusion), channel_id=1, source_target_pairs={{0,3},{1,2},{2,1},{3,0},{4,7},{5,6},{6,5},{7,4},{8,11},{9,10},{10,... | collective-permute-start | bytes 743432 | tf_op jit(solution)/shard_map/ppermute | solution.py:60
  13.2 2.4 %shard_map.37 = (f32[704,128]{1,0:T(8,128)S(1)}, f32[88,128]{1,0:T(8,128)S(1)}, bf16[800,128]{1,0:T(8,128)(2,1)S(1)}, bf16[720,128]{1,0:T(8,128)(2,1)}, bf16[720...) custom-call(s32[6]{0:T(128)S(1)} %stack.31.flags, f32[704,256]{1,0:T(8,128)S(1)} %pad.13.populations, ...), custom_call_target="tpu_custom_call" | custom-call | flops 761266176 | bytes 2786304 | tf_op jit(solution)/shard_map/pallas_call | solution.py:78
  16.4 10.2 %collective-permute-done.6 = bf16[88,1408]{1,0:T(8,128)(2,1)S(1)} collective-permute-done((bf16[88,1408]{1,0:T(8,128)(2,1)S(1)}, bf16[88,1408]{1,0:T(8,128)(2,1)S(1)}, u32[]{:S(2)}, u32[]{:S(2)}) %collective-permute-start.6) | collective-permute-done | bytes 247840 | tf_op jit(solution)/shard_map/ppermute | solution.py:60
  27.3 1.9 %collective-permute-start = (bf16[800,128]{1,0:T(8,128)(2,1)S(1)}, bf16[800,128]{1,0:T(8,128)(2,1)S(1)}, u32[]{:S(2)}, u32[]{:S(2)}) collective-permute-start(bf16[800,128]{1,0:T(8,128)(2,1)S(1)} %get-tuple-element.56), channel_id=1, source_target_pairs={{0,3},{1,2},{2,1},{3,0},{4,7},{5,6},{6,5},{7,4},{8,11},{9,10},{10,... | collective-permute-start | bytes 614408 | tf_op jit(solution)/shard_map/ppermute | solution.py:60
  29.2 14.1 %collective-permute-start.2 = (bf16[720,128]{1,0:T(8,128)(2,1)}, bf16[720,128]{1,0:T(8,128)(2,1)S(1)}, u32[]{:S(2)}, u32[]{:S(2)}) collective-permute-start(bf16[720,128]{1,0:T(8,128)(2,1)} %get-tuple-element.60), channel_id=1, source_target_pairs={{0,511},{1,510},{2,5},{3,4},{4,3},{5,2},{6,9},{7,8},{8,7},{9,6},{1... | collective-permute-start | bytes 552968 | tf_op jit(solution)/shard_map/ppermute | solution.py:47
  43.4 5.4 %fusion.6 = bf16[704,2744]{1,0:T(8,128)(2,1)S(1)} fusion(bf16[686,2744]{1,0:T(8,128)(2,1)} %param.5, s32[704]{0:T(1024)S(1)} %select_select_fusion), kind=kOutput, calls=%fused_computation.13 | convolution fusion | flops 2650879488 | bytes 7631136 | tf_op jit(solution)/shard_map/dot_general | solution.py:560
  49.1 5.0 %collective-permute-start.1 = (bf16[720,128]{1,0:T(8,128)(2,1)}, bf16[720,128]{1,0:T(8,128)(2,1)S(1)}, u32[]{:S(2)}, u32[]{:S(2)}) collective-permute-start(bf16[720,128]{1,0:T(8,128)(2,1)} %get-tuple-element.59), channel_id=1, source_target_pairs={{0,508},{1,509},{2,6},{3,7},{4,0},{5,1},{6,10},{7,11},{8,4},{9,5},... | collective-permute-start | bytes 552968 | tf_op jit(solution)/shard_map/ppermute | solution.py:47
  59.2 2.6 %shard_map.38 = (bf16[1408,128]{1,0:T(8,128)(2,1)S(1)}, f32[8,128]{1,0:T(8,128)S(1)}, bf16[352,128]{1,0:T(8,128)(2,1)S(1)}) custom-call(s32[6]{0:T(128)S(1)} %stack.31.flags, f32[704,128]{1,0:T(8,128)S(1)} %copy-done.5, f32[88,128]{1,0:T(8,128)S(1)} %get-tuple-element.55.own_edge, bf16[800,128]{1,0:T(8,128)(2,1)S(1)} %collective-permute-done.received, ...), custom_call_target="tpu_custom_call" | custom-call | flops 18022400 | bytes 2519040 | tf_op jit(solution)/shard_map/pallas_call | solution.py:78
  61.8 1.9 %collective-permute-start.3 = (bf16[1408,128]{1,0:T(8,128)(2,1)S(1)}, bf16[1408,128]{1,0:T(8,128)(2,1)S(1)}, u32[]{:S(2)}, u32[]{:S(2)}) collective-permute-start(bf16[1408,128]{1,0:T(8,128)(2,1)S(1)} %get-tuple-element.64.lowered), channel_id=1, source_target_pairs={{0,1},{1,0},{2,3},{3,2},{4,5},{5,4},{6,7},{7,6},{8,9},{9,8},{10,11... | collective-permute-start | bytes 1081352 | tf_op jit(solution)/shard_map/ppermute | solution.py:68
  63.7 1.9 %collective-permute-start.5 = (bf16[352,128]{1,0:T(8,128)(2,1)S(1)}, bf16[352,128]{1,0:T(8,128)(2,1)S(1)}, u32[]{:S(2)}, u32[]{:S(2)}) collective-permute-start(bf16[352,128]{1,0:T(8,128)(2,1)S(1)} %get-tuple-element.65), channel_id=1, source_target_pairs={{0,2},{1,3},{2,0},{3,1},{4,6},{5,7},{6,4},{7,5},{8,10},{9,11},{10,... | collective-permute-start | bytes 270344 | tf_op jit(solution)/shard_map/ppermute | solution.py:64
  65.7 5.4 %collective-permute-start.4 = (bf16[352,128]{1,0:T(8,128)(2,1)S(1)}, bf16[352,128]{1,0:T(8,128)(2,1)S(1)}, u32[]{:S(2)}, u32[]{:S(2)}) collective-permute-start(bf16[352,128]{1,0:T(8,128)(2,1)S(1)} %get-tuple-element.65), channel_id=1, source_target_pairs={{0,3},{1,2},{2,1},{3,0},{4,7},{5,6},{6,5},{7,4},{8,11},{9,10},{10,... | collective-permute-start | bytes 270344 | tf_op jit(solution)/shard_map/ppermute | solution.py:60
  71.9 3.2 %collective-permute-done.4.bands = bf16[352,128]{1,0:T(8,128)(2,1)S(1)} collective-permute-done((bf16[352,128]{1,0:T(8,128)(2,1)S(1)}, bf16[352,128]{1,0:T(8,128)(2,1)S(1)}, u32[]{:S(2)}, u32[]{:S(2)}) %collective-permute-start.4) | collective-permute-done | bytes 90144 | tf_op jit(solution)/shard_map/ppermute | solution.py:60
  75.1 3.1 %shard_map.39 = (f32[704,128]{1,0:T(8,128)}, bf16[96,128]{1,0:T(8,128)(2,1)}, bf16[2816,128]{1,0:T(8,128)(2,1)}, bf16[704,128]{1,0:T(8,128)(2,1)}) custom-call(s32[6]{0:T(128)S(1)} %stack.31.flags, bf16[1408,128]{1,0:T(8,128)(2,1)S(1)} %get-tuple-element.64.lowered, bf16[1408,128]{1,0:T(8,128)(2,1)S(1)} %collective-permute-done.3.other, ...), custom_call_target="tpu_custom_call" | custom-call | flops 1015021568 | bytes 7233536 | tf_op jit(solution)/shard_map/pallas_call | solution.py:78
  78.2 5.7 %shard_map.40 = (f32[704,128]{1,0:T(8,128)S(1)}, f32[704,128]{1,0:T(8,128)S(1)}, bf16[704,128]{1,0:T(8,128)(2,1)S(1)}, bf16[704,128]{1,0:T(8,128)(2,1)S(1)}, bf16[192,128]{1,0:T(8,128)(2,1)S(1)}) custom-call(s32[6]{0:T(128)S(1)} %stack.31.flags, f32[3,704,128]{2,1,0:T(8,128)S(1)} %get-tuple-element.53.factors, bf16[96,128]{1,0:T(8,128)(2,1)} %get-tuple-element.70.own_packed, ...), custom_call_target="tpu_custom_call" | custom-call | flops 1015021568 | bytes 7462912 | tf_op jit(solution)/shard_map/pallas_call | solution.py:78
  83.9 8.8 %collective-permute-start.7 = (bf16[704,128]{1,0:T(8,128)(2,1)S(1)}, bf16[704,128]{1,0:T(8,128)(2,1)S(1)}, u32[]{:S(2)}, u32[]{:S(2)}) collective-permute-start(bf16[704,128]{1,0:T(8,128)(2,1)S(1)} %get-tuple-element.84), channel_id=1, source_target_pairs={{0,511},{1,510},{2,509},{3,508},{4,8},{5,9},{6,10},{7,11},{8,4},{9... | collective-permute-start | bytes 540680 | tf_op jit(solution)/shard_map/ppermute | solution.py:56
  92.7 2.1 %all_gather.13.sibling = bf16[1408,128]{1,0:T(8,128)(2,1)S(1)} all-gather(bf16[704,128]{1,0:T(8,128)(2,1)S(1)} %get-tuple-element.80), channel_id=1, replica_groups={{0,4},{8,12},{16,20},{24,28},{32,36},{40,44},{48,52},{56,60},{64,68},{7..., dimensions={0}, use_global_device_ids=true | all-gather | bytes 540672 | tf_op jit(solution)/shard_map/all_gather | solution.py:40
  96.4 4.0 %collective-permute-start.8 = (bf16[704,128]{1,0:T(8,128)(2,1)S(1)}, bf16[704,128]{1,0:T(8,128)(2,1)S(1)}, u32[]{:S(2)}, u32[]{:S(2)}) collective-permute-start(bf16[704,128]{1,0:T(8,128)(2,1)S(1)} %get-tuple-element.88), channel_id=1, source_target_pairs={{0,511},{1,510},{2,509},{3,508},{4,8},{5,9},{6,10},{7,11},{8,4},{9... | collective-permute-start | bytes 540680 | tf_op jit(solution)/shard_map/ppermute | solution.py:56
  102.0 4.4 %collective-permute-start.9 = (bf16[192,128]{1,0:T(8,128)(2,1)S(1)}, bf16[192,128]{1,0:T(8,128)(2,1)S(1)}, u32[]{:S(2)}, u32[]{:S(2)}) collective-permute-start(bf16[192,128]{1,0:T(8,128)(2,1)S(1)} %get-tuple-element.89), channel_id=1, source_target_pairs={{0,3},{1,2},{2,1},{3,0},{4,7},{5,6},{6,5},{7,4},{8,11},{9,10},{10,... | collective-permute-start | bytes 147464 | tf_op jit(solution)/shard_map/ppermute | solution.py:60
  106.4 2.3 %all_gather.14.sibling = bf16[1408,128]{1,0:T(8,128)(2,1)S(1)} all-gather(bf16[704,128]{1,0:T(8,128)(2,1)S(1)} %get-tuple-element.87), channel_id=1, replica_groups={{0,4},{8,12},{16,20},{24,28},{32,36},{40,44},{48,52},{56,60},{64,68},{7..., dimensions={0}, use_global_device_ids=true | all-gather | bytes 540672 | tf_op jit(solution)/shard_map/all_gather | solution.py:40
  108.7 1.9 %collective-permute-done.8.neighbour = bf16[704,128]{1,0:T(8,128)(2,1)S(1)} collective-permute-done((bf16[704,128]{1,0:T(8,128)(2,1)S(1)}, bf16[704,128]{1,0:T(8,128)(2,1)S(1)}, u32[]{:S(2)}, u32[]{:S(2)}) %collective-permute-start.8) | collective-permute-done | bytes 180256 | tf_op jit(solution)/shard_map/ppermute | solution.py:56
  110.6 2.2 %shard_map.43.lowered = bf16[1408,128]{1,0:T(8,128)(2,1)S(1)} custom-call(s32[6]{0:T(128)S(1)} %stack.31.flags, f32[704,128]{1,0:T(8,128)S(1)} %get-tuple-element.83.near, f32[704,128]{1,0:T(8,128)S(1)} %get-tuple-element.86.far, bf16[1408,128]{1,0:T(8,128)(2,1)S(1)} %all_gather.14.sibling, bf16[704,128]{1,0:T(8,128)(2,1)S(1)} %collective-permute-done.8.neighbour, ...), custom_call_target="tpu_custom_call" | custom-call | flops 9011200 | bytes 2756608 | tf_op jit(solution)/shard_map/pallas_call | solution.py:78
  112.8 1.9 %collective-permute-start.10 = (bf16[1408,128]{1,0:T(8,128)(2,1)S(1)}, bf16[1408,128]{1,0:T(8,128)(2,1)S(1)}, u32[]{:S(2)}, u32[]{:S(2)}) collective-permute-start(bf16[1408,128]{1,0:T(8,128)(2,1)S(1)} %shard_map.43.lowered), channel_id=1, source_target_pairs={{0,1},{1,0},{2,3},{3,2},{4,5},{5,4},{6,7},{7,6},{8,9},{9,8},{10,11... | collective-permute-start | bytes 1081352 | tf_op jit(solution)/shard_map/ppermute | solution.py:68
  114.7 4.0 %shard_map.44 = (f32[704,128]{1,0:T(8,128)S(1)}, f32[704,128]{1,0:T(8,128)S(1)}, bf16[2,704,704]{2,1,0:T(8,128)(2,1)S(1)}, bf16[704,1408]{1,0:T(8,128)(2,1)S(1)}) custom-call(s32[6]{0:T(128)S(1)} %stack.31.flags, bf16[1408,128]{1,0:T(8,128)(2,1)S(1)} %shard_map.43.lowered, bf16[704,704]{1,0:T(8,128)(2,1)} %copy-done.3, bf16[704,704]{1,0:T(8,128)(2,1)} %copy-done.2, ...), custom_call_target="tpu_custom_call" | custom-call | flops 507510784 | bytes 12976128 | tf_op jit(solution)/shard_map/pallas_call | solution.py:78
  118.7 4.5 %collective-permute-done.10.other = bf16[1408,128]{1,0:T(8,128)(2,1)S(1)} collective-permute-done((bf16[1408,128]{1,0:T(8,128)(2,1)S(1)}, bf16[1408,128]{1,0:T(8,128)(2,1)S(1)}, u32[]{:S(2)}, u32[]{:S(2)}) %collective-permute-start.10) | collective-permute-done | bytes 360480 | tf_op jit(solution)/shard_map/ppermute | solution.py:68
  123.3 2.0 %shard_map.45 = (f32[704,128]{1,0:T(8,128)S(1)}, f32[704,128]{1,0:T(8,128)S(1)}, bf16[704,128]{1,0:T(8,128)(2,1)S(1)}, bf16[704,128]{1,0:T(8,128)(2,1)S(1)}, bf16[192,128]{1,0:T(8,128)(2,1)S(1)}) custom-call(s32[6]{0:T(128)S(1)} %stack.31.flags, bf16[1408,128]{1,0:T(8,128)(2,1)S(1)} %collective-permute-done.10.other, f32[704,128]{1,0:T(8,128)S(1)} %get-tuple-element.90.own, ...), custom_call_target="tpu_custom_call" | custom-call | flops 507510784 | bytes 7258112 | tf_op jit(solution)/shard_map/pallas_call | solution.py:78
  125.2 6.8 %collective-permute-start.11 = (bf16[704,128]{1,0:T(8,128)(2,1)S(1)}, bf16[704,128]{1,0:T(8,128)(2,1)S(1)}, u32[]{:S(2)}, u32[]{:S(2)}) collective-permute-start(bf16[704,128]{1,0:T(8,128)(2,1)S(1)} %get-tuple-element.97), channel_id=1, source_target_pairs={{0,511},{1,510},{2,509},{3,508},{4,8},{5,9},{6,10},{7,11},{8,4},{9... | collective-permute-start | bytes 540680 | tf_op jit(solution)/shard_map/ppermute | solution.py:56
  132.0 3.7 %collective-permute-start.12 = (bf16[192,128]{1,0:T(8,128)(2,1)S(1)}, bf16[192,128]{1,0:T(8,128)(2,1)S(1)}, u32[]{:S(2)}, u32[]{:S(2)}) collective-permute-start(bf16[192,128]{1,0:T(8,128)(2,1)S(1)} %get-tuple-element.98), channel_id=1, source_target_pairs={{0,3},{1,2},{2,1},{3,0},{4,7},{5,6},{6,5},{7,4},{8,11},{9,10},{10,... | collective-permute-start | bytes 147464 | tf_op jit(solution)/shard_map/ppermute | solution.py:60
  135.8 2.1 %all_gather.15.sibling = bf16[1408,128]{1,0:T(8,128)(2,1)S(1)} all-gather(bf16[704,128]{1,0:T(8,128)(2,1)S(1)} %get-tuple-element.96), channel_id=1, replica_groups={{0,4},{8,12},{16,20},{24,28},{32,36},{40,44},{48,52},{56,60},{64,68},{7..., dimensions={0}, use_global_device_ids=true | all-gather | bytes 540672 | tf_op jit(solution)/shard_map/all_gather | solution.py:40
  141.2 2.0 %collective-permute-start.13 = (bf16[704,128]{1,0:T(8,128)(2,1)S(1)}, bf16[704,128]{1,0:T(8,128)(2,1)S(1)}, u32[]{:S(2)}, u32[]{:S(2)}) collective-permute-start(bf16[704,128]{1,0:T(8,128)(2,1)S(1)} %shard_map.47), channel_id=1, source_target_pairs={{0,3},{1,2},{2,1},{3,0},{4,7},{5,6},{6,5},{7,4},{8,11},{9,10},{10,... | collective-permute-start | bytes 540680 | tf_op jit(solution)/shard_map/ppermute | solution.py:60
  143.2 2.3 %shard_map.46.kept = f32[704,128]{1,0:T(8,128)S(1)} custom-call(s32[6]{0:T(128)S(1)} %stack.31.flags, f32[704,128]{1,0:T(8,128)S(1)} %get-tuple-element.94.near, f32[704,128]{1,0:T(8,128)S(1)} %get-tuple-element.95.far, bf16[1408,128]{1,0:T(8,128)(2,1)S(1)} %all_gather.15.sibling, bf16[704,128]{1,0:T(8,128)(2,1)S(1)} %collective-permute-done.11.neighbour, ...), custom_call_target="tpu_custom_call" | custom-call | flops 507510784 | bytes 2756608 | tf_op jit(solution)/shard_map/pallas_call | solution.py:78
  145.5 6.2 %collective-permute-done.13.received = bf16[704,128]{1,0:T(8,128)(2,1)S(1)} collective-permute-done((bf16[704,128]{1,0:T(8,128)(2,1)S(1)}, bf16[704,128]{1,0:T(8,128)(2,1)S(1)}, u32[]{:S(2)}, u32[]{:S(2)}) %collective-permute-start.13) | collective-permute-done | bytes 180256 | tf_op jit(solution)/shard_map/ppermute | solution.py:60
  151.6 2.1 %shard_map.48 = f32[686,1,256]{2,1,0:T(1,128)} custom-call(s32[6]{0:T(128)S(1)} %stack.31.flags, f32[704,128]{1,0:T(8,128)S(1)} %shard_map.46.kept, bf16[704,128]{1,0:T(8,128)(2,1)S(1)} %collective-permute-done.13.received), custom_call_target="tpu_custom_call" | custom-call | flops 126877696 | bytes 1243136 | tf_op jit(solution)/shard_map/pallas_call | solution.py:78
  (53 shorter events, 17.2 us)
Async XLA Ops:
  6.5 6.5 %copy-start.7 = (f32[686,1,256]{2,1,0:T(1,128)S(1)}, f32[686,1,256]{2,1,0:T(1,128)}, u32[]{:S(2)}) copy-start(f32[686,1,256]{2,1,0:T(1,128)} %param.3) | copy-start | bytes 2107396
  6.5 71.6 %all-gather.2.cloned.1.call-start = ((), (), s32[]{:S(2)}) async-start(), calls=%async_computation | async-start | bytes 4212736 | tf_op jit(solution)/shard_map/all_gather | solution.py:615
  8.7 4.5 %copy-start.6 = (s32[1,256]{1,0:T(1,128)S(1)}, s32[1,256]{1,0:T(1,128)}, u32[]{:S(2)}) copy-start(s32[1,256]{1,0:T(1,128)} %solid.1) | copy-start | bytes 3076
  9.4 17.1 %collective-permute-start.6 = (bf16[88,1408]{1,0:T(8,128)(2,1)S(1)}, bf16[88,1408]{1,0:T(8,128)(2,1)S(1)}, u32[]{:S(2)}, u32[]{:S(2)}) collective-permute-start(bf16[88,1408]{1,0:T(8,128)(2,1)S(1)} %pad_maximum_fusion), channel_id=1, source_target_pairs={{0,3},{1,2},{2,1},{3,0},{4,7},{5,6},{6,5},{7,4},{8,11},{9,10},{10,... | collective-permute-start | bytes 743432 | tf_op jit(solution)/shard_map/ppermute | solution.py:60
  15.7 0.7 copy-start.4
  26.6 0.7 copy-start.8
  27.3 31.8 %collective-permute-start = (bf16[800,128]{1,0:T(8,128)(2,1)S(1)}, bf16[800,128]{1,0:T(8,128)(2,1)S(1)}, u32[]{:S(2)}, u32[]{:S(2)}) collective-permute-start(bf16[800,128]{1,0:T(8,128)(2,1)S(1)} %get-tuple-element.56), channel_id=1, source_target_pairs={{0,3},{1,2},{2,1},{3,0},{4,7},{5,6},{6,5},{7,4},{8,11},{9,10},{10,... | collective-permute-start | bytes 614408 | tf_op jit(solution)/shard_map/ppermute | solution.py:60
  29.2 29.9 %collective-permute-start.2 = (bf16[720,128]{1,0:T(8,128)(2,1)}, bf16[720,128]{1,0:T(8,128)(2,1)S(1)}, u32[]{:S(2)}, u32[]{:S(2)}) collective-permute-start(bf16[720,128]{1,0:T(8,128)(2,1)} %get-tuple-element.60), channel_id=1, source_target_pairs={{0,511},{1,510},{2,5},{3,4},{4,3},{5,2},{6,9},{7,8},{8,7},{9,6},{1... | collective-permute-start | bytes 552968 | tf_op jit(solution)/shard_map/ppermute | solution.py:47
  49.1 10.0 %collective-permute-start.1 = (bf16[720,128]{1,0:T(8,128)(2,1)}, bf16[720,128]{1,0:T(8,128)(2,1)S(1)}, u32[]{:S(2)}, u32[]{:S(2)}) collective-permute-start(bf16[720,128]{1,0:T(8,128)(2,1)} %get-tuple-element.59), channel_id=1, source_target_pairs={{0,508},{1,509},{2,6},{3,7},{4,0},{5,1},{6,10},{7,11},{8,4},{9,5},... | collective-permute-start | bytes 552968 | tf_op jit(solution)/shard_map/ppermute | solution.py:47
  55.2 19.8 %copy-start = (bf16[704,704]{1,0:T(8,128)(2,1)}, bf16[704,704]{1,0:T(8,128)(2,1)S(1)}, u32[]{:S(2)}) copy-start(bf16[704,704]{1,0:T(8,128)(2,1)S(1)} %fusion.4.m2) | copy-start | bytes 2973700
  56.6 18.5 %copy-start.1 = (bf16[704,704]{1,0:T(8,128)(2,1)}, bf16[704,704]{1,0:T(8,128)(2,1)S(1)}, u32[]{:S(2)}) copy-start(bf16[704,704]{1,0:T(8,128)(2,1)S(1)} %fusion.1.m3) | copy-start | bytes 2973700
  57.9 17.1 %copy-start.2 = (bf16[704,704]{1,0:T(8,128)(2,1)}, bf16[704,704]{1,0:T(8,128)(2,1)S(1)}, u32[]{:S(2)}) copy-start(bf16[704,704]{1,0:T(8,128)(2,1)S(1)} %fusion.m1) | copy-start | bytes 2973700
  57.9 1.2 copy-start.5
  59.0 16.0 %copy-start.3 = (bf16[704,704]{1,0:T(8,128)(2,1)}, bf16[704,704]{1,0:T(8,128)(2,1)S(1)}, u32[]{:S(2)}) copy-start(bf16[704,704]{1,0:T(8,128)(2,1)S(1)} %fusion.3.m0) | copy-start | bytes 2973700
  61.8 13.2 %collective-permute-start.3 = (bf16[1408,128]{1,0:T(8,128)(2,1)S(1)}, bf16[1408,128]{1,0:T(8,128)(2,1)S(1)}, u32[]{:S(2)}, u32[]{:S(2)}) collective-permute-start(bf16[1408,128]{1,0:T(8,128)(2,1)S(1)} %get-tuple-element.64.lowered), channel_id=1, source_target_pairs={{0,1},{1,0},{2,3},{3,2},{4,5},{5,4},{6,7},{7,6},{8,9},{9,8},{10,11... | collective-permute-start | bytes 1081352 | tf_op jit(solution)/shard_map/ppermute | solution.py:68
  63.7 8.1 %collective-permute-start.5 = (bf16[352,128]{1,0:T(8,128)(2,1)S(1)}, bf16[352,128]{1,0:T(8,128)(2,1)S(1)}, u32[]{:S(2)}, u32[]{:S(2)}) collective-permute-start(bf16[352,128]{1,0:T(8,128)(2,1)S(1)} %get-tuple-element.65), channel_id=1, source_target_pairs={{0,2},{1,3},{2,0},{3,1},{4,6},{5,7},{6,4},{7,5},{8,10},{9,11},{10,... | collective-permute-start | bytes 270344 | tf_op jit(solution)/shard_map/ppermute | solution.py:64
  65.7 9.4 %collective-permute-start.4 = (bf16[352,128]{1,0:T(8,128)(2,1)S(1)}, bf16[352,128]{1,0:T(8,128)(2,1)S(1)}, u32[]{:S(2)}, u32[]{:S(2)}) collective-permute-start(bf16[352,128]{1,0:T(8,128)(2,1)S(1)} %get-tuple-element.65), channel_id=1, source_target_pairs={{0,3},{1,2},{2,1},{3,0},{4,7},{5,6},{6,5},{7,4},{8,11},{9,10},{10,... | collective-permute-start | bytes 270344 | tf_op jit(solution)/shard_map/ppermute | solution.py:60
  83.9 16.5 %collective-permute-start.7 = (bf16[704,128]{1,0:T(8,128)(2,1)S(1)}, bf16[704,128]{1,0:T(8,128)(2,1)S(1)}, u32[]{:S(2)}, u32[]{:S(2)}) collective-permute-start(bf16[704,128]{1,0:T(8,128)(2,1)S(1)} %get-tuple-element.84), channel_id=1, source_target_pairs={{0,511},{1,510},{2,509},{3,508},{4,8},{5,9},{6,10},{7,11},{8,4},{9... | collective-permute-start | bytes 540680 | tf_op jit(solution)/shard_map/ppermute | solution.py:56
  96.4 14.2 %collective-permute-start.8 = (bf16[704,128]{1,0:T(8,128)(2,1)S(1)}, bf16[704,128]{1,0:T(8,128)(2,1)S(1)}, u32[]{:S(2)}, u32[]{:S(2)}) collective-permute-start(bf16[704,128]{1,0:T(8,128)(2,1)S(1)} %get-tuple-element.88), channel_id=1, source_target_pairs={{0,511},{1,510},{2,509},{3,508},{4,8},{5,9},{6,10},{7,11},{8,4},{9... | collective-permute-start | bytes 540680 | tf_op jit(solution)/shard_map/ppermute | solution.py:56
  102.0 8.5 %collective-permute-start.9 = (bf16[192,128]{1,0:T(8,128)(2,1)S(1)}, bf16[192,128]{1,0:T(8,128)(2,1)S(1)}, u32[]{:S(2)}, u32[]{:S(2)}) collective-permute-start(bf16[192,128]{1,0:T(8,128)(2,1)S(1)} %get-tuple-element.89), channel_id=1, source_target_pairs={{0,3},{1,2},{2,1},{3,0},{4,7},{5,6},{6,5},{7,4},{8,11},{9,10},{10,... | collective-permute-start | bytes 147464 | tf_op jit(solution)/shard_map/ppermute | solution.py:60
  112.8 10.5 %collective-permute-start.10 = (bf16[1408,128]{1,0:T(8,128)(2,1)S(1)}, bf16[1408,128]{1,0:T(8,128)(2,1)S(1)}, u32[]{:S(2)}, u32[]{:S(2)}) collective-permute-start(bf16[1408,128]{1,0:T(8,128)(2,1)S(1)} %shard_map.43.lowered), channel_id=1, source_target_pairs={{0,1},{1,0},{2,3},{3,2},{4,5},{5,4},{6,7},{7,6},{8,9},{9,8},{10,11... | collective-permute-start | bytes 1081352 | tf_op jit(solution)/shard_map/ppermute | solution.py:68
  125.2 14.6 %collective-permute-start.11 = (bf16[704,128]{1,0:T(8,128)(2,1)S(1)}, bf16[704,128]{1,0:T(8,128)(2,1)S(1)}, u32[]{:S(2)}, u32[]{:S(2)}) collective-permute-start(bf16[704,128]{1,0:T(8,128)(2,1)S(1)} %get-tuple-element.97), channel_id=1, source_target_pairs={{0,511},{1,510},{2,509},{3,508},{4,8},{5,9},{6,10},{7,11},{8,4},{9... | collective-permute-start | bytes 540680 | tf_op jit(solution)/shard_map/ppermute | solution.py:56
  132.0 6.0 %collective-permute-start.12 = (bf16[192,128]{1,0:T(8,128)(2,1)S(1)}, bf16[192,128]{1,0:T(8,128)(2,1)S(1)}, u32[]{:S(2)}, u32[]{:S(2)}) collective-permute-start(bf16[192,128]{1,0:T(8,128)(2,1)S(1)} %get-tuple-element.98), channel_id=1, source_target_pairs={{0,3},{1,2},{2,1},{3,0},{4,7},{5,6},{6,5},{7,4},{8,11},{9,10},{10,... | collective-permute-start | bytes 147464 | tf_op jit(solution)/shard_map/ppermute | solution.py:60
  141.2 10.4 %collective-permute-start.13 = (bf16[704,128]{1,0:T(8,128)(2,1)S(1)}, bf16[704,128]{1,0:T(8,128)(2,1)S(1)}, u32[]{:S(2)}, u32[]{:S(2)}) collective-permute-start(bf16[704,128]{1,0:T(8,128)(2,1)S(1)} %shard_map.47), channel_id=1, source_target_pairs={{0,3},{1,2},{2,1},{3,0},{4,7},{5,6},{6,5},{7,4},{8,11},{9,10},{10,... | collective-permute-start | bytes 540680 | tf_op jit(solution)/shard_map/ppermute | solution.py:60
Sparse Core Ops, SparseCore 0:
  27.4 44.0 all-gather.1

commit v13 on v12

--- a/solution.py
+++ b/solution.py
@@ -623,8 +623,6 @@
 
     straight, ordered = lax.optimization_barrier((straight, ordered))
     straight = to_layer(straight, False)
-    matrix = *column_half(ordered, 0), *column_half(ordered, 1)
-    turned, *matrix = lax.optimization_barrier((turned, *matrix))
     lowered, masks, bands = call(
         first_kernel,
         [((2 * PAD, LANES), BF16), ((8, LANES), F32), ((BAND, LANES), BF16)],
@@ -635,6 +633,8 @@
     multiply = 2 * PAD * 4 * PAD * LANES
     work = 100 * PAD * LANES
 
+    lowered, bands, ordered = lax.optimization_barrier((lowered, bands, ordered))
+    matrix = *column_half(ordered, 0), *column_half(ordered, 1)
     other = to_side(lowered)
     bands = to_mirror(bands), to_opposite(bands)
     own, own_packed, all_rows, all_bands = call(

time: 161 us -> 165 us (1.025)
  waiting for transfers between devices: 28.7 us -> 31.9 us
    ppermute x2, waiting for transfers between devices: 0.01 us -> 3.95 us  [to_layer(): return lax.ppermute(array, BOTH, pairs_of(target))]
    ppermute x6, starting transfers between devices: 20.8 us -> 17 us  [to_mirror(): return lax.ppermute(array, 'vel', [(i, 3 - i) for i in range(4)])]
    ppermute x2, starting transfers between devices: 3.84 us -> 7.19 us  [to_side(): return lax.ppermute(array, 'vel', [(i, i ^ 1) for i in range(4)])]
    ppermute x3, waiting for transfers between devices: 3.62 us -> 5.85 us  [to_neighbour(): return lax.ppermute(array, BOTH, pairs_of(neighbour_of))]
  transfers between devices with their start and end apart: 15 -> 15, of which waited for: 8 -> 7; matrix products, arithmetic and copies ran while one was open for 7% -> 7% of each run, Pallas kernels for 11% -> 11%
where the time goes in v13:
time: 165 us; the launch traced here: 164 us
  starting transfers between devices  66 us (40%)
  waiting for transfers between devices  31.9 us (19%)
  Pallas kernels  30.8 us (19%)
  between operations  13.9 us (8%)
  matrix products  12.9 us (8%)
  blocking collectives  6.19 us (4%)
  local copies, waits for them, and re-layouts  2.28 us (1%)
    pallas_call x12, Pallas kernels, call(): pl.pallas_call(kernel, out_shape=[(pltpu.HBM if leave else jax.ShapeDtype...  30.8 us
    ppermute x3, starting transfers between devices, to_neighbour(): return lax.ppermute(array, BOTH, pairs_of(neighbour_of))  20.9 us
    ppermute x2, starting transfers between devices, to_layer(): return lax.ppermute(array, BOTH, pairs_of(target))  19 us
    ppermute x6, waiting for transfers between devices, to_mirror(): return lax.ppermute(array, 'vel', [(i, 3 - i) for i in range(4)])  18.6 us
    ppermute x6, starting transfers between devices, to_mirror(): return lax.ppermute(array, 'vel', [(i, 3 - i) for i in range(4)])  17 us
    dot_general x8, matrix products, chosen(): return jnp.dot(left, right, preferred_element_type=BF16)  12.9 us
    ppermute x2, starting transfers between devices, to_side(): return lax.ppermute(array, 'vel', [(i, i ^ 1) for i in range(4)])  7.19 us
    all_gather x3, blocking collectives, with_sibling(): lax.all_gather(array, 'cells', axis=0, tiled=True, axis_index_groups=groups)  6.19 us
  transfers between devices with their start and end apart: 15, of which 7 were waited for; matrix products, arithmetic and copies ran while one was open for 7% of the time, Pallas kernels for 11%

profile of v13, /device:TPU:8, one launch (start us, length us, event | category | flops | bytes accessed | tf_op | source)
XLA Modules:
  0.0 164.1 jit_solution(15052959387950986954)
XLA Ops:
  9.4 3.5 %collective-permute-start.6 = (bf16[88,1408]{1,0:T(8,128)(2,1)S(1)}, bf16[88,1408]{1,0:T(8,128)(2,1)S(1)}, u32[]{:S(2)}, u32[]{:S(2)}) collective-permute-start(bf16[88,1408]{1,0:T(8,128)(2,1)S(1)} %pad_maximum_fusion), channel_id=1, source_target_pairs={{0,3},{1,2},{2,1},{3,0},{4,7},{5,6},{6,5},{7,4},{8,11},{9,10},{10,... | collective-permute-start | bytes 743432 | tf_op jit(solution)/shard_map/ppermute | solution.py:60
  13.2 2.0 %shard_map.37 = (f32[704,128]{1,0:T(8,128)S(1)}, f32[88,128]{1,0:T(8,128)S(1)}, bf16[800,128]{1,0:T(8,128)(2,1)S(1)}, bf16[720,128]{1,0:T(8,128)(2,1)S(1)}, bf16...) custom-call(s32[6]{0:T(128)S(1)} %stack.31.flags, f32[704,256]{1,0:T(8,128)S(1)} %pad.13.populations, ...), custom_call_target="tpu_custom_call" | custom-call | flops 761266176 | bytes 2786304 | tf_op jit(solution)/shard_map/pallas_call | solution.py:78
  15.2 11.3 %collective-permute-done.6 = bf16[88,1408]{1,0:T(8,128)(2,1)S(1)} collective-permute-done((bf16[88,1408]{1,0:T(8,128)(2,1)S(1)}, bf16[88,1408]{1,0:T(8,128)(2,1)S(1)}, u32[]{:S(2)}, u32[]{:S(2)}) %collective-permute-start.6) | collective-permute-done | bytes 247840 | tf_op jit(solution)/shard_map/ppermute | solution.py:60
  27.3 1.9 %collective-permute-start = (bf16[800,128]{1,0:T(8,128)(2,1)S(1)}, bf16[800,128]{1,0:T(8,128)(2,1)S(1)}, u32[]{:S(2)}, u32[]{:S(2)}) collective-permute-start(bf16[800,128]{1,0:T(8,128)(2,1)S(1)} %get-tuple-element.54), channel_id=1, source_target_pairs={{0,3},{1,2},{2,1},{3,0},{4,7},{5,6},{6,5},{7,4},{8,11},{9,10},{10,... | collective-permute-start | bytes 614408 | tf_op jit(solution)/shard_map/ppermute | solution.py:60
  29.2 14.1 %collective-permute-start.2 = (bf16[720,128]{1,0:T(8,128)(2,1)S(1)}, bf16[720,128]{1,0:T(8,128)(2,1)S(1)}, u32[]{:S(2)}, u32[]{:S(2)}) collective-permute-start(bf16[720,128]{1,0:T(8,128)(2,1)S(1)} %get-tuple-element.58), channel_id=1, source_target_pairs={{0,511},{1,510},{2,5},{3,4},{4,3},{5,2},{6,9},{7,8},{8,7},{9,6},{1... | collective-permute-start | bytes 552968 | tf_op jit(solution)/shard_map/ppermute | solution.py:47
  43.4 5.4 %fusion.6 = bf16[704,2744]{1,0:T(8,128)(2,1)S(1)} fusion(bf16[686,2744]{1,0:T(8,128)(2,1)} %param.5, s32[704]{0:T(1024)S(1)} %select_select_fusion), kind=kOutput, calls=%fused_computation.13 | convolution fusion | flops 2650879488 | bytes 7631136 | tf_op jit(solution)/shard_map/dot_general | solution.py:560
  49.1 4.8 %collective-permute-start.1 = (bf16[720,128]{1,0:T(8,128)(2,1)S(1)}, bf16[720,128]{1,0:T(8,128)(2,1)S(1)}, u32[]{:S(2)}, u32[]{:S(2)}) collective-permute-start(bf16[720,128]{1,0:T(8,128)(2,1)S(1)} %get-tuple-element.57), channel_id=1, source_target_pairs={{0,508},{1,509},{2,6},{3,7},{4,0},{5,1},{6,10},{7,11},{8,4},{9,5},... | collective-permute-start | bytes 552968 | tf_op jit(solution)/shard_map/ppermute | solution.py:47
  54.0 3.9 %collective-permute-done.1.straight = bf16[720,128]{1,0:T(8,128)(2,1)S(1)} collective-permute-done((bf16[720,128]{1,0:T(8,128)(2,1)S(1)}, bf16[720,128]{1,0:T(8,128)(2,1)S(1)}, u32[]{:S(2)}, u32[]{:S(2)}) %collective-permute-start.1) | collective-permute-done | bytes 184352 | tf_op jit(solution)/shard_map/ppermute | solution.py:47
  57.9 2.6 %shard_map.38 = (bf16[1408,128]{1,0:T(8,128)(2,1)S(1)}, f32[8,128]{1,0:T(8,128)S(1)}, bf16[352,128]{1,0:T(8,128)(2,1)S(1)}) custom-call(s32[6]{0:T(128)S(1)} %stack.31.flags, f32[704,128]{1,0:T(8,128)S(1)} %get-tuple-element.52.own, f32[88,128]{1,0:T(8,128)S(1)} %get-tuple-element.53.own_edge, bf16[800,128]{1,0:T(8,128)(2,1)S(1)} %collective-permute-done.received, ...), custom_call_target="tpu_custom_call" | custom-call | flops 18022400 | bytes 2519040 | tf_op jit(solution)/shard_map/pallas_call | solution.py:78
  60.5 1.9 %collective-permute-start.5 = (bf16[352,128]{1,0:T(8,128)(2,1)S(1)}, bf16[352,128]{1,0:T(8,128)(2,1)S(1)}, u32[]{:S(2)}, u32[]{:S(2)}) collective-permute-start(bf16[352,128]{1,0:T(8,128)(2,1)S(1)} %get-tuple-element.64), channel_id=1, source_target_pairs={{0,2},{1,3},{2,0},{3,1},{4,6},{5,7},{6,4},{7,5},{8,10},{9,11},{10,... | collective-permute-start | bytes 270344 | tf_op jit(solution)/shard_map/ppermute | solution.py:64
  62.5 3.1 %collective-permute-start.4 = (bf16[352,128]{1,0:T(8,128)(2,1)S(1)}, bf16[352,128]{1,0:T(8,128)(2,1)S(1)}, u32[]{:S(2)}, u32[]{:S(2)}) collective-permute-start(bf16[352,128]{1,0:T(8,128)(2,1)S(1)} %get-tuple-element.64), channel_id=1, source_target_pairs={{0,3},{1,2},{2,1},{3,0},{4,7},{5,6},{6,5},{7,4},{8,11},{9,10},{10,... | collective-permute-start | bytes 270344 | tf_op jit(solution)/shard_map/ppermute | solution.py:60
  65.6 5.3 %collective-permute-start.3 = (bf16[1408,128]{1,0:T(8,128)(2,1)S(1)}, bf16[1408,128]{1,0:T(8,128)(2,1)S(1)}, u32[]{:S(2)}, u32[]{:S(2)}) collective-permute-start(bf16[1408,128]{1,0:T(8,128)(2,1)S(1)} %get-tuple-element.63.lowered), channel_id=1, source_target_pairs={{0,1},{1,0},{2,3},{3,2},{4,5},{5,4},{6,7},{7,6},{8,9},{9,8},{10,11... | collective-permute-start | bytes 1081352 | tf_op jit(solution)/shard_map/ppermute | solution.py:68
  76.1 3.1 %shard_map.39 = (f32[704,128]{1,0:T(8,128)}, bf16[96,128]{1,0:T(8,128)(2,1)}, bf16[2816,128]{1,0:T(8,128)(2,1)}, bf16[704,128]{1,0:T(8,128)(2,1)}) custom-call(s32[6]{0:T(128)S(1)} %stack.31.flags, bf16[1408,128]{1,0:T(8,128)(2,1)S(1)} %get-tuple-element.63.lowered, bf16[1408,128]{1,0:T(8,128)(2,1)S(1)} %collective-permute-done.3.other, ...), custom_call_target="tpu_custom_call" | custom-call | flops 1015021568 | bytes 7233536 | tf_op jit(solution)/shard_map/pallas_call | solution.py:78
  80.2 5.7 %shard_map.40 = (f32[704,128]{1,0:T(8,128)S(1)}, f32[704,128]{1,0:T(8,128)S(1)}, bf16[704,128]{1,0:T(8,128)(2,1)S(1)}, bf16[704,128]{1,0:T(8,128)(2,1)S(1)}, bf16[192,128]{1,0:T(8,128)(2,1)S(1)}) custom-call(s32[6]{0:T(128)S(1)} %stack.31.flags, f32[3,704,128]{2,1,0:T(8,128)S(1)} %get-tuple-element.51.factors, bf16[96,128]{1,0:T(8,128)(2,1)} %get-tuple-element.66.own_packed, ...), custom_call_target="tpu_custom_call" | custom-call | flops 1015021568 | bytes 7462912 | tf_op jit(solution)/shard_map/pallas_call | solution.py:78
  85.9 10.5 %collective-permute-start.7 = (bf16[704,128]{1,0:T(8,128)(2,1)S(1)}, bf16[704,128]{1,0:T(8,128)(2,1)S(1)}, u32[]{:S(2)}, u32[]{:S(2)}) collective-permute-start(bf16[704,128]{1,0:T(8,128)(2,1)S(1)} %get-tuple-element.80), channel_id=1, source_target_pairs={{0,511},{1,510},{2,509},{3,508},{4,8},{5,9},{6,10},{7,11},{8,4},{9... | collective-permute-start | bytes 540680 | tf_op jit(solution)/shard_map/ppermute | solution.py:56
  96.4 2.1 %all_gather.13.sibling = bf16[1408,128]{1,0:T(8,128)(2,1)S(1)} all-gather(bf16[704,128]{1,0:T(8,128)(2,1)S(1)} %get-tuple-element.76), channel_id=1, replica_groups={{0,4},{8,12},{16,20},{24,28},{32,36},{40,44},{48,52},{56,60},{64,68},{7..., dimensions={0}, use_global_device_ids=true | all-gather | bytes 540672 | tf_op jit(solution)/shard_map/all_gather | solution.py:40
  100.2 2.3 %collective-permute-start.8 = (bf16[704,128]{1,0:T(8,128)(2,1)S(1)}, bf16[704,128]{1,0:T(8,128)(2,1)S(1)}, u32[]{:S(2)}, u32[]{:S(2)}) collective-permute-start(bf16[704,128]{1,0:T(8,128)(2,1)S(1)} %get-tuple-element.84), channel_id=1, source_target_pairs={{0,511},{1,510},{2,509},{3,508},{4,8},{5,9},{6,10},{7,11},{8,4},{9... | collective-permute-start | bytes 540680 | tf_op jit(solution)/shard_map/ppermute | solution.py:56
  104.1 2.5 %collective-permute-start.9 = (bf16[192,128]{1,0:T(8,128)(2,1)S(1)}, bf16[192,128]{1,0:T(8,128)(2,1)S(1)}, u32[]{:S(2)}, u32[]{:S(2)}) collective-permute-start(bf16[192,128]{1,0:T(8,128)(2,1)S(1)} %get-tuple-element.85), channel_id=1, source_target_pairs={{0,3},{1,2},{2,1},{3,0},{4,7},{5,6},{6,5},{7,4},{8,11},{9,10},{10,... | collective-permute-start | bytes 147464 | tf_op jit(solution)/shard_map/ppermute | solution.py:60
  106.7 2.1 %all_gather.14.sibling = bf16[1408,128]{1,0:T(8,128)(2,1)S(1)} all-gather(bf16[704,128]{1,0:T(8,128)(2,1)S(1)} %get-tuple-element.83), channel_id=1, replica_groups={{0,4},{8,12},{16,20},{24,28},{32,36},{40,44},{48,52},{56,60},{64,68},{7..., dimensions={0}, use_global_device_ids=true | all-gather | bytes 540672 | tf_op jit(solution)/shard_map/all_gather | solution.py:40
  108.7 5.8 %collective-permute-done.8.neighbour = bf16[704,128]{1,0:T(8,128)(2,1)S(1)} collective-permute-done((bf16[704,128]{1,0:T(8,128)(2,1)S(1)}, bf16[704,128]{1,0:T(8,128)(2,1)S(1)}, u32[]{:S(2)}, u32[]{:S(2)}) %collective-permute-start.8) | collective-permute-done | bytes 180256 | tf_op jit(solution)/shard_map/ppermute | solution.py:56
  114.6 2.2 %shard_map.43.lowered = bf16[1408,128]{1,0:T(8,128)(2,1)S(1)} custom-call(s32[6]{0:T(128)S(1)} %stack.31.flags, f32[704,128]{1,0:T(8,128)S(1)} %get-tuple-element.79.near, f32[704,128]{1,0:T(8,128)S(1)} %get-tuple-element.82.far, bf16[1408,128]{1,0:T(8,128)(2,1)S(1)} %all_gather.14.sibling, bf16[704,128]{1,0:T(8,128)(2,1)S(1)} %collective-permute-done.8.neighbour, ...), custom_call_target="tpu_custom_call" | custom-call | flops 9011200 | bytes 2756608 | tf_op jit(solution)/shard_map/pallas_call | solution.py:78
  116.8 1.9 %collective-permute-start.10 = (bf16[1408,128]{1,0:T(8,128)(2,1)S(1)}, bf16[1408,128]{1,0:T(8,128)(2,1)S(1)}, u32[]{:S(2)}, u32[]{:S(2)}) collective-permute-start(bf16[1408,128]{1,0:T(8,128)(2,1)S(1)} %shard_map.43.lowered), channel_id=1, source_target_pairs={{0,1},{1,0},{2,3},{3,2},{4,5},{5,4},{6,7},{7,6},{8,9},{9,8},{10,11... | collective-permute-start | bytes 1081352 | tf_op jit(solution)/shard_map/ppermute | solution.py:68
  118.7 4.2 %shard_map.44 = (f32[704,128]{1,0:T(8,128)S(1)}, f32[704,128]{1,0:T(8,128)S(1)}, bf16[2,704,704]{2,1,0:T(8,128)(2,1)S(1)}, bf16[704,1408]{1,0:T(8,128)(2,1)S(1)}) custom-call(s32[6]{0:T(128)S(1)} %stack.31.flags, bf16[1408,128]{1,0:T(8,128)(2,1)S(1)} %shard_map.43.lowered, bf16[704,704]{1,0:T(8,128)(2,1)} %copy-done.3, bf16[704,704]{1,0:T(8,128)(2,1)} %copy-done.1, ...), custom_call_target="tpu_custom_call" | custom-call | flops 507510784 | bytes 12976128 | tf_op jit(solution)/shard_map/pallas_call | solution.py:78
  123.0 3.1 %collective-permute-done.10.other = bf16[1408,128]{1,0:T(8,128)(2,1)S(1)} collective-permute-done((bf16[1408,128]{1,0:T(8,128)(2,1)S(1)}, bf16[1408,128]{1,0:T(8,128)(2,1)S(1)}, u32[]{:S(2)}, u32[]{:S(2)}) %collective-permute-start.10) | collective-permute-done | bytes 360480 | tf_op jit(solution)/shard_map/ppermute | solution.py:68
  126.1 2.0 %shard_map.45 = (f32[704,128]{1,0:T(8,128)S(1)}, f32[704,128]{1,0:T(8,128)S(1)}, bf16[704,128]{1,0:T(8,128)(2,1)S(1)}, bf16[704,128]{1,0:T(8,128)(2,1)S(1)}, bf16[192,128]{1,0:T(8,128)(2,1)S(1)}) custom-call(s32[6]{0:T(128)S(1)} %stack.31.flags, bf16[1408,128]{1,0:T(8,128)(2,1)S(1)} %collective-permute-done.10.other, f32[704,128]{1,0:T(8,128)S(1)} %get-tuple-element.86.own, ...), custom_call_target="tpu_custom_call" | custom-call | flops 507510784 | bytes 7258112 | tf_op jit(solution)/shard_map/pallas_call | solution.py:78
  128.1 8.1 %collective-permute-start.11 = (bf16[704,128]{1,0:T(8,128)(2,1)S(1)}, bf16[704,128]{1,0:T(8,128)(2,1)S(1)}, u32[]{:S(2)}, u32[]{:S(2)}) collective-permute-start(bf16[704,128]{1,0:T(8,128)(2,1)S(1)} %get-tuple-element.93), channel_id=1, source_target_pairs={{0,511},{1,510},{2,509},{3,508},{4,8},{5,9},{6,10},{7,11},{8,4},{9... | collective-permute-start | bytes 540680 | tf_op jit(solution)/shard_map/ppermute | solution.py:56
  136.2 3.1 %collective-permute-start.12 = (bf16[192,128]{1,0:T(8,128)(2,1)S(1)}, bf16[192,128]{1,0:T(8,128)(2,1)S(1)}, u32[]{:S(2)}, u32[]{:S(2)}) collective-permute-start(bf16[192,128]{1,0:T(8,128)(2,1)S(1)} %get-tuple-element.94), channel_id=1, source_target_pairs={{0,3},{1,2},{2,1},{3,0},{4,7},{5,6},{6,5},{7,4},{8,11},{9,10},{10,... | collective-permute-start | bytes 147464 | tf_op jit(solution)/shard_map/ppermute | solution.py:60
  139.4 2.1 %all_gather.15.sibling = bf16[1408,128]{1,0:T(8,128)(2,1)S(1)} all-gather(bf16[704,128]{1,0:T(8,128)(2,1)S(1)} %get-tuple-element.92), channel_id=1, replica_groups={{0,4},{8,12},{16,20},{24,28},{32,36},{40,44},{48,52},{56,60},{64,68},{7..., dimensions={0}, use_global_device_ids=true | all-gather | bytes 540672 | tf_op jit(solution)/shard_map/all_gather | solution.py:40
  144.0 2.8 %collective-permute-start.13 = (bf16[704,128]{1,0:T(8,128)(2,1)S(1)}, bf16[704,128]{1,0:T(8,128)(2,1)S(1)}, u32[]{:S(2)}, u32[]{:S(2)}) collective-permute-start(bf16[704,128]{1,0:T(8,128)(2,1)S(1)} %shard_map.47), channel_id=1, source_target_pairs={{0,3},{1,2},{2,1},{3,0},{4,7},{5,6},{6,5},{7,4},{8,11},{9,10},{10,... | collective-permute-start | bytes 540680 | tf_op jit(solution)/shard_map/ppermute | solution.py:60
  146.8 2.3 %shard_map.46.kept = f32[704,128]{1,0:T(8,128)S(1)} custom-call(s32[6]{0:T(128)S(1)} %stack.31.flags, f32[704,128]{1,0:T(8,128)S(1)} %get-tuple-element.90.near, f32[704,128]{1,0:T(8,128)S(1)} %get-tuple-element.91.far, bf16[1408,128]{1,0:T(8,128)(2,1)S(1)} %all_gather.15.sibling, bf16[704,128]{1,0:T(8,128)(2,1)S(1)} %collective-permute-done.11.neighbour, ...), custom_call_target="tpu_custom_call" | custom-call | flops 507510784 | bytes 2756608 | tf_op jit(solution)/shard_map/pallas_call | solution.py:78
  149.1 6.1 %collective-permute-done.13.received = bf16[704,128]{1,0:T(8,128)(2,1)S(1)} collective-permute-done((bf16[704,128]{1,0:T(8,128)(2,1)S(1)}, bf16[704,128]{1,0:T(8,128)(2,1)S(1)}, u32[]{:S(2)}, u32[]{:S(2)}) %collective-permute-start.13) | collective-permute-done | bytes 180256 | tf_op jit(solution)/shard_map/ppermute | solution.py:60
  155.2 2.1 %shard_map.48 = f32[686,1,256]{2,1,0:T(1,128)} custom-call(s32[6]{0:T(128)S(1)} %stack.31.flags, f32[704,128]{1,0:T(8,128)S(1)} %shard_map.46.kept, bf16[704,128]{1,0:T(8,128)(2,1)S(1)} %collective-permute-done.13.received), custom_call_target="tpu_custom_call" | custom-call | flops 126877696 | bytes 1243136 | tf_op jit(solution)/shard_map/pallas_call | solution.py:78
  (49 shorter events, 16.2 us)
Async XLA Ops:
  6.5 6.5 %copy-start.5 = (f32[686,1,256]{2,1,0:T(1,128)S(1)}, f32[686,1,256]{2,1,0:T(1,128)}, u32[]{:S(2)}) copy-start(f32[686,1,256]{2,1,0:T(1,128)} %param.3) | copy-start | bytes 2107396
  6.5 73.7 %all-gather.2.cloned.1.call-start = ((), (), s32[]{:S(2)}) async-start(), calls=%async_computation | async-start | bytes 4212736 | tf_op jit(solution)/shard_map/all_gather | solution.py:615
  8.7 4.5 %copy-start.4 = (s32[1,256]{1,0:T(1,128)S(1)}, s32[1,256]{1,0:T(1,128)}, u32[]{:S(2)}) copy-start(s32[1,256]{1,0:T(1,128)} %solid.1) | copy-start | bytes 3076
  9.4 17.1 %collective-permute-start.6 = (bf16[88,1408]{1,0:T(8,128)(2,1)S(1)}, bf16[88,1408]{1,0:T(8,128)(2,1)S(1)}, u32[]{:S(2)}, u32[]{:S(2)}) collective-permute-start(bf16[88,1408]{1,0:T(8,128)(2,1)S(1)} %pad_maximum_fusion), channel_id=1, source_target_pairs={{0,3},{1,2},{2,1},{3,0},{4,7},{5,6},{6,5},{7,4},{8,11},{9,10},{10,... | collective-permute-start | bytes 743432 | tf_op jit(solution)/shard_map/ppermute | solution.py:60
  26.6 0.7 copy-start.6
  27.3 30.6 %collective-permute-start = (bf16[800,128]{1,0:T(8,128)(2,1)S(1)}, bf16[800,128]{1,0:T(8,128)(2,1)S(1)}, u32[]{:S(2)}, u32[]{:S(2)}) collective-permute-start(bf16[800,128]{1,0:T(8,128)(2,1)S(1)} %get-tuple-element.54), channel_id=1, source_target_pairs={{0,3},{1,2},{2,1},{3,0},{4,7},{5,6},{6,5},{7,4},{8,11},{9,10},{10,... | collective-permute-start | bytes 614408 | tf_op jit(solution)/shard_map/ppermute | solution.py:60
  29.2 24.7 %collective-permute-start.2 = (bf16[720,128]{1,0:T(8,128)(2,1)S(1)}, bf16[720,128]{1,0:T(8,128)(2,1)S(1)}, u32[]{:S(2)}, u32[]{:S(2)}) collective-permute-start(bf16[720,128]{1,0:T(8,128)(2,1)S(1)} %get-tuple-element.58), channel_id=1, source_target_pairs={{0,511},{1,510},{2,5},{3,4},{4,3},{5,2},{6,9},{7,8},{8,7},{9,6},{1... | collective-permute-start | bytes 552968 | tf_op jit(solution)/shard_map/ppermute | solution.py:47
  49.1 8.8 %collective-permute-start.1 = (bf16[720,128]{1,0:T(8,128)(2,1)S(1)}, bf16[720,128]{1,0:T(8,128)(2,1)S(1)}, u32[]{:S(2)}, u32[]{:S(2)}) collective-permute-start(bf16[720,128]{1,0:T(8,128)(2,1)S(1)} %get-tuple-element.57), channel_id=1, source_target_pairs={{0,508},{1,509},{2,6},{3,7},{4,0},{5,1},{6,10},{7,11},{8,4},{9,5},... | collective-permute-start | bytes 552968 | tf_op jit(solution)/shard_map/ppermute | solution.py:47
  60.5 15.2 %collective-permute-start.5 = (bf16[352,128]{1,0:T(8,128)(2,1)S(1)}, bf16[352,128]{1,0:T(8,128)(2,1)S(1)}, u32[]{:S(2)}, u32[]{:S(2)}) collective-permute-start(bf16[352,128]{1,0:T(8,128)(2,1)S(1)} %get-tuple-element.64), channel_id=1, source_target_pairs={{0,2},{1,3},{2,0},{3,1},{4,6},{5,7},{6,4},{7,5},{8,10},{9,11},{10,... | collective-permute-start | bytes 270344 | tf_op jit(solution)/shard_map/ppermute | solution.py:64
  62.5 13.3 %collective-permute-start.4 = (bf16[352,128]{1,0:T(8,128)(2,1)S(1)}, bf16[352,128]{1,0:T(8,128)(2,1)S(1)}, u32[]{:S(2)}, u32[]{:S(2)}) collective-permute-start(bf16[352,128]{1,0:T(8,128)(2,1)S(1)} %get-tuple-element.64), channel_id=1, source_target_pairs={{0,3},{1,2},{2,1},{3,0},{4,7},{5,6},{6,5},{7,4},{8,11},{9,10},{10,... | collective-permute-start | bytes 270344 | tf_op jit(solution)/shard_map/ppermute | solution.py:60
  65.6 10.5 %collective-permute-start.3 = (bf16[1408,128]{1,0:T(8,128)(2,1)S(1)}, bf16[1408,128]{1,0:T(8,128)(2,1)S(1)}, u32[]{:S(2)}, u32[]{:S(2)}) collective-permute-start(bf16[1408,128]{1,0:T(8,128)(2,1)S(1)} %get-tuple-element.63.lowered), channel_id=1, source_target_pairs={{0,1},{1,0},{2,3},{3,2},{4,5},{5,4},{6,7},{7,6},{8,9},{9,8},{10,11... | collective-permute-start | bytes 1081352 | tf_op jit(solution)/shard_map/ppermute | solution.py:68
  72.2 3.9 %copy-start = (bf16[704,704]{1,0:T(8,128)(2,1)}, bf16[704,704]{1,0:T(8,128)(2,1)S(1)}, u32[]{:S(2)}) copy-start(bf16[704,704]{1,0:T(8,128)(2,1)S(1)} %fusion.1.m3) | copy-start | bytes 2973700
  73.5 2.5 %copy-start.1 = (bf16[704,704]{1,0:T(8,128)(2,1)}, bf16[704,704]{1,0:T(8,128)(2,1)S(1)}, u32[]{:S(2)}) copy-start(bf16[704,704]{1,0:T(8,128)(2,1)S(1)} %fusion.m1) | copy-start | bytes 2973700
  74.6 1.4 copy-start.2
  79.1 1.1 copy-start.3
  85.9 16.5 %collective-permute-start.7 = (bf16[704,128]{1,0:T(8,128)(2,1)S(1)}, bf16[704,128]{1,0:T(8,128)(2,1)S(1)}, u32[]{:S(2)}, u32[]{:S(2)}) collective-permute-start(bf16[704,128]{1,0:T(8,128)(2,1)S(1)} %get-tuple-element.80), channel_id=1, source_target_pairs={{0,511},{1,510},{2,509},{3,508},{4,8},{5,9},{6,10},{7,11},{8,4},{9... | collective-permute-start | bytes 540680 | tf_op jit(solution)/shard_map/ppermute | solution.py:56
  100.2 14.4 %collective-permute-start.8 = (bf16[704,128]{1,0:T(8,128)(2,1)S(1)}, bf16[704,128]{1,0:T(8,128)(2,1)S(1)}, u32[]{:S(2)}, u32[]{:S(2)}) collective-permute-start(bf16[704,128]{1,0:T(8,128)(2,1)S(1)} %get-tuple-element.84), channel_id=1, source_target_pairs={{0,511},{1,510},{2,509},{3,508},{4,8},{5,9},{6,10},{7,11},{8,4},{9... | collective-permute-start | bytes 540680 | tf_op jit(solution)/shard_map/ppermute | solution.py:56
  104.1 10.5 %collective-permute-start.9 = (bf16[192,128]{1,0:T(8,128)(2,1)S(1)}, bf16[192,128]{1,0:T(8,128)(2,1)S(1)}, u32[]{:S(2)}, u32[]{:S(2)}) collective-permute-start(bf16[192,128]{1,0:T(8,128)(2,1)S(1)} %get-tuple-element.85), channel_id=1, source_target_pairs={{0,3},{1,2},{2,1},{3,0},{4,7},{5,6},{6,5},{7,4},{8,11},{9,10},{10,... | collective-permute-start | bytes 147464 | tf_op jit(solution)/shard_map/ppermute | solution.py:60
  116.8 9.3 %collective-permute-start.10 = (bf16[1408,128]{1,0:T(8,128)(2,1)S(1)}, bf16[1408,128]{1,0:T(8,128)(2,1)S(1)}, u32[]{:S(2)}, u32[]{:S(2)}) collective-permute-start(bf16[1408,128]{1,0:T(8,128)(2,1)S(1)} %shard_map.43.lowered), channel_id=1, source_target_pairs={{0,1},{1,0},{2,3},{3,2},{4,5},{5,4},{6,7},{7,6},{8,9},{9,8},{10,11... | collective-permute-start | bytes 1081352 | tf_op jit(solution)/shard_map/ppermute | solution.py:68
  128.1 14.5 %collective-permute-start.11 = (bf16[704,128]{1,0:T(8,128)(2,1)S(1)}, bf16[704,128]{1,0:T(8,128)(2,1)S(1)}, u32[]{:S(2)}, u32[]{:S(2)}) collective-permute-start(bf16[704,128]{1,0:T(8,128)(2,1)S(1)} %get-tuple-element.93), channel_id=1, source_target_pairs={{0,511},{1,510},{2,509},{3,508},{4,8},{5,9},{6,10},{7,11},{8,4},{9... | collective-permute-start | bytes 540680 | tf_op jit(solution)/shard_map/ppermute | solution.py:56
  136.2 6.4 %collective-permute-start.12 = (bf16[192,128]{1,0:T(8,128)(2,1)S(1)}, bf16[192,128]{1,0:T(8,128)(2,1)S(1)}, u32[]{:S(2)}, u32[]{:S(2)}) collective-permute-start(bf16[192,128]{1,0:T(8,128)(2,1)S(1)} %get-tuple-element.94), channel_id=1, source_target_pairs={{0,3},{1,2},{2,1},{3,0},{4,7},{5,6},{6,5},{7,4},{8,11},{9,10},{10,... | collective-permute-start | bytes 147464 | tf_op jit(solution)/shard_map/ppermute | solution.py:60
  144.0 11.2 %collective-permute-start.13 = (bf16[704,128]{1,0:T(8,128)(2,1)S(1)}, bf16[704,128]{1,0:T(8,128)(2,1)S(1)}, u32[]{:S(2)}, u32[]{:S(2)}) collective-permute-start(bf16[704,128]{1,0:T(8,128)(2,1)S(1)} %shard_map.47), channel_id=1, source_target_pairs={{0,3},{1,2},{2,1},{3,0},{4,7},{5,6},{6,5},{7,4},{8,11},{9,10},{10,... | collective-permute-start | bytes 540680 | tf_op jit(solution)/shard_map/ppermute | solution.py:60
Sparse Core Ops, SparseCore 0:
  27.4 44.1 all-gather.1

commit v14 on v12

--- a/solution.py
+++ b/solution.py
@@ -606,7 +606,7 @@
          ((PAD + 16, LANES), BF16), ((PAD + 16, LANES), BF16), ((8, LANES), F32), ((3, *rows), F32)],
         flags, padded, solid_mask, flops=2 * 3 * PAD * PAD * 256,
     )
-    piece, _ = lax.optimization_barrier((piece, message))
+    piece, straight, turned = lax.optimization_barrier((piece, straight, turned))
     groups = [
         [x * 32 + y * 16 + 4 * pair + 2 * odd + side for side in range(2) for odd in range(2) for x in range(4)]
         for y in range(2)

time: 161 us -> 162 us (level)
    ppermute x1, starting transfers between devices: 1.92 us -> 4.11 us  [to_opposite(): return lax.ppermute(array, 'vel', [(i, i ^ 2) for i in range(4)])]
    ppermute x6, starting transfers between devices: 20.8 us -> 19.1 us  [to_mirror(): return lax.ppermute(array, 'vel', [(i, 3 - i) for i in range(4)])]
    ppermute x1, waiting for transfers between devices: 0.82 us -> 2.48 us  [to_opposite(): return lax.ppermute(array, 'vel', [(i, i ^ 2) for i in range(4)])]
  transfers between devices with their start and end apart: 15 -> 15, of which waited for: 8 -> 7; matrix products, arithmetic and copies ran while one was open for 7% -> 7% of each run, Pallas kernels for 11% -> 11%
where the time goes in v14:
time: 162 us; the launch traced here: 161 us
  starting transfers between devices  66.9 us (41%)
  Pallas kernels  31.1 us (19%)
  waiting for transfers between devices  27.9 us (17%)
  between operations  13.9 us (9%)
  matrix products  13 us (8%)
  blocking collectives  6.41 us (4%)
  local copies, waits for them, and re-layouts  2.05 us (1%)
    pallas_call x12, Pallas kernels, call(): pl.pallas_call(kernel, out_shape=[(pltpu.HBM if leave else jax.ShapeDtype...  31.1 us
    ppermute x3, starting transfers between devices, to_neighbour(): return lax.ppermute(array, BOTH, pairs_of(neighbour_of))  20.7 us
    ppermute x2, starting transfers between devices, to_layer(): return lax.ppermute(array, BOTH, pairs_of(target))  19.1 us
    ppermute x6, starting transfers between devices, to_mirror(): return lax.ppermute(array, 'vel', [(i, 3 - i) for i in range(4)])  19.1 us
    ppermute x6, waiting for transfers between devices, to_mirror(): return lax.ppermute(array, 'vel', [(i, 3 - i) for i in range(4)])  19 us
    dot_general x8, matrix products, chosen(): return jnp.dot(left, right, preferred_element_type=BF16)  13 us
    all_gather x3, blocking collectives, with_sibling(): lax.all_gather(array, 'cells', axis=0, tiled=True, axis_index_groups=groups)  6.41 us
    ppermute x2, waiting for transfers between devices, to_side(): return lax.ppermute(array, 'vel', [(i, i ^ 1) for i in range(4)])  4.4 us
  transfers between devices with their start and end apart: 15, of which 7 were waited for; matrix products, arithmetic and copies ran while one was open for 7% of the time, Pallas kernels for 11%

profile of v14, /device:TPU:8, one launch (start us, length us, event | category | flops | bytes accessed | tf_op | source)
XLA Modules:
  0.0 161.3 jit_solution(6161831955599193694)
XLA Ops:
  9.4 3.5 %collective-permute-start.1 = (bf16[88,1408]{1,0:T(8,128)(2,1)S(1)}, bf16[88,1408]{1,0:T(8,128)(2,1)S(1)}, u32[]{:S(2)}, u32[]{:S(2)}) collective-permute-start(bf16[88,1408]{1,0:T(8,128)(2,1)S(1)} %pad_maximum_fusion), channel_id=1, source_target_pairs={{0,3},{1,2},{2,1},{3,0},{4,7},{5,6},{6,5},{7,4},{8,11},{9,10},{10,... | collective-permute-start | bytes 743432 | tf_op jit(solution)/shard_map/ppermute | solution.py:60
  13.2 2.4 %shard_map.37 = (f32[704,128]{1,0:T(8,128)S(1)}, f32[88,128]{1,0:T(8,128)S(1)}, bf16[800,128]{1,0:T(8,128)(2,1)S(1)}, bf16[720,128]{1,0:T(8,128)(2,1)}, bf16[720...) custom-call(s32[6]{0:T(128)S(1)} %stack.31.flags, f32[704,256]{1,0:T(8,128)S(1)} %pad.13.populations, ...), custom_call_target="tpu_custom_call" | custom-call | flops 761266176 | bytes 2786304 | tf_op jit(solution)/shard_map/pallas_call | solution.py:78
  16.4 10.2 %collective-permute-done.1 = bf16[88,1408]{1,0:T(8,128)(2,1)S(1)} collective-permute-done((bf16[88,1408]{1,0:T(8,128)(2,1)S(1)}, bf16[88,1408]{1,0:T(8,128)(2,1)S(1)}, u32[]{:S(2)}, u32[]{:S(2)}) %collective-permute-start.1) | collective-permute-done | bytes 247840 | tf_op jit(solution)/shard_map/ppermute | solution.py:60
  27.3 1.9 %collective-permute-start = (bf16[800,128]{1,0:T(8,128)(2,1)S(1)}, bf16[800,128]{1,0:T(8,128)(2,1)S(1)}, u32[]{:S(2)}, u32[]{:S(2)}) collective-permute-start(bf16[800,128]{1,0:T(8,128)(2,1)S(1)} %get-tuple-element.58), channel_id=1, source_target_pairs={{0,3},{1,2},{2,1},{3,0},{4,7},{5,6},{6,5},{7,4},{8,11},{9,10},{10,... | collective-permute-start | bytes 614408 | tf_op jit(solution)/shard_map/ppermute | solution.py:60
  29.2 5.4 %fusion.6 = bf16[704,2744]{1,0:T(8,128)(2,1)S(1)} fusion(bf16[686,2744]{1,0:T(8,128)(2,1)} %param.5, s32[704]{0:T(1024)S(1)} %select_select_fusion), kind=kOutput, calls=%fused_computation.13 | convolution fusion | flops 2650879488 | bytes 7631136 | tf_op jit(solution)/shard_map/dot_general | solution.py:560
  35.0 14.1 %collective-permute-start.3 = (bf16[720,128]{1,0:T(8,128)(2,1)}, bf16[720,128]{1,0:T(8,128)(2,1)S(1)}, u32[]{:S(2)}, u32[]{:S(2)}) collective-permute-start(bf16[720,128]{1,0:T(8,128)(2,1)} %get-tuple-element.65), channel_id=1, source_target_pairs={{0,511},{1,510},{2,5},{3,4},{4,3},{5,2},{6,9},{7,8},{8,7},{9,6},{1... | collective-permute-start | bytes 552968 | tf_op jit(solution)/shard_map/ppermute | solution.py:47
  49.1 5.0 %collective-permute-start.2 = (bf16[720,128]{1,0:T(8,128)(2,1)}, bf16[720,128]{1,0:T(8,128)(2,1)S(1)}, u32[]{:S(2)}, u32[]{:S(2)}) collective-permute-start(bf16[720,128]{1,0:T(8,128)(2,1)} %get-tuple-element.64), channel_id=1, source_target_pairs={{0,508},{1,509},{2,6},{3,7},{4,0},{5,1},{6,10},{7,11},{8,4},{9,5},... | collective-permute-start | bytes 552968 | tf_op jit(solution)/shard_map/ppermute | solution.py:47
  59.2 2.6 %shard_map.38 = (bf16[1408,128]{1,0:T(8,128)(2,1)S(1)}, f32[8,128]{1,0:T(8,128)S(1)}, bf16[352,128]{1,0:T(8,128)(2,1)S(1)}) custom-call(s32[6]{0:T(128)S(1)} %stack.31.flags, f32[704,128]{1,0:T(8,128)S(1)} %copy-done.5, f32[88,128]{1,0:T(8,128)S(1)} %get-tuple-element.57.own_edge, bf16[800,128]{1,0:T(8,128)(2,1)S(1)} %collective-permute-done.received, ...), custom_call_target="tpu_custom_call" | custom-call | flops 18022400 | bytes 2519040 | tf_op jit(solution)/shard_map/pallas_call | solution.py:78
  61.8 1.9 %collective-permute-start.4 = (bf16[1408,128]{1,0:T(8,128)(2,1)S(1)}, bf16[1408,128]{1,0:T(8,128)(2,1)S(1)}, u32[]{:S(2)}, u32[]{:S(2)}) collective-permute-start(bf16[1408,128]{1,0:T(8,128)(2,1)S(1)} %get-tuple-element.69.lowered), channel_id=1, source_target_pairs={{0,1},{1,0},{2,3},{3,2},{4,5},{5,4},{6,7},{7,6},{8,9},{9,8},{10,11... | collective-permute-start | bytes 1081352 | tf_op jit(solution)/shard_map/ppermute | solution.py:68
  63.7 4.1 %collective-permute-start.6 = (bf16[352,128]{1,0:T(8,128)(2,1)S(1)}, bf16[352,128]{1,0:T(8,128)(2,1)S(1)}, u32[]{:S(2)}, u32[]{:S(2)}) collective-permute-start(bf16[352,128]{1,0:T(8,128)(2,1)S(1)} %get-tuple-element.70), channel_id=1, source_target_pairs={{0,2},{1,3},{2,0},{3,1},{4,6},{5,7},{6,4},{7,5},{8,10},{9,11},{10,... | collective-permute-start | bytes 270344 | tf_op jit(solution)/shard_map/ppermute | solution.py:64
  67.8 3.2 %collective-permute-start.5 = (bf16[352,128]{1,0:T(8,128)(2,1)S(1)}, bf16[352,128]{1,0:T(8,128)(2,1)S(1)}, u32[]{:S(2)}, u32[]{:S(2)}) collective-permute-start(bf16[352,128]{1,0:T(8,128)(2,1)S(1)} %get-tuple-element.70), channel_id=1, source_target_pairs={{0,3},{1,2},{2,1},{3,0},{4,7},{5,6},{6,5},{7,4},{8,11},{9,10},{10,... | collective-permute-start | bytes 270344 | tf_op jit(solution)/shard_map/ppermute | solution.py:60
  71.0 2.5 %collective-permute-done.6.other_bands = bf16[352,128]{1,0:T(8,128)(2,1)S(1)} collective-permute-done((bf16[352,128]{1,0:T(8,128)(2,1)S(1)}, bf16[352,128]{1,0:T(8,128)(2,1)S(1)}, u32[]{:S(2)}, u32[]{:S(2)}) %collective-permute-start.6) | collective-permute-done | bytes 90144 | tf_op jit(solution)/shard_map/ppermute | solution.py:64
  75.5 3.1 %shard_map.39 = (f32[704,128]{1,0:T(8,128)}, bf16[96,128]{1,0:T(8,128)(2,1)}, bf16[2816,128]{1,0:T(8,128)(2,1)}, bf16[704,128]{1,0:T(8,128)(2,1)}) custom-call(s32[6]{0:T(128)S(1)} %stack.31.flags, bf16[1408,128]{1,0:T(8,128)(2,1)S(1)} %get-tuple-element.69.lowered, bf16[1408,128]{1,0:T(8,128)(2,1)S(1)} %collective-permute-done.4.other, ...), custom_call_target="tpu_custom_call" | custom-call | flops 1015021568 | bytes 7233536 | tf_op jit(solution)/shard_map/pallas_call | solution.py:78
  78.6 5.7 %shard_map.40 = (f32[704,128]{1,0:T(8,128)S(1)}, f32[704,128]{1,0:T(8,128)S(1)}, bf16[704,128]{1,0:T(8,128)(2,1)S(1)}, bf16[704,128]{1,0:T(8,128)(2,1)S(1)}, bf16[192,128]{1,0:T(8,128)(2,1)S(1)}) custom-call(s32[6]{0:T(128)S(1)} %stack.31.flags, f32[3,704,128]{2,1,0:T(8,128)S(1)} %get-tuple-element.55.factors, bf16[96,128]{1,0:T(8,128)(2,1)} %get-tuple-element.75.own_packed, ...), custom_call_target="tpu_custom_call" | custom-call | flops 1015021568 | bytes 7462912 | tf_op jit(solution)/shard_map/pallas_call | solution.py:78
  84.3 8.7 %collective-permute-start.7 = (bf16[704,128]{1,0:T(8,128)(2,1)S(1)}, bf16[704,128]{1,0:T(8,128)(2,1)S(1)}, u32[]{:S(2)}, u32[]{:S(2)}) collective-permute-start(bf16[704,128]{1,0:T(8,128)(2,1)S(1)} %get-tuple-element.88), channel_id=1, source_target_pairs={{0,511},{1,510},{2,509},{3,508},{4,8},{5,9},{6,10},{7,11},{8,4},{9... | collective-permute-start | bytes 540680 | tf_op jit(solution)/shard_map/ppermute | solution.py:56
  92.9 2.1 %all_gather.13.sibling = bf16[1408,128]{1,0:T(8,128)(2,1)S(1)} all-gather(bf16[704,128]{1,0:T(8,128)(2,1)S(1)} %get-tuple-element.84), channel_id=1, replica_groups={{0,4},{8,12},{16,20},{24,28},{32,36},{40,44},{48,52},{56,60},{64,68},{7..., dimensions={0}, use_global_device_ids=true | all-gather | bytes 540672 | tf_op jit(solution)/shard_map/all_gather | solution.py:40
  96.7 4.1 %collective-permute-start.8 = (bf16[704,128]{1,0:T(8,128)(2,1)S(1)}, bf16[704,128]{1,0:T(8,128)(2,1)S(1)}, u32[]{:S(2)}, u32[]{:S(2)}) collective-permute-start(bf16[704,128]{1,0:T(8,128)(2,1)S(1)} %get-tuple-element.92), channel_id=1, source_target_pairs={{0,511},{1,510},{2,509},{3,508},{4,8},{5,9},{6,10},{7,11},{8,4},{9... | collective-permute-start | bytes 540680 | tf_op jit(solution)/shard_map/ppermute | solution.py:56
  102.5 3.9 %collective-permute-start.9 = (bf16[192,128]{1,0:T(8,128)(2,1)S(1)}, bf16[192,128]{1,0:T(8,128)(2,1)S(1)}, u32[]{:S(2)}, u32[]{:S(2)}) collective-permute-start(bf16[192,128]{1,0:T(8,128)(2,1)S(1)} %get-tuple-element.93), channel_id=1, source_target_pairs={{0,3},{1,2},{2,1},{3,0},{4,7},{5,6},{6,5},{7,4},{8,11},{9,10},{10,... | collective-permute-start | bytes 147464 | tf_op jit(solution)/shard_map/ppermute | solution.py:60
  106.4 2.3 %all_gather.14.sibling = bf16[1408,128]{1,0:T(8,128)(2,1)S(1)} all-gather(bf16[704,128]{1,0:T(8,128)(2,1)S(1)} %get-tuple-element.91), channel_id=1, replica_groups={{0,4},{8,12},{16,20},{24,28},{32,36},{40,44},{48,52},{56,60},{64,68},{7..., dimensions={0}, use_global_device_ids=true | all-gather | bytes 540672 | tf_op jit(solution)/shard_map/all_gather | solution.py:40
  108.7 2.0 %collective-permute-done.8.neighbour = bf16[704,128]{1,0:T(8,128)(2,1)S(1)} collective-permute-done((bf16[704,128]{1,0:T(8,128)(2,1)S(1)}, bf16[704,128]{1,0:T(8,128)(2,1)S(1)}, u32[]{:S(2)}, u32[]{:S(2)}) %collective-permute-start.8) | collective-permute-done | bytes 180256 | tf_op jit(solution)/shard_map/ppermute | solution.py:56
  110.7 2.2 %shard_map.43.lowered = bf16[1408,128]{1,0:T(8,128)(2,1)S(1)} custom-call(s32[6]{0:T(128)S(1)} %stack.31.flags, f32[704,128]{1,0:T(8,128)S(1)} %get-tuple-element.87.near, f32[704,128]{1,0:T(8,128)S(1)} %get-tuple-element.90.far, bf16[1408,128]{1,0:T(8,128)(2,1)S(1)} %all_gather.14.sibling, bf16[704,128]{1,0:T(8,128)(2,1)S(1)} %collective-permute-done.8.neighbour, ...), custom_call_target="tpu_custom_call" | custom-call | flops 9011200 | bytes 2756608 | tf_op jit(solution)/shard_map/pallas_call | solution.py:78
  112.9 1.9 %collective-permute-start.10 = (bf16[1408,128]{1,0:T(8,128)(2,1)S(1)}, bf16[1408,128]{1,0:T(8,128)(2,1)S(1)}, u32[]{:S(2)}, u32[]{:S(2)}) collective-permute-start(bf16[1408,128]{1,0:T(8,128)(2,1)S(1)} %shard_map.43.lowered), channel_id=1, source_target_pairs={{0,1},{1,0},{2,3},{3,2},{4,5},{5,4},{6,7},{7,6},{8,9},{9,8},{10,11... | collective-permute-start | bytes 1081352 | tf_op jit(solution)/shard_map/ppermute | solution.py:68
  114.8 4.0 %shard_map.44 = (f32[704,128]{1,0:T(8,128)S(1)}, f32[704,128]{1,0:T(8,128)S(1)}, bf16[2,704,704]{2,1,0:T(8,128)(2,1)S(1)}, bf16[704,1408]{1,0:T(8,128)(2,1)S(1)}) custom-call(s32[6]{0:T(128)S(1)} %stack.31.flags, bf16[1408,128]{1,0:T(8,128)(2,1)S(1)} %shard_map.43.lowered, bf16[704,704]{1,0:T(8,128)(2,1)} %copy-done.3, bf16[704,704]{1,0:T(8,128)(2,1)} %copy-done.2, ...), custom_call_target="tpu_custom_call" | custom-call | flops 507510784 | bytes 12976128 | tf_op jit(solution)/shard_map/pallas_call | solution.py:78
  118.9 4.4 %collective-permute-done.10.other = bf16[1408,128]{1,0:T(8,128)(2,1)S(1)} collective-permute-done((bf16[1408,128]{1,0:T(8,128)(2,1)S(1)}, bf16[1408,128]{1,0:T(8,128)(2,1)S(1)}, u32[]{:S(2)}, u32[]{:S(2)}) %collective-permute-start.10) | collective-permute-done | bytes 360480 | tf_op jit(solution)/shard_map/ppermute | solution.py:68
  123.3 2.0 %shard_map.45 = (f32[704,128]{1,0:T(8,128)S(1)}, f32[704,128]{1,0:T(8,128)S(1)}, bf16[704,128]{1,0:T(8,128)(2,1)S(1)}, bf16[704,128]{1,0:T(8,128)(2,1)S(1)}, bf16[192,128]{1,0:T(8,128)(2,1)S(1)}) custom-call(s32[6]{0:T(128)S(1)} %stack.31.flags, bf16[1408,128]{1,0:T(8,128)(2,1)S(1)} %collective-permute-done.10.other, f32[704,128]{1,0:T(8,128)S(1)} %get-tuple-element.94.own, ...), custom_call_target="tpu_custom_call" | custom-call | flops 507510784 | bytes 7258112 | tf_op jit(solution)/shard_map/pallas_call | solution.py:78
  125.2 8.0 %collective-permute-start.11 = (bf16[704,128]{1,0:T(8,128)(2,1)S(1)}, bf16[704,128]{1,0:T(8,128)(2,1)S(1)}, u32[]{:S(2)}, u32[]{:S(2)}) collective-permute-start(bf16[704,128]{1,0:T(8,128)(2,1)S(1)} %get-tuple-element.101), channel_id=1, source_target_pairs={{0,511},{1,510},{2,509},{3,508},{4,8},{5,9},{6,10},{7,11},{8,4},{9... | collective-permute-start | bytes 540680 | tf_op jit(solution)/shard_map/ppermute | solution.py:56
  133.2 3.4 %collective-permute-start.12 = (bf16[192,128]{1,0:T(8,128)(2,1)S(1)}, bf16[192,128]{1,0:T(8,128)(2,1)S(1)}, u32[]{:S(2)}, u32[]{:S(2)}) collective-permute-start(bf16[192,128]{1,0:T(8,128)(2,1)S(1)} %get-tuple-element.102), channel_id=1, source_target_pairs={{0,3},{1,2},{2,1},{3,0},{4,7},{5,6},{6,5},{7,4},{8,11},{9,10},{10,... | collective-permute-start | bytes 147464 | tf_op jit(solution)/shard_map/ppermute | solution.py:60
  136.6 2.1 %all_gather.15.sibling = bf16[1408,128]{1,0:T(8,128)(2,1)S(1)} all-gather(bf16[704,128]{1,0:T(8,128)(2,1)S(1)} %get-tuple-element.100), channel_id=1, replica_groups={{0,4},{8,12},{16,20},{24,28},{32,36},{40,44},{48,52},{56,60},{64,68},{7..., dimensions={0}, use_global_device_ids=true | all-gather | bytes 540672 | tf_op jit(solution)/shard_map/all_gather | solution.py:40
  141.1 3.2 %collective-permute-start.13 = (bf16[704,128]{1,0:T(8,128)(2,1)S(1)}, bf16[704,128]{1,0:T(8,128)(2,1)S(1)}, u32[]{:S(2)}, u32[]{:S(2)}) collective-permute-start(bf16[704,128]{1,0:T(8,128)(2,1)S(1)} %shard_map.47), channel_id=1, source_target_pairs={{0,3},{1,2},{2,1},{3,0},{4,7},{5,6},{6,5},{7,4},{8,11},{9,10},{10,... | collective-permute-start | bytes 540680 | tf_op jit(solution)/shard_map/ppermute | solution.py:60
  144.3 2.3 %shard_map.46.kept = f32[704,128]{1,0:T(8,128)S(1)} custom-call(s32[6]{0:T(128)S(1)} %stack.31.flags, f32[704,128]{1,0:T(8,128)S(1)} %get-tuple-element.98.near, f32[704,128]{1,0:T(8,128)S(1)} %get-tuple-element.99.far, bf16[1408,128]{1,0:T(8,128)(2,1)S(1)} %all_gather.15.sibling, bf16[704,128]{1,0:T(8,128)(2,1)S(1)} %collective-permute-done.11.neighbour, ...), custom_call_target="tpu_custom_call" | custom-call | flops 507510784 | bytes 2756608 | tf_op jit(solution)/shard_map/pallas_call | solution.py:78
  146.6 5.8 %collective-permute-done.13.received = bf16[704,128]{1,0:T(8,128)(2,1)S(1)} collective-permute-done((bf16[704,128]{1,0:T(8,128)(2,1)S(1)}, bf16[704,128]{1,0:T(8,128)(2,1)S(1)}, u32[]{:S(2)}, u32[]{:S(2)}) %collective-permute-start.13) | collective-permute-done | bytes 180256 | tf_op jit(solution)/shard_map/ppermute | solution.py:60
  152.4 2.1 %shard_map.48 = f32[686,1,256]{2,1,0:T(1,128)} custom-call(s32[6]{0:T(128)S(1)} %stack.31.flags, f32[704,128]{1,0:T(8,128)S(1)} %shard_map.46.kept, bf16[704,128]{1,0:T(8,128)(2,1)S(1)} %collective-permute-done.13.received), custom_call_target="tpu_custom_call" | custom-call | flops 126877696 | bytes 1243136 | tf_op jit(solution)/shard_map/pallas_call | solution.py:78
  (53 shorter events, 17.4 us)
Async XLA Ops:
  6.5 6.5 %copy-start.7 = (f32[686,1,256]{2,1,0:T(1,128)S(1)}, f32[686,1,256]{2,1,0:T(1,128)}, u32[]{:S(2)}) copy-start(f32[686,1,256]{2,1,0:T(1,128)} %param.3) | copy-start | bytes 2107396
  6.5 72.0 %all-gather.2.cloned.1.call-start = ((), (), s32[]{:S(2)}) async-start(), calls=%async_computation | async-start | bytes 4212736 | tf_op jit(solution)/shard_map/all_gather | solution.py:615
  8.7 4.5 %copy-start.6 = (s32[1,256]{1,0:T(1,128)S(1)}, s32[1,256]{1,0:T(1,128)}, u32[]{:S(2)}) copy-start(s32[1,256]{1,0:T(1,128)} %solid.1) | copy-start | bytes 3076
  9.4 17.1 %collective-permute-start.1 = (bf16[88,1408]{1,0:T(8,128)(2,1)S(1)}, bf16[88,1408]{1,0:T(8,128)(2,1)S(1)}, u32[]{:S(2)}, u32[]{:S(2)}) collective-permute-start(bf16[88,1408]{1,0:T(8,128)(2,1)S(1)} %pad_maximum_fusion), channel_id=1, source_target_pairs={{0,3},{1,2},{2,1},{3,0},{4,7},{5,6},{6,5},{7,4},{8,11},{9,10},{10,... | collective-permute-start | bytes 743432 | tf_op jit(solution)/shard_map/ppermute | solution.py:60
  15.7 0.7 copy-start.4
  26.6 0.7 copy-start.8
  27.3 31.8 %collective-permute-start = (bf16[800,128]{1,0:T(8,128)(2,1)S(1)}, bf16[800,128]{1,0:T(8,128)(2,1)S(1)}, u32[]{:S(2)}, u32[]{:S(2)}) collective-permute-start(bf16[800,128]{1,0:T(8,128)(2,1)S(1)} %get-tuple-element.58), channel_id=1, source_target_pairs={{0,3},{1,2},{2,1},{3,0},{4,7},{5,6},{6,5},{7,4},{8,11},{9,10},{10,... | collective-permute-start | bytes 614408 | tf_op jit(solution)/shard_map/ppermute | solution.py:60
  35.0 24.1 %collective-permute-start.3 = (bf16[720,128]{1,0:T(8,128)(2,1)}, bf16[720,128]{1,0:T(8,128)(2,1)S(1)}, u32[]{:S(2)}, u32[]{:S(2)}) collective-permute-start(bf16[720,128]{1,0:T(8,128)(2,1)} %get-tuple-element.65), channel_id=1, source_target_pairs={{0,511},{1,510},{2,5},{3,4},{4,3},{5,2},{6,9},{7,8},{8,7},{9,6},{1... | collective-permute-start | bytes 552968 | tf_op jit(solution)/shard_map/ppermute | solution.py:47
  49.1 9.9 %collective-permute-start.2 = (bf16[720,128]{1,0:T(8,128)(2,1)}, bf16[720,128]{1,0:T(8,128)(2,1)S(1)}, u32[]{:S(2)}, u32[]{:S(2)}) collective-permute-start(bf16[720,128]{1,0:T(8,128)(2,1)} %get-tuple-element.64), channel_id=1, source_target_pairs={{0,508},{1,509},{2,6},{3,7},{4,0},{5,1},{6,10},{7,11},{8,4},{9,5},... | collective-permute-start | bytes 552968 | tf_op jit(solution)/shard_map/ppermute | solution.py:47
  55.2 20.2 %copy-start = (bf16[704,704]{1,0:T(8,128)(2,1)}, bf16[704,704]{1,0:T(8,128)(2,1)S(1)}, u32[]{:S(2)}) copy-start(bf16[704,704]{1,0:T(8,128)(2,1)S(1)} %fusion.4.m2) | copy-start | bytes 2973700
  56.6 18.9 %copy-start.1 = (bf16[704,704]{1,0:T(8,128)(2,1)}, bf16[704,704]{1,0:T(8,128)(2,1)S(1)}, u32[]{:S(2)}) copy-start(bf16[704,704]{1,0:T(8,128)(2,1)S(1)} %fusion.1.m3) | copy-start | bytes 2973700
  57.9 17.5 %copy-start.2 = (bf16[704,704]{1,0:T(8,128)(2,1)}, bf16[704,704]{1,0:T(8,128)(2,1)S(1)}, u32[]{:S(2)}) copy-start(bf16[704,704]{1,0:T(8,128)(2,1)S(1)} %fusion.m1) | copy-start | bytes 2973700
  57.9 1.2 copy-start.5
  59.0 16.4 %copy-start.3 = (bf16[704,704]{1,0:T(8,128)(2,1)}, bf16[704,704]{1,0:T(8,128)(2,1)S(1)}, u32[]{:S(2)}) copy-start(bf16[704,704]{1,0:T(8,128)(2,1)S(1)} %fusion.3.m0) | copy-start | bytes 2973700
  61.8 13.6 %collective-permute-start.4 = (bf16[1408,128]{1,0:T(8,128)(2,1)S(1)}, bf16[1408,128]{1,0:T(8,128)(2,1)S(1)}, u32[]{:S(2)}, u32[]{:S(2)}) collective-permute-start(bf16[1408,128]{1,0:T(8,128)(2,1)S(1)} %get-tuple-element.69.lowered), channel_id=1, source_target_pairs={{0,1},{1,0},{2,3},{3,2},{4,5},{5,4},{6,7},{7,6},{8,9},{9,8},{10,11... | collective-permute-start | bytes 1081352 | tf_op jit(solution)/shard_map/ppermute | solution.py:68
  63.7 9.8 %collective-permute-start.6 = (bf16[352,128]{1,0:T(8,128)(2,1)S(1)}, bf16[352,128]{1,0:T(8,128)(2,1)S(1)}, u32[]{:S(2)}, u32[]{:S(2)}) collective-permute-start(bf16[352,128]{1,0:T(8,128)(2,1)S(1)} %get-tuple-element.70), channel_id=1, source_target_pairs={{0,2},{1,3},{2,0},{3,1},{4,6},{5,7},{6,4},{7,5},{8,10},{9,11},{10,... | collective-permute-start | bytes 270344 | tf_op jit(solution)/shard_map/ppermute | solution.py:64
  67.8 7.6 %collective-permute-start.5 = (bf16[352,128]{1,0:T(8,128)(2,1)S(1)}, bf16[352,128]{1,0:T(8,128)(2,1)S(1)}, u32[]{:S(2)}, u32[]{:S(2)}) collective-permute-start(bf16[352,128]{1,0:T(8,128)(2,1)S(1)} %get-tuple-element.70), channel_id=1, source_target_pairs={{0,3},{1,2},{2,1},{3,0},{4,7},{5,6},{6,5},{7,4},{8,11},{9,10},{10,... | collective-permute-start | bytes 270344 | tf_op jit(solution)/shard_map/ppermute | solution.py:60
  84.3 16.5 %collective-permute-start.7 = (bf16[704,128]{1,0:T(8,128)(2,1)S(1)}, bf16[704,128]{1,0:T(8,128)(2,1)S(1)}, u32[]{:S(2)}, u32[]{:S(2)}) collective-permute-start(bf16[704,128]{1,0:T(8,128)(2,1)S(1)} %get-tuple-element.88), channel_id=1, source_target_pairs={{0,511},{1,510},{2,509},{3,508},{4,8},{5,9},{6,10},{7,11},{8,4},{9... | collective-permute-start | bytes 540680 | tf_op jit(solution)/shard_map/ppermute | solution.py:56
  96.7 14.0 %collective-permute-start.8 = (bf16[704,128]{1,0:T(8,128)(2,1)S(1)}, bf16[704,128]{1,0:T(8,128)(2,1)S(1)}, u32[]{:S(2)}, u32[]{:S(2)}) collective-permute-start(bf16[704,128]{1,0:T(8,128)(2,1)S(1)} %get-tuple-element.92), channel_id=1, source_target_pairs={{0,511},{1,510},{2,509},{3,508},{4,8},{5,9},{6,10},{7,11},{8,4},{9... | collective-permute-start | bytes 540680 | tf_op jit(solution)/shard_map/ppermute | solution.py:56
  102.5 8.2 %collective-permute-start.9 = (bf16[192,128]{1,0:T(8,128)(2,1)S(1)}, bf16[192,128]{1,0:T(8,128)(2,1)S(1)}, u32[]{:S(2)}, u32[]{:S(2)}) collective-permute-start(bf16[192,128]{1,0:T(8,128)(2,1)S(1)} %get-tuple-element.93), channel_id=1, source_target_pairs={{0,3},{1,2},{2,1},{3,0},{4,7},{5,6},{6,5},{7,4},{8,11},{9,10},{10,... | collective-permute-start | bytes 147464 | tf_op jit(solution)/shard_map/ppermute | solution.py:60
  112.9 10.4 %collective-permute-start.10 = (bf16[1408,128]{1,0:T(8,128)(2,1)S(1)}, bf16[1408,128]{1,0:T(8,128)(2,1)S(1)}, u32[]{:S(2)}, u32[]{:S(2)}) collective-permute-start(bf16[1408,128]{1,0:T(8,128)(2,1)S(1)} %shard_map.43.lowered), channel_id=1, source_target_pairs={{0,1},{1,0},{2,3},{3,2},{4,5},{5,4},{6,7},{7,6},{8,9},{9,8},{10,11... | collective-permute-start | bytes 1081352 | tf_op jit(solution)/shard_map/ppermute | solution.py:68
  125.2 14.5 %collective-permute-start.11 = (bf16[704,128]{1,0:T(8,128)(2,1)S(1)}, bf16[704,128]{1,0:T(8,128)(2,1)S(1)}, u32[]{:S(2)}, u32[]{:S(2)}) collective-permute-start(bf16[704,128]{1,0:T(8,128)(2,1)S(1)} %get-tuple-element.101), channel_id=1, source_target_pairs={{0,511},{1,510},{2,509},{3,508},{4,8},{5,9},{6,10},{7,11},{8,4},{9... | collective-permute-start | bytes 540680 | tf_op jit(solution)/shard_map/ppermute | solution.py:56
  133.2 6.5 %collective-permute-start.12 = (bf16[192,128]{1,0:T(8,128)(2,1)S(1)}, bf16[192,128]{1,0:T(8,128)(2,1)S(1)}, u32[]{:S(2)}, u32[]{:S(2)}) collective-permute-start(bf16[192,128]{1,0:T(8,128)(2,1)S(1)} %get-tuple-element.102), channel_id=1, source_target_pairs={{0,3},{1,2},{2,1},{3,0},{4,7},{5,6},{6,5},{7,4},{8,11},{9,10},{10,... | collective-permute-start | bytes 147464 | tf_op jit(solution)/shard_map/ppermute | solution.py:60
  141.1 11.3 %collective-permute-start.13 = (bf16[704,128]{1,0:T(8,128)(2,1)S(1)}, bf16[704,128]{1,0:T(8,128)(2,1)S(1)}, u32[]{:S(2)}, u32[]{:S(2)}) collective-permute-start(bf16[704,128]{1,0:T(8,128)(2,1)S(1)} %shard_map.47), channel_id=1, source_target_pairs={{0,3},{1,2},{2,1},{3,0},{4,7},{5,6},{6,5},{7,4},{8,11},{9,10},{10,... | collective-permute-start | bytes 540680 | tf_op jit(solution)/shard_map/ppermute | solution.py:60
Sparse Core Ops, SparseCore 0:
  27.4 45.0 all-gather.1
